TPU v7x, 32 devices: a whole 2x2x4 slice. The times are simulated.
32 devices in a mesh: blk: 4 (over y, x), grp: 8 (over z, core).
Axes of the slice: x: 2, y: 2, z: 4, core: 2. Of those that a mesh axis runs over, the one named last changes fastest.
Arguments:
- amplitudes: bfloat16 [4, 512, 1024], P(None, 'blk'), may hold values from -6 to 6
- pair_screen: int32 [4, 32], P(None, 'blk'), may hold values 0 or 1
- integrals: bfloat16 [32, 1024, 1024], P(('blk', 'grp')), may hold values from -0.1875 to 0.1875
- tile_ab: int32 [4, 8], replicated, may hold values from 0 to 49, as said below
- tile_cd: int32 [4, 8], replicated, may hold values from 0 to 3
- residual_in: float32 [512, 50, 1024], P(('blk', 'grp')), may hold values from -6 to 6
Outputs:
- residual: float32 [512, 50, 1024], P(('blk', 'grp'))
Inputs may be any that keep to these rules, and one draw needn't show every extreme that they name: `tile_ab`: the 4 integral tiles that share a column g name 2 to 4 distinct b tiles, and in every draw some column names exactly 4.
All inputs are finite; a program needn't handle non-finite values. No bound on the sum of `pair_screen` on one device may be relied on, other than what follows from the above.
Results may differ from a plain program's by a relative error of at most 0.0003.
Values may be sent and summed in bfloat16 or wider, within the bound.
No kernel may reach another device: no remote copies, remote signals or barrier semaphores. Data moves between devices by JAX's collectives and lax.ppermute only.
A program may use at most 128 MiB of HBM per device.

v0:
```python
import jax
import jax.numpy as jnp
from jax import lax
from jax.sharding import PartitionSpec as P


def contract(masked, panel, cd_index):
    rows_in = lax.dynamic_index_in_dim(masked, cd_index, 0, keepdims=False)
    return jnp.dot(rows_in, panel, preferred_element_type=jnp.float32)


def shards(amplitudes, pair_screen, integrals, tile_ab, tile_cd, residual_in):
    blk_count = lax.axis_size("blk")
    grp_count = lax.axis_size("grp")
    grp_position = lax.axis_index("grp")
    owner_rows, ab_tiles, tile_width = residual_in.shape
    group_rows = amplitudes.shape[1]
    row_mask = jnp.repeat(pair_screen, owner_rows, axis=1).astype(jnp.bfloat16)
    masked = amplitudes * row_mask[:, :, None]
    column_cd = lax.dynamic_index_in_dim(tile_cd, grp_position, 1, keepdims=False)
    initial = jnp.zeros((blk_count, group_rows, tile_width), jnp.float32)
    running = initial
    portion = lax.all_gather(integrals, "blk", axis=0, tiled=True)
    first_row = jnp.int32(0)
    for offset in range(portion.shape[0]):
        position = first_row + offset
        product = contract(masked, portion[offset], column_cd[position])
        earlier = lax.dynamic_index_in_dim(running, position, 0, keepdims=False)
        running = lax.dynamic_update_index_in_dim(running, earlier + product, position, 0)
    arrived = lax.all_to_all(
        running.reshape(blk_count, grp_count, owner_rows, tile_width),
        "grp",
        split_axis=1,
        concat_axis=1,
        tiled=True,
    )
    blocks = arrived.reshape(blk_count * grp_count, owner_rows, tile_width)
    summed = jax.ops.segment_sum(blocks, tile_ab.reshape(-1), num_segments=ab_tiles)
    return residual_in + jnp.transpose(summed, (1, 0, 2))


def solution(mesh):
    in_specs = (
        P(None, "blk", None),
        P(None, "blk"),
        P(("blk", "grp"), None, None),
        P(),
        P(),
        P(("blk", "grp"), None, None),
    )
    out_specs = P(("blk", "grp"), None, None)
    return jax.shard_map(shards, mesh=mesh, in_specs=in_specs, out_specs=out_specs, check_vma=False)
```

profile of v0, /device:TPU:0, one launch (start us, length us, event | category | flops | bytes accessed | tf_op | source)
XLA Modules:
  0.0 178.7 jit_solution(13328309618190691948)
XLA Ops:
  6.5 0.0 copy-start
  6.5 0.0 copy-start.4
  6.5 0.0 copy-start.2
  6.5 0.0 all-gather.2.cloned.1.call-start
  6.5 0.7 all-gather.2.cloned.1.call-update
  7.3 0.0 copy-done
  7.3 0.1 constant_dynamic-slice_fusion
  7.4 0.6 fusion.25
  13.1 0.0 copy-done.4
  13.1 0.1 broadcast_in_dim.22
  13.2 0.1 convert_element_type.12
  15.9 0.0 copy-done.2
  15.9 0.1 broadcast_multiply_fusion
  16.0 83.5 %all-gather.2.cloned.1.call-done = bf16[4,1024,1024]{2,1,0:T(8,128)(2,1)} async-done(((bf16[1,1024,1024]{2,1,0:T(8,128)(2,1)}), bf16[4,1024,1024]{2,1,0:T(8,128)(2,1)}) %all-gather.2.cloned.1.call-update) | async-done | bytes 8388624 | tf_op jit(solution)/shard_map/all_gather | solution.py:23
  99.6 0.0 copy-start.1
  99.6 2.2 %fusion.4 = f32[1,128,1024]{2,1,0:T(8,128)S(1)} fusion(bf16[4,1024,1024]{2,1,0:T(8,128)(2,1)} %all-gather.2.cloned.1.call-done, bf16[4,128,1024]{2,1,0:T(8,128)(2,1)S(1)} %broadcast_multiply_fusion, s32[]{:T(128)S(6)} %select_n.28), kind=kOutput, calls=%fused_computation.10 | convolution fusion | flops 268435456 | bytes 2883588 | tf_op jit(solution)/shard_map/dot_general | solution.py:9
  101.8 0.2 dynamic_update_slice.13
  102.0 2.6 %fusion.6 = f32[4,128,1024]{2,1,0:T(8,128)S(1)} fusion(f32[4,128,1024]{2,1,0:T(8,128)S(1)} %dynamic_update_slice.13, bf16[4,1024,1024]{2,1,0:T(8,128)(2,1)} %all-gather.2.cloned.1.call-done, bf16[4,128,1024]{2,1,0:T(8,128)(2,1)S(1)} %broadcast_multiply_fusion, s32[]{:T(128)S(6)} %select_n.29), kind=kOutput, calls=%fused_computation.12 | convolution fusion | flops 268435456 | bytes 2883588 | tf_op jit(solution)/shard_map/dot_general | solution.py:9
  104.6 0.0 copy-done.1
  104.6 0.5 fusion.9
  105.2 0.5 fusion.12
  105.7 1.5 copy.8
  107.1 0.0 copy-start.3
  107.1 4.7 %all-to-all-start = ((f32[4,8,16,1024]{3,2,0,1:T(8,128)}), f32[4,8,16,1024]{3,2,0,1:T(8,128)S(1)}, u32[]{:S(2)}, u32[]{:S(2)}) async-start(f32[4,8,16,1024]{3,2,0,1:T(8,128)} %copy.8), calls=%async_computation | async-start | bytes 4194304 | tf_op jit(solution)/shard_map/all_to_all | solution.py:30
  111.9 0.0 copy-done.3
  111.9 0.1 reshape.25
  111.9 49.0 %all-to-all-done = f32[4,8,16,1024]{3,2,0,1:T(8,128)S(1)} async-done(((f32[4,8,16,1024]{3,2,0,1:T(8,128)}), f32[4,8,16,1024]{3,2,0,1:T(8,128)S(1)}, u32[]{:S(2)}, u32[]{:S(2)}) %all-to-all-start) | async-done | bytes 2097184 | tf_op jit(solution)/shard_map/all_to_all | solution.py:30
  160.9 1.5 copy.9
  162.4 0.4 broadcast_in_dim.21
  162.8 4.7 %scatter_fusion = f32[50,16,1024]{2,1,0:T(8,128)S(1)} fusion(f32[50,16,1024]{2,1,0:T(8,128)S(1)} %broadcast_in_dim.21, s32[32]{0:T(128)S(1)} %reshape.25, f32[32,16,1024]{2,1,0:T(8,128)} %bitcast.69), kind=kCustom, calls=%fused_computation | custom fusion | flops 524288 | bytes 6291584 | tf_op jit(solution)/shard_map/scatter-add | solution.py:38
  167.5 4.4 %bitcast_add_fusion = f32[16,50,1024]{2,0,1:T(8,128)} fusion(f32[16,50,1024]{2,0,1:T(8,128)} %param.11, f32[50,16,1024]{2,1,0:T(8,128)S(1)} %scatter_fusion), kind=kLoop, calls=%fused_computation.1 | loop fusion | flops 819200 | bytes 9830400 | tf_op jit(solution)/shard_map/add | solution.py:39
  (3 shorter events, 0.1 us)
Async XLA Ops:
  6.5 0.7 copy-start
  6.5 6.6 %copy-start.4 = (s32[4,8]{1,0:T(4,128)S(1)}, s32[4,8]{1,0:T(4,128)}, u32[]{:S(2)}) copy-start(s32[4,8]{1,0:T(4,128)} %param.7) | copy-start | bytes 388
  6.5 9.3 %copy-start.2 = (bf16[4,128,1024]{2,1,0:T(8,128)(2,1)S(1)}, bf16[4,128,1024]{2,1,0:T(8,128)(2,1)}, u32[]{:S(2)}) copy-start(bf16[4,128,1024]{2,1,0:T(8,128)(2,1)} %param.6) | copy-start | bytes 3145732
  6.5 93.0 %all-gather.2.cloned.1.call-start = ((), (), s32[]{:S(2)}) async-start(), calls=%async_computation.1 | async-start | bytes 10485760 | tf_op jit(solution)/shard_map/all_gather | solution.py:23
  99.6 5.1 %copy-start.1 = (bf16[4,1024,1024]{2,1,0:T(8,128)(2,1)S(1)}, bf16[4,1024,1024]{2,1,0:T(8,128)(2,1)}, u32[]{:S(2)}) copy-start(bf16[4,1024,1024]{2,1,0:T(8,128)(2,1)} %all-gather.2.cloned.1.call-done) | copy-start | bytes 25165828
  107.1 4.7 %copy-start.3 = (s32[4,8]{1,0:T(4,128)S(1)}, s32[4,8]{1,0:T(4,128)}, u32[]{:S(2)}) copy-start(s32[4,8]{1,0:T(4,128)} %param.9) | copy-start | bytes 388
  107.1 53.8 %all-to-all-start = ((f32[4,8,16,1024]{3,2,0,1:T(8,128)}), f32[4,8,16,1024]{3,2,0,1:T(8,128)S(1)}, u32[]{:S(2)}, u32[]{:S(2)}) async-start(f32[4,8,16,1024]{3,2,0,1:T(8,128)} %copy.8), calls=%async_computation | async-start | bytes 4194304 | tf_op jit(solution)/shard_map/all_to_all | solution.py:30
Sparse Core Ops, SparseCore 0:
  9.2 90.2 all-gather.1
where the time goes:
time: 179 us
  waiting for transfers between devices  133 us (74%)
  between operations  21.3 us (12%)
  other arithmetic  9.22 us (5%)
  matrix products  5.73 us (3%)
  starting transfers between devices  4.74 us (3%)
  local copies, waits for them, and re-layouts  4.56 us (3%)
    all_gather x1, waiting for transfers between devices, shards(): portion = lax.all_gather(integrals, 'blk', axis=0, tiled=True)  83.5 us
    all_to_all x1, waiting for transfers between devices, shards(): lax.all_to_all(running.reshape(blk_count, grp_count, owner_rows, tile_wid...  49 us
    dot_general x4, matrix products, contract(): return jnp.dot(rows_in, panel, preferred_element_type=jnp.float32)  5.73 us
    all_to_all x1, starting transfers between devices, shards(): lax.all_to_all(running.reshape(blk_count, grp_count, owner_rows, tile_wid...  4.74 us
    scatter-add x1, other arithmetic, shards(): jax.ops.segment_sum(blocks, tile_ab.reshape(-1), num_segments=ab_tiles)  4.67 us
    add x1, other arithmetic, shards(): return residual_in + jnp.transpose(summed, (1, 0, 2))  4.41 us
  transfers between devices with their start and end apart: 2, of which 2 were waited for; matrix products, arithmetic and copies ran while one was open for 1% of the time, Pallas kernels for 0%

commit v1 on v0

v1 whole, which is shorter than its diff:
```python
import jax
import jax.numpy as jnp
from jax import lax
from jax.sharding import PartitionSpec as P


def shards(amplitudes, pair_screen, integrals, tile_ab, tile_cd, residual_in):
    blk_count = lax.axis_size("blk")
    grp_count = lax.axis_size("grp")
    grp_position = lax.axis_index("grp")
    owner_rows, ab_tiles, tile_width = residual_in.shape
    group_rows = amplitudes.shape[1]
    row_mask = jnp.repeat(pair_screen, owner_rows, axis=1).astype(jnp.bfloat16)
    masked = amplitudes * row_mask[:, :, None]
    column_cd = lax.dynamic_index_in_dim(tile_cd, grp_position, 1, keepdims=False)
    outgoing = jnp.stack(
        [lax.dynamic_index_in_dim(masked, column_cd[p], 0, keepdims=False) for p in range(blk_count)]
    )
    rows_in = lax.all_to_all(outgoing, "blk", split_axis=0, concat_axis=0, tiled=True)
    rows_in = rows_in.reshape(blk_count * group_rows, -1)
    product = jnp.dot(rows_in, integrals[0], preferred_element_type=jnp.float32)
    coded = product.astype(jnp.float16).reshape(blk_count * grp_count, owner_rows, tile_width)
    arrived = lax.all_to_all(coded, ("blk", "grp"), split_axis=0, concat_axis=0, tiled=True)
    blocks = arrived.astype(jnp.float32)
    summed = jax.ops.segment_sum(blocks, tile_ab.reshape(-1), num_segments=ab_tiles)
    return residual_in + jnp.transpose(summed, (1, 0, 2))


def solution(mesh):
    in_specs = (
        P(None, "blk", None),
        P(None, "blk"),
        P(("blk", "grp"), None, None),
        P(),
        P(),
        P(("blk", "grp"), None, None),
    )
    out_specs = P(("blk", "grp"), None, None)
    return jax.shard_map(shards, mesh=mesh, in_specs=in_specs, out_specs=out_specs, check_vma=False)
```

time: 179 us -> 81.2 us (0.45)
  waiting for transfers between devices: 133 us -> 27.5 us
  blocking collectives: 0 us -> 19.1 us
  between operations: 21.3 us -> 7.36 us
  other arithmetic: 9.22 us -> 16.2 us
  matrix products: 5.73 us -> 2.24 us
    all_gather x1 -> x0, waiting for transfers between devices: 83.5 us -> none  [shards(): portion = lax.all_gather(integrals, 'blk', axis=0, tiled=True)]
    all_to_all x1, waiting for transfers between devices: 49 us -> 27.5 us  [shards(): lax.all_to_all(coded, ('blk', 'grp'), split_axis=0, concat_axis=0, tiled=...]
    all_to_all x0 -> x1, blocking collectives: none -> 19.1 us  [shards(): lax.all_to_all(outgoing, 'blk', split_axis=0, concat_axis=0, tiled=True)]
    dot_general x4 -> x1, matrix products: 5.73 us -> 2.24 us  [shards(): product = jnp.dot(rows_in, integrals[0], preferred_element_type=jnp.float32)]
    scatter-add x1, other arithmetic: 4.67 us -> 6.87 us  [shards(): jax.ops.segment_sum(blocks, tile_ab.reshape(-1), num_segments=ab_tiles)]
  transfers between devices with their start and end apart: 2 -> 1, of which waited for: 2 -> 1; matrix products, arithmetic and copies ran while one was open for 1% -> 0% of each run, Pallas kernels for 0% -> 0%
where the time goes in v1:
time: 81.2 us; the launch traced here: 80.7 us
  waiting for transfers between devices  27.5 us (34%)
  blocking collectives  19.1 us (24%)
  other arithmetic  16.2 us (20%)
  between operations  7.36 us (9%)
  starting transfers between devices  4.32 us (5%)
  local copies, waits for them, and re-layouts  3.92 us (5%)
  matrix products  2.24 us (3%)
    all_to_all x1, waiting for transfers between devices, shards(): lax.all_to_all(coded, ('blk', 'grp'), split_axis=0, concat_axis=0, tiled=...  27.5 us
    all_to_all x1, blocking collectives, shards(): lax.all_to_all(outgoing, 'blk', split_axis=0, concat_axis=0, tiled=True)  19.1 us
    scatter-add x1, other arithmetic, shards(): jax.ops.segment_sum(blocks, tile_ab.reshape(-1), num_segments=ab_tiles)  6.87 us
    add x1, other arithmetic, shards(): return residual_in + jnp.transpose(summed, (1, 0, 2))  5.64 us
    all_to_all x1, starting transfers between devices, shards(): lax.all_to_all(coded, ('blk', 'grp'), split_axis=0, concat_axis=0, tiled=...  4.32 us
    dot_general x1, matrix products, shards(): product = jnp.dot(rows_in, integrals[0], preferred_element_type=jnp.float32)  2.24 us
    broadcast_in_dim x1, local copies, waits for them, and re-layouts, shards(): jax.ops.segment_sum(blocks, tile_ab.reshape(-1), num_segments=ab_tiles)  2.12 us
  transfers between devices with their start and end apart: 1, of which 1 were waited for; matrix products, arithmetic and copies ran while one was open for 0% of the time, Pallas kernels for 0%

profile of v1, /device:TPU:0, one launch (start us, length us, event | category | flops | bytes accessed | tf_op | source)
XLA Modules:
  0.0 80.7 jit_solution(12578225890066903139)
XLA Ops:
  0.0 0.0 copy-start
  0.0 0.9 %constant_dynamic-slice_fusion.4 = s32[4,1]{1,0:T(4,128)S(1)} fusion(s32[4,8]{1,0:T(4,128)} %param.10, s32[]{:T(128)S(6)} %select_n.17), kind=kLoop, calls=%fused_computation.11 | loop fusion | bytes 36 | tf_op jit(solution)/shard_map/jit(dynamic_index_in_dim)/dynamic_slice | solution.py:15
  0.9 0.6 fusion.5
  6.3 0.7 convert_element_type.17
  7.0 0.1 broadcast_in_dim.8
  7.1 0.1 convert_element_type.18
  9.6 1.4 %broadcast_multiply_fusion = bf16[4,128,1024]{2,1,0:T(8,128)(2,1)S(1)} fusion(bf16[4,128,1024]{2,1,0:T(8,128)(2,1)} %param.6, bf16[4,128]{1,0:T(4,128)(2,1)S(1)} %convert_element_type.18), kind=kLoop, calls=%fused_computation.6 | loop fusion | flops 524288 | bytes 2098176 | tf_op jit(solution)/shard_map/mul | solution.py:14
  11.0 0.1 constant_dynamic-slice_fusion.3
  11.1 0.1 pad_maximum_fusion
  11.2 19.1 %all_to_all.10 = bf16[4,128,1024]{2,1,0:T(8,128)(2,1)S(1)} all-to-all(bf16[4,128,1024]{2,1,0:T(8,128)(2,1)S(1)} %pad_maximum_fusion), channel_id=1, replica_groups=mesh['blk'=4,'grp'=8] {'blk'}, dimensions={0} | all-to-all | bytes 2097152 | tf_op jit(solution)/shard_map/all_to_all | solution.py:19
  30.3 0.0 copy-done
  30.3 0.0 copy-start.1
  30.3 2.2 %fusion.2 = f16[512,1024]{1,0:T(8,128)(2,1)} fusion(bf16[512,1024]{1,0:T(8,128)(2,1)S(1)} %bitcast.15, bf16[1,1024,1024]{2,1,0:T(8,128)(2,1)S(1)} %copy-done), kind=kOutput, calls=%fused_computation.4 | convolution fusion | flops 1074266112 | bytes 4194304 | tf_op jit(solution)/shard_map/dot_general | solution.py:21
  32.6 4.3 %all-to-all-start.1 = ((f16[32,16,1024]{2,1,0:T(8,128)(2,1)}), f16[32,16,1024]{2,1,0:T(8,128)(2,1)S(1)}, u32[]{:S(2)}, u32[]{:S(2)}) async-start(f16[32,16,1024]{2,1,0:T(8,128)(2,1)} %bitcast.14), calls=%async_computation.1 | async-start | bytes 2097152 | tf_op jit(solution)/shard_map/all_to_all | solution.py:23
  36.9 0.0 copy-done.1
  36.9 0.1 reshape.25
  37.0 27.5 %all-to-all-done.1 = f16[32,16,1024]{2,1,0:T(8,128)(2,1)S(1)} async-done(((f16[32,16,1024]{2,1,0:T(8,128)(2,1)}), f16[32,16,1024]{2,1,0:T(8,128)(2,1)S(1)}, u32[]{:S(2)}, u32[]{:S(2)}) %all-to-all-start.1) | async-done | bytes 1048608 | tf_op jit(solution)/shard_map/all_to_all | solution.py:23
  64.5 1.5 %convert_element_type.20 = f32[32,16,1024]{2,1,0:T(8,128)} convert(f16[32,16,1024]{2,1,0:T(8,128)(2,1)S(1)} %all-to-all-done.1) | non-fusion elementwise | flops 524288 | bytes 3145728 | tf_op jit(solution)/shard_map/convert_element_type | solution.py:24
  66.0 2.1 %broadcast_in_dim.7 = f32[50,16,1024]{2,1,0:T(8,128)} broadcast(f32[]{:T(128)} %constant.18.clone.1), dimensions={} | broadcast | bytes 3276804 | tf_op jit(solution)/shard_map/broadcast_in_dim | solution.py:25
  68.1 6.9 %scatter_fusion = f32[50,16,1024]{2,1,0:T(8,128)} fusion(f32[50,16,1024]{2,1,0:T(8,128)} %broadcast_in_dim.7, s32[32]{0:T(128)S(1)} %reshape.25, f32[32,16,1024]{2,1,0:T(8,128)} %convert_element_type.20), kind=kCustom, calls=%fused_computation | custom fusion | flops 524288 | bytes 6291584 | tf_op jit(solution)/shard_map/scatter-add | solution.py:25
  75.0 5.6 %bitcast_add_fusion = f32[16,50,1024]{2,0,1:T(8,128)} fusion(f32[16,50,1024]{2,0,1:T(8,128)} %param.11, f32[50,16,1024]{2,1,0:T(8,128)} %scatter_fusion), kind=kLoop, calls=%fused_computation.1 | loop fusion | flops 819200 | bytes 9830400 | tf_op jit(solution)/shard_map/add | solution.py:26
Async XLA Ops:
  0.0 30.3 %copy-start = (bf16[1,1024,1024]{2,1,0:T(8,128)(2,1)S(1)}, bf16[1,1024,1024]{2,1,0:T(8,128)(2,1)}, u32[]{:S(2)}) copy-start(bf16[1,1024,1024]{2,1,0:T(8,128)(2,1)} %param.8) | copy-start | bytes 6291460
  30.3 6.6 %copy-start.1 = (s32[4,8]{1,0:T(4,128)S(1)}, s32[4,8]{1,0:T(4,128)}, u32[]{:S(2)}) copy-start(s32[4,8]{1,0:T(4,128)} %param.9) | copy-start | bytes 388
  32.6 31.9 %all-to-all-start.1 = ((f16[32,16,1024]{2,1,0:T(8,128)(2,1)}), f16[32,16,1024]{2,1,0:T(8,128)(2,1)S(1)}, u32[]{:S(2)}, u32[]{:S(2)}) async-start(f16[32,16,1024]{2,1,0:T(8,128)(2,1)} %bitcast.14), calls=%async_computation.1 | async-start | bytes 2097152 | tf_op jit(solution)/shard_map/all_to_all | solution.py:23

commit v2 on v1

v2 whole, which is shorter than its diff:
```python
import jax
import jax.numpy as jnp
from jax import lax
from jax.experimental import pallas as pl
from jax.experimental.pallas import tpu as pltpu
from jax.sharding import PartitionSpec as P


def pick_kernel(tile_cd, amplitudes, outgoing, sems):
    grp = lax.axis_index("grp")
    copies = []
    for p in range(outgoing.shape[0]):
        copies.append(pltpu.make_async_copy(amplitudes.at[tile_cd[p, grp]], outgoing.at[p], sems.at[p]))
    for copy in copies:
        copy.start()
    for copy in copies:
        copy.wait()


def pick(tile_cd, amplitudes):
    columns = tile_cd.shape[0]
    return pl.pallas_call(
        pick_kernel,
        out_shape=jax.ShapeDtypeStruct((columns,) + amplitudes.shape[1:], amplitudes.dtype),
        in_specs=[pl.BlockSpec(memory_space=pltpu.SMEM), pl.BlockSpec(memory_space=pl.ANY)],
        out_specs=pl.BlockSpec(memory_space=pl.ANY),
        scratch_shapes=[pltpu.SemaphoreType.DMA((columns,))],
        name="pick_cd_blocks",
    )(tile_cd, amplitudes)


def add_kernel(pieces, tile_ab, tile_cd, pair_screen, blocks, residual_in, residual, held, in_sems, out_sems):
    grp = lax.axis_index("grp")
    ab_tiles = residual.shape[0]
    columns, grp_count = tile_ab.shape
    bounds = [ab_tiles * piece // pieces for piece in range(pieces + 1)]
    parts = [pl.ds(low, high - low) for low, high in zip(bounds[:-1], bounds[1:])]
    arrivals = [pltpu.make_async_copy(residual_in.at[part], held.at[part], in_sems.at[i]) for i, part in enumerate(parts)]
    leaves = [pltpu.make_async_copy(held.at[part], residual.at[part], out_sems.at[i]) for i, part in enumerate(parts)]
    for copy in arrivals:
        copy.start()
    for copy in arrivals:
        copy.wait()

    def add_tile(tile, carry):
        p, g = tile // grp_count, tile % grp_count

        @pl.when(pair_screen[tile_cd[p, g], grp] != 0)
        def _():
            ab = tile_ab[p, g]
            held[ab] = held[ab] + blocks[tile]

        return carry

    lax.fori_loop(0, columns * grp_count, add_tile, 0)
    for copy in leaves:
        copy.start()
    for copy in leaves:
        copy.wait()


def add_blocks(tile_ab, tile_cd, pair_screen, blocks, residual_in):
    pieces = 5
    smem = pl.BlockSpec(memory_space=pltpu.SMEM)
    return pl.pallas_call(
        lambda *refs: add_kernel(pieces, *refs),
        out_shape=jax.ShapeDtypeStruct(residual_in.shape, residual_in.dtype),
        in_specs=[smem, smem, smem, pl.BlockSpec(memory_space=pltpu.VMEM), pl.BlockSpec(memory_space=pl.ANY)],
        out_specs=pl.BlockSpec(memory_space=pl.ANY),
        scratch_shapes=[
            pltpu.VMEM(residual_in.shape, residual_in.dtype),
            pltpu.SemaphoreType.DMA((pieces,)),
            pltpu.SemaphoreType.DMA((pieces,)),
        ],
        compiler_params=pltpu.CompilerParams(vmem_limit_bytes=32 * 1024 * 1024),
        name="add_contributions",
    )(tile_ab, tile_cd, pair_screen, blocks, residual_in)


def shards(amplitudes, pair_screen, integrals, tile_ab, tile_cd, residual_in):
    blk_count = lax.axis_size("blk")
    grp_count = lax.axis_size("grp")
    owner_rows, ab_tiles, tile_width = residual_in.shape
    group_rows = amplitudes.shape[1]
    outgoing = pick(tile_cd, amplitudes)
    rows_in = lax.all_to_all(outgoing, "blk", split_axis=0, concat_axis=0, tiled=True)
    rows_in = rows_in.reshape(blk_count * group_rows, -1)
    product = jnp.dot(rows_in, integrals[0], preferred_element_type=jnp.float32)
    coded = product.astype(jnp.float16).reshape(blk_count * grp_count, owner_rows, tile_width)
    arrived = lax.all_to_all(coded, ("blk", "grp"), split_axis=0, concat_axis=0, tiled=True)
    blocks = arrived.astype(jnp.float32)
    by_tile = jnp.transpose(residual_in, (1, 0, 2))
    return jnp.transpose(add_blocks(tile_ab, tile_cd, pair_screen, blocks, by_tile), (1, 0, 2))


def solution(mesh):
    in_specs = (
        P(None, "blk", None),
        P(None, "blk"),
        P(("blk", "grp"), None, None),
        P(),
        P(),
        P(("blk", "grp"), None, None),
    )
    out_specs = P(("blk", "grp"), None, None)
    return jax.shard_map(shards, mesh=mesh, in_specs=in_specs, out_specs=out_specs, check_vma=False)
```

time: 81.2 us -> 91.5 us (1.13)
  Pallas kernels: 0 us -> 38.2 us
  blocking collectives: 19.1 us -> 51.1 us
  waiting for transfers between devices: 27.5 us -> 0 us
  other arithmetic: 16.2 us -> 0.21 us
  between operations: 7.36 us -> 0.05 us
  starting transfers between devices: 4.32 us -> 0 us
  local copies, waits for them, and re-layouts: 3.92 us -> 0.5 us
  matrix products: 2.24 us -> 1.26 us
    pallas_call x0 -> x2, Pallas kernels: none -> 38.2 us  [the longest x1 33.7 us: pick(): pl.pallas_call(pick_kernel, out_shape=jax.ShapeDtypeStruct((columns,) + a...]
    all_to_all x0 -> x1, blocking collectives: none -> 31.8 us  [shards(): lax.all_to_all(coded, ('blk', 'grp'), split_axis=0, concat_axis=0, tiled=...]
    all_to_all x1 -> x0, waiting for transfers between devices: 27.5 us -> none  [shards(): lax.all_to_all(coded, ('blk', 'grp'), split_axis=0, concat_axis=0, tiled=...]
    scatter-add x1 -> x0, other arithmetic: 6.87 us -> none  [shards(): jax.ops.segment_sum(blocks, tile_ab.reshape(-1), num_segments=ab_tiles)]
    add x1 -> x0, other arithmetic: 5.64 us -> none  [shards(): return residual_in + jnp.transpose(summed, (1, 0, 2))]
    all_to_all x1 -> x0, starting transfers between devices: 4.32 us -> none  [shards(): lax.all_to_all(coded, ('blk', 'grp'), split_axis=0, concat_axis=0, tiled=...]
    broadcast_in_dim x2 -> x0, local copies, waits for them, and re-layouts: 2.19 us -> none  [the longest x1 2.12 us: shards(): jax.ops.segment_sum(blocks, tile_ab.reshape(-1), num_segments=ab_tiles)]
    mul x1 -> x0, other arithmetic: 1.36 us -> none  [shards(): masked = amplitudes * row_mask[:, :, None]]
  transfers between devices with their start and end apart: 1 -> 0, of which waited for: 1 -> 0; matrix products, arithmetic and copies ran while one was open for 0% -> 0% of each run, Pallas kernels for 0% -> 0%
where the time goes in v2:
time: 91.5 us; the launch traced here: 91.3 us
  blocking collectives  51.1 us (56%)
  Pallas kernels  38.2 us (42%)
  matrix products  1.26 us (1%)
    pallas_call x1, Pallas kernels, pick(): pl.pallas_call(pick_kernel, out_shape=jax.ShapeDtypeStruct((columns,) + a...  33.7 us
    all_to_all x1, blocking collectives, shards(): lax.all_to_all(coded, ('blk', 'grp'), split_axis=0, concat_axis=0, tiled=...  31.8 us
    all_to_all x1, blocking collectives, shards(): lax.all_to_all(outgoing, 'blk', split_axis=0, concat_axis=0, tiled=True)  19.3 us
    pallas_call x1, Pallas kernels, add_blocks(): pl.pallas_call(lambda *refs: add_kernel(pieces, *refs), out_shape=jax.Sha...  4.49 us

profile of v2, /device:TPU:0, one launch (start us, length us, event | category | flops | bytes accessed | tf_op | source)
XLA Modules:
  0.0 91.3 jit_solution(12150751047323184124)
XLA Ops:
  0.0 0.0 copy-start
  0.0 33.7 %pick_cd_blocks.1 = bf16[4,128,1024]{2,1,0:T(8,128)(2,1)} custom-call(s32[4,8]{1,0:T(4,128)} %refs_1_.1, bf16[4,128,1024]{2,1,0:T(8,128)(2,1)} %amplitudes.1), custom_call_target="tpu_custom_call" | custom-call | tf_op jit(solution)/shard_map/pick_cd_blocks/pallas_call | solution.py:22
  33.7 19.3 %all_to_all.10 = bf16[4,128,1024]{2,1,0:T(8,128)(2,1)S(1)} all-to-all(bf16[4,128,1024]{2,1,0:T(8,128)(2,1)} %pick_cd_blocks.1), channel_id=1, replica_groups=mesh['blk'=4,'grp'=8] {'blk'}, dimensions={0} | all-to-all | bytes 2097152 | tf_op jit(solution)/shard_map/all_to_all | solution.py:86
  53.1 0.0 copy-done
  53.1 1.3 %fusion.2 = f16[512,1024]{1,0:T(8,128)(2,1)S(1)} fusion(bf16[512,1024]{1,0:T(8,128)(2,1)S(1)} %bitcast.11, bf16[1,1024,1024]{2,1,0:T(8,128)(2,1)S(1)} %copy-done), kind=kOutput, calls=%fused_computation.2 | convolution fusion | flops 1074266112 | bytes 4194304 | tf_op jit(solution)/shard_map/dot_general | solution.py:88
  54.3 0.0 copy-start.1
  54.3 31.8 %all_to_all.11 = f16[32,16,1024]{2,1,0:T(8,128)(2,1)S(1)} all-to-all(f16[32,16,1024]{2,1,0:T(8,128)(2,1)S(1)} %bitcast.12), channel_id=1, replica_groups=mesh['blk'=4,'grp'=8] {'blk','grp'}, dimensions={0} | all-to-all | bytes 2097152 | tf_op jit(solution)/shard_map/all_to_all | solution.py:90
  86.1 0.0 copy-start.2
  86.1 0.0 copy-start.3
  86.1 0.0 copy-start.4
  86.1 0.2 convert_element_type.7.refs_3_
  86.3 0.0 copy-done.1
  86.3 0.5 copy-done.2
  86.8 0.0 copy-done.3
  86.8 0.0 copy-done.4
  86.8 4.5 %add_contributions.1 = f32[50,16,1024]{2,1,0:T(8,128)} custom-call(s32[4,8]{1,0:T(4,128)S(1)} %copy-done.3, s32[4,8]{1,0:T(4,128)S(1)} %copy-done.2, s32[4,8]{1,0:T(4,128)S(1)} %copy-done.4, f32[32,16,1024]{2,1,0:T(8,128)S(1)} %convert_element_type.7.refs_3_, f32[50,16,1024]{2,1,0:T(8,128)S(1)} %bitcast.10), custom_call_target="tpu_custom_call" | custom-call | tf_op jit(solution)/shard_map/add_contributions/pallas_call | solution.py:65
Async XLA Ops:
  0.0 53.1 %copy-start = (bf16[1,1024,1024]{2,1,0:T(8,128)(2,1)S(1)}, bf16[1,1024,1024]{2,1,0:T(8,128)(2,1)}, u32[]{:S(2)}) copy-start(bf16[1,1024,1024]{2,1,0:T(8,128)(2,1)} %param.8) | copy-start | bytes 6291460
  54.3 32.0 %copy-start.1 = (f32[16,50,1024]{2,0,1:T(8,128)S(1)}, f32[16,50,1024]{2,0,1:T(8,128)}, u32[]{:S(2)}) copy-start(f32[16,50,1024]{2,0,1:T(8,128)} %param.11) | copy-start | bytes 9830404
  86.1 0.7 copy-start.2
  86.1 0.7 copy-start.3
  86.1 0.7 copy-start.4

commit v3 on v2

--- a/solution.py
+++ b/solution.py
@@ -23,7 +23,7 @@
         pick_kernel,
         out_shape=jax.ShapeDtypeStruct((columns,) + amplitudes.shape[1:], amplitudes.dtype),
         in_specs=[pl.BlockSpec(memory_space=pltpu.SMEM), pl.BlockSpec(memory_space=pl.ANY)],
-        out_specs=pl.BlockSpec(memory_space=pl.ANY),
+        out_specs=pl.BlockSpec(memory_space=pltpu.VMEM),
         scratch_shapes=[pltpu.SemaphoreType.DMA((columns,))],
         name="pick_cd_blocks",
     )(tile_cd, amplitudes)

time: 91.5 us -> 60.8 us (0.66)
  Pallas kernels: 38.2 us -> 7.39 us
    pallas_call x1, Pallas kernels: 33.7 us -> 3.02 us  [pick(): pl.pallas_call(pick_kernel, out_shape=jax.ShapeDtypeStruct((columns,) + a...]
where the time goes in v3:
time: 60.8 us; the launch traced here: 60.5 us
  blocking collectives  51.1 us (84%)
  Pallas kernels  7.39 us (12%)
  matrix products  1.26 us (2%)
    all_to_all x1, blocking collectives, shards(): lax.all_to_all(coded, ('blk', 'grp'), split_axis=0, concat_axis=0, tiled=...  31.8 us
    all_to_all x1, blocking collectives, shards(): lax.all_to_all(outgoing, 'blk', split_axis=0, concat_axis=0, tiled=True)  19.3 us
    pallas_call x1, Pallas kernels, add_blocks(): pl.pallas_call(lambda *refs: add_kernel(pieces, *refs), out_shape=jax.Sha...  4.37 us
    pallas_call x1, Pallas kernels, pick(): pl.pallas_call(pick_kernel, out_shape=jax.ShapeDtypeStruct((columns,) + a...  3.02 us
    dot_general x1, matrix products, shards(): product = jnp.dot(rows_in, integrals[0], preferred_element_type=jnp.float32)  1.26 us

profile of v3, /device:TPU:0, one launch (start us, length us, event | category | flops | bytes accessed | tf_op | source)
XLA Modules:
  0.0 60.5 jit_solution(8367011333399520937)
XLA Ops:
  0.0 0.0 copy-start
  0.0 3.0 %pick_cd_blocks.1 = bf16[4,128,1024]{2,1,0:T(8,128)(2,1)} custom-call(s32[4,8]{1,0:T(4,128)} %refs_1_.1, bf16[4,128,1024]{2,1,0:T(8,128)(2,1)} %amplitudes.1), custom_call_target="tpu_custom_call" | custom-call | tf_op jit(solution)/shard_map/pick_cd_blocks/pallas_call | solution.py:22
  3.0 19.3 %all_to_all.10 = bf16[4,128,1024]{2,1,0:T(8,128)(2,1)S(1)} all-to-all(bf16[4,128,1024]{2,1,0:T(8,128)(2,1)} %pick_cd_blocks.1), channel_id=1, replica_groups=mesh['blk'=4,'grp'=8] {'blk'}, dimensions={0} | all-to-all | bytes 2097152 | tf_op jit(solution)/shard_map/all_to_all | solution.py:86
  22.3 0.0 copy-done
  22.3 1.3 %fusion.2 = f16[512,1024]{1,0:T(8,128)(2,1)S(1)} fusion(bf16[512,1024]{1,0:T(8,128)(2,1)S(1)} %bitcast.11, bf16[1,1024,1024]{2,1,0:T(8,128)(2,1)S(1)} %copy-done), kind=kOutput, calls=%fused_computation.2 | convolution fusion | flops 1074266112 | bytes 4194304 | tf_op jit(solution)/shard_map/dot_general | solution.py:88
  23.6 0.0 copy-start.1
  23.6 31.8 %all_to_all.11 = f16[32,16,1024]{2,1,0:T(8,128)(2,1)S(1)} all-to-all(f16[32,16,1024]{2,1,0:T(8,128)(2,1)S(1)} %bitcast.12), channel_id=1, replica_groups=mesh['blk'=4,'grp'=8] {'blk','grp'}, dimensions={0} | all-to-all | bytes 2097152 | tf_op jit(solution)/shard_map/all_to_all | solution.py:90
  55.4 0.0 copy-start.2
  55.4 0.0 copy-start.3
  55.4 0.0 copy-start.4
  55.4 0.2 convert_element_type.7.refs_3_
  55.7 0.0 copy-done.1
  55.7 0.5 copy-done.2
  56.1 0.0 copy-done.3
  56.1 0.0 copy-done.4
  56.1 4.4 %add_contributions.1 = f32[50,16,1024]{2,1,0:T(8,128)} custom-call(s32[4,8]{1,0:T(4,128)S(1)} %copy-done.3, s32[4,8]{1,0:T(4,128)S(1)} %copy-done.2, s32[4,8]{1,0:T(4,128)S(1)} %copy-done.4, f32[32,16,1024]{2,1,0:T(8,128)S(1)} %convert_element_type.7.refs_3_, f32[50,16,1024]{2,1,0:T(8,128)S(1)} %bitcast.10), custom_call_target="tpu_custom_call" | custom-call | tf_op jit(solution)/shard_map/add_contributions/pallas_call | solution.py:65
Async XLA Ops:
  0.0 22.3 %copy-start = (bf16[1,1024,1024]{2,1,0:T(8,128)(2,1)S(1)}, bf16[1,1024,1024]{2,1,0:T(8,128)(2,1)}, u32[]{:S(2)}) copy-start(bf16[1,1024,1024]{2,1,0:T(8,128)(2,1)} %param.8) | copy-start | bytes 6291460
  23.6 32.0 %copy-start.1 = (f32[16,50,1024]{2,0,1:T(8,128)S(1)}, f32[16,50,1024]{2,0,1:T(8,128)}, u32[]{:S(2)}) copy-start(f32[16,50,1024]{2,0,1:T(8,128)} %param.11) | copy-start | bytes 9830404
  55.4 0.7 %copy-start.2 = (s32[4,8]{1,0:T(4,128)S(1)}, s32[4,8]{1,0:T(4,128)}, u32[]{:S(2)}) copy-start(s32[4,8]{1,0:T(4,128)} %refs_1_.1) | copy-start | bytes 388
  55.4 0.7 %copy-start.3 = (s32[4,8]{1,0:T(4,128)S(1)}, s32[4,8]{1,0:T(4,128)}, u32[]{:S(2)}) copy-start(s32[4,8]{1,0:T(4,128)} %refs_0_.1) | copy-start | bytes 388
  55.4 0.7 %copy-start.4 = (s32[4,8]{1,0:T(4,128)S(1)}, s32[4,8]{1,0:T(4,128)}, u32[]{:S(2)}) copy-start(s32[4,8]{1,0:T(4,128)} %refs_2_.1) | copy-start | bytes 388

commit v4 on v3

v4 whole, which is shorter than its diff:
```python
import jax
import jax.numpy as jnp
from jax import lax
from jax.experimental import pallas as pl
from jax.experimental.pallas import tpu as pltpu
from jax.sharding import PartitionSpec as P


def pick_kernel(tile_cd, amplitudes, *rest):
    outgoing, sems = rest[:-1], rest[-1]
    blk, grp = lax.axis_index("blk"), lax.axis_index("grp")
    copies = []
    for step, picked in enumerate(outgoing):
        cd = tile_cd[jnp.bitwise_xor(blk, step), grp]
        copies.append(pltpu.make_async_copy(amplitudes.at[cd], picked, sems.at[step]))
    for copy in copies:
        copy.start()
    for copy in copies:
        copy.wait()


def pick(tile_cd, amplitudes):
    columns = tile_cd.shape[0]
    block = jax.ShapeDtypeStruct(amplitudes.shape[1:], amplitudes.dtype)
    return pl.pallas_call(
        pick_kernel,
        out_shape=[block] * columns,
        in_specs=[pl.BlockSpec(memory_space=pltpu.SMEM), pl.BlockSpec(memory_space=pl.ANY)],
        out_specs=[pl.BlockSpec(memory_space=pltpu.VMEM)] * columns,
        scratch_shapes=[pltpu.SemaphoreType.DMA((columns,))],
        name="pick_cd_blocks",
    )(tile_cd, amplitudes)


def add_kernel(pieces, tile_ab, tile_cd, pair_screen, *rest):
    blocks, (residual_in, residual, held, in_sems, out_sems) = rest[:-5], rest[-5:]
    blk, grp = lax.axis_index("blk"), lax.axis_index("grp")
    ab_tiles = residual.shape[0]
    columns, grp_count = tile_ab.shape
    bounds = [ab_tiles * piece // pieces for piece in range(pieces + 1)]
    parts = [pl.ds(low, high - low) for low, high in zip(bounds[:-1], bounds[1:])]
    arrivals = [pltpu.make_async_copy(residual_in.at[part], held.at[part], in_sems.at[i]) for i, part in enumerate(parts)]
    leaves = [pltpu.make_async_copy(held.at[part], residual.at[part], out_sems.at[i]) for i, part in enumerate(parts)]
    for copy in arrivals:
        copy.start()
    for copy in arrivals:
        copy.wait()

    for step, group_blocks in enumerate(blocks):
        p = jnp.bitwise_xor(blk, step)

        def add_tile(g, carry):
            @pl.when(pair_screen[tile_cd[p, g], grp] != 0)
            def _():
                ab = tile_ab[p, g]
                held[ab] = held[ab] + group_blocks[g]

            return carry

        lax.fori_loop(0, grp_count, add_tile, 0)
    for copy in leaves:
        copy.start()
    for copy in leaves:
        copy.wait()


def add_blocks(tile_ab, tile_cd, pair_screen, blocks, residual_in):
    pieces = 5
    smem = pl.BlockSpec(memory_space=pltpu.SMEM)
    vmem = pl.BlockSpec(memory_space=pltpu.VMEM)
    return pl.pallas_call(
        lambda *refs: add_kernel(pieces, *refs),
        out_shape=jax.ShapeDtypeStruct(residual_in.shape, residual_in.dtype),
        in_specs=[smem, smem, smem] + [vmem] * len(blocks) + [pl.BlockSpec(memory_space=pl.ANY)],
        out_specs=pl.BlockSpec(memory_space=pl.ANY),
        scratch_shapes=[
            pltpu.VMEM(residual_in.shape, residual_in.dtype),
            pltpu.SemaphoreType.DMA((pieces,)),
            pltpu.SemaphoreType.DMA((pieces,)),
        ],
        compiler_params=pltpu.CompilerParams(vmem_limit_bytes=32 * 1024 * 1024),
        name="add_contributions",
    )(tile_ab, tile_cd, pair_screen, *blocks, residual_in)


def shards(amplitudes, pair_screen, integrals, tile_ab, tile_cd, residual_in):
    blk_count = lax.axis_size("blk")
    grp_count = lax.axis_size("grp")
    owner_rows, ab_tiles, tile_width = residual_in.shape

    def swap(value, step):
        return lax.ppermute(value, "blk", [(b, b ^ step) for b in range(blk_count)])

    picked = pick(tile_cd, amplitudes)
    rows_in = [picked[0]] + [swap(picked[step], step) for step in range(1, blk_count)]
    blocks = []
    for step in range(blk_count):
        product = jnp.dot(rows_in[step], integrals[0], preferred_element_type=jnp.float32)
        coded = product.astype(jnp.float16).reshape(grp_count, owner_rows, tile_width)
        spread = lax.all_to_all(coded, "grp", split_axis=0, concat_axis=0, tiled=True)
        blocks.append((swap(spread, step) if step else spread).astype(jnp.float32))
    by_tile = jnp.transpose(residual_in, (1, 0, 2))
    return jnp.transpose(add_blocks(tile_ab, tile_cd, pair_screen, blocks, by_tile), (1, 0, 2))


def solution(mesh):
    in_specs = (
        P(None, "blk", None),
        P(None, "blk"),
        P(("blk", "grp"), None, None),
        P(),
        P(),
        P(("blk", "grp"), None, None),
    )
    out_specs = P(("blk", "grp"), None, None)
    return jax.shard_map(shards, mesh=mesh, in_specs=in_specs, out_specs=out_specs, check_vma=False)
```

time: 60.8 us -> 81.4 us (1.34)
  blocking collectives: 51.1 us -> 0 us
  waiting for transfers between devices: 0 us -> 40.1 us
  starting transfers between devices: 0 us -> 26 us
  matrix products: 1.26 us -> 4.62 us
  local copies, waits for them, and re-layouts: 0.5 us -> 2.64 us
    all_to_all x2 -> x0, blocking collectives: 51.1 us -> none  [the longest x1 31.8 us: shards(): lax.all_to_all(coded, ('blk', 'grp'), split_axis=0, concat_axis=0, tiled=...]
    all_to_all x0 -> x4, waiting for transfers between devices: none -> 29.1 us  [shards(): lax.all_to_all(coded, 'grp', split_axis=0, concat_axis=0, tiled=True)]
    all_to_all x0 -> x4, starting transfers between devices: none -> 15.4 us  [shards(): lax.all_to_all(coded, 'grp', split_axis=0, concat_axis=0, tiled=True)]
    ppermute x0 -> x6, waiting for transfers between devices: none -> 10.9 us  [swap(): return lax.ppermute(value, 'blk', [(b, b ^ step) for b in range(blk_count)])]
    ppermute x0 -> x6, starting transfers between devices: none -> 10.6 us  [swap(): return lax.ppermute(value, 'blk', [(b, b ^ step) for b in range(blk_count)])]
    dot_general x1 -> x4, matrix products: 1.26 us -> 4.62 us  [shards(): jnp.dot(rows_in[step], integrals[0], preferred_element_type=jnp.float32)]
    unnamed x10 -> x18, local copies, waits for them, and re-layouts: 0.5 us -> 2.64 us
  transfers between devices with their start and end apart: 0 -> 10, of which waited for: 0 -> 6; matrix products, arithmetic and copies ran while one was open for 0% -> 6% of each run, Pallas kernels for 0% -> 0%
where the time goes in v4:
time: 81.4 us; the launch traced here: 80.8 us
  waiting for transfers between devices  40.1 us (49%)
  starting transfers between devices  26 us (32%)
  Pallas kernels  7.23 us (9%)
  matrix products  4.62 us (6%)
  local copies, waits for them, and re-layouts  2.64 us (3%)
    all_to_all x4, waiting for transfers between devices, shards(): lax.all_to_all(coded, 'grp', split_axis=0, concat_axis=0, tiled=True)  29.1 us
    all_to_all x4, starting transfers between devices, shards(): lax.all_to_all(coded, 'grp', split_axis=0, concat_axis=0, tiled=True)  15.4 us
    ppermute x6, waiting for transfers between devices, swap(): return lax.ppermute(value, 'blk', [(b, b ^ step) for b in range(blk_count)])  10.9 us
    ppermute x6, starting transfers between devices, swap(): return lax.ppermute(value, 'blk', [(b, b ^ step) for b in range(blk_count)])  10.6 us
    dot_general x4, matrix products, shards(): jnp.dot(rows_in[step], integrals[0], preferred_element_type=jnp.float32)  4.62 us
    pallas_call x1, Pallas kernels, add_blocks(): pl.pallas_call(lambda *refs: add_kernel(pieces, *refs), out_shape=jax.Sha...  4.22 us
    pallas_call x1, Pallas kernels, pick(): pl.pallas_call(pick_kernel, out_shape=[block] * columns, in_specs=[pl.Blo...  3.01 us
    unnamed x18, local copies, waits for them, and re-layouts  2.64 us
  transfers between devices with their start and end apart: 10, of which 6 were waited for; matrix products, arithmetic and copies ran while one was open for 6% of the time, Pallas kernels for 0%

profile of v4, /device:TPU:0, one launch (start us, length us, event | category | flops | bytes accessed | tf_op | source)
XLA Modules:
  0.0 80.8 jit_solution(6378884867083799427)
XLA Ops:
  0.0 0.0 copy-start
  0.0 3.0 %pick_cd_blocks.1 = (bf16[128,1024]{1,0:T(8,128)(2,1)}, bf16[128,1024]{1,0:T(8,128)(2,1)}, bf16[128,1024]{1,0:T(8,128)(2,1)}, bf16[128,1024]{1,0:T(8,128)(2,1)}) custom-call(s32[4,8]{1,0:T(4,128)} %refs_1_.1, bf16[4,128,1024]{2,1,0:T(8,128)(2,1)} %amplitudes.1), custom_call_target="tpu_custom_call" | custom-call | tf_op jit(solution)/shard_map/pick_cd_blocks/pallas_call | solution.py:25
  3.0 0.0 copy-start.8
  3.0 3.0 %collective-permute-start = (bf16[128,1024]{1,0:T(8,128)(2,1)}, bf16[128,1024]{1,0:T(8,128)(2,1)S(1)}, u32[]{:S(2)}, u32[]{:S(2)}) collective-permute-start(bf16[128,1024]{1,0:T(8,128)(2,1)} %get-tuple-element.10), channel_id=1, source_target_pairs={{0,8},{8,0},{16,24},{24,16},{1,9},{9,1},{17,25},{25,17},{2,10},{10... | collective-permute-start | bytes 786440 | tf_op jit(solution)/shard_map/ppermute | solution.py:92
  6.0 1.5 %collective-permute-start.2 = (bf16[128,1024]{1,0:T(8,128)(2,1)}, bf16[128,1024]{1,0:T(8,128)(2,1)S(1)}, u32[]{:S(2)}, u32[]{:S(2)}) collective-permute-start(bf16[128,1024]{1,0:T(8,128)(2,1)} %get-tuple-element.11), channel_id=1, source_target_pairs={{0,16},{8,24},{16,0},{24,8},{1,17},{9,25},{17,1},{25,9},{2,18},{10... | collective-permute-start | bytes 786440 | tf_op jit(solution)/shard_map/ppermute | solution.py:92
  7.6 5.0 %collective-permute-done = bf16[128,1024]{1,0:T(8,128)(2,1)S(1)} collective-permute-done((bf16[128,1024]{1,0:T(8,128)(2,1)}, bf16[128,1024]{1,0:T(8,128)(2,1)S(1)}, u32[]{:S(2)}, u32[]{:S(2)}) %collective-permute-start) | collective-permute-done | bytes 262176 | tf_op jit(solution)/shard_map/ppermute | solution.py:92
  12.6 0.0 copy-done
  12.6 1.1 %fusion.11 = f16[128,1024]{1,0:T(8,128)(2,1)} fusion(bf16[128,1024]{1,0:T(8,128)(2,1)S(1)} %collective-permute-done, bf16[1,1024,1024]{2,1,0:T(8,128)(2,1)S(1)} %copy-done), kind=kOutput, calls=%fused_computation.9 | convolution fusion | flops 268566528 | bytes 2621440 | tf_op jit(solution)/shard_map/dot_general | solution.py:98
  13.7 5.2 %all-to-all-start.1 = ((f16[8,16,1024]{2,1,0:T(8,128)(2,1)}), f16[8,16,1024]{2,1,0:T(8,128)(2,1)S(1)}, u32[]{:S(2)}, u32[]{:S(2)}) async-start(f16[8,16,1024]{2,1,0:T(8,128)(2,1)} %bitcast.2), calls=%async_computation.1 | async-start | bytes 524288 | tf_op jit(solution)/shard_map/all_to_all | solution.py:100
  18.9 0.0 copy-done.8
  18.9 2.5 %collective-permute-start.4 = (bf16[128,1024]{1,0:T(8,128)(2,1)S(1)}, bf16[128,1024]{1,0:T(8,128)(2,1)S(1)}, u32[]{:S(2)}, u32[]{:S(2)}) collective-permute-start(bf16[128,1024]{1,0:T(8,128)(2,1)S(1)} %copy-done.8), channel_id=1, source_target_pairs={{0,24},{8,16},{16,8},{24,0},{1,25},{9,17},{17,9},{25,1},{2,26},{10... | collective-permute-start | bytes 786440 | tf_op jit(solution)/shard_map/ppermute | solution.py:92
  21.4 0.0 collective-permute-done.2
  21.4 1.1 %fusion.14 = f16[128,1024]{1,0:T(8,128)(2,1)} fusion(bf16[128,1024]{1,0:T(8,128)(2,1)S(1)} %collective-permute-done.2, bf16[1,1024,1024]{2,1,0:T(8,128)(2,1)S(1)} %copy-done), kind=kOutput, calls=%fused_computation.10 | convolution fusion | flops 268566528 | bytes 2621440 | tf_op jit(solution)/shard_map/dot_general | solution.py:98
  22.5 0.0 copy-start.5
  22.5 6.1 %all-to-all-done.1 = f16[8,16,1024]{2,1,0:T(8,128)(2,1)S(1)} async-done(((f16[8,16,1024]{2,1,0:T(8,128)(2,1)}), f16[8,16,1024]{2,1,0:T(8,128)(2,1)S(1)}, u32[]{:S(2)}, u32[]{:S(2)}) %all-to-all-start.1) | async-done | bytes 262176 | tf_op jit(solution)/shard_map/all_to_all | solution.py:100
  28.6 3.4 %all-to-all-start.2 = ((f16[8,16,1024]{2,1,0:T(8,128)(2,1)}), f16[8,16,1024]{2,1,0:T(8,128)(2,1)S(1)}, u32[]{:S(2)}, u32[]{:S(2)}) async-start(f16[8,16,1024]{2,1,0:T(8,128)(2,1)} %bitcast.3), calls=%async_computation.2 | async-start | bytes 524288 | tf_op jit(solution)/shard_map/all_to_all | solution.py:100
  32.0 0.0 collective-permute-done.4
  32.0 1.2 %fusion.17 = f16[128,1024]{1,0:T(8,128)(2,1)} fusion(bf16[128,1024]{1,0:T(8,128)(2,1)S(1)} %collective-permute-done.4, bf16[1,1024,1024]{2,1,0:T(8,128)(2,1)S(1)} %copy-done), kind=kOutput, calls=%fused_computation.11 | convolution fusion | flops 268566528 | bytes 2621440 | tf_op jit(solution)/shard_map/dot_general | solution.py:98
  33.2 8.5 %all-to-all-done.2 = f16[8,16,1024]{2,1,0:T(8,128)(2,1)S(1)} async-done(((f16[8,16,1024]{2,1,0:T(8,128)(2,1)}), f16[8,16,1024]{2,1,0:T(8,128)(2,1)S(1)}, u32[]{:S(2)}, u32[]{:S(2)}) %all-to-all-start.2) | async-done | bytes 262176 | tf_op jit(solution)/shard_map/all_to_all | solution.py:100
  41.7 0.0 copy-start.6
  41.7 3.4 %all-to-all-start.3 = ((f16[8,16,1024]{2,1,0:T(8,128)(2,1)}), f16[8,16,1024]{2,1,0:T(8,128)(2,1)S(1)}, u32[]{:S(2)}, u32[]{:S(2)}) async-start(f16[8,16,1024]{2,1,0:T(8,128)(2,1)} %bitcast.4), calls=%async_computation.3 | async-start | bytes 524288 | tf_op jit(solution)/shard_map/all_to_all | solution.py:100
  45.1 0.0 copy-done.5
  45.1 1.2 %fusion.8 = f16[128,1024]{1,0:T(8,128)(2,1)} fusion(bf16[128,1024]{1,0:T(8,128)(2,1)S(1)} %copy-done.5, bf16[1,1024,1024]{2,1,0:T(8,128)(2,1)S(1)} %copy-done), kind=kOutput, calls=%fused_computation.8 | convolution fusion | flops 268566528 | bytes 2621440 | tf_op jit(solution)/shard_map/dot_general | solution.py:98
  46.3 0.0 copy-start.2
  46.3 0.0 copy-start.3
  46.3 0.0 copy-start.4
  46.3 8.5 %all-to-all-done.3 = f16[8,16,1024]{2,1,0:T(8,128)(2,1)S(1)} async-done(((f16[8,16,1024]{2,1,0:T(8,128)(2,1)}), f16[8,16,1024]{2,1,0:T(8,128)(2,1)S(1)}, u32[]{:S(2)}, u32[]{:S(2)}) %all-to-all-start.3) | async-done | bytes 262176 | tf_op jit(solution)/shard_map/all_to_all | solution.py:100
  54.8 0.0 copy-start.7
  54.8 0.0 copy-done.6
  54.8 0.7 copy-done.7
  55.5 3.4 %all-to-all-start = ((f16[8,16,1024]{2,1,0:T(8,128)(2,1)}), f16[8,16,1024]{2,1,0:T(8,128)(2,1)S(1)}, u32[]{:S(2)}, u32[]{:S(2)}) async-start(f16[8,16,1024]{2,1,0:T(8,128)(2,1)} %bitcast.1), calls=%async_computation | async-start | bytes 524288 | tf_op jit(solution)/shard_map/all_to_all | solution.py:100
  58.9 1.6 %collective-permute-start.1 = (f16[8,16,1024]{2,1,0:T(8,128)(2,1)S(1)}, f16[8,16,1024]{2,1,0:T(8,128)(2,1)S(1)}, u32[]{:S(2)}, u32[]{:S(2)}) collective-permute-start(f16[8,16,1024]{2,1,0:T(8,128)(2,1)S(1)} %all-to-all-done.1), channel_id=1, source_target_pairs={{0,8},{8,0},{16,24},{24,16},{1,9},{9,1},{17,25},{25,17},{2,10},{10... | collective-permute-start | bytes 786440 | tf_op jit(solution)/shard_map/ppermute | solution.py:92
  60.4 1.5 %collective-permute-start.3 = (f16[8,16,1024]{2,1,0:T(8,128)(2,1)}, f16[8,16,1024]{2,1,0:T(8,128)(2,1)S(1)}, u32[]{:S(2)}, u32[]{:S(2)}) collective-permute-start(f16[8,16,1024]{2,1,0:T(8,128)(2,1)} %copy-done.6), channel_id=1, source_target_pairs={{0,16},{8,24},{16,0},{24,8},{1,17},{9,25},{17,1},{25,9},{2,18},{10... | collective-permute-start | bytes 786440 | tf_op jit(solution)/shard_map/ppermute | solution.py:92
  62.0 0.5 collective-permute-start.5
  62.4 6.1 %all-to-all-done = f16[8,16,1024]{2,1,0:T(8,128)(2,1)S(1)} async-done(((f16[8,16,1024]{2,1,0:T(8,128)(2,1)}), f16[8,16,1024]{2,1,0:T(8,128)(2,1)S(1)}, u32[]{:S(2)}, u32[]{:S(2)}) %all-to-all-start) | async-done | bytes 262176 | tf_op jit(solution)/shard_map/all_to_all | solution.py:100
  68.6 0.0 collective-permute-done.1
  68.6 5.9 %collective-permute-done.3 = f16[8,16,1024]{2,1,0:T(8,128)(2,1)S(1)} collective-permute-done((f16[8,16,1024]{2,1,0:T(8,128)(2,1)}, f16[8,16,1024]{2,1,0:T(8,128)(2,1)S(1)}, u32[]{:S(2)}, u32[]{:S(2)}) %collective-permute-start.3) | collective-permute-done | bytes 262176 | tf_op jit(solution)/shard_map/ppermute | solution.py:92
  74.6 0.0 collective-permute-done.5
  74.6 0.0 copy-done.2
  74.6 0.0 copy-done.3
  74.7 0.0 copy-done.4
  74.7 0.0 copy-start.1
  74.7 1.9 %copy-done.1 = f32[16,50,1024]{2,0,1:T(8,128)S(1)} copy-done((f32[16,50,1024]{2,0,1:T(8,128)S(1)}, f32[16,50,1024]{2,0,1:T(8,128)}, u32[]{:S(2)}) %copy-start.1) | copy-done | bytes 3276824
  76.6 4.2 %add_contributions.1 = f32[50,16,1024]{2,1,0:T(8,128)} custom-call(s32[4,8]{1,0:T(4,128)S(1)} %copy-done.3, s32[4,8]{1,0:T(4,128)S(1)} %copy-done.2, s32[4,8]{1,0:T(4,128)S(1)} %copy-done.4, f32[8,16,1024]{2,1,0:T(8,128)S(1)} %convert_element_type.25.refs_3_, f32[8,16,1024]{2,1,0:T(8,128)S(1)} %convert_element_type.27.refs_4_, ...), custom_call_target="tpu_custom_call" | custom-call | tf_op jit(solution)/shard_map/add_contributions/pallas_call | solution.py:71
  (4 shorter events, 0.1 us)
Async XLA Ops:
  0.0 12.6 %copy-start = (bf16[1,1024,1024]{2,1,0:T(8,128)(2,1)S(1)}, bf16[1,1024,1024]{2,1,0:T(8,128)(2,1)}, u32[]{:S(2)}) copy-start(bf16[1,1024,1024]{2,1,0:T(8,128)(2,1)} %param.8) | copy-start | bytes 6291460
  3.0 15.8 %copy-start.8 = (bf16[128,1024]{1,0:T(8,128)(2,1)S(1)}, bf16[128,1024]{1,0:T(8,128)(2,1)}, u32[]{:S(2)}) copy-start(bf16[128,1024]{1,0:T(8,128)(2,1)} %get-tuple-element.12) | copy-start | bytes 786436
  3.0 9.5 %collective-permute-start = (bf16[128,1024]{1,0:T(8,128)(2,1)}, bf16[128,1024]{1,0:T(8,128)(2,1)S(1)}, u32[]{:S(2)}, u32[]{:S(2)}) collective-permute-start(bf16[128,1024]{1,0:T(8,128)(2,1)} %get-tuple-element.10), channel_id=1, source_target_pairs={{0,8},{8,0},{16,24},{24,16},{1,9},{9,1},{17,25},{25,17},{2,10},{10... | collective-permute-start | bytes 786440 | tf_op jit(solution)/shard_map/ppermute | solution.py:92
  6.0 15.3 %collective-permute-start.2 = (bf16[128,1024]{1,0:T(8,128)(2,1)}, bf16[128,1024]{1,0:T(8,128)(2,1)S(1)}, u32[]{:S(2)}, u32[]{:S(2)}) collective-permute-start(bf16[128,1024]{1,0:T(8,128)(2,1)} %get-tuple-element.11), channel_id=1, source_target_pairs={{0,16},{8,24},{16,0},{24,8},{1,17},{9,25},{17,1},{25,9},{2,18},{10... | collective-permute-start | bytes 786440 | tf_op jit(solution)/shard_map/ppermute | solution.py:92
  13.7 14.9 %all-to-all-start.1 = ((f16[8,16,1024]{2,1,0:T(8,128)(2,1)}), f16[8,16,1024]{2,1,0:T(8,128)(2,1)S(1)}, u32[]{:S(2)}, u32[]{:S(2)}) async-start(f16[8,16,1024]{2,1,0:T(8,128)(2,1)} %bitcast.2), calls=%async_computation.1 | async-start | bytes 524288 | tf_op jit(solution)/shard_map/all_to_all | solution.py:100
  18.9 13.2 %collective-permute-start.4 = (bf16[128,1024]{1,0:T(8,128)(2,1)S(1)}, bf16[128,1024]{1,0:T(8,128)(2,1)S(1)}, u32[]{:S(2)}, u32[]{:S(2)}) collective-permute-start(bf16[128,1024]{1,0:T(8,128)(2,1)S(1)} %copy-done.8), channel_id=1, source_target_pairs={{0,24},{8,16},{16,8},{24,0},{1,25},{9,17},{17,9},{25,1},{2,26},{10... | collective-permute-start | bytes 786440 | tf_op jit(solution)/shard_map/ppermute | solution.py:92
  22.5 22.6 %copy-start.5 = (bf16[128,1024]{1,0:T(8,128)(2,1)S(1)}, bf16[128,1024]{1,0:T(8,128)(2,1)}, u32[]{:S(2)}) copy-start(bf16[128,1024]{1,0:T(8,128)(2,1)} %get-tuple-element.9) | copy-start | bytes 786436
  28.6 13.1 %all-to-all-start.2 = ((f16[8,16,1024]{2,1,0:T(8,128)(2,1)}), f16[8,16,1024]{2,1,0:T(8,128)(2,1)S(1)}, u32[]{:S(2)}, u32[]{:S(2)}) async-start(f16[8,16,1024]{2,1,0:T(8,128)(2,1)} %bitcast.3), calls=%async_computation.2 | async-start | bytes 524288 | tf_op jit(solution)/shard_map/all_to_all | solution.py:100
  41.7 13.1 %copy-start.6 = (f16[8,16,1024]{2,1,0:T(8,128)(2,1)}, f16[8,16,1024]{2,1,0:T(8,128)(2,1)S(1)}, u32[]{:S(2)}) copy-start(f16[8,16,1024]{2,1,0:T(8,128)(2,1)S(1)} %all-to-all-done.2) | copy-start | bytes 786436
  41.7 13.1 %all-to-all-start.3 = ((f16[8,16,1024]{2,1,0:T(8,128)(2,1)}), f16[8,16,1024]{2,1,0:T(8,128)(2,1)S(1)}, u32[]{:S(2)}, u32[]{:S(2)}) async-start(f16[8,16,1024]{2,1,0:T(8,128)(2,1)} %bitcast.4), calls=%async_computation.3 | async-start | bytes 524288 | tf_op jit(solution)/shard_map/all_to_all | solution.py:100
  46.3 28.4 %copy-start.2 = (s32[4,8]{1,0:T(4,128)S(1)}, s32[4,8]{1,0:T(4,128)}, u32[]{:S(2)}) copy-start(s32[4,8]{1,0:T(4,128)} %refs_1_.1) | copy-start | bytes 388
  46.3 28.4 %copy-start.3 = (s32[4,8]{1,0:T(4,128)S(1)}, s32[4,8]{1,0:T(4,128)}, u32[]{:S(2)}) copy-start(s32[4,8]{1,0:T(4,128)} %refs_0_.1) | copy-start | bytes 388
  46.3 28.4 %copy-start.4 = (s32[4,8]{1,0:T(4,128)S(1)}, s32[4,8]{1,0:T(4,128)}, u32[]{:S(2)}) copy-start(s32[4,8]{1,0:T(4,128)} %refs_2_.1) | copy-start | bytes 388
  54.8 0.7 copy-start.7
  55.5 13.1 %all-to-all-start = ((f16[8,16,1024]{2,1,0:T(8,128)(2,1)}), f16[8,16,1024]{2,1,0:T(8,128)(2,1)S(1)}, u32[]{:S(2)}, u32[]{:S(2)}) async-start(f16[8,16,1024]{2,1,0:T(8,128)(2,1)} %bitcast.1), calls=%async_computation | async-start | bytes 524288 | tf_op jit(solution)/shard_map/all_to_all | solution.py:100
  58.9 9.7 %collective-permute-start.1 = (f16[8,16,1024]{2,1,0:T(8,128)(2,1)S(1)}, f16[8,16,1024]{2,1,0:T(8,128)(2,1)S(1)}, u32[]{:S(2)}, u32[]{:S(2)}) collective-permute-start(f16[8,16,1024]{2,1,0:T(8,128)(2,1)S(1)} %all-to-all-done.1), channel_id=1, source_target_pairs={{0,8},{8,0},{16,24},{24,16},{1,9},{9,1},{17,25},{25,17},{2,10},{10... | collective-permute-start | bytes 786440 | tf_op jit(solution)/shard_map/ppermute | solution.py:92
  60.4 14.1 %collective-permute-start.3 = (f16[8,16,1024]{2,1,0:T(8,128)(2,1)}, f16[8,16,1024]{2,1,0:T(8,128)(2,1)S(1)}, u32[]{:S(2)}, u32[]{:S(2)}) collective-permute-start(f16[8,16,1024]{2,1,0:T(8,128)(2,1)} %copy-done.6), channel_id=1, source_target_pairs={{0,16},{8,24},{16,0},{24,8},{1,17},{9,25},{17,1},{25,9},{2,18},{10... | collective-permute-start | bytes 786440 | tf_op jit(solution)/shard_map/ppermute | solution.py:92
  62.0 12.6 %collective-permute-start.5 = (f16[8,16,1024]{2,1,0:T(8,128)(2,1)}, f16[8,16,1024]{2,1,0:T(8,128)(2,1)S(1)}, u32[]{:S(2)}, u32[]{:S(2)}) collective-permute-start(f16[8,16,1024]{2,1,0:T(8,128)(2,1)} %copy-done.7), channel_id=1, source_target_pairs={{0,24},{8,16},{16,8},{24,0},{1,25},{9,17},{17,9},{25,1},{2,26},{10... | collective-permute-start | bytes 786440 | tf_op jit(solution)/shard_map/ppermute | solution.py:92
  74.7 1.9 %copy-start.1 = (f32[16,50,1024]{2,0,1:T(8,128)S(1)}, f32[16,50,1024]{2,0,1:T(8,128)}, u32[]{:S(2)}) copy-start(f32[16,50,1024]{2,0,1:T(8,128)} %param.11) | copy-start | bytes 9830404

commit v5 on v4

--- a/solution.py
+++ b/solution.py
@@ -4,6 +4,39 @@
 from jax.experimental import pallas as pl
 from jax.experimental.pallas import tpu as pltpu
 from jax.sharding import PartitionSpec as P
+
+LARGEST = 32766.0
+SCALE_STEPS = 64.0
+SCALE_SHIFT = 8192
+SCALE_BITS = 16
+LANES = 128
+
+
+def encode(values):
+    largest = jnp.max(jnp.abs(values), axis=1, keepdims=True)
+    logarithm = jnp.log2(jnp.maximum(largest, 2.0**-100))
+    exponent = jnp.floor(logarithm * SCALE_STEPS) + 2.0
+    scaled = values * (LARGEST * jnp.exp2(exponent * (-1.0 / SCALE_STEPS)))
+    scaled = jnp.clip(scaled, -LARGEST, LARGEST)
+    code = jnp.floor(scaled + 0.5).astype(jnp.int32)
+    head = code[:, :LANES]
+    lane = lax.broadcasted_iota(jnp.int32, head.shape, 1)
+    stored = exponent.astype(jnp.int32) + SCALE_SHIFT
+    stored = jnp.broadcast_to(stored, head.shape)
+    bit = lax.shift_right_logical(stored, jnp.minimum(lane, SCALE_BITS)) & 1
+    head = jnp.where(lane < SCALE_BITS, (head & -2) | bit, head)
+    return head.astype(jnp.int16), code[:, LANES:].astype(jnp.int16)
+
+
+def decode(code):
+    code = code.astype(jnp.int32)
+    head = code[:, :LANES]
+    lane = lax.broadcasted_iota(jnp.int32, head.shape, 1)
+    bits = lax.shift_left(head & 1, jnp.minimum(lane, SCALE_BITS))
+    bits = jnp.where(lane < SCALE_BITS, bits, 0).astype(jnp.float32)
+    stored = jnp.sum(bits, axis=1, keepdims=True)
+    scale = jnp.exp2((stored - SCALE_SHIFT) * (1.0 / SCALE_STEPS)) * (1.0 / LARGEST)
+    return code.astype(jnp.float32) * scale
 
 
 def pick_kernel(tile_cd, amplitudes, *rest):
@@ -32,6 +65,38 @@
     )(tile_cd, amplitudes)
 
 
+def product_kernel(rows, tile, *rest):
+    outgoing, product = rest[:-1], rest[-1]
+    grp = lax.axis_index("grp")
+    owner_rows = outgoing[0].shape[0]
+    product[...] = jnp.dot(rows[...], tile[0], preferred_element_type=jnp.float32)
+    for step, coded in enumerate(outgoing):
+        first = pl.multiple_of(jnp.bitwise_xor(grp, step) * owner_rows, owner_rows)
+        head, tail = encode(product[pl.ds(first, owner_rows), :])
+        coded[:, :LANES] = head
+        coded[:, LANES:] = tail
+
+
+def contract(rows, tile, owner_rows):
+    group_rows, tile_width = rows.shape[0], tile.shape[2]
+    owners = group_rows // owner_rows
+    vmem = pl.BlockSpec(memory_space=pltpu.VMEM)
+    return pl.pallas_call(
+        product_kernel,
+        out_shape=[jax.ShapeDtypeStruct((owner_rows, tile_width), jnp.int16)] * owners,
+        in_specs=[vmem, vmem],
+        out_specs=[vmem] * owners,
+        scratch_shapes=[pltpu.VMEM((group_rows, tile_width), jnp.float32)],
+        compiler_params=pltpu.CompilerParams(vmem_limit_bytes=32 * 1024 * 1024),
+        cost_estimate=pl.CostEstimate(
+            flops=2 * group_rows * tile.shape[1] * tile_width,
+            bytes_accessed=2 * tile.shape[1] * tile_width,
+            transcendentals=0,
+        ),
+        name="contract_group",
+    )(rows, tile)
+
+
 def add_kernel(pieces, tile_ab, tile_cd, pair_screen, *rest):
     blocks, (residual_in, residual, held, in_sems, out_sems) = rest[:-5], rest[-5:]
     blk, grp = lax.axis_index("blk"), lax.axis_index("grp")
@@ -46,18 +111,15 @@
     for copy in arrivals:
         copy.wait()
 
-    for step, group_blocks in enumerate(blocks):
-        p = jnp.bitwise_xor(blk, step)
+    for index, coded in enumerate(blocks):
+        p = jnp.bitwise_xor(blk, index // grp_count)
+        g = jnp.bitwise_xor(grp, index % grp_count)
 
-        def add_tile(g, carry):
-            @pl.when(pair_screen[tile_cd[p, g], grp] != 0)
-            def _():
-                ab = tile_ab[p, g]
-                held[ab] = held[ab] + group_blocks[g]
+        @pl.when(pair_screen[tile_cd[p, g], grp] != 0)
+        def _():
+            ab = tile_ab[p, g]
+            held[ab] = held[ab] + decode(coded[...])
 
-            return carry
-
-        lax.fori_loop(0, grp_count, add_tile, 0)
     for copy in leaves:
         copy.start()
     for copy in leaves:
@@ -86,19 +148,23 @@
 def shards(amplitudes, pair_screen, integrals, tile_ab, tile_cd, residual_in):
     blk_count = lax.axis_size("blk")
     grp_count = lax.axis_size("grp")
-    owner_rows, ab_tiles, tile_width = residual_in.shape
+    owner_rows = residual_in.shape[0]
 
-    def swap(value, step):
-        return lax.ppermute(value, "blk", [(b, b ^ step) for b in range(blk_count)])
+    def swap(value, blk_step, grp_step):
+        step = blk_step * grp_count + grp_step
+        pairs = [(device, device ^ step) for device in range(blk_count * grp_count)]
+        return lax.ppermute(value, ("blk", "grp"), pairs)
 
     picked = pick(tile_cd, amplitudes)
-    rows_in = [picked[0]] + [swap(picked[step], step) for step in range(1, blk_count)]
+    rows_in = [picked[0]] + [swap(picked[step], step, 0) for step in range(1, blk_count)]
     blocks = []
-    for step in range(blk_count):
-        product = jnp.dot(rows_in[step], integrals[0], preferred_element_type=jnp.float32)
-        coded = product.astype(jnp.float16).reshape(grp_count, owner_rows, tile_width)
-        spread = lax.all_to_all(coded, "grp", split_axis=0, concat_axis=0, tiled=True)
-        blocks.append((swap(spread, step) if step else spread).astype(jnp.float32))
+    for blk_step in range(blk_count):
+        coded = contract(rows_in[blk_step], integrals, owner_rows)
+        arrived = {}
+        for grp_step in reversed(range(grp_count)):
+            own = blk_step == 0 and grp_step == 0
+            arrived[grp_step] = coded[grp_step] if own else swap(coded[grp_step], blk_step, grp_step)
+        blocks += [arrived[grp_step] for grp_step in range(grp_count)]
     by_tile = jnp.transpose(residual_in, (1, 0, 2))
     return jnp.transpose(add_blocks(tile_ab, tile_cd, pair_screen, blocks, by_tile), (1, 0, 2))
 

time: 81.4 us -> 82.1 us (level)
  starting transfers between devices: 26 us -> 56.4 us
  waiting for transfers between devices: 40.1 us -> 10.4 us
  matrix products: 4.62 us -> 0 us
  Pallas kernels: 7.23 us -> 11.6 us
    ppermute x6 -> x34, starting transfers between devices: 10.6 us -> 56.4 us  [swap(): return lax.ppermute(value, ('blk', 'grp'), pairs)]
    all_to_all x4 -> x0, waiting for transfers between devices: 29.1 us -> none  [shards(): lax.all_to_all(coded, 'grp', split_axis=0, concat_axis=0, tiled=True)]
    all_to_all x4 -> x0, starting transfers between devices: 15.4 us -> none  [shards(): lax.all_to_all(coded, 'grp', split_axis=0, concat_axis=0, tiled=True)]
    dot_general x4 -> x0, matrix products: 4.62 us -> none  [shards(): jnp.dot(rows_in[step], integrals[0], preferred_element_type=jnp.float32)]
    pallas_call x0 -> x4, Pallas kernels: none -> 2.78 us  [contract(): pl.pallas_call(product_kernel, out_shape=[jax.ShapeDtypeStruct((owner_row...]
    pallas_call x1, Pallas kernels: 4.22 us -> 5.9 us  [add_blocks(): pl.pallas_call(lambda *refs: add_kernel(pieces, *refs), out_shape=jax.Sha...]
    ppermute x6 -> x34, waiting for transfers between devices: 10.9 us -> 10.4 us  [swap(): return lax.ppermute(value, ('blk', 'grp'), pairs)]
    unnamed x18 -> x14, local copies, waits for them, and re-layouts: 2.64 us -> 2.56 us
  transfers between devices with their start and end apart: 10 -> 34, of which waited for: 6 -> 6; matrix products, arithmetic and copies ran while one was open for 6% -> 0% of each run, Pallas kernels for 0% -> 3%
where the time goes in v5:
time: 82.1 us; the launch traced here: 81.1 us
  starting transfers between devices  56.4 us (69%)
  Pallas kernels  11.6 us (14%)
  waiting for transfers between devices  10.4 us (13%)
  local copies, waits for them, and re-layouts  2.56 us (3%)
    ppermute x34, starting transfers between devices, swap(): return lax.ppermute(value, ('blk', 'grp'), pairs)  56.4 us
    ppermute x34, waiting for transfers between devices, swap(): return lax.ppermute(value, ('blk', 'grp'), pairs)  10.4 us
    pallas_call x1, Pallas kernels, add_blocks(): pl.pallas_call(lambda *refs: add_kernel(pieces, *refs), out_shape=jax.Sha...  5.9 us
    pallas_call x1, Pallas kernels, pick(): pl.pallas_call(pick_kernel, out_shape=[block] * columns, in_specs=[pl.Blo...  2.93 us
    pallas_call x4, Pallas kernels, contract(): pl.pallas_call(product_kernel, out_shape=[jax.ShapeDtypeStruct((owner_row...  2.78 us
    unnamed x14, local copies, waits for them, and re-layouts  2.56 us
  transfers between devices with their start and end apart: 34, of which 6 were waited for; matrix products, arithmetic and copies ran while one was open for 0% of the time, Pallas kernels for 3%

profile of v5, /device:TPU:0, one launch (start us, length us, event | category | flops | bytes accessed | tf_op | source)
XLA Modules:
  0.0 81.1 jit_solution(5088763849671740397)
XLA Ops:
  0.0 2.9 %pick_cd_blocks.1 = (bf16[128,1024]{1,0:T(8,128)(2,1)}, bf16[128,1024]{1,0:T(8,128)(2,1)}, bf16[128,1024]{1,0:T(8,128)(2,1)}, bf16[128,1024]{1,0:T(8,128)(2,1)}) custom-call(s32[4,8]{1,0:T(4,128)} %refs_1_.1, bf16[4,128,1024]{2,1,0:T(8,128)(2,1)} %amplitudes.1), custom_call_target="tpu_custom_call" | custom-call | tf_op jit(solution)/shard_map/pick_cd_blocks/pallas_call | solution.py:58
  2.9 3.0 %collective-permute-start.7 = (bf16[128,1024]{1,0:T(8,128)(2,1)}, bf16[128,1024]{1,0:T(8,128)(2,1)S(1)}, u32[]{:S(2)}, u32[]{:S(2)}) collective-permute-start(bf16[128,1024]{1,0:T(8,128)(2,1)} %get-tuple-element.50), channel_id=1, source_target_pairs={{0,8},{1,9},{2,10},{3,11},{4,12},{5,13},{6,14},{7,15},{8,0},{9,1},... | collective-permute-start | bytes 786440 | tf_op jit(solution)/shard_map/ppermute | solution.py:156
  5.9 1.5 %collective-permute-start.16 = (bf16[128,1024]{1,0:T(8,128)(2,1)}, bf16[128,1024]{1,0:T(8,128)(2,1)S(1)}, u32[]{:S(2)}, u32[]{:S(2)}) collective-permute-start(bf16[128,1024]{1,0:T(8,128)(2,1)} %get-tuple-element.59), channel_id=1, source_target_pairs={{0,16},{1,17},{2,18},{3,19},{4,20},{5,21},{6,22},{7,23},{8,24},{9,... | collective-permute-start | bytes 786440 | tf_op jit(solution)/shard_map/ppermute | solution.py:156
  7.5 0.0 collective-permute-start.25
  7.5 1.6 %copy-done = bf16[1,1024,1024]{2,1,0:T(8,128)(2,1)S(1)} copy-done((bf16[1,1024,1024]{2,1,0:T(8,128)(2,1)S(1)}, bf16[1,1024,1024]{2,1,0:T(8,128)(2,1)}, u32[]{:S(2)}) %copy-start) | copy-done | bytes 2097176
  9.1 0.9 %copy-done.3 = bf16[128,1024]{1,0:T(8,128)(2,1)S(1)} copy-done((bf16[128,1024]{1,0:T(8,128)(2,1)S(1)}, bf16[128,1024]{1,0:T(8,128)(2,1)}, u32[]{:S(2)}) %copy-start.3) | copy-done | bytes 262168
  10.0 0.7 contract_group.4
  10.7 0.1 collective-permute-start
  10.8 2.1 %collective-permute-start.1 = (s16[16,1024]{1,0:T(8,128)(2,1)S(1)}, s16[16,1024]{1,0:T(8,128)(2,1)S(1)}, u32[]{:S(2)}, u32[]{:S(2)}) collective-permute-start(s16[16,1024]{1,0:T(8,128)(2,1)S(1)} %get-tuple-element.44), channel_id=1, source_target_pairs={{0,2},{1,3},{2,0},{3,1},{4,6},{5,7},{6,4},{7,5},{8,10},{9,11},{10,... | collective-permute-start | bytes 98312 | tf_op jit(solution)/shard_map/ppermute | solution.py:156
  12.9 0.0 collective-permute-done.refs_4_
  12.9 0.9 %collective-permute-start.2 = (s16[16,1024]{1,0:T(8,128)(2,1)S(1)}, s16[16,1024]{1,0:T(8,128)(2,1)S(1)}, u32[]{:S(2)}, u32[]{:S(2)}) collective-permute-start(s16[16,1024]{1,0:T(8,128)(2,1)S(1)} %get-tuple-element.45), channel_id=1, source_target_pairs={{0,3},{1,2},{2,1},{3,0},{4,7},{5,6},{6,5},{7,4},{8,11},{9,10},{10,... | collective-permute-start | bytes 98312 | tf_op jit(solution)/shard_map/ppermute | solution.py:156
  13.8 1.1 %collective-permute-done.1.refs_5_ = s16[16,1024]{1,0:T(8,128)(2,1)S(1)} collective-permute-done((s16[16,1024]{1,0:T(8,128)(2,1)S(1)}, s16[16,1024]{1,0:T(8,128)(2,1)S(1)}, u32[]{:S(2)}, u32[]{:S(2)}) %collective-permute-start.1) | collective-permute-done | bytes 32800 | tf_op jit(solution)/shard_map/ppermute | solution.py:156
  14.9 2.9 %collective-permute-start.3 = (s16[16,1024]{1,0:T(8,128)(2,1)S(1)}, s16[16,1024]{1,0:T(8,128)(2,1)S(1)}, u32[]{:S(2)}, u32[]{:S(2)}) collective-permute-start(s16[16,1024]{1,0:T(8,128)(2,1)S(1)} %get-tuple-element.46), channel_id=1, source_target_pairs={{0,4},{1,5},{2,6},{3,7},{4,0},{5,1},{6,2},{7,3},{8,12},{9,13},{10,... | collective-permute-start | bytes 98312 | tf_op jit(solution)/shard_map/ppermute | solution.py:156
  17.8 0.0 collective-permute-done.2.refs_6_
  17.8 1.1 %collective-permute-start.4 = (s16[16,1024]{1,0:T(8,128)(2,1)S(1)}, s16[16,1024]{1,0:T(8,128)(2,1)S(1)}, u32[]{:S(2)}, u32[]{:S(2)}) collective-permute-start(s16[16,1024]{1,0:T(8,128)(2,1)S(1)} %get-tuple-element.47), channel_id=1, source_target_pairs={{0,5},{1,4},{2,7},{3,6},{4,1},{5,0},{6,3},{7,2},{8,13},{9,12},{10,... | collective-permute-start | bytes 98312 | tf_op jit(solution)/shard_map/ppermute | solution.py:156
  18.9 1.1 %collective-permute-done.3.refs_7_ = s16[16,1024]{1,0:T(8,128)(2,1)S(1)} collective-permute-done((s16[16,1024]{1,0:T(8,128)(2,1)S(1)}, s16[16,1024]{1,0:T(8,128)(2,1)S(1)}, u32[]{:S(2)}, u32[]{:S(2)}) %collective-permute-start.3) | collective-permute-done | bytes 32800 | tf_op jit(solution)/shard_map/ppermute | solution.py:156
  20.0 4.9 %collective-permute-start.5 = (s16[16,1024]{1,0:T(8,128)(2,1)S(1)}, s16[16,1024]{1,0:T(8,128)(2,1)S(1)}, u32[]{:S(2)}, u32[]{:S(2)}) collective-permute-start(s16[16,1024]{1,0:T(8,128)(2,1)S(1)} %get-tuple-element.48), channel_id=1, source_target_pairs={{0,6},{1,7},{2,4},{3,5},{4,2},{5,3},{6,0},{7,1},{8,14},{9,15},{10,... | collective-permute-start | bytes 98312 | tf_op jit(solution)/shard_map/ppermute | solution.py:156
  24.9 0.0 collective-permute-done.7.rows
  24.9 0.0 copy-start.6
  24.9 0.1 collective-permute-start.6
  25.0 0.7 contract_group.5
  25.7 0.0 collective-permute-done.4.refs_8_
  25.7 1.6 %collective-permute-start.8 = (s16[16,1024]{1,0:T(8,128)(2,1)S(1)}, s16[16,1024]{1,0:T(8,128)(2,1)S(1)}, u32[]{:S(2)}, u32[]{:S(2)}) collective-permute-start(s16[16,1024]{1,0:T(8,128)(2,1)S(1)} %get-tuple-element.51), channel_id=1, source_target_pairs={{0,8},{1,9},{2,10},{3,11},{4,12},{5,13},{6,14},{7,15},{8,0},{9,1},... | collective-permute-start | bytes 98312 | tf_op jit(solution)/shard_map/ppermute | solution.py:156
  27.3 0.0 collective-permute-done.5.refs_9_
  27.3 0.0 collective-permute-start.9
  27.3 2.8 %collective-permute-done.6.refs_10_ = s16[16,1024]{1,0:T(8,128)(2,1)S(1)} collective-permute-done((s16[16,1024]{1,0:T(8,128)(2,1)S(1)}, s16[16,1024]{1,0:T(8,128)(2,1)S(1)}, u32[]{:S(2)}, u32[]{:S(2)}) %collective-permute-start.6) | collective-permute-done | bytes 32800 | tf_op jit(solution)/shard_map/ppermute | solution.py:156
  30.1 0.0 collective-permute-start.10
  30.1 0.0 collective-permute-done.16.rows
  30.2 0.5 collective-permute-start.11
  30.7 0.7 contract_group.6
  31.4 0.0 collective-permute-done.25.rows
  31.4 2.8 %collective-permute-start.12 = (s16[16,1024]{1,0:T(8,128)(2,1)S(1)}, s16[16,1024]{1,0:T(8,128)(2,1)S(1)}, u32[]{:S(2)}, u32[]{:S(2)}) collective-permute-start(s16[16,1024]{1,0:T(8,128)(2,1)S(1)} %get-tuple-element.55), channel_id=1, source_target_pairs={{0,12},{1,13},{2,14},{3,15},{4,8},{5,9},{6,10},{7,11},{8,4},{9,5},... | collective-permute-start | bytes 98312 | tf_op jit(solution)/shard_map/ppermute | solution.py:156
  34.2 0.0 collective-permute-done.8.refs_11_
  34.2 3.0 %collective-permute-start.13 = (s16[16,1024]{1,0:T(8,128)(2,1)S(1)}, s16[16,1024]{1,0:T(8,128)(2,1)S(1)}, u32[]{:S(2)}, u32[]{:S(2)}) collective-permute-start(s16[16,1024]{1,0:T(8,128)(2,1)S(1)} %get-tuple-element.56), channel_id=1, source_target_pairs={{0,13},{1,12},{2,15},{3,14},{4,9},{5,8},{6,11},{7,10},{8,5},{9,4},... | collective-permute-start | bytes 98312 | tf_op jit(solution)/shard_map/ppermute | solution.py:156
  37.1 1.9 %collective-permute-start.14 = (s16[16,1024]{1,0:T(8,128)(2,1)S(1)}, s16[16,1024]{1,0:T(8,128)(2,1)S(1)}, u32[]{:S(2)}, u32[]{:S(2)}) collective-permute-start(s16[16,1024]{1,0:T(8,128)(2,1)S(1)} %get-tuple-element.57), channel_id=1, source_target_pairs={{0,14},{1,15},{2,12},{3,13},{4,10},{5,11},{6,8},{7,9},{8,6},{9,7},... | collective-permute-start | bytes 98312 | tf_op jit(solution)/shard_map/ppermute | solution.py:156
  39.0 0.0 collective-permute-done.10.refs_13_
  39.0 0.4 collective-permute-start.15
  39.4 0.0 collective-permute-done.11.refs_14_
  39.5 1.5 %collective-permute-start.17 = (s16[16,1024]{1,0:T(8,128)(2,1)S(1)}, s16[16,1024]{1,0:T(8,128)(2,1)S(1)}, u32[]{:S(2)}, u32[]{:S(2)}) collective-permute-start(s16[16,1024]{1,0:T(8,128)(2,1)S(1)} %get-tuple-element.60), channel_id=1, source_target_pairs={{0,16},{1,17},{2,18},{3,19},{4,20},{5,21},{6,22},{7,23},{8,24},{9,... | collective-permute-start | bytes 98312 | tf_op jit(solution)/shard_map/ppermute | solution.py:156
  41.0 2.4 %collective-permute-start.18 = (s16[16,1024]{1,0:T(8,128)(2,1)S(1)}, s16[16,1024]{1,0:T(8,128)(2,1)S(1)}, u32[]{:S(2)}, u32[]{:S(2)}) collective-permute-start(s16[16,1024]{1,0:T(8,128)(2,1)S(1)} %get-tuple-element.61), channel_id=1, source_target_pairs={{0,17},{1,16},{2,19},{3,18},{4,21},{5,20},{6,23},{7,22},{8,25},{9,... | collective-permute-start | bytes 98312 | tf_op jit(solution)/shard_map/ppermute | solution.py:156
  43.3 0.4 collective-permute-done.14.refs_17_
  43.7 1.8 %collective-permute-start.20 = (s16[16,1024]{1,0:T(8,128)(2,1)S(1)}, s16[16,1024]{1,0:T(8,128)(2,1)S(1)}, u32[]{:S(2)}, u32[]{:S(2)}) collective-permute-start(s16[16,1024]{1,0:T(8,128)(2,1)S(1)} %get-tuple-element.63), channel_id=1, source_target_pairs={{0,19},{1,18},{2,17},{3,16},{4,23},{5,22},{6,21},{7,20},{8,27},{9,... | collective-permute-start | bytes 98312 | tf_op jit(solution)/shard_map/ppermute | solution.py:156
  45.5 1.0 %collective-permute-start.21 = (s16[16,1024]{1,0:T(8,128)(2,1)S(1)}, s16[16,1024]{1,0:T(8,128)(2,1)S(1)}, u32[]{:S(2)}, u32[]{:S(2)}) collective-permute-start(s16[16,1024]{1,0:T(8,128)(2,1)S(1)} %get-tuple-element.64), channel_id=1, source_target_pairs={{0,20},{1,21},{2,22},{3,23},{4,16},{5,17},{6,18},{7,19},{8,28},{9,... | collective-permute-start | bytes 98312 | tf_op jit(solution)/shard_map/ppermute | solution.py:156
  46.6 3.0 %collective-permute-start.22 = (s16[16,1024]{1,0:T(8,128)(2,1)S(1)}, s16[16,1024]{1,0:T(8,128)(2,1)S(1)}, u32[]{:S(2)}, u32[]{:S(2)}) collective-permute-start(s16[16,1024]{1,0:T(8,128)(2,1)S(1)} %get-tuple-element.65), channel_id=1, source_target_pairs={{0,21},{1,20},{2,23},{3,22},{4,17},{5,16},{6,19},{7,18},{8,29},{9,... | collective-permute-start | bytes 98312 | tf_op jit(solution)/shard_map/ppermute | solution.py:156
  49.5 0.7 contract_group.7
  50.2 0.0 collective-permute-done.18.refs_20_
  50.2 2.0 %collective-permute-start.23 = (s16[16,1024]{1,0:T(8,128)(2,1)S(1)}, s16[16,1024]{1,0:T(8,128)(2,1)S(1)}, u32[]{:S(2)}, u32[]{:S(2)}) collective-permute-start(s16[16,1024]{1,0:T(8,128)(2,1)S(1)} %get-tuple-element.66), channel_id=1, source_target_pairs={{0,22},{1,23},{2,20},{3,21},{4,18},{5,19},{6,16},{7,17},{8,30},{9,... | collective-permute-start | bytes 98312 | tf_op jit(solution)/shard_map/ppermute | solution.py:156
  52.2 0.0 collective-permute-done.19.refs_21_
  52.2 2.1 %collective-permute-start.24 = (s16[16,1024]{1,0:T(8,128)(2,1)S(1)}, s16[16,1024]{1,0:T(8,128)(2,1)S(1)}, u32[]{:S(2)}, u32[]{:S(2)}) collective-permute-start(s16[16,1024]{1,0:T(8,128)(2,1)S(1)} %get-tuple-element.67), channel_id=1, source_target_pairs={{0,23},{1,22},{2,21},{3,20},{4,19},{5,18},{6,17},{7,16},{8,31},{9,... | collective-permute-start | bytes 98312 | tf_op jit(solution)/shard_map/ppermute | solution.py:156
  54.3 0.0 collective-permute-done.20.refs_22_
  54.3 1.4 %collective-permute-start.26 = (s16[16,1024]{1,0:T(8,128)(2,1)S(1)}, s16[16,1024]{1,0:T(8,128)(2,1)S(1)}, u32[]{:S(2)}, u32[]{:S(2)}) collective-permute-start(s16[16,1024]{1,0:T(8,128)(2,1)S(1)} %get-tuple-element.69), channel_id=1, source_target_pairs={{0,24},{1,25},{2,26},{3,27},{4,28},{5,29},{6,30},{7,31},{8,16},{9,... | collective-permute-start | bytes 98312 | tf_op jit(solution)/shard_map/ppermute | solution.py:156
  55.8 1.7 %collective-permute-start.27 = (s16[16,1024]{1,0:T(8,128)(2,1)S(1)}, s16[16,1024]{1,0:T(8,128)(2,1)S(1)}, u32[]{:S(2)}, u32[]{:S(2)}) collective-permute-start(s16[16,1024]{1,0:T(8,128)(2,1)S(1)} %get-tuple-element.70), channel_id=1, source_target_pairs={{0,25},{1,24},{2,27},{3,26},{4,29},{5,28},{6,31},{7,30},{8,17},{9,... | collective-permute-start | bytes 98312 | tf_op jit(solution)/shard_map/ppermute | solution.py:156
  57.4 0.0 collective-permute-done.23.refs_25_
  57.4 3.1 %collective-permute-start.29 = (s16[16,1024]{1,0:T(8,128)(2,1)S(1)}, s16[16,1024]{1,0:T(8,128)(2,1)S(1)}, u32[]{:S(2)}, u32[]{:S(2)}) collective-permute-start(s16[16,1024]{1,0:T(8,128)(2,1)S(1)} %get-tuple-element.72), channel_id=1, source_target_pairs={{0,27},{1,26},{2,25},{3,24},{4,31},{5,30},{6,29},{7,28},{8,19},{9,... | collective-permute-start | bytes 98312 | tf_op jit(solution)/shard_map/ppermute | solution.py:156
  60.5 0.0 collective-permute-done.24.refs_26_
  60.6 1.2 %collective-permute-start.30 = (s16[16,1024]{1,0:T(8,128)(2,1)S(1)}, s16[16,1024]{1,0:T(8,128)(2,1)S(1)}, u32[]{:S(2)}, u32[]{:S(2)}) collective-permute-start(s16[16,1024]{1,0:T(8,128)(2,1)S(1)} %get-tuple-element.73), channel_id=1, source_target_pairs={{0,28},{1,29},{2,30},{3,31},{4,24},{5,25},{6,26},{7,27},{8,20},{9,... | collective-permute-start | bytes 98312 | tf_op jit(solution)/shard_map/ppermute | solution.py:156
  61.8 3.6 %collective-permute-start.31 = (s16[16,1024]{1,0:T(8,128)(2,1)S(1)}, s16[16,1024]{1,0:T(8,128)(2,1)S(1)}, u32[]{:S(2)}, u32[]{:S(2)}) collective-permute-start(s16[16,1024]{1,0:T(8,128)(2,1)S(1)} %get-tuple-element.74), channel_id=1, source_target_pairs={{0,29},{1,28},{2,31},{3,30},{4,25},{5,24},{6,27},{7,26},{8,21},{9,... | collective-permute-start | bytes 98312 | tf_op jit(solution)/shard_map/ppermute | solution.py:156
  65.4 2.8 %collective-permute-start.32 = (s16[16,1024]{1,0:T(8,128)(2,1)S(1)}, s16[16,1024]{1,0:T(8,128)(2,1)S(1)}, u32[]{:S(2)}, u32[]{:S(2)}) collective-permute-start(s16[16,1024]{1,0:T(8,128)(2,1)S(1)} %get-tuple-element.75), channel_id=1, source_target_pairs={{0,30},{1,31},{2,28},{3,29},{4,26},{5,27},{6,24},{7,25},{8,22},{9,... | collective-permute-start | bytes 98312 | tf_op jit(solution)/shard_map/ppermute | solution.py:156
  68.3 0.0 collective-permute-done.28.refs_29_
  68.3 2.1 %collective-permute-start.33 = (s16[16,1024]{1,0:T(8,128)(2,1)S(1)}, s16[16,1024]{1,0:T(8,128)(2,1)S(1)}, u32[]{:S(2)}, u32[]{:S(2)}) collective-permute-start(s16[16,1024]{1,0:T(8,128)(2,1)S(1)} %get-tuple-element.76), channel_id=1, source_target_pairs={{0,31},{1,30},{2,29},{3,28},{4,27},{5,26},{6,25},{7,24},{8,23},{9,... | collective-permute-start | bytes 98312 | tf_op jit(solution)/shard_map/ppermute | solution.py:156
  70.4 0.0 collective-permute-done.31.refs_32_
  70.4 2.6 %collective-permute-done.32.refs_33_ = s16[16,1024]{1,0:T(8,128)(2,1)S(1)} collective-permute-done((s16[16,1024]{1,0:T(8,128)(2,1)S(1)}, s16[16,1024]{1,0:T(8,128)(2,1)S(1)}, u32[]{:S(2)}, u32[]{:S(2)}) %collective-permute-start.32) | collective-permute-done | bytes 32800 | tf_op jit(solution)/shard_map/ppermute | solution.py:156
  72.9 2.3 %collective-permute-done.33.refs_34_ = s16[16,1024]{1,0:T(8,128)(2,1)S(1)} collective-permute-done((s16[16,1024]{1,0:T(8,128)(2,1)S(1)}, s16[16,1024]{1,0:T(8,128)(2,1)S(1)}, u32[]{:S(2)}, u32[]{:S(2)}) %collective-permute-start.33) | collective-permute-done | bytes 32800 | tf_op jit(solution)/shard_map/ppermute | solution.py:156
  75.2 5.9 %add_contributions.1 = f32[50,16,1024]{2,1,0:T(8,128)} custom-call(s32[4,8]{1,0:T(4,128)S(1)} %copy-done.5, s32[4,8]{1,0:T(4,128)S(1)} %copy-done.4, s32[4,8]{1,0:T(4,128)S(1)} %copy-done.6, s16[16,1024]{1,0:T(8,128)(2,1)S(1)} %get-tuple-element.42.refs_3_, s16[16,1024]{1,0:T(8,128)(2,1)S(1)} %collective-permute-done.refs_4_, ...), custom_call_target="tpu_custom_call" | custom-call | tf_op jit(solution)/shard_map/add_contributions/pallas_call | solution.py:133
  (24 shorter events, 0.1 us)
Async XLA Ops:
  2.9 22.0 %collective-permute-start.7 = (bf16[128,1024]{1,0:T(8,128)(2,1)}, bf16[128,1024]{1,0:T(8,128)(2,1)S(1)}, u32[]{:S(2)}, u32[]{:S(2)}) collective-permute-start(bf16[128,1024]{1,0:T(8,128)(2,1)} %get-tuple-element.50), channel_id=1, source_target_pairs={{0,8},{1,9},{2,10},{3,11},{4,12},{5,13},{6,14},{7,15},{8,0},{9,1},... | collective-permute-start | bytes 786440 | tf_op jit(solution)/shard_map/ppermute | solution.py:156
  5.9 24.2 %collective-permute-start.16 = (bf16[128,1024]{1,0:T(8,128)(2,1)}, bf16[128,1024]{1,0:T(8,128)(2,1)S(1)}, u32[]{:S(2)}, u32[]{:S(2)}) collective-permute-start(bf16[128,1024]{1,0:T(8,128)(2,1)} %get-tuple-element.59), channel_id=1, source_target_pairs={{0,16},{1,17},{2,18},{3,19},{4,20},{5,21},{6,22},{7,23},{8,24},{9,... | collective-permute-start | bytes 786440 | tf_op jit(solution)/shard_map/ppermute | solution.py:156
  7.5 23.9 %collective-permute-start.25 = (bf16[128,1024]{1,0:T(8,128)(2,1)}, bf16[128,1024]{1,0:T(8,128)(2,1)S(1)}, u32[]{:S(2)}, u32[]{:S(2)}) collective-permute-start(bf16[128,1024]{1,0:T(8,128)(2,1)} %get-tuple-element.68), channel_id=1, source_target_pairs={{0,24},{1,25},{2,26},{3,27},{4,28},{5,29},{6,30},{7,31},{8,16},{9,... | collective-permute-start | bytes 786440 | tf_op jit(solution)/shard_map/ppermute | solution.py:156
  7.5 1.6 %copy-start = (bf16[1,1024,1024]{2,1,0:T(8,128)(2,1)S(1)}, bf16[1,1024,1024]{2,1,0:T(8,128)(2,1)}, u32[]{:S(2)}) copy-start(bf16[1,1024,1024]{2,1,0:T(8,128)(2,1)} %tile.7) | copy-start | bytes 6291460
  9.1 0.9 %copy-start.3 = (bf16[128,1024]{1,0:T(8,128)(2,1)S(1)}, bf16[128,1024]{1,0:T(8,128)(2,1)}, u32[]{:S(2)}) copy-start(bf16[128,1024]{1,0:T(8,128)(2,1)} %get-tuple-element.41.rows) | copy-start | bytes 786436
  10.0 15.0 %copy-start.1 = (bf16[1,1024,1024]{2,1,0:T(8,128)(2,1)S(1)}, bf16[1,1024,1024]{2,1,0:T(8,128)(2,1)}, u32[]{:S(2)}) copy-start(bf16[1,1024,1024]{2,1,0:T(8,128)(2,1)} %tile.7) | copy-start | bytes 6291460
  10.7 2.1 %collective-permute-start = (s16[16,1024]{1,0:T(8,128)(2,1)S(1)}, s16[16,1024]{1,0:T(8,128)(2,1)S(1)}, u32[]{:S(2)}, u32[]{:S(2)}) collective-permute-start(s16[16,1024]{1,0:T(8,128)(2,1)S(1)} %get-tuple-element.43), channel_id=1, source_target_pairs={{0,1},{1,0},{2,3},{3,2},{4,5},{5,4},{6,7},{7,6},{8,9},{9,8},{10,11... | collective-permute-start | bytes 98312 | tf_op jit(solution)/shard_map/ppermute | solution.py:156
  10.8 4.0 %collective-permute-start.1 = (s16[16,1024]{1,0:T(8,128)(2,1)S(1)}, s16[16,1024]{1,0:T(8,128)(2,1)S(1)}, u32[]{:S(2)}, u32[]{:S(2)}) collective-permute-start(s16[16,1024]{1,0:T(8,128)(2,1)S(1)} %get-tuple-element.44), channel_id=1, source_target_pairs={{0,2},{1,3},{2,0},{3,1},{4,6},{5,7},{6,4},{7,5},{8,10},{9,11},{10,... | collective-permute-start | bytes 98312 | tf_op jit(solution)/shard_map/ppermute | solution.py:156
  12.9 4.9 %collective-permute-start.2 = (s16[16,1024]{1,0:T(8,128)(2,1)S(1)}, s16[16,1024]{1,0:T(8,128)(2,1)S(1)}, u32[]{:S(2)}, u32[]{:S(2)}) collective-permute-start(s16[16,1024]{1,0:T(8,128)(2,1)S(1)} %get-tuple-element.45), channel_id=1, source_target_pairs={{0,3},{1,2},{2,1},{3,0},{4,7},{5,6},{6,5},{7,4},{8,11},{9,10},{10,... | collective-permute-start | bytes 98312 | tf_op jit(solution)/shard_map/ppermute | solution.py:156
  14.9 5.2 %collective-permute-start.3 = (s16[16,1024]{1,0:T(8,128)(2,1)S(1)}, s16[16,1024]{1,0:T(8,128)(2,1)S(1)}, u32[]{:S(2)}, u32[]{:S(2)}) collective-permute-start(s16[16,1024]{1,0:T(8,128)(2,1)S(1)} %get-tuple-element.46), channel_id=1, source_target_pairs={{0,4},{1,5},{2,6},{3,7},{4,0},{5,1},{6,2},{7,3},{8,12},{9,13},{10,... | collective-permute-start | bytes 98312 | tf_op jit(solution)/shard_map/ppermute | solution.py:156
  17.8 7.9 %collective-permute-start.4 = (s16[16,1024]{1,0:T(8,128)(2,1)S(1)}, s16[16,1024]{1,0:T(8,128)(2,1)S(1)}, u32[]{:S(2)}, u32[]{:S(2)}) collective-permute-start(s16[16,1024]{1,0:T(8,128)(2,1)S(1)} %get-tuple-element.47), channel_id=1, source_target_pairs={{0,5},{1,4},{2,7},{3,6},{4,1},{5,0},{6,3},{7,2},{8,13},{9,12},{10,... | collective-permute-start | bytes 98312 | tf_op jit(solution)/shard_map/ppermute | solution.py:156
  20.0 7.3 %collective-permute-start.5 = (s16[16,1024]{1,0:T(8,128)(2,1)S(1)}, s16[16,1024]{1,0:T(8,128)(2,1)S(1)}, u32[]{:S(2)}, u32[]{:S(2)}) collective-permute-start(s16[16,1024]{1,0:T(8,128)(2,1)S(1)} %get-tuple-element.48), channel_id=1, source_target_pairs={{0,6},{1,7},{2,4},{3,5},{4,2},{5,3},{6,0},{7,1},{8,14},{9,15},{10,... | collective-permute-start | bytes 98312 | tf_op jit(solution)/shard_map/ppermute | solution.py:156
  24.9 50.3 %copy-start.2 = (f32[16,50,1024]{2,0,1:T(8,128)S(1)}, f32[16,50,1024]{2,0,1:T(8,128)}, u32[]{:S(2)}) copy-start(f32[16,50,1024]{2,0,1:T(8,128)} %param.11) | copy-start | bytes 9830404
  24.9 50.3 %copy-start.4 = (s32[4,8]{1,0:T(4,128)S(1)}, s32[4,8]{1,0:T(4,128)}, u32[]{:S(2)}) copy-start(s32[4,8]{1,0:T(4,128)} %refs_1_.1) | copy-start | bytes 388
  24.9 50.3 %copy-start.5 = (s32[4,8]{1,0:T(4,128)S(1)}, s32[4,8]{1,0:T(4,128)}, u32[]{:S(2)}) copy-start(s32[4,8]{1,0:T(4,128)} %refs_0_.1) | copy-start | bytes 388
  24.9 50.3 %copy-start.6 = (s32[4,8]{1,0:T(4,128)S(1)}, s32[4,8]{1,0:T(4,128)}, u32[]{:S(2)}) copy-start(s32[4,8]{1,0:T(4,128)} %refs_2_.1) | copy-start | bytes 388
  24.9 5.2 %collective-permute-start.6 = (s16[16,1024]{1,0:T(8,128)(2,1)S(1)}, s16[16,1024]{1,0:T(8,128)(2,1)S(1)}, u32[]{:S(2)}, u32[]{:S(2)}) collective-permute-start(s16[16,1024]{1,0:T(8,128)(2,1)S(1)} %get-tuple-element.49), channel_id=1, source_target_pairs={{0,7},{1,6},{2,5},{3,4},{4,3},{5,2},{6,1},{7,0},{8,15},{9,14},{10,... | collective-permute-start | bytes 98312 | tf_op jit(solution)/shard_map/ppermute | solution.py:156
  25.7 8.4 %collective-permute-start.8 = (s16[16,1024]{1,0:T(8,128)(2,1)S(1)}, s16[16,1024]{1,0:T(8,128)(2,1)S(1)}, u32[]{:S(2)}, u32[]{:S(2)}) collective-permute-start(s16[16,1024]{1,0:T(8,128)(2,1)S(1)} %get-tuple-element.51), channel_id=1, source_target_pairs={{0,8},{1,9},{2,10},{3,11},{4,12},{5,13},{6,14},{7,15},{8,0},{9,1},... | collective-permute-start | bytes 98312 | tf_op jit(solution)/shard_map/ppermute | solution.py:156
  27.3 9.8 %collective-permute-start.9 = (s16[16,1024]{1,0:T(8,128)(2,1)S(1)}, s16[16,1024]{1,0:T(8,128)(2,1)S(1)}, u32[]{:S(2)}, u32[]{:S(2)}) collective-permute-start(s16[16,1024]{1,0:T(8,128)(2,1)S(1)} %get-tuple-element.52), channel_id=1, source_target_pairs={{0,9},{1,8},{2,11},{3,10},{4,13},{5,12},{6,15},{7,14},{8,1},{9,0},... | collective-permute-start | bytes 98312 | tf_op jit(solution)/shard_map/ppermute | solution.py:156
  30.1 8.9 %collective-permute-start.10 = (s16[16,1024]{1,0:T(8,128)(2,1)S(1)}, s16[16,1024]{1,0:T(8,128)(2,1)S(1)}, u32[]{:S(2)}, u32[]{:S(2)}) collective-permute-start(s16[16,1024]{1,0:T(8,128)(2,1)S(1)} %get-tuple-element.53), channel_id=1, source_target_pairs={{0,10},{1,11},{2,8},{3,9},{4,14},{5,15},{6,12},{7,13},{8,2},{9,3},... | collective-permute-start | bytes 98312 | tf_op jit(solution)/shard_map/ppermute | solution.py:156
  30.2 9.3 %collective-permute-start.11 = (s16[16,1024]{1,0:T(8,128)(2,1)S(1)}, s16[16,1024]{1,0:T(8,128)(2,1)S(1)}, u32[]{:S(2)}, u32[]{:S(2)}) collective-permute-start(s16[16,1024]{1,0:T(8,128)(2,1)S(1)} %get-tuple-element.54), channel_id=1, source_target_pairs={{0,11},{1,10},{2,9},{3,8},{4,15},{5,14},{6,13},{7,12},{8,3},{9,2},... | collective-permute-start | bytes 98312 | tf_op jit(solution)/shard_map/ppermute | solution.py:156
  31.4 9.6 %collective-permute-start.12 = (s16[16,1024]{1,0:T(8,128)(2,1)S(1)}, s16[16,1024]{1,0:T(8,128)(2,1)S(1)}, u32[]{:S(2)}, u32[]{:S(2)}) collective-permute-start(s16[16,1024]{1,0:T(8,128)(2,1)S(1)} %get-tuple-element.55), channel_id=1, source_target_pairs={{0,12},{1,13},{2,14},{3,15},{4,8},{5,9},{6,10},{7,11},{8,4},{9,5},... | collective-permute-start | bytes 98312 | tf_op jit(solution)/shard_map/ppermute | solution.py:156
  34.2 9.2 %collective-permute-start.13 = (s16[16,1024]{1,0:T(8,128)(2,1)S(1)}, s16[16,1024]{1,0:T(8,128)(2,1)S(1)}, u32[]{:S(2)}, u32[]{:S(2)}) collective-permute-start(s16[16,1024]{1,0:T(8,128)(2,1)S(1)} %get-tuple-element.56), channel_id=1, source_target_pairs={{0,13},{1,12},{2,15},{3,14},{4,9},{5,8},{6,11},{7,10},{8,5},{9,4},... | collective-permute-start | bytes 98312 | tf_op jit(solution)/shard_map/ppermute | solution.py:156
  37.1 6.6 %collective-permute-start.14 = (s16[16,1024]{1,0:T(8,128)(2,1)S(1)}, s16[16,1024]{1,0:T(8,128)(2,1)S(1)}, u32[]{:S(2)}, u32[]{:S(2)}) collective-permute-start(s16[16,1024]{1,0:T(8,128)(2,1)S(1)} %get-tuple-element.57), channel_id=1, source_target_pairs={{0,14},{1,15},{2,12},{3,13},{4,10},{5,11},{6,8},{7,9},{8,6},{9,7},... | collective-permute-start | bytes 98312 | tf_op jit(solution)/shard_map/ppermute | solution.py:156
  39.0 6.5 %collective-permute-start.15 = (s16[16,1024]{1,0:T(8,128)(2,1)S(1)}, s16[16,1024]{1,0:T(8,128)(2,1)S(1)}, u32[]{:S(2)}, u32[]{:S(2)}) collective-permute-start(s16[16,1024]{1,0:T(8,128)(2,1)S(1)} %get-tuple-element.58), channel_id=1, source_target_pairs={{0,15},{1,14},{2,13},{3,12},{4,11},{5,10},{6,9},{7,8},{8,7},{9,6},... | collective-permute-start | bytes 98312 | tf_op jit(solution)/shard_map/ppermute | solution.py:156
  39.5 7.1 %collective-permute-start.17 = (s16[16,1024]{1,0:T(8,128)(2,1)S(1)}, s16[16,1024]{1,0:T(8,128)(2,1)S(1)}, u32[]{:S(2)}, u32[]{:S(2)}) collective-permute-start(s16[16,1024]{1,0:T(8,128)(2,1)S(1)} %get-tuple-element.60), channel_id=1, source_target_pairs={{0,16},{1,17},{2,18},{3,19},{4,20},{5,21},{6,22},{7,23},{8,24},{9,... | collective-permute-start | bytes 98312 | tf_op jit(solution)/shard_map/ppermute | solution.py:156
  41.0 9.3 %collective-permute-start.18 = (s16[16,1024]{1,0:T(8,128)(2,1)S(1)}, s16[16,1024]{1,0:T(8,128)(2,1)S(1)}, u32[]{:S(2)}, u32[]{:S(2)}) collective-permute-start(s16[16,1024]{1,0:T(8,128)(2,1)S(1)} %get-tuple-element.61), channel_id=1, source_target_pairs={{0,17},{1,16},{2,19},{3,18},{4,21},{5,20},{6,23},{7,22},{8,25},{9,... | collective-permute-start | bytes 98312 | tf_op jit(solution)/shard_map/ppermute | solution.py:156
  43.3 8.9 %collective-permute-start.19 = (s16[16,1024]{1,0:T(8,128)(2,1)S(1)}, s16[16,1024]{1,0:T(8,128)(2,1)S(1)}, u32[]{:S(2)}, u32[]{:S(2)}) collective-permute-start(s16[16,1024]{1,0:T(8,128)(2,1)S(1)} %get-tuple-element.62), channel_id=1, source_target_pairs={{0,18},{1,19},{2,16},{3,17},{4,22},{5,23},{6,20},{7,21},{8,26},{9,... | collective-permute-start | bytes 98312 | tf_op jit(solution)/shard_map/ppermute | solution.py:156
  43.7 10.6 %collective-permute-start.20 = (s16[16,1024]{1,0:T(8,128)(2,1)S(1)}, s16[16,1024]{1,0:T(8,128)(2,1)S(1)}, u32[]{:S(2)}, u32[]{:S(2)}) collective-permute-start(s16[16,1024]{1,0:T(8,128)(2,1)S(1)} %get-tuple-element.63), channel_id=1, source_target_pairs={{0,19},{1,18},{2,17},{3,16},{4,23},{5,22},{6,21},{7,20},{8,27},{9,... | collective-permute-start | bytes 98312 | tf_op jit(solution)/shard_map/ppermute | solution.py:156
  45.5 10.2 %collective-permute-start.21 = (s16[16,1024]{1,0:T(8,128)(2,1)S(1)}, s16[16,1024]{1,0:T(8,128)(2,1)S(1)}, u32[]{:S(2)}, u32[]{:S(2)}) collective-permute-start(s16[16,1024]{1,0:T(8,128)(2,1)S(1)} %get-tuple-element.64), channel_id=1, source_target_pairs={{0,20},{1,21},{2,22},{3,23},{4,16},{5,17},{6,18},{7,19},{8,28},{9,... | collective-permute-start | bytes 98312 | tf_op jit(solution)/shard_map/ppermute | solution.py:156
  46.6 10.8 %collective-permute-start.22 = (s16[16,1024]{1,0:T(8,128)(2,1)S(1)}, s16[16,1024]{1,0:T(8,128)(2,1)S(1)}, u32[]{:S(2)}, u32[]{:S(2)}) collective-permute-start(s16[16,1024]{1,0:T(8,128)(2,1)S(1)} %get-tuple-element.65), channel_id=1, source_target_pairs={{0,21},{1,20},{2,23},{3,22},{4,17},{5,16},{6,19},{7,18},{8,29},{9,... | collective-permute-start | bytes 98312 | tf_op jit(solution)/shard_map/ppermute | solution.py:156
  50.2 7.2 %collective-permute-start.23 = (s16[16,1024]{1,0:T(8,128)(2,1)S(1)}, s16[16,1024]{1,0:T(8,128)(2,1)S(1)}, u32[]{:S(2)}, u32[]{:S(2)}) collective-permute-start(s16[16,1024]{1,0:T(8,128)(2,1)S(1)} %get-tuple-element.66), channel_id=1, source_target_pairs={{0,22},{1,23},{2,20},{3,21},{4,18},{5,19},{6,16},{7,17},{8,30},{9,... | collective-permute-start | bytes 98312 | tf_op jit(solution)/shard_map/ppermute | solution.py:156
  52.2 8.3 %collective-permute-start.24 = (s16[16,1024]{1,0:T(8,128)(2,1)S(1)}, s16[16,1024]{1,0:T(8,128)(2,1)S(1)}, u32[]{:S(2)}, u32[]{:S(2)}) collective-permute-start(s16[16,1024]{1,0:T(8,128)(2,1)S(1)} %get-tuple-element.67), channel_id=1, source_target_pairs={{0,23},{1,22},{2,21},{3,20},{4,19},{5,18},{6,17},{7,16},{8,31},{9,... | collective-permute-start | bytes 98312 | tf_op jit(solution)/shard_map/ppermute | solution.py:156
  54.3 7.5 %collective-permute-start.26 = (s16[16,1024]{1,0:T(8,128)(2,1)S(1)}, s16[16,1024]{1,0:T(8,128)(2,1)S(1)}, u32[]{:S(2)}, u32[]{:S(2)}) collective-permute-start(s16[16,1024]{1,0:T(8,128)(2,1)S(1)} %get-tuple-element.69), channel_id=1, source_target_pairs={{0,24},{1,25},{2,26},{3,27},{4,28},{5,29},{6,30},{7,31},{8,16},{9,... | collective-permute-start | bytes 98312 | tf_op jit(solution)/shard_map/ppermute | solution.py:156
  55.8 9.7 %collective-permute-start.27 = (s16[16,1024]{1,0:T(8,128)(2,1)S(1)}, s16[16,1024]{1,0:T(8,128)(2,1)S(1)}, u32[]{:S(2)}, u32[]{:S(2)}) collective-permute-start(s16[16,1024]{1,0:T(8,128)(2,1)S(1)} %get-tuple-element.70), channel_id=1, source_target_pairs={{0,25},{1,24},{2,27},{3,26},{4,29},{5,28},{6,31},{7,30},{8,17},{9,... | collective-permute-start | bytes 98312 | tf_op jit(solution)/shard_map/ppermute | solution.py:156
  57.4 10.8 %collective-permute-start.28 = (s16[16,1024]{1,0:T(8,128)(2,1)S(1)}, s16[16,1024]{1,0:T(8,128)(2,1)S(1)}, u32[]{:S(2)}, u32[]{:S(2)}) collective-permute-start(s16[16,1024]{1,0:T(8,128)(2,1)S(1)} %get-tuple-element.71), channel_id=1, source_target_pairs={{0,26},{1,27},{2,24},{3,25},{4,30},{5,31},{6,28},{7,29},{8,18},{9,... | collective-permute-start | bytes 98312 | tf_op jit(solution)/shard_map/ppermute | solution.py:156
  57.4 12.9 %collective-permute-start.29 = (s16[16,1024]{1,0:T(8,128)(2,1)S(1)}, s16[16,1024]{1,0:T(8,128)(2,1)S(1)}, u32[]{:S(2)}, u32[]{:S(2)}) collective-permute-start(s16[16,1024]{1,0:T(8,128)(2,1)S(1)} %get-tuple-element.72), channel_id=1, source_target_pairs={{0,27},{1,26},{2,25},{3,24},{4,31},{5,30},{6,29},{7,28},{8,19},{9,... | collective-permute-start | bytes 98312 | tf_op jit(solution)/shard_map/ppermute | solution.py:156
  60.6 9.8 %collective-permute-start.30 = (s16[16,1024]{1,0:T(8,128)(2,1)S(1)}, s16[16,1024]{1,0:T(8,128)(2,1)S(1)}, u32[]{:S(2)}, u32[]{:S(2)}) collective-permute-start(s16[16,1024]{1,0:T(8,128)(2,1)S(1)} %get-tuple-element.73), channel_id=1, source_target_pairs={{0,28},{1,29},{2,30},{3,31},{4,24},{5,25},{6,26},{7,27},{8,20},{9,... | collective-permute-start | bytes 98312 | tf_op jit(solution)/shard_map/ppermute | solution.py:156
  61.8 8.6 %collective-permute-start.31 = (s16[16,1024]{1,0:T(8,128)(2,1)S(1)}, s16[16,1024]{1,0:T(8,128)(2,1)S(1)}, u32[]{:S(2)}, u32[]{:S(2)}) collective-permute-start(s16[16,1024]{1,0:T(8,128)(2,1)S(1)} %get-tuple-element.74), channel_id=1, source_target_pairs={{0,29},{1,28},{2,31},{3,30},{4,25},{5,24},{6,27},{7,26},{8,21},{9,... | collective-permute-start | bytes 98312 | tf_op jit(solution)/shard_map/ppermute | solution.py:156
  65.4 7.5 %collective-permute-start.32 = (s16[16,1024]{1,0:T(8,128)(2,1)S(1)}, s16[16,1024]{1,0:T(8,128)(2,1)S(1)}, u32[]{:S(2)}, u32[]{:S(2)}) collective-permute-start(s16[16,1024]{1,0:T(8,128)(2,1)S(1)} %get-tuple-element.75), channel_id=1, source_target_pairs={{0,30},{1,31},{2,28},{3,29},{4,26},{5,27},{6,24},{7,25},{8,22},{9,... | collective-permute-start | bytes 98312 | tf_op jit(solution)/shard_map/ppermute | solution.py:156
  68.3 6.9 %collective-permute-start.33 = (s16[16,1024]{1,0:T(8,128)(2,1)S(1)}, s16[16,1024]{1,0:T(8,128)(2,1)S(1)}, u32[]{:S(2)}, u32[]{:S(2)}) collective-permute-start(s16[16,1024]{1,0:T(8,128)(2,1)S(1)} %get-tuple-element.76), channel_id=1, source_target_pairs={{0,31},{1,30},{2,29},{3,28},{4,27},{5,26},{6,25},{7,24},{8,23},{9,... | collective-permute-start | bytes 98312 | tf_op jit(solution)/shard_map/ppermute | solution.py:156

commit v6 on v5

--- a/solution.py
+++ b/solution.py
@@ -10,6 +10,7 @@
 SCALE_SHIFT = 8192
 SCALE_BITS = 16
 LANES = 128
+CORES = 2
 
 
 def encode(values):
@@ -68,24 +69,25 @@
 def product_kernel(rows, tile, *rest):
     outgoing, product = rest[:-1], rest[-1]
     grp = lax.axis_index("grp")
-    owner_rows = outgoing[0].shape[0]
+    chip_rows = outgoing[0].shape[0]
     product[...] = jnp.dot(rows[...], tile[0], preferred_element_type=jnp.float32)
     for step, coded in enumerate(outgoing):
-        first = pl.multiple_of(jnp.bitwise_xor(grp, step) * owner_rows, owner_rows)
-        head, tail = encode(product[pl.ds(first, owner_rows), :])
+        chip = jnp.bitwise_xor(grp // CORES, step)
+        first = pl.multiple_of(chip * chip_rows, chip_rows)
+        head, tail = encode(product[pl.ds(first, chip_rows), :])
         coded[:, :LANES] = head
         coded[:, LANES:] = tail
 
 
-def contract(rows, tile, owner_rows):
+def contract(rows, tile, chip_rows):
     group_rows, tile_width = rows.shape[0], tile.shape[2]
-    owners = group_rows // owner_rows
+    chips = group_rows // chip_rows
     vmem = pl.BlockSpec(memory_space=pltpu.VMEM)
     return pl.pallas_call(
         product_kernel,
-        out_shape=[jax.ShapeDtypeStruct((owner_rows, tile_width), jnp.int16)] * owners,
+        out_shape=[jax.ShapeDtypeStruct((chip_rows, tile_width), jnp.int16)] * chips,
         in_specs=[vmem, vmem],
-        out_specs=[vmem] * owners,
+        out_specs=[vmem] * chips,
         scratch_shapes=[pltpu.VMEM((group_rows, tile_width), jnp.float32)],
         compiler_params=pltpu.CompilerParams(vmem_limit_bytes=32 * 1024 * 1024),
         cost_estimate=pl.CostEstimate(
@@ -97,11 +99,39 @@
     )(rows, tile)
 
 
+def other_core_kernel(*refs):
+    blocks, (halves, sems) = refs[:-2], refs[-2:]
+    owner_rows = blocks[0].shape[0] // CORES
+    other = 1 - lax.axis_index("grp") % CORES
+    first = pl.multiple_of(other * owner_rows, owner_rows)
+    copies = []
+    for index, coded in enumerate(blocks):
+        place = halves.at[pl.ds(index * owner_rows, owner_rows)]
+        copies.append(pltpu.make_async_copy(coded.at[pl.ds(first, owner_rows)], place, sems.at[index]))
+    for copy in copies:
+        copy.start()
+    for copy in copies:
+        copy.wait()
+
+
+def other_core_rows(blocks):
+    chip_rows, tile_width = blocks[0].shape
+    vmem = pl.BlockSpec(memory_space=pltpu.VMEM)
+    return pl.pallas_call(
+        other_core_kernel,
+        out_shape=jax.ShapeDtypeStruct((len(blocks) * chip_rows // CORES, tile_width), blocks[0].dtype),
+        in_specs=[vmem] * len(blocks),
+        out_specs=vmem,
+        scratch_shapes=[pltpu.SemaphoreType.DMA((len(blocks),))],
+        name="rows_of_other_core",
+    )(*blocks)
+
+
 def add_kernel(pieces, tile_ab, tile_cd, pair_screen, *rest):
-    blocks, (residual_in, residual, held, in_sems, out_sems) = rest[:-5], rest[-5:]
+    blocks, (swapped, residual_in, residual, held, in_sems, out_sems) = rest[:-6], rest[-6:]
     blk, grp = lax.axis_index("blk"), lax.axis_index("grp")
-    ab_tiles = residual.shape[0]
-    columns, grp_count = tile_ab.shape
+    ab_tiles, owner_rows, _ = residual.shape
+    chips = tile_ab.shape[1] // CORES
     bounds = [ab_tiles * piece // pieces for piece in range(pieces + 1)]
     parts = [pl.ds(low, high - low) for low, high in zip(bounds[:-1], bounds[1:])]
     arrivals = [pltpu.make_async_copy(residual_in.at[part], held.at[part], in_sems.at[i]) for i, part in enumerate(parts)]
@@ -111,14 +141,18 @@
     for copy in arrivals:
         copy.wait()
 
-    for index, coded in enumerate(blocks):
-        p = jnp.bitwise_xor(blk, index // grp_count)
-        g = jnp.bitwise_xor(grp, index % grp_count)
-
+    def add_tile(p, g, rows):
         @pl.when(pair_screen[tile_cd[p, g], grp] != 0)
         def _():
             ab = tile_ab[p, g]
-            held[ab] = held[ab] + decode(coded[...])
+            held[ab] = held[ab] + decode(rows())
+
+    own_first = pl.multiple_of(grp % CORES * owner_rows, owner_rows)
+    for index, coded in enumerate(blocks):
+        p = jnp.bitwise_xor(blk, index // chips)
+        g = jnp.bitwise_xor(grp, index % chips * CORES)
+        add_tile(p, g, lambda: coded[pl.ds(own_first, owner_rows), :])
+        add_tile(p, jnp.bitwise_xor(g, 1), lambda: swapped[pl.ds(index * owner_rows, owner_rows), :])
 
     for copy in leaves:
         copy.start()
@@ -126,14 +160,14 @@
         copy.wait()
 
 
-def add_blocks(tile_ab, tile_cd, pair_screen, blocks, residual_in):
+def add_blocks(tile_ab, tile_cd, pair_screen, blocks, swapped, residual_in):
     pieces = 5
     smem = pl.BlockSpec(memory_space=pltpu.SMEM)
     vmem = pl.BlockSpec(memory_space=pltpu.VMEM)
     return pl.pallas_call(
         lambda *refs: add_kernel(pieces, *refs),
         out_shape=jax.ShapeDtypeStruct(residual_in.shape, residual_in.dtype),
-        in_specs=[smem, smem, smem] + [vmem] * len(blocks) + [pl.BlockSpec(memory_space=pl.ANY)],
+        in_specs=[smem, smem, smem] + [vmem] * (len(blocks) + 1) + [pl.BlockSpec(memory_space=pl.ANY)],
         out_specs=pl.BlockSpec(memory_space=pl.ANY),
         scratch_shapes=[
             pltpu.VMEM(residual_in.shape, residual_in.dtype),
@@ -142,7 +176,7 @@
         ],
         compiler_params=pltpu.CompilerParams(vmem_limit_bytes=32 * 1024 * 1024),
         name="add_contributions",
-    )(tile_ab, tile_cd, pair_screen, *blocks, residual_in)
+    )(tile_ab, tile_cd, pair_screen, *blocks, swapped, residual_in)
 
 
 def shards(amplitudes, pair_screen, integrals, tile_ab, tile_cd, residual_in):
@@ -158,15 +192,17 @@
     picked = pick(tile_cd, amplitudes)
     rows_in = [picked[0]] + [swap(picked[step], step, 0) for step in range(1, blk_count)]
     blocks = []
+    chips = grp_count // CORES
     for blk_step in range(blk_count):
-        coded = contract(rows_in[blk_step], integrals, owner_rows)
+        coded = contract(rows_in[blk_step], integrals, CORES * owner_rows)
         arrived = {}
-        for grp_step in reversed(range(grp_count)):
-            own = blk_step == 0 and grp_step == 0
-            arrived[grp_step] = coded[grp_step] if own else swap(coded[grp_step], blk_step, grp_step)
-        blocks += [arrived[grp_step] for grp_step in range(grp_count)]
+        for chip_step in reversed(range(chips)):
+            own = blk_step == 0 and chip_step == 0
+            arrived[chip_step] = coded[chip_step] if own else swap(coded[chip_step], blk_step, CORES * chip_step)
+        blocks += [arrived[chip_step] for chip_step in range(chips)]
+    swapped = swap(other_core_rows(blocks), 0, 1)
     by_tile = jnp.transpose(residual_in, (1, 0, 2))
-    return jnp.transpose(add_blocks(tile_ab, tile_cd, pair_screen, blocks, by_tile), (1, 0, 2))
+    return jnp.transpose(add_blocks(tile_ab, tile_cd, pair_screen, blocks, swapped, by_tile), (1, 0, 2))
 
 
 def solution(mesh):

time: 82.1 us -> 66.9 us (0.81)
  starting transfers between devices: 56.4 us -> 32.9 us
  local copies, waits for them, and re-layouts: 2.56 us -> 8.85 us
  Pallas kernels: 11.6 us -> 14.4 us
    ppermute x34 -> x19, starting transfers between devices: 56.4 us -> 32.9 us  [swap(): return lax.ppermute(value, ('blk', 'grp'), pairs)]
    unnamed x14 -> x42, local copies, waits for them, and re-layouts: 2.56 us -> 8.85 us
    pallas_call x4 -> x5, Pallas kernels: 2.78 us -> 5.66 us  [the longest x1 2.85 us: other_core_rows(): pl.pallas_call(other_core_kernel, out_shape=jax.ShapeDtypeStruct((len(blo...]
    ppermute x34 -> x19, waiting for transfers between devices: 10.4 us -> 9.66 us  [swap(): return lax.ppermute(value, ('blk', 'grp'), pairs)]
  transfers between devices with their start and end apart: 34 -> 19, of which waited for: 6 -> 4; matrix products, arithmetic and copies ran while one was open for 0% -> 0% of each run, Pallas kernels for 3% -> 4%
where the time goes in v6:
time: 66.9 us; the launch traced here: 66.1 us
  starting transfers between devices  32.9 us (49%)
  Pallas kernels  14.4 us (22%)
  waiting for transfers between devices  9.66 us (14%)
  local copies, waits for them, and re-layouts  8.85 us (13%)
    ppermute x19, starting transfers between devices, swap(): return lax.ppermute(value, ('blk', 'grp'), pairs)  32.9 us
    ppermute x19, waiting for transfers between devices, swap(): return lax.ppermute(value, ('blk', 'grp'), pairs)  9.66 us
    unnamed x42, local copies, waits for them, and re-layouts  8.85 us
    pallas_call x1, Pallas kernels, add_blocks(): pl.pallas_call(lambda *refs: add_kernel(pieces, *refs), out_shape=jax.Sha...  5.89 us
    pallas_call x1, Pallas kernels, pick(): pl.pallas_call(pick_kernel, out_shape=[block] * columns, in_specs=[pl.Blo...  2.87 us
    pallas_call x1, Pallas kernels, other_core_rows(): pl.pallas_call(other_core_kernel, out_shape=jax.ShapeDtypeStruct((len(blo...  2.85 us
    pallas_call x4, Pallas kernels, contract(): pl.pallas_call(product_kernel, out_shape=[jax.ShapeDtypeStruct((chip_rows...  2.81 us
  transfers between devices with their start and end apart: 19, of which 4 were waited for; matrix products, arithmetic and copies ran while one was open for 0% of the time, Pallas kernels for 4%

profile of v6, /device:TPU:0, one launch (start us, length us, event | category | flops | bytes accessed | tf_op | source)
XLA Modules:
  0.0 66.1 jit_solution(5899255483485295292)
XLA Ops:
  0.0 2.9 %pick_cd_blocks.1 = (bf16[128,1024]{1,0:T(8,128)(2,1)}, bf16[128,1024]{1,0:T(8,128)(2,1)}, bf16[128,1024]{1,0:T(8,128)(2,1)}, bf16[128,1024]{1,0:T(8,128)(2,1)}) custom-call(s32[4,8]{1,0:T(4,128)} %refs_1_.1, bf16[4,128,1024]{2,1,0:T(8,128)(2,1)} %amplitudes.1), custom_call_target="tpu_custom_call" | custom-call | tf_op jit(solution)/shard_map/pick_cd_blocks/pallas_call | solution.py:59
  2.9 3.0 %collective-permute-start.3 = (bf16[128,1024]{1,0:T(8,128)(2,1)}, bf16[128,1024]{1,0:T(8,128)(2,1)S(1)}, u32[]{:S(2)}, u32[]{:S(2)}) collective-permute-start(bf16[128,1024]{1,0:T(8,128)(2,1)} %get-tuple-element.30), channel_id=1, source_target_pairs={{0,8},{1,9},{2,10},{3,11},{4,12},{5,13},{6,14},{7,15},{8,0},{9,1},... | collective-permute-start | bytes 786440 | tf_op jit(solution)/shard_map/ppermute | solution.py:190
  5.9 1.5 %collective-permute-start.8 = (bf16[128,1024]{1,0:T(8,128)(2,1)}, bf16[128,1024]{1,0:T(8,128)(2,1)S(1)}, u32[]{:S(2)}, u32[]{:S(2)}) collective-permute-start(bf16[128,1024]{1,0:T(8,128)(2,1)} %get-tuple-element.35), channel_id=1, source_target_pairs={{0,16},{1,17},{2,18},{3,19},{4,20},{5,21},{6,22},{7,23},{8,24},{9,... | collective-permute-start | bytes 786440 | tf_op jit(solution)/shard_map/ppermute | solution.py:190
  7.4 0.0 collective-permute-start.13
  7.4 1.6 %copy-done = bf16[1,1024,1024]{2,1,0:T(8,128)(2,1)S(1)} copy-done((bf16[1,1024,1024]{2,1,0:T(8,128)(2,1)S(1)}, bf16[1,1024,1024]{2,1,0:T(8,128)(2,1)}, u32[]{:S(2)}) %copy-start) | copy-done | bytes 2097176
  9.0 0.9 %copy-done.17 = bf16[128,1024]{1,0:T(8,128)(2,1)S(1)} copy-done((bf16[128,1024]{1,0:T(8,128)(2,1)S(1)}, bf16[128,1024]{1,0:T(8,128)(2,1)}, u32[]{:S(2)}) %copy-start.17) | copy-done | bytes 262168
  10.0 0.7 %contract_group.4 = (s16[32,1024]{1,0:T(8,128)(2,1)S(1)}, s16[32,1024]{1,0:T(8,128)(2,1)S(1)}, s16[32,1024]{1,0:T(8,128)(2,1)S(1)}, s16[32,1024]{1,0:T(8,128)(2,1)S(1)}) custom-call(bf16[128,1024]{1,0:T(8,128)(2,1)S(1)} %copy-done.17, bf16[1,1024,1024]{2,1,0:T(8,128)(2,1)S(1)} %copy-done), custom_call_target="tpu_custom_call" | custom-call | flops 268435456 | bytes 2097152 | tf_op jit(solution)/shard_map/contract_group/pallas_call | solution.py:86
  10.7 0.6 copy-done.3
  11.3 2.1 %collective-permute-start = (s16[32,1024]{1,0:T(8,128)(2,1)S(1)}, s16[32,1024]{1,0:T(8,128)(2,1)S(1)}, u32[]{:S(2)}, u32[]{:S(2)}) collective-permute-start(s16[32,1024]{1,0:T(8,128)(2,1)S(1)} %get-tuple-element.27), channel_id=1, source_target_pairs={{0,2},{1,3},{2,0},{3,1},{4,6},{5,7},{6,4},{7,5},{8,10},{9,11},{10,... | collective-permute-start | bytes 196616 | tf_op jit(solution)/shard_map/ppermute | solution.py:190
  13.4 2.6 %collective-permute-start.1 = (s16[32,1024]{1,0:T(8,128)(2,1)S(1)}, s16[32,1024]{1,0:T(8,128)(2,1)S(1)}, u32[]{:S(2)}, u32[]{:S(2)}) collective-permute-start(s16[32,1024]{1,0:T(8,128)(2,1)S(1)} %get-tuple-element.28), channel_id=1, source_target_pairs={{0,4},{1,5},{2,6},{3,7},{4,0},{5,1},{6,2},{7,3},{8,12},{9,13},{10,... | collective-permute-start | bytes 196616 | tf_op jit(solution)/shard_map/ppermute | solution.py:190
  16.0 0.0 collective-permute-done.3.rows
  16.0 1.5 %collective-permute-start.2 = (s16[32,1024]{1,0:T(8,128)(2,1)S(1)}, s16[32,1024]{1,0:T(8,128)(2,1)S(1)}, u32[]{:S(2)}, u32[]{:S(2)}) collective-permute-start(s16[32,1024]{1,0:T(8,128)(2,1)S(1)} %get-tuple-element.29), channel_id=1, source_target_pairs={{0,6},{1,7},{2,4},{3,5},{4,2},{5,3},{6,0},{7,1},{8,14},{9,15},{10,... | collective-permute-start | bytes 196616 | tf_op jit(solution)/shard_map/ppermute | solution.py:190
  17.4 0.7 %contract_group.5 = (s16[32,1024]{1,0:T(8,128)(2,1)S(1)}, s16[32,1024]{1,0:T(8,128)(2,1)S(1)}, s16[32,1024]{1,0:T(8,128)(2,1)S(1)}, s16[32,1024]{1,0:T(8,128)(2,1)S(1)}) custom-call(bf16[128,1024]{1,0:T(8,128)(2,1)S(1)} %collective-permute-done.3.rows, bf16[1,1024,1024]{2,1,0:T(8,128)(2,1)S(1)} %copy-done.1), custom_call_target="tpu_custom_call" | custom-call | flops 268435456 | bytes 2097152 | tf_op jit(solution)/shard_map/contract_group/pallas_call | solution.py:86
  18.1 0.0 copy-start.2
  18.2 0.0 copy-start.18
  18.2 0.0 copy-start.19
  18.2 0.0 copy-start.20
  18.2 0.0 collective-permute-done.refs_1_.refs_4_
  18.2 1.6 %collective-permute-start.4 = (s16[32,1024]{1,0:T(8,128)(2,1)S(1)}, s16[32,1024]{1,0:T(8,128)(2,1)S(1)}, u32[]{:S(2)}, u32[]{:S(2)}) collective-permute-start(s16[32,1024]{1,0:T(8,128)(2,1)S(1)} %get-tuple-element.31), channel_id=1, source_target_pairs={{0,8},{1,9},{2,10},{3,11},{4,12},{5,13},{6,14},{7,15},{8,0},{9,1},... | collective-permute-start | bytes 196616 | tf_op jit(solution)/shard_map/ppermute | solution.py:190
  19.8 0.0 collective-permute-done.8.rows
  19.8 0.0 collective-permute-start.5
  19.8 0.7 %contract_group.6 = (s16[32,1024]{1,0:T(8,128)(2,1)S(1)}, s16[32,1024]{1,0:T(8,128)(2,1)S(1)}, s16[32,1024]{1,0:T(8,128)(2,1)S(1)}, s16[32,1024]{1,0:T(8,128)(2,1)S(1)}) custom-call(bf16[128,1024]{1,0:T(8,128)(2,1)S(1)} %collective-permute-done.8.rows, bf16[1,1024,1024]{2,1,0:T(8,128)(2,1)S(1)} %copy-done.1), custom_call_target="tpu_custom_call" | custom-call | flops 268435456 | bytes 2097152 | tf_op jit(solution)/shard_map/contract_group/pallas_call | solution.py:86
  20.5 0.0 collective-permute-done.1.refs_2_.refs_5_
  20.5 0.0 copy-start.7
  20.5 4.5 %collective-permute-start.6 = (s16[32,1024]{1,0:T(8,128)(2,1)S(1)}, s16[32,1024]{1,0:T(8,128)(2,1)S(1)}, u32[]{:S(2)}, u32[]{:S(2)}) collective-permute-start(s16[32,1024]{1,0:T(8,128)(2,1)S(1)} %get-tuple-element.33), channel_id=1, source_target_pairs={{0,12},{1,13},{2,14},{3,15},{4,8},{5,9},{6,10},{7,11},{8,4},{9,5},... | collective-permute-start | bytes 196616 | tf_op jit(solution)/shard_map/ppermute | solution.py:190
  25.1 0.0 collective-permute-done.2.refs_3_.refs_6_
  25.1 0.8 %collective-permute-start.7 = (s16[32,1024]{1,0:T(8,128)(2,1)S(1)}, s16[32,1024]{1,0:T(8,128)(2,1)}, u32[]{:S(2)}, u32[]{:S(2)}) collective-permute-start(s16[32,1024]{1,0:T(8,128)(2,1)S(1)} %get-tuple-element.34), channel_id=1, source_target_pairs={{0,14},{1,15},{2,12},{3,13},{4,10},{5,11},{6,8},{7,9},{8,6},{9,7},... | collective-permute-start | bytes 196616 | tf_op jit(solution)/shard_map/ppermute | solution.py:190
  25.8 0.0 collective-permute-done.13.rows
  25.8 1.5 %collective-permute-start.9 = (s16[32,1024]{1,0:T(8,128)(2,1)S(1)}, s16[32,1024]{1,0:T(8,128)(2,1)}, u32[]{:S(2)}, u32[]{:S(2)}) collective-permute-start(s16[32,1024]{1,0:T(8,128)(2,1)S(1)} %get-tuple-element.36), channel_id=1, source_target_pairs={{0,16},{1,17},{2,18},{3,19},{4,20},{5,21},{6,22},{7,23},{8,24},{9,... | collective-permute-start | bytes 196616 | tf_op jit(solution)/shard_map/ppermute | solution.py:190
  27.4 0.0 collective-permute-done.4.refs_4_.refs_7_
  27.4 0.0 collective-permute-start.10
  27.4 0.0 collective-permute-done.5.refs_5_.refs_8_
  27.4 0.0 copy-start.13
  27.4 4.5 %collective-permute-start.11 = (s16[32,1024]{1,0:T(8,128)(2,1)S(1)}, s16[32,1024]{1,0:T(8,128)(2,1)}, u32[]{:S(2)}, u32[]{:S(2)}) collective-permute-start(s16[32,1024]{1,0:T(8,128)(2,1)S(1)} %get-tuple-element.38), channel_id=1, source_target_pairs={{0,20},{1,21},{2,22},{3,23},{4,16},{5,17},{6,18},{7,19},{8,28},{9,... | collective-permute-start | bytes 196616 | tf_op jit(solution)/shard_map/ppermute | solution.py:190
  31.9 0.7 %contract_group.7 = (s16[32,1024]{1,0:T(8,128)(2,1)S(1)}, s16[32,1024]{1,0:T(8,128)(2,1)S(1)}, s16[32,1024]{1,0:T(8,128)(2,1)S(1)}, s16[32,1024]{1,0:T(8,128)(2,1)S(1)}) custom-call(bf16[128,1024]{1,0:T(8,128)(2,1)S(1)} %collective-permute-done.13.rows, bf16[1,1024,1024]{2,1,0:T(8,128)(2,1)S(1)} %copy-done.1), custom_call_target="tpu_custom_call" | custom-call | flops 268435456 | bytes 2097152 | tf_op jit(solution)/shard_map/contract_group/pallas_call | solution.py:86
  32.6 0.0 copy-done.11
  32.6 0.0 collective-permute-done.6.refs_6_.refs_9_
  32.7 0.6 copy-done.15
  33.3 0.7 %collective-permute-start.12 = (s16[32,1024]{1,0:T(8,128)(2,1)S(1)}, s16[32,1024]{1,0:T(8,128)(2,1)}, u32[]{:S(2)}, u32[]{:S(2)}) collective-permute-start(s16[32,1024]{1,0:T(8,128)(2,1)S(1)} %get-tuple-element.39), channel_id=1, source_target_pairs={{0,22},{1,23},{2,20},{3,21},{4,18},{5,19},{6,16},{7,17},{8,30},{9,... | collective-permute-start | bytes 196616 | tf_op jit(solution)/shard_map/ppermute | solution.py:190
  34.0 0.0 collective-permute-done.7.refs_7_.refs_10_
  34.0 2.4 %collective-permute-start.14 = (s16[32,1024]{1,0:T(8,128)(2,1)S(1)}, s16[32,1024]{1,0:T(8,128)(2,1)}, u32[]{:S(2)}, u32[]{:S(2)}) collective-permute-start(s16[32,1024]{1,0:T(8,128)(2,1)S(1)} %get-tuple-element.41), channel_id=1, source_target_pairs={{0,24},{1,25},{2,26},{3,27},{4,28},{5,29},{6,30},{7,31},{8,16},{9,... | collective-permute-start | bytes 196616 | tf_op jit(solution)/shard_map/ppermute | solution.py:190
  36.4 0.0 collective-permute-done.9.refs_8_.refs_11_
  36.4 0.0 collective-permute-start.15
  36.4 0.0 collective-permute-done.10.refs_9_.refs_12_
  36.4 5.7 %collective-permute-start.16 = (s16[32,1024]{1,0:T(8,128)(2,1)S(1)}, s16[32,1024]{1,0:T(8,128)(2,1)}, u32[]{:S(2)}, u32[]{:S(2)}) collective-permute-start(s16[32,1024]{1,0:T(8,128)(2,1)S(1)} %get-tuple-element.43), channel_id=1, source_target_pairs={{0,28},{1,29},{2,30},{3,31},{4,24},{5,25},{6,26},{7,27},{8,20},{9,... | collective-permute-start | bytes 196616 | tf_op jit(solution)/shard_map/ppermute | solution.py:190
  42.1 0.0 collective-permute-done.11.refs_10_.refs_13_
  42.1 0.4 collective-permute-start.17
  42.5 0.0 collective-permute-done.12.refs_11_.refs_14_
  42.5 0.0 collective-permute-done.14.refs_12_.refs_15_
  42.5 0.1 collective-permute-done.15.refs_13_.refs_16_
  42.6 2.5 %collective-permute-done.16.refs_14_.refs_17_ = s16[32,1024]{1,0:T(8,128)(2,1)} collective-permute-done((s16[32,1024]{1,0:T(8,128)(2,1)S(1)}, s16[32,1024]{1,0:T(8,128)(2,1)}, u32[]{:S(2)}, u32[]{:S(2)}) %collective-permute-start.16) | collective-permute-done | bytes 65568 | tf_op jit(solution)/shard_map/ppermute | solution.py:190
  45.1 4.9 %collective-permute-done.17.refs_15_.refs_18_ = s16[32,1024]{1,0:T(8,128)(2,1)} collective-permute-done((s16[32,1024]{1,0:T(8,128)(2,1)S(1)}, s16[32,1024]{1,0:T(8,128)(2,1)}, u32[]{:S(2)}, u32[]{:S(2)}) %collective-permute-start.17) | collective-permute-done | bytes 65568 | tf_op jit(solution)/shard_map/ppermute | solution.py:190
  50.1 0.0 copy-done.9
  50.1 2.9 %rows_of_other_core.1 = s16[256,1024]{1,0:T(8,128)(2,1)} custom-call(s16[32,1024]{1,0:T(8,128)(2,1)} %copy-done.3, s16[32,1024]{1,0:T(8,128)(2,1)} %copy-done.5, s16[32,1024]{1,0:T(8,128)(2,1)} %copy-done.7, s16[32,1024]{1,0:T(8,128)(2,1)} %copy-done.9, s16[32,1024]{1,0:T(8,128)(2,1)} %copy-done.11, s16[32,1024]{1,0:T(8,128)(2,1)} %copy-done.13, ...), custom_call_target="tpu_custom_call" | custom-call | tf_op jit(solution)/shard_map/rows_of_other_core/pallas_call | solution.py:120
  52.9 0.1 collective-permute-start.18
  53.0 2.1 %collective-permute-done.18.refs_19_ = s16[256,1024]{1,0:T(8,128)(2,1)S(1)} collective-permute-done((s16[256,1024]{1,0:T(8,128)(2,1)}, s16[256,1024]{1,0:T(8,128)(2,1)S(1)}, u32[]{:S(2)}, u32[]{:S(2)}) %collective-permute-start.18) | collective-permute-done | bytes 524320 | tf_op jit(solution)/shard_map/ppermute | solution.py:190
  55.1 0.0 copy-done.2
  55.1 0.8 %copy-done.6 = s16[32,1024]{1,0:T(8,128)(2,1)S(1)} copy-done((s16[32,1024]{1,0:T(8,128)(2,1)S(1)}, s16[32,1024]{1,0:T(8,128)(2,1)}, u32[]{:S(2)}) %copy-start.6) | copy-done | bytes 65560
  56.0 0.8 %copy-done.8 = s16[32,1024]{1,0:T(8,128)(2,1)S(1)} copy-done((s16[32,1024]{1,0:T(8,128)(2,1)S(1)}, s16[32,1024]{1,0:T(8,128)(2,1)}, u32[]{:S(2)}) %copy-start.8) | copy-done | bytes 65560
  56.8 0.8 %copy-done.10 = s16[32,1024]{1,0:T(8,128)(2,1)S(1)} copy-done((s16[32,1024]{1,0:T(8,128)(2,1)S(1)}, s16[32,1024]{1,0:T(8,128)(2,1)}, u32[]{:S(2)}) %copy-start.10) | copy-done | bytes 65560
  57.7 0.8 %copy-done.12 = s16[32,1024]{1,0:T(8,128)(2,1)S(1)} copy-done((s16[32,1024]{1,0:T(8,128)(2,1)S(1)}, s16[32,1024]{1,0:T(8,128)(2,1)}, u32[]{:S(2)}) %copy-start.12) | copy-done | bytes 65560
  58.5 0.8 %copy-done.14 = s16[32,1024]{1,0:T(8,128)(2,1)S(1)} copy-done((s16[32,1024]{1,0:T(8,128)(2,1)S(1)}, s16[32,1024]{1,0:T(8,128)(2,1)}, u32[]{:S(2)}) %copy-start.14) | copy-done | bytes 65560
  59.3 0.8 %copy-done.16 = s16[32,1024]{1,0:T(8,128)(2,1)S(1)} copy-done((s16[32,1024]{1,0:T(8,128)(2,1)S(1)}, s16[32,1024]{1,0:T(8,128)(2,1)}, u32[]{:S(2)}) %copy-start.16) | copy-done | bytes 65560
  60.2 5.9 %add_contributions.1 = f32[50,16,1024]{2,1,0:T(8,128)} custom-call(s32[4,8]{1,0:T(4,128)S(1)} %copy-done.19, s32[4,8]{1,0:T(4,128)S(1)} %copy-done.18, s32[4,8]{1,0:T(4,128)S(1)} %copy-done.20, s16[32,1024]{1,0:T(8,128)(2,1)S(1)} %copy-done.4, s16[32,1024]{1,0:T(8,128)(2,1)S(1)} %copy-done.6, s16[32,1024]{1,0:T(8,128)(2,1)S(1)} %copy-done.8, ...), custom_call_target="tpu_custom_call" | custom-call | tf_op jit(solution)/shard_map/add_contributions/pallas_call | solution.py:167
  (23 shorter events, 0.0 us)
Async XLA Ops:
  2.9 13.1 %collective-permute-start.3 = (bf16[128,1024]{1,0:T(8,128)(2,1)}, bf16[128,1024]{1,0:T(8,128)(2,1)S(1)}, u32[]{:S(2)}, u32[]{:S(2)}) collective-permute-start(bf16[128,1024]{1,0:T(8,128)(2,1)} %get-tuple-element.30), channel_id=1, source_target_pairs={{0,8},{1,9},{2,10},{3,11},{4,12},{5,13},{6,14},{7,15},{8,0},{9,1},... | collective-permute-start | bytes 786440 | tf_op jit(solution)/shard_map/ppermute | solution.py:190
  5.9 13.9 %collective-permute-start.8 = (bf16[128,1024]{1,0:T(8,128)(2,1)}, bf16[128,1024]{1,0:T(8,128)(2,1)S(1)}, u32[]{:S(2)}, u32[]{:S(2)}) collective-permute-start(bf16[128,1024]{1,0:T(8,128)(2,1)} %get-tuple-element.35), channel_id=1, source_target_pairs={{0,16},{1,17},{2,18},{3,19},{4,20},{5,21},{6,22},{7,23},{8,24},{9,... | collective-permute-start | bytes 786440 | tf_op jit(solution)/shard_map/ppermute | solution.py:190
  7.4 18.4 %collective-permute-start.13 = (bf16[128,1024]{1,0:T(8,128)(2,1)}, bf16[128,1024]{1,0:T(8,128)(2,1)S(1)}, u32[]{:S(2)}, u32[]{:S(2)}) collective-permute-start(bf16[128,1024]{1,0:T(8,128)(2,1)} %get-tuple-element.40), channel_id=1, source_target_pairs={{0,24},{1,25},{2,26},{3,27},{4,28},{5,29},{6,30},{7,31},{8,16},{9,... | collective-permute-start | bytes 786440 | tf_op jit(solution)/shard_map/ppermute | solution.py:190
  7.4 1.6 %copy-start = (bf16[1,1024,1024]{2,1,0:T(8,128)(2,1)S(1)}, bf16[1,1024,1024]{2,1,0:T(8,128)(2,1)}, u32[]{:S(2)}) copy-start(bf16[1,1024,1024]{2,1,0:T(8,128)(2,1)} %tile.7) | copy-start | bytes 6291460
  9.0 0.9 %copy-start.17 = (bf16[128,1024]{1,0:T(8,128)(2,1)S(1)}, bf16[128,1024]{1,0:T(8,128)(2,1)}, u32[]{:S(2)}) copy-start(bf16[128,1024]{1,0:T(8,128)(2,1)} %get-tuple-element.25.rows) | copy-start | bytes 786436
  10.0 7.5 %copy-start.1 = (bf16[1,1024,1024]{2,1,0:T(8,128)(2,1)S(1)}, bf16[1,1024,1024]{2,1,0:T(8,128)(2,1)}, u32[]{:S(2)}) copy-start(bf16[1,1024,1024]{2,1,0:T(8,128)(2,1)} %tile.7) | copy-start | bytes 6291460
  10.7 0.6 copy-start.3
  11.3 6.9 %collective-permute-start = (s16[32,1024]{1,0:T(8,128)(2,1)S(1)}, s16[32,1024]{1,0:T(8,128)(2,1)S(1)}, u32[]{:S(2)}, u32[]{:S(2)}) collective-permute-start(s16[32,1024]{1,0:T(8,128)(2,1)S(1)} %get-tuple-element.27), channel_id=1, source_target_pairs={{0,2},{1,3},{2,0},{3,1},{4,6},{5,7},{6,4},{7,5},{8,10},{9,11},{10,... | collective-permute-start | bytes 196616 | tf_op jit(solution)/shard_map/ppermute | solution.py:190
  13.4 7.1 %collective-permute-start.1 = (s16[32,1024]{1,0:T(8,128)(2,1)S(1)}, s16[32,1024]{1,0:T(8,128)(2,1)S(1)}, u32[]{:S(2)}, u32[]{:S(2)}) collective-permute-start(s16[32,1024]{1,0:T(8,128)(2,1)S(1)} %get-tuple-element.28), channel_id=1, source_target_pairs={{0,4},{1,5},{2,6},{3,7},{4,0},{5,1},{6,2},{7,3},{8,12},{9,13},{10,... | collective-permute-start | bytes 196616 | tf_op jit(solution)/shard_map/ppermute | solution.py:190
  16.0 9.1 %collective-permute-start.2 = (s16[32,1024]{1,0:T(8,128)(2,1)S(1)}, s16[32,1024]{1,0:T(8,128)(2,1)S(1)}, u32[]{:S(2)}, u32[]{:S(2)}) collective-permute-start(s16[32,1024]{1,0:T(8,128)(2,1)S(1)} %get-tuple-element.29), channel_id=1, source_target_pairs={{0,6},{1,7},{2,4},{3,5},{4,2},{5,3},{6,0},{7,1},{8,14},{9,15},{10,... | collective-permute-start | bytes 196616 | tf_op jit(solution)/shard_map/ppermute | solution.py:190
  18.1 37.0 %copy-start.2 = (f32[16,50,1024]{2,0,1:T(8,128)S(1)}, f32[16,50,1024]{2,0,1:T(8,128)}, u32[]{:S(2)}) copy-start(f32[16,50,1024]{2,0,1:T(8,128)} %param.11) | copy-start | bytes 9830404
  18.2 36.9 %copy-start.4 = (s16[32,1024]{1,0:T(8,128)(2,1)S(1)}, s16[32,1024]{1,0:T(8,128)(2,1)}, u32[]{:S(2)}) copy-start(s16[32,1024]{1,0:T(8,128)(2,1)} %copy-done.3) | copy-start | bytes 196612
  18.2 36.9 %copy-start.18 = (s32[4,8]{1,0:T(4,128)S(1)}, s32[4,8]{1,0:T(4,128)}, u32[]{:S(2)}) copy-start(s32[4,8]{1,0:T(4,128)} %refs_1_.1) | copy-start | bytes 388
  18.2 36.9 %copy-start.19 = (s32[4,8]{1,0:T(4,128)S(1)}, s32[4,8]{1,0:T(4,128)}, u32[]{:S(2)}) copy-start(s32[4,8]{1,0:T(4,128)} %refs_0_.1) | copy-start | bytes 388
  18.2 36.9 %copy-start.20 = (s32[4,8]{1,0:T(4,128)S(1)}, s32[4,8]{1,0:T(4,128)}, u32[]{:S(2)}) copy-start(s32[4,8]{1,0:T(4,128)} %refs_2_.1) | copy-start | bytes 388
  18.2 31.8 %copy-start.5 = (s16[32,1024]{1,0:T(8,128)(2,1)}, s16[32,1024]{1,0:T(8,128)(2,1)S(1)}, u32[]{:S(2)}) copy-start(s16[32,1024]{1,0:T(8,128)(2,1)S(1)} %collective-permute-done.refs_1_.refs_4_) | copy-start | bytes 196612
  18.2 9.1 %collective-permute-start.4 = (s16[32,1024]{1,0:T(8,128)(2,1)S(1)}, s16[32,1024]{1,0:T(8,128)(2,1)S(1)}, u32[]{:S(2)}, u32[]{:S(2)}) collective-permute-start(s16[32,1024]{1,0:T(8,128)(2,1)S(1)} %get-tuple-element.31), channel_id=1, source_target_pairs={{0,8},{1,9},{2,10},{3,11},{4,12},{5,13},{6,14},{7,15},{8,0},{9,1},... | collective-permute-start | bytes 196616 | tf_op jit(solution)/shard_map/ppermute | solution.py:190
  19.8 7.6 %collective-permute-start.5 = (s16[32,1024]{1,0:T(8,128)(2,1)S(1)}, s16[32,1024]{1,0:T(8,128)(2,1)S(1)}, u32[]{:S(2)}, u32[]{:S(2)}) collective-permute-start(s16[32,1024]{1,0:T(8,128)(2,1)S(1)} %get-tuple-element.32), channel_id=1, source_target_pairs={{0,10},{1,11},{2,8},{3,9},{4,14},{5,15},{6,12},{7,13},{8,2},{9,3},... | collective-permute-start | bytes 196616 | tf_op jit(solution)/shard_map/ppermute | solution.py:190
  20.5 29.5 %copy-start.7 = (s16[32,1024]{1,0:T(8,128)(2,1)}, s16[32,1024]{1,0:T(8,128)(2,1)S(1)}, u32[]{:S(2)}) copy-start(s16[32,1024]{1,0:T(8,128)(2,1)S(1)} %collective-permute-done.1.refs_2_.refs_5_) | copy-start | bytes 196612
  20.5 12.1 %collective-permute-start.6 = (s16[32,1024]{1,0:T(8,128)(2,1)S(1)}, s16[32,1024]{1,0:T(8,128)(2,1)S(1)}, u32[]{:S(2)}, u32[]{:S(2)}) collective-permute-start(s16[32,1024]{1,0:T(8,128)(2,1)S(1)} %get-tuple-element.33), channel_id=1, source_target_pairs={{0,12},{1,13},{2,14},{3,15},{4,8},{5,9},{6,10},{7,11},{8,4},{9,5},... | collective-permute-start | bytes 196616 | tf_op jit(solution)/shard_map/ppermute | solution.py:190
  25.1 25.0 %copy-start.9 = (s16[32,1024]{1,0:T(8,128)(2,1)}, s16[32,1024]{1,0:T(8,128)(2,1)S(1)}, u32[]{:S(2)}) copy-start(s16[32,1024]{1,0:T(8,128)(2,1)S(1)} %collective-permute-done.2.refs_3_.refs_6_) | copy-start | bytes 196612
  25.1 8.9 %collective-permute-start.7 = (s16[32,1024]{1,0:T(8,128)(2,1)S(1)}, s16[32,1024]{1,0:T(8,128)(2,1)}, u32[]{:S(2)}, u32[]{:S(2)}) collective-permute-start(s16[32,1024]{1,0:T(8,128)(2,1)S(1)} %get-tuple-element.34), channel_id=1, source_target_pairs={{0,14},{1,15},{2,12},{3,13},{4,10},{5,11},{6,8},{7,9},{8,6},{9,7},... | collective-permute-start | bytes 196616 | tf_op jit(solution)/shard_map/ppermute | solution.py:190
  25.8 10.6 %collective-permute-start.9 = (s16[32,1024]{1,0:T(8,128)(2,1)S(1)}, s16[32,1024]{1,0:T(8,128)(2,1)}, u32[]{:S(2)}, u32[]{:S(2)}) collective-permute-start(s16[32,1024]{1,0:T(8,128)(2,1)S(1)} %get-tuple-element.36), channel_id=1, source_target_pairs={{0,16},{1,17},{2,18},{3,19},{4,20},{5,21},{6,22},{7,23},{8,24},{9,... | collective-permute-start | bytes 196616 | tf_op jit(solution)/shard_map/ppermute | solution.py:190
  27.4 5.3 %copy-start.11 = (s16[32,1024]{1,0:T(8,128)(2,1)}, s16[32,1024]{1,0:T(8,128)(2,1)S(1)}, u32[]{:S(2)}) copy-start(s16[32,1024]{1,0:T(8,128)(2,1)S(1)} %collective-permute-done.4.refs_4_.refs_7_) | copy-start | bytes 196612
  27.4 9.1 %collective-permute-start.10 = (s16[32,1024]{1,0:T(8,128)(2,1)S(1)}, s16[32,1024]{1,0:T(8,128)(2,1)}, u32[]{:S(2)}, u32[]{:S(2)}) collective-permute-start(s16[32,1024]{1,0:T(8,128)(2,1)S(1)} %get-tuple-element.37), channel_id=1, source_target_pairs={{0,18},{1,19},{2,16},{3,17},{4,22},{5,23},{6,20},{7,21},{8,26},{9,... | collective-permute-start | bytes 196616 | tf_op jit(solution)/shard_map/ppermute | solution.py:190
  27.4 5.3 %copy-start.13 = (s16[32,1024]{1,0:T(8,128)(2,1)}, s16[32,1024]{1,0:T(8,128)(2,1)S(1)}, u32[]{:S(2)}) copy-start(s16[32,1024]{1,0:T(8,128)(2,1)S(1)} %collective-permute-done.5.refs_5_.refs_8_) | copy-start | bytes 196612
  27.4 14.7 %collective-permute-start.11 = (s16[32,1024]{1,0:T(8,128)(2,1)S(1)}, s16[32,1024]{1,0:T(8,128)(2,1)}, u32[]{:S(2)}, u32[]{:S(2)}) collective-permute-start(s16[32,1024]{1,0:T(8,128)(2,1)S(1)} %get-tuple-element.38), channel_id=1, source_target_pairs={{0,20},{1,21},{2,22},{3,23},{4,16},{5,17},{6,18},{7,19},{8,28},{9,... | collective-permute-start | bytes 196616 | tf_op jit(solution)/shard_map/ppermute | solution.py:190
  32.7 0.6 copy-start.15
  33.3 9.3 %collective-permute-start.12 = (s16[32,1024]{1,0:T(8,128)(2,1)S(1)}, s16[32,1024]{1,0:T(8,128)(2,1)}, u32[]{:S(2)}, u32[]{:S(2)}) collective-permute-start(s16[32,1024]{1,0:T(8,128)(2,1)S(1)} %get-tuple-element.39), channel_id=1, source_target_pairs={{0,22},{1,23},{2,20},{3,21},{4,18},{5,19},{6,16},{7,17},{8,30},{9,... | collective-permute-start | bytes 196616 | tf_op jit(solution)/shard_map/ppermute | solution.py:190
  34.0 8.6 %collective-permute-start.14 = (s16[32,1024]{1,0:T(8,128)(2,1)S(1)}, s16[32,1024]{1,0:T(8,128)(2,1)}, u32[]{:S(2)}, u32[]{:S(2)}) collective-permute-start(s16[32,1024]{1,0:T(8,128)(2,1)S(1)} %get-tuple-element.41), channel_id=1, source_target_pairs={{0,24},{1,25},{2,26},{3,27},{4,28},{5,29},{6,30},{7,31},{8,16},{9,... | collective-permute-start | bytes 196616 | tf_op jit(solution)/shard_map/ppermute | solution.py:190
  36.4 6.2 %collective-permute-start.15 = (s16[32,1024]{1,0:T(8,128)(2,1)S(1)}, s16[32,1024]{1,0:T(8,128)(2,1)}, u32[]{:S(2)}, u32[]{:S(2)}) collective-permute-start(s16[32,1024]{1,0:T(8,128)(2,1)S(1)} %get-tuple-element.42), channel_id=1, source_target_pairs={{0,26},{1,27},{2,24},{3,25},{4,30},{5,31},{6,28},{7,29},{8,18},{9,... | collective-permute-start | bytes 196616 | tf_op jit(solution)/shard_map/ppermute | solution.py:190
  36.4 8.7 %collective-permute-start.16 = (s16[32,1024]{1,0:T(8,128)(2,1)S(1)}, s16[32,1024]{1,0:T(8,128)(2,1)}, u32[]{:S(2)}, u32[]{:S(2)}) collective-permute-start(s16[32,1024]{1,0:T(8,128)(2,1)S(1)} %get-tuple-element.43), channel_id=1, source_target_pairs={{0,28},{1,29},{2,30},{3,31},{4,24},{5,25},{6,26},{7,27},{8,20},{9,... | collective-permute-start | bytes 196616 | tf_op jit(solution)/shard_map/ppermute | solution.py:190
  42.1 8.0 %collective-permute-start.17 = (s16[32,1024]{1,0:T(8,128)(2,1)S(1)}, s16[32,1024]{1,0:T(8,128)(2,1)}, u32[]{:S(2)}, u32[]{:S(2)}) collective-permute-start(s16[32,1024]{1,0:T(8,128)(2,1)S(1)} %get-tuple-element.44), channel_id=1, source_target_pairs={{0,30},{1,31},{2,28},{3,29},{4,26},{5,27},{6,24},{7,25},{8,22},{9,... | collective-permute-start | bytes 196616 | tf_op jit(solution)/shard_map/ppermute | solution.py:190
  52.9 2.2 %collective-permute-start.18 = (s16[256,1024]{1,0:T(8,128)(2,1)}, s16[256,1024]{1,0:T(8,128)(2,1)S(1)}, u32[]{:S(2)}, u32[]{:S(2)}) collective-permute-start(s16[256,1024]{1,0:T(8,128)(2,1)} %rows_of_other_core.1), channel_id=1, source_target_pairs={{0,1},{1,0},{2,3},{3,2},{4,5},{5,4},{6,7},{7,6},{8,9},{9,8},{10,11... | collective-permute-start | bytes 1572872 | tf_op jit(solution)/shard_map/ppermute | solution.py:190
  55.1 0.8 %copy-start.6 = (s16[32,1024]{1,0:T(8,128)(2,1)S(1)}, s16[32,1024]{1,0:T(8,128)(2,1)}, u32[]{:S(2)}) copy-start(s16[32,1024]{1,0:T(8,128)(2,1)} %copy-done.5) | copy-start | bytes 196612
  56.0 0.8 %copy-start.8 = (s16[32,1024]{1,0:T(8,128)(2,1)S(1)}, s16[32,1024]{1,0:T(8,128)(2,1)}, u32[]{:S(2)}) copy-start(s16[32,1024]{1,0:T(8,128)(2,1)} %copy-done.7) | copy-start | bytes 196612
  56.8 0.8 %copy-start.10 = (s16[32,1024]{1,0:T(8,128)(2,1)S(1)}, s16[32,1024]{1,0:T(8,128)(2,1)}, u32[]{:S(2)}) copy-start(s16[32,1024]{1,0:T(8,128)(2,1)} %copy-done.9) | copy-start | bytes 196612
  57.7 0.8 %copy-start.12 = (s16[32,1024]{1,0:T(8,128)(2,1)S(1)}, s16[32,1024]{1,0:T(8,128)(2,1)}, u32[]{:S(2)}) copy-start(s16[32,1024]{1,0:T(8,128)(2,1)} %copy-done.11) | copy-start | bytes 196612
  58.5 0.8 %copy-start.14 = (s16[32,1024]{1,0:T(8,128)(2,1)S(1)}, s16[32,1024]{1,0:T(8,128)(2,1)}, u32[]{:S(2)}) copy-start(s16[32,1024]{1,0:T(8,128)(2,1)} %copy-done.13) | copy-start | bytes 196612
  59.3 0.8 %copy-start.16 = (s16[32,1024]{1,0:T(8,128)(2,1)S(1)}, s16[32,1024]{1,0:T(8,128)(2,1)}, u32[]{:S(2)}) copy-start(s16[32,1024]{1,0:T(8,128)(2,1)} %copy-done.15) | copy-start | bytes 196612

commit v7 on v4

v7 whole, which is shorter than its diff:
```python
import math

import jax
import jax.numpy as jnp
from jax import lax
from jax.experimental import pallas as pl
from jax.experimental.pallas import tpu as pltpu
from jax.sharding import PartitionSpec as P

LARGEST = 32766.0
SCALE_STEPS = 64.0
SCALE_SHIFT = 8192
SCALE_BITS = 16
LANES = 128
MEBIBYTE = 1 << 20
SMEM = pl.BlockSpec(memory_space=pltpu.SMEM)
VMEM = pl.BlockSpec(memory_space=pltpu.VMEM)


def vmem_limit(*arrays):
    total = sum(math.prod(array.shape) * jnp.dtype(array.dtype).itemsize for array in arrays)
    return pltpu.CompilerParams(vmem_limit_bytes=total + 4 * MEBIBYTE)


def encode(values):
    largest = jnp.max(jnp.abs(values), axis=1, keepdims=True)
    logarithm = jnp.log2(jnp.maximum(largest, 2.0**-100))
    exponent = jnp.floor(logarithm * SCALE_STEPS) + 2.0
    scaled = values * (LARGEST * jnp.exp2(exponent * (-1.0 / SCALE_STEPS)))
    scaled = jnp.clip(scaled, -LARGEST, LARGEST)
    code = jnp.floor(scaled + 0.5).astype(jnp.int32)
    head = code[:, :LANES]
    lane = lax.broadcasted_iota(jnp.int32, head.shape, 1)
    stored = exponent.astype(jnp.int32) + SCALE_SHIFT
    stored = jnp.broadcast_to(stored, head.shape)
    bit = lax.shift_right_logical(stored, jnp.minimum(lane, SCALE_BITS)) & 1
    head = jnp.where(lane < SCALE_BITS, (head & -2) | bit, head)
    return head.astype(jnp.int16), code[:, LANES:].astype(jnp.int16)


def row_scale(head):
    head = head.astype(jnp.int32)
    lane = lax.broadcasted_iota(jnp.int32, head.shape, 1)
    bits = lax.shift_left(head & 1, jnp.minimum(lane, SCALE_BITS))
    bits = jnp.where(lane < SCALE_BITS, bits, 0).astype(jnp.float32)
    stored = jnp.broadcast_to(jnp.sum(bits, axis=1, keepdims=True), head.shape)
    return jnp.exp2((stored - SCALE_SHIFT) * (1.0 / SCALE_STEPS)) * (1.0 / LARGEST)


def pick_kernel(tile_cd, amplitudes, *rest):
    outgoing, sems = rest[:-1], rest[-1]
    blk, grp = lax.axis_index("blk"), lax.axis_index("grp")
    copies = []
    for step, picked in enumerate(outgoing):
        cd = tile_cd[jnp.bitwise_xor(blk, step), grp]
        copies.append(pltpu.make_async_copy(amplitudes.at[cd], picked, sems.at[step]))
    for copy in copies:
        copy.start()
    for copy in copies:
        copy.wait()


def pick(tile_cd, amplitudes):
    columns = tile_cd.shape[0]
    block = jax.ShapeDtypeStruct(amplitudes.shape[1:], amplitudes.dtype)
    return pl.pallas_call(
        pick_kernel,
        out_shape=[block] * columns,
        in_specs=[SMEM, pl.BlockSpec(memory_space=pl.ANY)],
        out_specs=[VMEM] * columns,
        scratch_shapes=[pltpu.SemaphoreType.DMA((columns,))],
        compiler_params=vmem_limit(*[block] * columns),
        name="pick_cd_blocks",
    )(tile_cd, amplitudes)


def code_rows(rows, tile, product, coded, first):
    group_rows = rows.shape[0]
    product[...] = jnp.dot(rows[...], tile[0], preferred_element_type=jnp.float32)
    for part in range(0, group_rows, 16):
        head, tail = encode(product[part : part + 16, :])
        place = pl.ds(first + part, 16)
        coded[place, :LANES] = head
        coded[place, LANES:] = tail


def early_kernel(*refs):
    groups, (tile, coded, product) = refs[:-3], refs[-3:]
    for index, rows in enumerate(groups):
        code_rows(rows, tile, product, coded, index * rows.shape[0])


def last_kernel(rows, tile, early, coded, product):
    blk = lax.axis_index("blk")
    group_rows = rows.shape[0]
    groups = coded.shape[0] // group_rows
    for step in range(groups - 1):
        first = pl.multiple_of(jnp.bitwise_xor(blk, step) * group_rows, group_rows)
        coded[pl.ds(first, group_rows), :] = early[step * group_rows : (step + 1) * group_rows, :]
    first = pl.multiple_of(jnp.bitwise_xor(blk, groups - 1) * group_rows, group_rows)
    code_rows(rows, tile, product, coded, first)


def cost(rows, tile):
    flops = 2 * rows * tile.shape[1] * tile.shape[2]
    return pl.CostEstimate(flops=flops, bytes_accessed=2 * tile.shape[1] * tile.shape[2], transcendentals=0)


def contract_early(groups, tile):
    group_rows, tile_width = groups[0].shape[0], tile.shape[2]
    coded = jax.ShapeDtypeStruct((len(groups) * group_rows, tile_width), jnp.int16)
    product = jax.ShapeDtypeStruct((group_rows, tile_width), jnp.float32)
    return pl.pallas_call(
        early_kernel,
        out_shape=coded,
        in_specs=[VMEM] * (len(groups) + 1),
        out_specs=VMEM,
        scratch_shapes=[pltpu.VMEM(product.shape, product.dtype)],
        compiler_params=vmem_limit(*groups, tile, coded, product),
        cost_estimate=cost(len(groups) * group_rows, tile),
        name="contract_early_groups",
    )(*groups, tile)


def contract_last(rows, tile, early):
    group_rows, tile_width = rows.shape[0], tile.shape[2]
    coded = jax.ShapeDtypeStruct((early.shape[0] + group_rows, tile_width), early.dtype)
    product = jax.ShapeDtypeStruct((group_rows, tile_width), jnp.float32)
    return pl.pallas_call(
        last_kernel,
        out_shape=coded,
        in_specs=[VMEM] * 3,
        out_specs=VMEM,
        scratch_shapes=[pltpu.VMEM(product.shape, product.dtype)],
        compiler_params=vmem_limit(rows, tile, early, coded, product),
        cost_estimate=cost(group_rows, tile),
        name="contract_last_group",
    )(rows, tile, early)


def add_kernel(pieces, tile_ab, tile_cd, pair_screen, arrived, residual_in, residual, held, sems):
    grp = lax.axis_index("grp")
    ab_tiles, _, tile_width = residual.shape
    columns, grp_count = tile_ab.shape
    bounds = [ab_tiles * piece // pieces for piece in range(pieces + 1)]
    parts = [pl.ds(low, high - low) for low, high in zip(bounds[:-1], bounds[1:])]
    leaves = [pltpu.make_async_copy(held.at[part], residual.at[part], sems.at[i]) for i, part in enumerate(parts)]

    def hold(ab, carry):
        held[ab] = residual_in[ab]
        return carry

    lax.fori_loop(0, ab_tiles, hold, 0)

    def add_group(p, carry):
        scales = []
        for g in range(grp_count):
            kept = pair_screen[tile_cd[p, g], grp].astype(jnp.float32)
            scales.append(row_scale(arrived[p * grp_count + g, :, :LANES]) * kept)
        for g in range(grp_count):
            ab = tile_ab[p, g]
            for lane in range(0, tile_width, LANES):
                code = arrived[p * grp_count + g, :, lane : lane + LANES]
                term = code.astype(jnp.float32) * scales[g]
                held[ab, :, lane : lane + LANES] = held[ab, :, lane : lane + LANES] + term
        return carry

    lax.fori_loop(0, columns, add_group, 0)
    for copy in leaves:
        copy.start()
    for copy in leaves:
        copy.wait()


def add_blocks(tile_ab, tile_cd, pair_screen, arrived, residual_in):
    pieces = 5
    return pl.pallas_call(
        lambda *refs: add_kernel(pieces, *refs),
        out_shape=jax.ShapeDtypeStruct(residual_in.shape, residual_in.dtype),
        in_specs=[SMEM] * 3 + [VMEM] * 2,
        out_specs=pl.BlockSpec(memory_space=pl.ANY),
        scratch_shapes=[pltpu.VMEM(residual_in.shape, residual_in.dtype), pltpu.SemaphoreType.DMA((pieces,))],
        compiler_params=vmem_limit(arrived, residual_in, residual_in),
        name="add_contributions",
    )(tile_ab, tile_cd, pair_screen, arrived, residual_in)


def shards(amplitudes, pair_screen, integrals, tile_ab, tile_cd, residual_in):
    blk_count = lax.axis_size("blk")
    grp_count = lax.axis_size("grp")
    owner_rows, _, tile_width = residual_in.shape

    def swap(value, step):
        return lax.ppermute(value, "blk", [(b, b ^ step) for b in range(blk_count)])

    picked = pick(tile_cd, amplitudes)
    rows_in = [picked[0]] + [swap(picked[step], step) for step in range(1, blk_count)]
    early = contract_early(rows_in[:-1], integrals)
    coded = contract_last(rows_in[-1], integrals, early)
    coded = coded.reshape(blk_count * grp_count, owner_rows, tile_width)
    arrived = lax.all_to_all(coded, ("blk", "grp"), split_axis=0, concat_axis=0, tiled=True)
    by_tile = jnp.transpose(residual_in, (1, 0, 2))
    return jnp.transpose(add_blocks(tile_ab, tile_cd, pair_screen, arrived, by_tile), (1, 0, 2))


def solution(mesh):
    in_specs = (
        P(None, "blk", None),
        P(None, "blk"),
        P(("blk", "grp"), None, None),
        P(),
        P(),
        P(("blk", "grp"), None, None),
    )
    out_specs = P(("blk", "grp"), None, None)
    return jax.shard_map(shards, mesh=mesh, in_specs=in_specs, out_specs=out_specs, check_vma=False)
```

time: 81.4 us -> 58.8 us (0.72)
  blocking collectives: 0 us -> 32.3 us
  waiting for transfers between devices: 40.1 us -> 11.8 us
  starting transfers between devices: 26 us -> 4.54 us
  matrix products: 4.62 us -> 0 us
  Pallas kernels: 7.23 us -> 6.2 us
  local copies, waits for them, and re-layouts: 2.64 us -> 3.55 us
    all_to_all x0 -> x1, blocking collectives: none -> 32.3 us  [shards(): lax.all_to_all(coded, ('blk', 'grp'), split_axis=0, concat_axis=0, tiled=...]
    all_to_all x4 -> x0, waiting for transfers between devices: 29.1 us -> none  [shards(): lax.all_to_all(coded, 'grp', split_axis=0, concat_axis=0, tiled=True)]
    all_to_all x4 -> x0, starting transfers between devices: 15.4 us -> none  [shards(): lax.all_to_all(coded, 'grp', split_axis=0, concat_axis=0, tiled=True)]
    ppermute x6 -> x3, starting transfers between devices: 10.6 us -> 4.54 us  [swap(): return lax.ppermute(value, 'blk', [(b, b ^ step) for b in range(blk_count)])]
    dot_general x4 -> x0, matrix products: 4.62 us -> none  [shards(): jnp.dot(rows_in[step], integrals[0], preferred_element_type=jnp.float32)]
    ppermute x6 -> x3, waiting for transfers between devices: 10.9 us -> 11.8 us  [swap(): return lax.ppermute(value, 'blk', [(b, b ^ step) for b in range(blk_count)])]
    unnamed x18 -> x16, local copies, waits for them, and re-layouts: 2.64 us -> 3.55 us
    pallas_call x1, Pallas kernels: 4.22 us -> 3.35 us  [add_blocks(): pl.pallas_call(lambda *refs: add_kernel(pieces, *refs), out_shape=jax.Sha...]
  transfers between devices with their start and end apart: 10 -> 3, of which waited for: 6 -> 2; matrix products, arithmetic and copies ran while one was open for 6% -> 0% of each run, Pallas kernels for 0% -> 3%
where the time goes in v7:
time: 58.8 us; the launch traced here: 58.5 us
  blocking collectives  32.3 us (55%)
  waiting for transfers between devices  11.8 us (20%)
  Pallas kernels  6.2 us (11%)
  starting transfers between devices  4.54 us (8%)
  local copies, waits for them, and re-layouts  3.55 us (6%)
    all_to_all x1, blocking collectives, shards(): lax.all_to_all(coded, ('blk', 'grp'), split_axis=0, concat_axis=0, tiled=...  32.3 us
    ppermute x3, waiting for transfers between devices, swap(): return lax.ppermute(value, 'blk', [(b, b ^ step) for b in range(blk_count)])  11.8 us
    ppermute x3, starting transfers between devices, swap(): return lax.ppermute(value, 'blk', [(b, b ^ step) for b in range(blk_count)])  4.54 us
    unnamed x16, local copies, waits for them, and re-layouts  3.55 us
    pallas_call x1, Pallas kernels, add_blocks(): pl.pallas_call(lambda *refs: add_kernel(pieces, *refs), out_shape=jax.Sha...  3.35 us
    pallas_call x1, Pallas kernels, contract_early(): pl.pallas_call(early_kernel, out_shape=coded, in_specs=[VMEM] * (len(grou...  1.49 us
  transfers between devices with their start and end apart: 3, of which 2 were waited for; matrix products, arithmetic and copies ran while one was open for 0% of the time, Pallas kernels for 3%

profile of v7, /device:TPU:0, one launch (start us, length us, event | category | flops | bytes accessed | tf_op | source)
XLA Modules:
  0.0 58.5 jit_solution(18110564928636588096)
XLA Ops:
  0.0 0.0 copy-start.3
  0.0 1.2 %copy-done.3 = bf16[4,128,1024]{2,1,0:T(8,128)(2,1)S(1)} copy-done((bf16[4,128,1024]{2,1,0:T(8,128)(2,1)S(1)}, bf16[4,128,1024]{2,1,0:T(8,128)(2,1)}, u32[]{:S(2)}) %copy-start.3) | copy-done | bytes 1048600
  1.2 0.0 copy-start.4
  1.2 0.7 %copy-done.4 = s32[4,8]{1,0:T(4,128)S(1)} copy-done((s32[4,8]{1,0:T(4,128)S(1)}, s32[4,8]{1,0:T(4,128)}, u32[]{:S(2)}) %copy-start.4) | copy-done | bytes 152
  1.9 0.7 %pick_cd_blocks.1 = (bf16[128,1024]{1,0:T(8,128)(2,1)S(1)}, bf16[128,1024]{1,0:T(8,128)(2,1)S(1)}, bf16[128,1024]{1,0:T(8,128)(2,1)S(1)}, bf16[128,1024]{1,0:T(8,128)(2,1)S(1)}) custom-call(s32[4,8]{1,0:T(4,128)S(1)} %copy-done.4, bf16[4,128,1024]{2,1,0:T(8,128)(2,1)S(1)} %copy-done.3), custom_call_target="tpu_custom_call" | custom-call | tf_op jit(solution)/shard_map/pick_cd_blocks/pallas_call | solution.py:66
  2.6 3.0 %collective-permute-start.1 = (bf16[128,1024]{1,0:T(8,128)(2,1)S(1)}, bf16[128,1024]{1,0:T(8,128)(2,1)S(1)}, u32[]{:S(2)}, u32[]{:S(2)}) collective-permute-start(bf16[128,1024]{1,0:T(8,128)(2,1)S(1)} %get-tuple-element.11), channel_id=1, source_target_pairs={{0,8},{8,0},{16,24},{24,16},{1,9},{9,1},{17,25},{25,17},{2,10},{10... | collective-permute-start | bytes 786440 | tf_op jit(solution)/shard_map/ppermute | solution.py:194
  5.6 1.5 %collective-permute-start.2 = (bf16[128,1024]{1,0:T(8,128)(2,1)S(1)}, bf16[128,1024]{1,0:T(8,128)(2,1)S(1)}, u32[]{:S(2)}, u32[]{:S(2)}) collective-permute-start(bf16[128,1024]{1,0:T(8,128)(2,1)S(1)} %get-tuple-element.12), channel_id=1, source_target_pairs={{0,16},{8,24},{16,0},{24,8},{1,17},{9,25},{17,1},{25,9},{2,18},{10... | collective-permute-start | bytes 786440 | tf_op jit(solution)/shard_map/ppermute | solution.py:194
  7.1 0.0 collective-permute-start
  7.2 5.6 %collective-permute-done.1.refs_1_ = bf16[128,1024]{1,0:T(8,128)(2,1)S(1)} collective-permute-done((bf16[128,1024]{1,0:T(8,128)(2,1)S(1)}, bf16[128,1024]{1,0:T(8,128)(2,1)S(1)}, u32[]{:S(2)}, u32[]{:S(2)}) %collective-permute-start.1) | collective-permute-done | bytes 262176 | tf_op jit(solution)/shard_map/ppermute | solution.py:194
  12.8 6.2 %collective-permute-done.2.refs_2_ = bf16[128,1024]{1,0:T(8,128)(2,1)S(1)} collective-permute-done((bf16[128,1024]{1,0:T(8,128)(2,1)S(1)}, bf16[128,1024]{1,0:T(8,128)(2,1)S(1)}, u32[]{:S(2)}, u32[]{:S(2)}) %collective-permute-start.2) | collective-permute-done | bytes 262176 | tf_op jit(solution)/shard_map/ppermute | solution.py:194
  19.0 0.0 copy-start
  19.0 1.6 %copy-done = bf16[1,1024,1024]{2,1,0:T(8,128)(2,1)S(1)} copy-done((bf16[1,1024,1024]{2,1,0:T(8,128)(2,1)S(1)}, bf16[1,1024,1024]{2,1,0:T(8,128)(2,1)}, u32[]{:S(2)}) %copy-start) | copy-done | bytes 2097176
  20.6 0.0 copy-start.1
  20.6 1.5 %contract_early_groups.1.early = s16[384,1024]{1,0:T(8,128)(2,1)S(1)} custom-call(bf16[128,1024]{1,0:T(8,128)(2,1)S(1)} %get-tuple-element.10.refs_0_, bf16[128,1024]{1,0:T(8,128)(2,1)S(1)} %collective-permute-done.1.refs_1_, bf16[128,1024]{1,0:T(8,128)(2,1)S(1)} %collective-permute-done.2.refs_2_, bf16[1,1024,1024]{2,1,0:T(8,128)(2,1)S(1)} %copy-done), custom_call_target="tpu_custom_call" | custom-call | flops 805306368 | bytes 2097152 | tf_op jit(solution)/shard_map/contract_early_groups/pallas_call | solution.py:113
  22.1 0.0 copy-start.2
  22.1 0.0 copy-start.5
  22.1 0.0 copy-start.6
  22.1 0.0 copy-start.7
  22.1 0.0 collective-permute-done.rows
  22.2 0.0 copy-done.1
  22.2 0.7 %contract_last_group.1 = s16[512,1024]{1,0:T(8,128)(2,1)S(1)} custom-call(bf16[128,1024]{1,0:T(8,128)(2,1)S(1)} %collective-permute-done.rows, bf16[1,1024,1024]{2,1,0:T(8,128)(2,1)S(1)} %copy-done.1, s16[384,1024]{1,0:T(8,128)(2,1)S(1)} %contract_early_groups.1.early), custom_call_target="tpu_custom_call" | custom-call | flops 268435456 | bytes 2097152 | tf_op jit(solution)/shard_map/contract_last_group/pallas_call | solution.py:129
  22.9 32.3 %all_to_all.5.refs_3_ = s16[32,16,1024]{2,1,0:T(8,128)(2,1)S(1)} all-to-all(s16[32,16,1024]{2,1,0:T(8,128)(2,1)S(1)} %bitcast.3), channel_id=1, replica_groups=mesh['blk'=4,'grp'=8] {'blk','grp'}, dimensions={0} | all-to-all | bytes 2097152 | tf_op jit(solution)/shard_map/all_to_all | solution.py:201
  55.2 0.0 copy-done.2
  55.2 0.0 copy-done.5
  55.2 0.0 copy-done.6
  55.2 0.0 copy-done.7
  55.2 3.3 %add_contributions.1 = f32[50,16,1024]{2,1,0:T(8,128)} custom-call(s32[4,8]{1,0:T(4,128)S(1)} %copy-done.6, s32[4,8]{1,0:T(4,128)S(1)} %copy-done.5, s32[4,8]{1,0:T(4,128)S(1)} %copy-done.7, s16[32,16,1024]{2,1,0:T(8,128)(2,1)S(1)} %all_to_all.5.refs_3_, f32[50,16,1024]{2,1,0:T(8,128)S(1)} %bitcast.4), custom_call_target="tpu_custom_call" | custom-call | tf_op jit(solution)/shard_map/add_contributions/pallas_call | solution.py:177
Async XLA Ops:
  0.0 1.2 %copy-start.3 = (bf16[4,128,1024]{2,1,0:T(8,128)(2,1)S(1)}, bf16[4,128,1024]{2,1,0:T(8,128)(2,1)}, u32[]{:S(2)}) copy-start(bf16[4,128,1024]{2,1,0:T(8,128)(2,1)} %amplitudes.1) | copy-start | bytes 3145732
  1.2 0.7 %copy-start.4 = (s32[4,8]{1,0:T(4,128)S(1)}, s32[4,8]{1,0:T(4,128)}, u32[]{:S(2)}) copy-start(s32[4,8]{1,0:T(4,128)} %refs_1_.1) | copy-start | bytes 388
  2.6 10.1 %collective-permute-start.1 = (bf16[128,1024]{1,0:T(8,128)(2,1)S(1)}, bf16[128,1024]{1,0:T(8,128)(2,1)S(1)}, u32[]{:S(2)}, u32[]{:S(2)}) collective-permute-start(bf16[128,1024]{1,0:T(8,128)(2,1)S(1)} %get-tuple-element.11), channel_id=1, source_target_pairs={{0,8},{8,0},{16,24},{24,16},{1,9},{9,1},{17,25},{25,17},{2,10},{10... | collective-permute-start | bytes 786440 | tf_op jit(solution)/shard_map/ppermute | solution.py:194
  5.6 13.4 %collective-permute-start.2 = (bf16[128,1024]{1,0:T(8,128)(2,1)S(1)}, bf16[128,1024]{1,0:T(8,128)(2,1)S(1)}, u32[]{:S(2)}, u32[]{:S(2)}) collective-permute-start(bf16[128,1024]{1,0:T(8,128)(2,1)S(1)} %get-tuple-element.12), channel_id=1, source_target_pairs={{0,16},{8,24},{16,0},{24,8},{1,17},{9,25},{17,1},{25,9},{2,18},{10... | collective-permute-start | bytes 786440 | tf_op jit(solution)/shard_map/ppermute | solution.py:194
  7.1 15.0 %collective-permute-start = (bf16[128,1024]{1,0:T(8,128)(2,1)S(1)}, bf16[128,1024]{1,0:T(8,128)(2,1)S(1)}, u32[]{:S(2)}, u32[]{:S(2)}) collective-permute-start(bf16[128,1024]{1,0:T(8,128)(2,1)S(1)} %get-tuple-element.9), channel_id=1, source_target_pairs={{0,24},{8,16},{16,8},{24,0},{1,25},{9,17},{17,9},{25,1},{2,26},{10... | collective-permute-start | bytes 786440 | tf_op jit(solution)/shard_map/ppermute | solution.py:194
  19.0 1.6 %copy-start = (bf16[1,1024,1024]{2,1,0:T(8,128)(2,1)S(1)}, bf16[1,1024,1024]{2,1,0:T(8,128)(2,1)}, u32[]{:S(2)}) copy-start(bf16[1,1024,1024]{2,1,0:T(8,128)(2,1)} %tile.1) | copy-start | bytes 6291460
  20.6 1.6 %copy-start.1 = (bf16[1,1024,1024]{2,1,0:T(8,128)(2,1)S(1)}, bf16[1,1024,1024]{2,1,0:T(8,128)(2,1)}, u32[]{:S(2)}) copy-start(bf16[1,1024,1024]{2,1,0:T(8,128)(2,1)} %tile.1) | copy-start | bytes 6291460
  22.1 33.1 %copy-start.2 = (f32[16,50,1024]{2,0,1:T(8,128)S(1)}, f32[16,50,1024]{2,0,1:T(8,128)}, u32[]{:S(2)}) copy-start(f32[16,50,1024]{2,0,1:T(8,128)} %param.11) | copy-start | bytes 9830404
  22.1 33.1 %copy-start.5 = (s32[4,8]{1,0:T(4,128)S(1)}, s32[4,8]{1,0:T(4,128)}, u32[]{:S(2)}) copy-start(s32[4,8]{1,0:T(4,128)} %refs_1_.1) | copy-start | bytes 388
  22.1 33.1 %copy-start.6 = (s32[4,8]{1,0:T(4,128)S(1)}, s32[4,8]{1,0:T(4,128)}, u32[]{:S(2)}) copy-start(s32[4,8]{1,0:T(4,128)} %refs_0_.1) | copy-start | bytes 388
  22.1 33.1 %copy-start.7 = (s32[4,8]{1,0:T(4,128)S(1)}, s32[4,8]{1,0:T(4,128)}, u32[]{:S(2)}) copy-start(s32[4,8]{1,0:T(4,128)} %refs_2_.1) | copy-start | bytes 388

commit v8 on v1

v8 whole, which is shorter than its diff:
```python
import math

import jax
import jax.numpy as jnp
from jax import lax
from jax.experimental import pallas as pl
from jax.experimental.pallas import tpu as pltpu
from jax.sharding import PartitionSpec as P

LARGEST = 32766.0
SCALE_STEPS = 64.0
SCALE_SHIFT = 8192
SCALE_BITS = 16
LANES = 128
CORES = 2
MEBIBYTE = 1 << 20
SMEM = pl.BlockSpec(memory_space=pltpu.SMEM)
VMEM = pl.BlockSpec(memory_space=pltpu.VMEM)
ANY = pl.BlockSpec(memory_space=pl.ANY)


def vmem_limit(*arrays):
    total = sum(math.prod(array.shape) * jnp.dtype(array.dtype).itemsize for array in arrays)
    return pltpu.CompilerParams(vmem_limit_bytes=total + 4 * MEBIBYTE)


def encode(values):
    largest = jnp.max(jnp.abs(values), axis=1, keepdims=True)
    logarithm = jnp.log2(jnp.maximum(largest, 2.0**-100))
    exponent = jnp.floor(logarithm * SCALE_STEPS) + 2.0
    scaled = values * (LARGEST * jnp.exp2(exponent * (-1.0 / SCALE_STEPS)))
    scaled = jnp.clip(scaled, -LARGEST, LARGEST)
    code = jnp.floor(scaled + 0.5).astype(jnp.int32)
    head = code[:, :LANES]
    lane = lax.broadcasted_iota(jnp.int32, head.shape, 1)
    stored = exponent.astype(jnp.int32) + SCALE_SHIFT
    stored = jnp.broadcast_to(stored, head.shape)
    bit = lax.shift_right_logical(stored, jnp.minimum(lane, SCALE_BITS)) & 1
    head = jnp.where(lane < SCALE_BITS, (head & -2) | bit, head)
    return head.astype(jnp.int16), code[:, LANES:].astype(jnp.int16)


def row_scale(head):
    head = head.astype(jnp.int32)
    lane = lax.broadcasted_iota(jnp.int32, head.shape, 1)
    bits = lax.shift_left(head & 1, jnp.minimum(lane, SCALE_BITS))
    bits = jnp.where(lane < SCALE_BITS, bits, 0).astype(jnp.float32)
    stored = jnp.broadcast_to(jnp.sum(bits, axis=1, keepdims=True), head.shape)
    return jnp.exp2((stored - SCALE_SHIFT) * (1.0 / SCALE_STEPS)) * (1.0 / LARGEST)


def cost(rows, tile):
    flops = 2 * rows * tile.shape[-2] * tile.shape[-1]
    return pl.CostEstimate(flops=flops, bytes_accessed=2 * tile.shape[-2] * tile.shape[-1], transcendentals=0)


def start_all(copies):
    for copy in copies:
        copy.start()


def wait_all(copies):
    for copy in copies:
        copy.wait()


def pick_kernel(tile_cd, amplitudes, *rest):
    outgoing, sems = rest[:-1], rest[-1]
    blk, grp = lax.axis_index("blk"), lax.axis_index("grp")
    copies = []
    for step, picked in enumerate(outgoing):
        cd = tile_cd[jnp.bitwise_xor(blk, step), grp]
        copies.append(pltpu.make_async_copy(amplitudes.at[cd], picked, sems.at[step]))
    start_all(copies)
    wait_all(copies)


def pick(tile_cd, amplitudes):
    groups = tile_cd.shape[0]
    block = jax.ShapeDtypeStruct(amplitudes.shape[1:], amplitudes.dtype)
    return pl.pallas_call(
        pick_kernel,
        out_shape=[block] * groups,
        in_specs=[SMEM, ANY],
        out_specs=[VMEM] * groups,
        scratch_shapes=[pltpu.SemaphoreType.DMA((groups,))],
        compiler_params=vmem_limit(*[block] * groups),
        name="pick_cd_blocks",
    )(tile_cd, amplitudes)


def code_chips(rows, tile, product, outgoing, first):
    product[...] = jnp.dot(rows[...], tile[...], preferred_element_type=jnp.float32)
    chip_rows = product.shape[0] // len(outgoing)
    chip = lax.axis_index("grp") // CORES
    for step, coded in enumerate(outgoing):
        source = pl.multiple_of(jnp.bitwise_xor(chip, step) * chip_rows, chip_rows)
        code, tail = encode(product[pl.ds(source, chip_rows), :])
        coded[first : first + chip_rows, :LANES] = code
        coded[first : first + chip_rows, LANES:] = tail


def own_kernel(rows, far_picked, tile, *rest):
    outgoing, (far_rows, product) = rest[:-2], rest[-2:]
    far_rows[...] = far_picked[...]
    code_chips(rows, tile, product, outgoing, 0)


def contract_own(rows, far_picked, tile, chips):
    group_rows, tile_width = rows.shape[0], tile.shape[1]
    coded = jax.ShapeDtypeStruct((group_rows // chips, tile_width), jnp.int16)
    product = jax.ShapeDtypeStruct((group_rows, tile_width), jnp.float32)
    outputs = [coded] * chips + [jax.ShapeDtypeStruct(rows.shape, rows.dtype)]
    return pl.pallas_call(
        own_kernel,
        out_shape=outputs,
        in_specs=[VMEM] * 3,
        out_specs=[VMEM] * len(outputs),
        scratch_shapes=[pltpu.VMEM(product.shape, product.dtype)],
        compiler_params=vmem_limit(rows, far_picked, tile, *outputs, product),
        cost_estimate=cost(group_rows, tile),
        name="contract_own_group",
    )(rows, far_picked, tile)


def near_kernel(near, *refs):
    groups, tile, outgoing, product = refs[:near], refs[near], refs[near + 1 : -1], refs[-1]
    chip_rows = product.shape[0] // len(outgoing)
    for index, rows in enumerate(groups):
        code_chips(rows, tile, product, outgoing, index * chip_rows)


def contract_near(groups, tile, chips):
    group_rows, tile_width = groups[0].shape[0], tile.shape[1]
    coded = jax.ShapeDtypeStruct((len(groups) * group_rows // chips, tile_width), jnp.int16)
    product = jax.ShapeDtypeStruct((group_rows, tile_width), jnp.float32)
    return pl.pallas_call(
        lambda *refs: near_kernel(len(groups), *refs),
        out_shape=[coded] * chips,
        in_specs=[VMEM] * (len(groups) + 1),
        out_specs=[VMEM] * chips,
        scratch_shapes=[pltpu.VMEM(product.shape, product.dtype)],
        compiler_params=vmem_limit(*groups, tile, *[coded] * chips, product),
        cost_estimate=cost(len(groups) * group_rows, tile),
        name="contract_near_groups",
    )(*groups, tile)


def far_kernel(chips, rows, tile, *rest):
    coded, product = rest[-2:]
    chip_rows = product.shape[0] // chips
    parts = [coded.at[pl.ds(step * chip_rows, chip_rows)] for step in range(chips)]
    code_chips(rows, tile, product, parts, 0)


def contract_far(rows, tile, chips, earlier):
    coded = jax.ShapeDtypeStruct((rows.shape[0], tile.shape[1]), jnp.int16)
    product = jax.ShapeDtypeStruct(coded.shape, jnp.float32)
    return pl.pallas_call(
        lambda *refs: far_kernel(chips, *refs),
        out_shape=coded,
        in_specs=[VMEM] * 2 + [ANY] * len(earlier),
        out_specs=VMEM,
        scratch_shapes=[pltpu.VMEM(product.shape, product.dtype)],
        compiler_params=vmem_limit(rows, tile, coded, product),
        cost_estimate=cost(rows.shape[0], tile),
        name="contract_far_group",
    )(rows, tile, *earlier)


def regroup_kernel(count, *refs):
    sources, targets = refs[:count], refs[count:]
    part_rows = sources[0].shape[0] // len(targets)
    for j, source in enumerate(sources):
        for i, target in enumerate(targets):
            target[j * part_rows : (j + 1) * part_rows, :] = source[i * part_rows : (i + 1) * part_rows, :]


def regroup(sources, parts, name):
    rows, tile_width = sources[0].shape
    target = jax.ShapeDtypeStruct((len(sources) * rows // parts, tile_width), sources[0].dtype)
    return pl.pallas_call(
        lambda *refs: regroup_kernel(len(sources), *refs),
        out_shape=[target] * parts,
        in_specs=[VMEM] * len(sources),
        out_specs=[VMEM] * parts,
        compiler_params=vmem_limit(*sources, *[target] * parts),
        name=name,
    )(*sources)


def pieces_of(arrays, owner_rows):
    return [(array, first) for array in arrays for first in range(0, array.shape[0], CORES * owner_rows)]


def other_core_kernel(owner_rows, *refs):
    arrays, halves = refs[:-1], refs[-1]
    other = 1 - lax.axis_index("grp") % CORES
    for index, (array, first) in enumerate(pieces_of(arrays, owner_rows)):
        source = pl.multiple_of(first + other * owner_rows, owner_rows)
        halves[index * owner_rows : (index + 1) * owner_rows, :] = array[pl.ds(source, owner_rows), :]


def other_core_rows(arrays, owner_rows):
    rows = sum(array.shape[0] for array in arrays) // CORES
    halves = jax.ShapeDtypeStruct((rows, arrays[0].shape[1]), arrays[0].dtype)
    return pl.pallas_call(
        lambda *refs: other_core_kernel(owner_rows, *refs),
        out_shape=halves,
        in_specs=[VMEM] * len(arrays),
        out_specs=VMEM,
        compiler_params=vmem_limit(*arrays, halves),
        name="rows_of_other_core",
    )(*arrays)


def add_kernel(parts, tile_ab, tile_cd, pair_screen, *rest):
    arrays, (swapped, residual_in, residual, held, sems) = rest[:-5], rest[-5:]
    blk, grp = lax.axis_index("blk"), lax.axis_index("grp")
    ab_tiles, owner_rows, tile_width = residual.shape
    chips = tile_ab.shape[1] // CORES
    bounds = [ab_tiles * part // parts for part in range(parts + 1)]
    spans = [pl.ds(low, high - low) for low, high in zip(bounds[:-1], bounds[1:])]
    leaves = [pltpu.make_async_copy(held.at[span], residual.at[span], sems.at[i]) for i, span in enumerate(spans)]

    def hold(ab, carry):
        held[ab] = residual_in[ab]
        return carry

    lax.fori_loop(0, ab_tiles, hold, 0)
    pieces = pieces_of(arrays, owner_rows)
    own = grp % CORES * owner_rows
    for start in range(0, len(pieces), chips):
        terms = []
        for index in range(start, start + chips):
            array, first = pieces[index]
            p = jnp.bitwise_xor(blk, index // chips)
            g = jnp.bitwise_xor(grp, index % chips * CORES)
            here = pl.ds(pl.multiple_of(first + own, owner_rows), owner_rows)
            there = pl.ds(index * owner_rows, owner_rows)
            for source, span, column in ((array, here, g), (swapped, there, jnp.bitwise_xor(g, 1))):
                kept = pair_screen[tile_cd[p, column], grp].astype(jnp.float32)
                scale = row_scale(source[span, :LANES]) * kept
                terms.append((source, span, scale, tile_ab[p, column]))
        for source, span, scale, ab in terms:
            for lane in range(0, tile_width, LANES):
                term = source[span, lane : lane + LANES].astype(jnp.float32) * scale
                held[ab, :, lane : lane + LANES] = held[ab, :, lane : lane + LANES] + term
    start_all(leaves)
    wait_all(leaves)


def add_blocks(tile_ab, tile_cd, pair_screen, arrays, swapped, residual_in):
    parts = 5
    return pl.pallas_call(
        lambda *refs: add_kernel(parts, *refs),
        out_shape=jax.ShapeDtypeStruct(residual_in.shape, residual_in.dtype),
        in_specs=[SMEM] * 3 + [VMEM] * (len(arrays) + 2),
        out_specs=ANY,
        scratch_shapes=[pltpu.VMEM(residual_in.shape, residual_in.dtype), pltpu.SemaphoreType.DMA((parts,))],
        compiler_params=vmem_limit(*arrays, swapped, residual_in, residual_in),
        name="add_contributions",
    )(tile_ab, tile_cd, pair_screen, *arrays, swapped, residual_in)


def shards(amplitudes, pair_screen, integrals, tile_ab, tile_cd, residual_in):
    blk_count = lax.axis_size("blk")
    grp_count = lax.axis_size("grp")
    chips = grp_count // CORES
    owner_rows = residual_in.shape[0]
    far = blk_count - 1

    def swap(value, blk_step, chip_step, core_step=0):
        step = blk_step * grp_count + chip_step * CORES + core_step
        pairs = [(device, device ^ step) for device in range(blk_count * grp_count)]
        return lax.ppermute(value, ("blk", "grp"), pairs)

    def along_chips(outgoing):
        arrived = {step: swap(outgoing[step], 0, step) for step in reversed(range(1, chips))}
        return [outgoing[0]] + [arrived[step] for step in range(1, chips)]

    tile = integrals[0]
    own_rows, *near_picked, far_picked = pick(tile_cd, amplitudes)
    near_rows = [swap(rows, index + 1, 0) for index, rows in enumerate(near_picked)]
    *own_out, far_picked = contract_own(own_rows, far_picked, tile, chips)
    own_in = along_chips(own_out)
    far_rows = swap(far_picked, far, 0)
    near_in = along_chips(contract_near(near_rows, tile, chips))
    near_back = regroup(near_in, blk_count - 2, "regroup_by_group")
    near_in = [swap(rows, index + 1, 0) for index, rows in enumerate(near_back)]
    far_back = swap(contract_far(far_rows, tile, chips, own_in[1:]), far, 0)
    far_in = along_chips(regroup([far_back], chips, "regroup_by_chip"))
    arrays = [*own_in, *near_in, *far_in]
    swapped = swap(other_core_rows(arrays, owner_rows), 0, 0, 1)
    by_tile = jnp.transpose(residual_in, (1, 0, 2))
    added = add_blocks(tile_ab, tile_cd, pair_screen, arrays, swapped, by_tile)
    return jnp.transpose(added, (1, 0, 2))


def solution(mesh):
    in_specs = (
        P(None, "blk", None),
        P(None, "blk"),
        P(("blk", "grp"), None, None),
        P(),
        P(),
        P(("blk", "grp"), None, None),
    )
    out_specs = P(("blk", "grp"), None, None)
    return jax.shard_map(shards, mesh=mesh, in_specs=in_specs, out_specs=out_specs, check_vma=False)
```

time: 81.2 us -> 51.8 us (0.64)
  starting transfers between devices: 4.32 us -> 26.3 us
  blocking collectives: 19.1 us -> 0 us
  other arithmetic: 16.2 us -> 0 us
  waiting for transfers between devices: 27.5 us -> 13.6 us
  between operations: 7.36 us -> 0.1 us
  Pallas kernels: 0 us -> 6.47 us
  matrix products: 2.24 us -> 0 us
  local copies, waits for them, and re-layouts: 3.92 us -> 5.11 us
    all_to_all x1 -> x0, waiting for transfers between devices: 27.5 us -> none  [shards(): lax.all_to_all(coded, ('blk', 'grp'), split_axis=0, concat_axis=0, tiled=...]
    ppermute x0 -> x16, starting transfers between devices: none -> 26.3 us  [swap(): return lax.ppermute(value, ('blk', 'grp'), pairs)]
    all_to_all x1 -> x0, blocking collectives: 19.1 us -> none  [shards(): lax.all_to_all(outgoing, 'blk', split_axis=0, concat_axis=0, tiled=True)]
    ppermute x0 -> x16, waiting for transfers between devices: none -> 13.6 us  [swap(): return lax.ppermute(value, ('blk', 'grp'), pairs)]
    scatter-add x1 -> x0, other arithmetic: 6.87 us -> none  [shards(): jax.ops.segment_sum(blocks, tile_ab.reshape(-1), num_segments=ab_tiles)]
    pallas_call x0 -> x8, Pallas kernels: none -> 6.47 us  [the longest x1 3.12 us: add_blocks(): pl.pallas_call(lambda *refs: add_kernel(parts, *refs), out_shape=jax.Shap...]
    add x1 -> x0, other arithmetic: 5.64 us -> none  [shards(): return residual_in + jnp.transpose(summed, (1, 0, 2))]
    unnamed x4 -> x18, local copies, waits for them, and re-layouts: 0.01 us -> 5.11 us
  transfers between devices with their start and end apart: 1 -> 16, of which waited for: 1 -> 6; matrix products, arithmetic and copies ran while one was open for 0% -> 0% of each run, Pallas kernels for 0% -> 5%
where the time goes in v8:
time: 51.8 us; the launch traced here: 51.6 us
  starting transfers between devices  26.3 us (51%)
  waiting for transfers between devices  13.6 us (26%)
  Pallas kernels  6.47 us (12%)
  local copies, waits for them, and re-layouts  5.11 us (10%)
    ppermute x16, starting transfers between devices, swap(): return lax.ppermute(value, ('blk', 'grp'), pairs)  26.3 us
    ppermute x16, waiting for transfers between devices, swap(): return lax.ppermute(value, ('blk', 'grp'), pairs)  13.6 us
    unnamed x18, local copies, waits for them, and re-layouts  5.11 us
    pallas_call x1, Pallas kernels, add_blocks(): pl.pallas_call(lambda *refs: add_kernel(parts, *refs), out_shape=jax.Shap...  3.12 us
    pallas_call x1, Pallas kernels, contract_near(): pl.pallas_call(lambda *refs: near_kernel(len(groups), *refs), out_shape=[...  1.15 us
  transfers between devices with their start and end apart: 16, of which 6 were waited for; matrix products, arithmetic and copies ran while one was open for 0% of the time, Pallas kernels for 5%

profile of v8, /device:TPU:0, one launch (start us, length us, event | category | flops | bytes accessed | tf_op | source)
XLA Modules:
  0.0 51.6 jit_solution(5576994055899837933)
XLA Ops:
  0.0 0.0 copy-start.4
  0.0 1.2 %copy-done.4 = bf16[4,128,1024]{2,1,0:T(8,128)(2,1)S(1)} copy-done((bf16[4,128,1024]{2,1,0:T(8,128)(2,1)S(1)}, bf16[4,128,1024]{2,1,0:T(8,128)(2,1)}, u32[]{:S(2)}) %copy-start.4) | copy-done | bytes 1048600
  1.2 0.0 copy-start.5
  1.2 0.7 %copy-done.5 = s32[4,8]{1,0:T(4,128)S(1)} copy-done((s32[4,8]{1,0:T(4,128)S(1)}, s32[4,8]{1,0:T(4,128)}, u32[]{:S(2)}) %copy-start.5) | copy-done | bytes 152
  1.9 0.7 %pick_cd_blocks.1 = (bf16[128,1024]{1,0:T(8,128)(2,1)S(1)}, bf16[128,1024]{1,0:T(8,128)(2,1)S(1)}, bf16[128,1024]{1,0:T(8,128)(2,1)S(1)}, bf16[128,1024]{1,0:T(8,128)(2,1)S(1)}) custom-call(s32[4,8]{1,0:T(4,128)S(1)} %copy-done.5, bf16[4,128,1024]{2,1,0:T(8,128)(2,1)S(1)} %copy-done.4), custom_call_target="tpu_custom_call" | custom-call | tf_op jit(solution)/shard_map/pick_cd_blocks/pallas_call | solution.py:81
  2.6 3.0 %collective-permute-start.3 = (bf16[128,1024]{1,0:T(8,128)(2,1)S(1)}, bf16[128,1024]{1,0:T(8,128)(2,1)S(1)}, u32[]{:S(2)}, u32[]{:S(2)}) collective-permute-start(bf16[128,1024]{1,0:T(8,128)(2,1)S(1)} %get-tuple-element.30), channel_id=1, source_target_pairs={{0,8},{1,9},{2,10},{3,11},{4,12},{5,13},{6,14},{7,15},{8,0},{9,1},... | collective-permute-start | bytes 786440 | tf_op jit(solution)/shard_map/ppermute | solution.py:276
  5.6 1.5 %collective-permute-start.4 = (bf16[128,1024]{1,0:T(8,128)(2,1)S(1)}, bf16[128,1024]{1,0:T(8,128)(2,1)S(1)}, u32[]{:S(2)}, u32[]{:S(2)}) collective-permute-start(bf16[128,1024]{1,0:T(8,128)(2,1)S(1)} %get-tuple-element.31), channel_id=1, source_target_pairs={{0,16},{1,17},{2,18},{3,19},{4,20},{5,21},{6,22},{7,23},{8,24},{9,... | collective-permute-start | bytes 786440 | tf_op jit(solution)/shard_map/ppermute | solution.py:276
  7.1 0.0 copy-start
  7.1 1.6 %copy-done = bf16[1,1024,1024]{2,1,0:T(8,128)(2,1)S(1)} copy-done((bf16[1,1024,1024]{2,1,0:T(8,128)(2,1)S(1)}, bf16[1,1024,1024]{2,1,0:T(8,128)(2,1)}, u32[]{:S(2)}) %copy-start) | copy-done | bytes 2097176
  8.7 0.0 copy-start.2
  8.7 0.7 %contract_own_group.1 = (s16[32,1024]{1,0:T(8,128)(2,1)S(1)}, s16[32,1024]{1,0:T(8,128)(2,1)S(1)}, s16[32,1024]{1,0:T(8,128)(2,1)S(1)}, s16[32,1024]{1,0:T(8,128)(2,1)S(1)}, bf16[128,1024]{1,0:T(8,128)(2,1)S(1)}) custom-call(bf16[128,1024]{1,0:T(8,128)(2,1)S(1)} %get-tuple-element.24.rows, bf16[128,1024]{1,0:T(8,128)(2,1)S(1)} %get-tuple-element.25.far_picked, ...), custom_call_target="tpu_custom_call" | custom-call | flops 268435456 | bytes 2097152 | tf_op jit(solution)/shard_map/contract_own_group/pallas_call | solution.py:114
  9.5 0.1 collective-permute-start.10
  9.5 2.0 %collective-permute-start = (s16[32,1024]{1,0:T(8,128)(2,1)S(1)}, s16[32,1024]{1,0:T(8,128)(2,1)S(1)}, u32[]{:S(2)}, u32[]{:S(2)}) collective-permute-start(s16[32,1024]{1,0:T(8,128)(2,1)S(1)} %get-tuple-element.27), channel_id=1, source_target_pairs={{0,2},{1,3},{2,0},{3,1},{4,6},{5,7},{6,4},{7,5},{8,10},{9,11},{10,... | collective-permute-start | bytes 196616 | tf_op jit(solution)/shard_map/ppermute | solution.py:276
  11.6 2.6 %collective-permute-start.1 = (s16[32,1024]{1,0:T(8,128)(2,1)S(1)}, s16[32,1024]{1,0:T(8,128)(2,1)S(1)}, u32[]{:S(2)}, u32[]{:S(2)}) collective-permute-start(s16[32,1024]{1,0:T(8,128)(2,1)S(1)} %get-tuple-element.28), channel_id=1, source_target_pairs={{0,4},{1,5},{2,6},{3,7},{4,0},{5,1},{6,2},{7,3},{8,12},{9,13},{10,... | collective-permute-start | bytes 196616 | tf_op jit(solution)/shard_map/ppermute | solution.py:276
  14.2 0.0 collective-permute-done.3.refs_0_
  14.2 2.4 %collective-permute-start.2 = (s16[32,1024]{1,0:T(8,128)(2,1)S(1)}, s16[32,1024]{1,0:T(8,128)(2,1)S(1)}, u32[]{:S(2)}, u32[]{:S(2)}) collective-permute-start(s16[32,1024]{1,0:T(8,128)(2,1)S(1)} %get-tuple-element.29), channel_id=1, source_target_pairs={{0,6},{1,7},{2,4},{3,5},{4,2},{5,3},{6,0},{7,1},{8,14},{9,15},{10,... | collective-permute-start | bytes 196616 | tf_op jit(solution)/shard_map/ppermute | solution.py:276
  16.5 2.5 %collective-permute-done.4.refs_1_ = bf16[128,1024]{1,0:T(8,128)(2,1)S(1)} collective-permute-done((bf16[128,1024]{1,0:T(8,128)(2,1)S(1)}, bf16[128,1024]{1,0:T(8,128)(2,1)S(1)}, u32[]{:S(2)}, u32[]{:S(2)}) %collective-permute-start.4) | collective-permute-done | bytes 262176 | tf_op jit(solution)/shard_map/ppermute | solution.py:276
  19.0 0.0 copy-start.1
  19.0 1.6 %copy-done.1 = bf16[1,1024,1024]{2,1,0:T(8,128)(2,1)S(1)} copy-done((bf16[1,1024,1024]{2,1,0:T(8,128)(2,1)S(1)}, bf16[1,1024,1024]{2,1,0:T(8,128)(2,1)}, u32[]{:S(2)}) %copy-start.1) | copy-done | bytes 2097176
  20.6 0.0 copy-start.3
  20.6 0.0 copy-start.6
  20.6 0.0 copy-start.7
  20.6 0.0 copy-start.8
  20.6 1.2 %contract_near_groups.1 = (s16[64,1024]{1,0:T(8,128)(2,1)S(1)}, s16[64,1024]{1,0:T(8,128)(2,1)S(1)}, s16[64,1024]{1,0:T(8,128)(2,1)S(1)}, s16[64,1024]{1,0:T(8,128)(2,1)S(1)}) custom-call(bf16[128,1024]{1,0:T(8,128)(2,1)S(1)} %collective-permute-done.3.refs_0_, bf16[128,1024]{1,0:T(8,128)(2,1)S(1)} %collective-permute-done.4.refs_1_, ...), custom_call_target="tpu_custom_call" | custom-call | flops 536870912 | bytes 2097152 | tf_op jit(solution)/shard_map/contract_near_groups/pallas_call | solution.py:137
  21.8 1.6 %collective-permute-start.5 = (s16[64,1024]{1,0:T(8,128)(2,1)S(1)}, s16[64,1024]{1,0:T(8,128)(2,1)S(1)}, u32[]{:S(2)}, u32[]{:S(2)}) collective-permute-start(s16[64,1024]{1,0:T(8,128)(2,1)S(1)} %get-tuple-element.33), channel_id=1, source_target_pairs={{0,2},{1,3},{2,0},{3,1},{4,6},{5,7},{6,4},{7,5},{8,10},{9,11},{10,... | collective-permute-start | bytes 393224 | tf_op jit(solution)/shard_map/ppermute | solution.py:276
  23.4 0.0 collective-permute-done.refs_2_.refs_1_.refs_4_
  23.4 2.6 %collective-permute-start.6 = (s16[64,1024]{1,0:T(8,128)(2,1)S(1)}, s16[64,1024]{1,0:T(8,128)(2,1)S(1)}, u32[]{:S(2)}, u32[]{:S(2)}) collective-permute-start(s16[64,1024]{1,0:T(8,128)(2,1)S(1)} %get-tuple-element.34), channel_id=1, source_target_pairs={{0,4},{1,5},{2,6},{3,7},{4,0},{5,1},{6,2},{7,3},{8,12},{9,13},{10,... | collective-permute-start | bytes 393224 | tf_op jit(solution)/shard_map/ppermute | solution.py:276
  26.0 0.0 collective-permute-done.1.refs_3_.refs_2_.refs_5_
  26.0 0.2 collective-permute-start.7
  26.2 0.0 collective-permute-done.2.refs_4_.refs_3_.refs_6_
  26.2 0.0 collective-permute-done.10.refs_0_
  26.2 0.0 copy-done.2
  26.2 0.7 %contract_far_group.1 = s16[128,1024]{1,0:T(8,128)(2,1)S(1)} custom-call(bf16[128,1024]{1,0:T(8,128)(2,1)S(1)} %collective-permute-done.10.refs_0_, bf16[1024,1024]{1,0:T(8,128)(2,1)S(1)} %bitcast.5, s16[32,1024]{1,0:T(8,128)(2,1)S(1)} %collective-permute-done.refs_2_.refs_1_.refs_4_, s16[32,1024]{1,0:T(8,128)(2,1)S(1)} %collective-permute-done.1.refs_3_.refs_2_.refs_5_, ...), custom_call_target="tpu_custom_call" | custom-call | flops 268435456 | bytes 2097152 | tf_op jit(solution)/shard_map/contract_far_group/pallas_call | solution.py:159
  26.9 1.6 %collective-permute-start.11 = (s16[128,1024]{1,0:T(8,128)(2,1)S(1)}, s16[128,1024]{1,0:T(8,128)(2,1)S(1)}, u32[]{:S(2)}, u32[]{:S(2)}) collective-permute-start(s16[128,1024]{1,0:T(8,128)(2,1)S(1)} %contract_far_group.1), channel_id=1, source_target_pairs={{0,24},{1,25},{2,26},{3,27},{4,28},{5,29},{6,30},{7,31},{8,16},{9,... | collective-permute-start | bytes 786440 | tf_op jit(solution)/shard_map/ppermute | solution.py:276
  28.5 0.0 collective-permute-done.5.refs_1_
  28.5 2.2 %collective-permute-done.6.refs_2_ = s16[64,1024]{1,0:T(8,128)(2,1)S(1)} collective-permute-done((s16[64,1024]{1,0:T(8,128)(2,1)S(1)}, s16[64,1024]{1,0:T(8,128)(2,1)S(1)}, u32[]{:S(2)}, u32[]{:S(2)}) %collective-permute-start.6) | collective-permute-done | bytes 131104 | tf_op jit(solution)/shard_map/ppermute | solution.py:276
  30.7 2.2 %collective-permute-done.7.refs_3_ = s16[64,1024]{1,0:T(8,128)(2,1)S(1)} collective-permute-done((s16[64,1024]{1,0:T(8,128)(2,1)S(1)}, s16[64,1024]{1,0:T(8,128)(2,1)S(1)}, u32[]{:S(2)}, u32[]{:S(2)}) %collective-permute-start.7) | collective-permute-done | bytes 131104 | tf_op jit(solution)/shard_map/ppermute | solution.py:276
  33.0 0.1 collective-permute-start.8
  33.0 2.6 %collective-permute-start.9 = (s16[128,1024]{1,0:T(8,128)(2,1)S(1)}, s16[128,1024]{1,0:T(8,128)(2,1)S(1)}, u32[]{:S(2)}, u32[]{:S(2)}) collective-permute-start(s16[128,1024]{1,0:T(8,128)(2,1)S(1)} %get-tuple-element.37), channel_id=1, source_target_pairs={{0,16},{1,17},{2,18},{3,19},{4,20},{5,21},{6,22},{7,23},{8,24},{9,... | collective-permute-start | bytes 786440 | tf_op jit(solution)/shard_map/ppermute | solution.py:276
  35.7 0.0 collective-permute-done.11.refs_0_
  35.7 2.4 %collective-permute-start.12 = (s16[32,1024]{1,0:T(8,128)(2,1)S(1)}, s16[32,1024]{1,0:T(8,128)(2,1)S(1)}, u32[]{:S(2)}, u32[]{:S(2)}) collective-permute-start(s16[32,1024]{1,0:T(8,128)(2,1)S(1)} %get-tuple-element.40), channel_id=1, source_target_pairs={{0,2},{1,3},{2,0},{3,1},{4,6},{5,7},{6,4},{7,5},{8,10},{9,11},{10,... | collective-permute-start | bytes 196616 | tf_op jit(solution)/shard_map/ppermute | solution.py:276
  38.1 2.1 %collective-permute-start.13 = (s16[32,1024]{1,0:T(8,128)(2,1)S(1)}, s16[32,1024]{1,0:T(8,128)(2,1)S(1)}, u32[]{:S(2)}, u32[]{:S(2)}) collective-permute-start(s16[32,1024]{1,0:T(8,128)(2,1)S(1)} %get-tuple-element.41), channel_id=1, source_target_pairs={{0,4},{1,5},{2,6},{3,7},{4,0},{5,1},{6,2},{7,3},{8,12},{9,13},{10,... | collective-permute-start | bytes 196616 | tf_op jit(solution)/shard_map/ppermute | solution.py:276
  40.2 1.4 %collective-permute-start.14 = (s16[32,1024]{1,0:T(8,128)(2,1)S(1)}, s16[32,1024]{1,0:T(8,128)(2,1)S(1)}, u32[]{:S(2)}, u32[]{:S(2)}) collective-permute-start(s16[32,1024]{1,0:T(8,128)(2,1)S(1)} %get-tuple-element.42), channel_id=1, source_target_pairs={{0,6},{1,7},{2,4},{3,5},{4,2},{5,3},{6,0},{7,1},{8,14},{9,15},{10,... | collective-permute-start | bytes 196616 | tf_op jit(solution)/shard_map/ppermute | solution.py:276
  41.6 0.0 collective-permute-done.12.refs_7_.refs_10_
  41.6 1.7 %collective-permute-done.13.refs_8_.refs_11_ = s16[32,1024]{1,0:T(8,128)(2,1)S(1)} collective-permute-done((s16[32,1024]{1,0:T(8,128)(2,1)S(1)}, s16[32,1024]{1,0:T(8,128)(2,1)S(1)}, u32[]{:S(2)}, u32[]{:S(2)}) %collective-permute-start.13) | collective-permute-done | bytes 65568 | tf_op jit(solution)/shard_map/ppermute | solution.py:276
  43.3 3.1 %collective-permute-done.14.refs_9_.refs_12_ = s16[32,1024]{1,0:T(8,128)(2,1)S(1)} collective-permute-done((s16[32,1024]{1,0:T(8,128)(2,1)S(1)}, s16[32,1024]{1,0:T(8,128)(2,1)S(1)}, u32[]{:S(2)}, u32[]{:S(2)}) %collective-permute-start.14) | collective-permute-done | bytes 65568 | tf_op jit(solution)/shard_map/ppermute | solution.py:276
  46.4 0.0 collective-permute-done.8.refs_4_.refs_7_
  46.4 0.0 collective-permute-done.9.refs_5_.refs_8_
  46.4 0.1 collective-permute-start.15
  46.5 1.9 %collective-permute-done.15.refs_13_ = s16[256,1024]{1,0:T(8,128)(2,1)S(1)} collective-permute-done((s16[256,1024]{1,0:T(8,128)(2,1)S(1)}, s16[256,1024]{1,0:T(8,128)(2,1)S(1)}, u32[]{:S(2)}, u32[]{:S(2)}) %collective-permute-start.15) | collective-permute-done | bytes 524320 | tf_op jit(solution)/shard_map/ppermute | solution.py:276
  48.4 0.0 copy-done.3
  48.4 0.0 copy-done.6
  48.4 0.0 copy-done.7
  48.4 0.0 copy-done.8
  48.4 3.1 %add_contributions.1 = f32[50,16,1024]{2,1,0:T(8,128)} custom-call(s32[4,8]{1,0:T(4,128)S(1)} %copy-done.7, s32[4,8]{1,0:T(4,128)S(1)} %copy-done.6, s32[4,8]{1,0:T(4,128)S(1)} %copy-done.8, s16[32,1024]{1,0:T(8,128)(2,1)S(1)} %get-tuple-element.26.refs_0_.refs_3_, s16[32,1024]{1,0:T(8,128)(2,1)S(1)} %collective-permute-done.refs_2_.refs_1_.refs_4_, ...), custom_call_target="tpu_custom_call" | custom-call | tf_op jit(solution)/shard_map/add_contributions/pallas_call | solution.py:255
  (3 shorter events, 0.1 us)
Async XLA Ops:
  0.0 1.2 %copy-start.4 = (bf16[4,128,1024]{2,1,0:T(8,128)(2,1)S(1)}, bf16[4,128,1024]{2,1,0:T(8,128)(2,1)}, u32[]{:S(2)}) copy-start(bf16[4,128,1024]{2,1,0:T(8,128)(2,1)} %amplitudes.1) | copy-start | bytes 3145732
  1.2 0.7 %copy-start.5 = (s32[4,8]{1,0:T(4,128)S(1)}, s32[4,8]{1,0:T(4,128)}, u32[]{:S(2)}) copy-start(s32[4,8]{1,0:T(4,128)} %refs_1_.1) | copy-start | bytes 388
  2.6 11.5 %collective-permute-start.3 = (bf16[128,1024]{1,0:T(8,128)(2,1)S(1)}, bf16[128,1024]{1,0:T(8,128)(2,1)S(1)}, u32[]{:S(2)}, u32[]{:S(2)}) collective-permute-start(bf16[128,1024]{1,0:T(8,128)(2,1)S(1)} %get-tuple-element.30), channel_id=1, source_target_pairs={{0,8},{1,9},{2,10},{3,11},{4,12},{5,13},{6,14},{7,15},{8,0},{9,1},... | collective-permute-start | bytes 786440 | tf_op jit(solution)/shard_map/ppermute | solution.py:276
  5.6 13.4 %collective-permute-start.4 = (bf16[128,1024]{1,0:T(8,128)(2,1)S(1)}, bf16[128,1024]{1,0:T(8,128)(2,1)S(1)}, u32[]{:S(2)}, u32[]{:S(2)}) collective-permute-start(bf16[128,1024]{1,0:T(8,128)(2,1)S(1)} %get-tuple-element.31), channel_id=1, source_target_pairs={{0,16},{1,17},{2,18},{3,19},{4,20},{5,21},{6,22},{7,23},{8,24},{9,... | collective-permute-start | bytes 786440 | tf_op jit(solution)/shard_map/ppermute | solution.py:276
  7.1 1.6 %copy-start = (bf16[1,1024,1024]{2,1,0:T(8,128)(2,1)S(1)}, bf16[1,1024,1024]{2,1,0:T(8,128)(2,1)}, u32[]{:S(2)}) copy-start(bf16[1,1024,1024]{2,1,0:T(8,128)(2,1)} %param.8) | copy-start | bytes 6291460
  8.7 17.5 %copy-start.2 = (bf16[1,1024,1024]{2,1,0:T(8,128)(2,1)S(1)}, bf16[1,1024,1024]{2,1,0:T(8,128)(2,1)}, u32[]{:S(2)}) copy-start(bf16[1,1024,1024]{2,1,0:T(8,128)(2,1)} %param.8) | copy-start | bytes 6291460
  9.5 16.8 %collective-permute-start.10 = (bf16[128,1024]{1,0:T(8,128)(2,1)S(1)}, bf16[128,1024]{1,0:T(8,128)(2,1)S(1)}, u32[]{:S(2)}, u32[]{:S(2)}) collective-permute-start(bf16[128,1024]{1,0:T(8,128)(2,1)S(1)} %get-tuple-element.38), channel_id=1, source_target_pairs={{0,24},{1,25},{2,26},{3,27},{4,28},{5,29},{6,30},{7,31},{8,16},{9,... | collective-permute-start | bytes 786440 | tf_op jit(solution)/shard_map/ppermute | solution.py:276
  9.5 13.9 %collective-permute-start = (s16[32,1024]{1,0:T(8,128)(2,1)S(1)}, s16[32,1024]{1,0:T(8,128)(2,1)S(1)}, u32[]{:S(2)}, u32[]{:S(2)}) collective-permute-start(s16[32,1024]{1,0:T(8,128)(2,1)S(1)} %get-tuple-element.27), channel_id=1, source_target_pairs={{0,2},{1,3},{2,0},{3,1},{4,6},{5,7},{6,4},{7,5},{8,10},{9,11},{10,... | collective-permute-start | bytes 196616 | tf_op jit(solution)/shard_map/ppermute | solution.py:276
  11.6 14.4 %collective-permute-start.1 = (s16[32,1024]{1,0:T(8,128)(2,1)S(1)}, s16[32,1024]{1,0:T(8,128)(2,1)S(1)}, u32[]{:S(2)}, u32[]{:S(2)}) collective-permute-start(s16[32,1024]{1,0:T(8,128)(2,1)S(1)} %get-tuple-element.28), channel_id=1, source_target_pairs={{0,4},{1,5},{2,6},{3,7},{4,0},{5,1},{6,2},{7,3},{8,12},{9,13},{10,... | collective-permute-start | bytes 196616 | tf_op jit(solution)/shard_map/ppermute | solution.py:276
  14.2 12.1 %collective-permute-start.2 = (s16[32,1024]{1,0:T(8,128)(2,1)S(1)}, s16[32,1024]{1,0:T(8,128)(2,1)S(1)}, u32[]{:S(2)}, u32[]{:S(2)}) collective-permute-start(s16[32,1024]{1,0:T(8,128)(2,1)S(1)} %get-tuple-element.29), channel_id=1, source_target_pairs={{0,6},{1,7},{2,4},{3,5},{4,2},{5,3},{6,0},{7,1},{8,14},{9,15},{10,... | collective-permute-start | bytes 196616 | tf_op jit(solution)/shard_map/ppermute | solution.py:276
  19.0 1.6 %copy-start.1 = (bf16[1,1024,1024]{2,1,0:T(8,128)(2,1)S(1)}, bf16[1,1024,1024]{2,1,0:T(8,128)(2,1)}, u32[]{:S(2)}) copy-start(bf16[1,1024,1024]{2,1,0:T(8,128)(2,1)} %param.8) | copy-start | bytes 6291460
  20.6 27.8 %copy-start.3 = (f32[16,50,1024]{2,0,1:T(8,128)S(1)}, f32[16,50,1024]{2,0,1:T(8,128)}, u32[]{:S(2)}) copy-start(f32[16,50,1024]{2,0,1:T(8,128)} %param.11) | copy-start | bytes 9830404
  20.6 27.8 %copy-start.6 = (s32[4,8]{1,0:T(4,128)S(1)}, s32[4,8]{1,0:T(4,128)}, u32[]{:S(2)}) copy-start(s32[4,8]{1,0:T(4,128)} %refs_1_.1) | copy-start | bytes 388
  20.6 27.8 %copy-start.7 = (s32[4,8]{1,0:T(4,128)S(1)}, s32[4,8]{1,0:T(4,128)}, u32[]{:S(2)}) copy-start(s32[4,8]{1,0:T(4,128)} %refs_0_.1) | copy-start | bytes 388
  20.6 27.8 %copy-start.8 = (s32[4,8]{1,0:T(4,128)S(1)}, s32[4,8]{1,0:T(4,128)}, u32[]{:S(2)}) copy-start(s32[4,8]{1,0:T(4,128)} %refs_2_.1) | copy-start | bytes 388
  21.8 6.7 %collective-permute-start.5 = (s16[64,1024]{1,0:T(8,128)(2,1)S(1)}, s16[64,1024]{1,0:T(8,128)(2,1)S(1)}, u32[]{:S(2)}, u32[]{:S(2)}) collective-permute-start(s16[64,1024]{1,0:T(8,128)(2,1)S(1)} %get-tuple-element.33), channel_id=1, source_target_pairs={{0,2},{1,3},{2,0},{3,1},{4,6},{5,7},{6,4},{7,5},{8,10},{9,11},{10,... | collective-permute-start | bytes 393224 | tf_op jit(solution)/shard_map/ppermute | solution.py:276
  23.4 7.3 %collective-permute-start.6 = (s16[64,1024]{1,0:T(8,128)(2,1)S(1)}, s16[64,1024]{1,0:T(8,128)(2,1)S(1)}, u32[]{:S(2)}, u32[]{:S(2)}) collective-permute-start(s16[64,1024]{1,0:T(8,128)(2,1)S(1)} %get-tuple-element.34), channel_id=1, source_target_pairs={{0,4},{1,5},{2,6},{3,7},{4,0},{5,1},{6,2},{7,3},{8,12},{9,13},{10,... | collective-permute-start | bytes 393224 | tf_op jit(solution)/shard_map/ppermute | solution.py:276
  26.0 6.9 %collective-permute-start.7 = (s16[64,1024]{1,0:T(8,128)(2,1)S(1)}, s16[64,1024]{1,0:T(8,128)(2,1)S(1)}, u32[]{:S(2)}, u32[]{:S(2)}) collective-permute-start(s16[64,1024]{1,0:T(8,128)(2,1)S(1)} %get-tuple-element.35), channel_id=1, source_target_pairs={{0,6},{1,7},{2,4},{3,5},{4,2},{5,3},{6,0},{7,1},{8,14},{9,15},{10,... | collective-permute-start | bytes 393224 | tf_op jit(solution)/shard_map/ppermute | solution.py:276
  26.9 8.7 %collective-permute-start.11 = (s16[128,1024]{1,0:T(8,128)(2,1)S(1)}, s16[128,1024]{1,0:T(8,128)(2,1)S(1)}, u32[]{:S(2)}, u32[]{:S(2)}) collective-permute-start(s16[128,1024]{1,0:T(8,128)(2,1)S(1)} %contract_far_group.1), channel_id=1, source_target_pairs={{0,24},{1,25},{2,26},{3,27},{4,28},{5,29},{6,30},{7,31},{8,16},{9,... | collective-permute-start | bytes 786440 | tf_op jit(solution)/shard_map/ppermute | solution.py:276
  33.0 13.4 %collective-permute-start.8 = (s16[128,1024]{1,0:T(8,128)(2,1)S(1)}, s16[128,1024]{1,0:T(8,128)(2,1)S(1)}, u32[]{:S(2)}, u32[]{:S(2)}) collective-permute-start(s16[128,1024]{1,0:T(8,128)(2,1)S(1)} %get-tuple-element.36), channel_id=1, source_target_pairs={{0,8},{1,9},{2,10},{3,11},{4,12},{5,13},{6,14},{7,15},{8,0},{9,1},... | collective-permute-start | bytes 786440 | tf_op jit(solution)/shard_map/ppermute | solution.py:276
  33.0 13.4 %collective-permute-start.9 = (s16[128,1024]{1,0:T(8,128)(2,1)S(1)}, s16[128,1024]{1,0:T(8,128)(2,1)S(1)}, u32[]{:S(2)}, u32[]{:S(2)}) collective-permute-start(s16[128,1024]{1,0:T(8,128)(2,1)S(1)} %get-tuple-element.37), channel_id=1, source_target_pairs={{0,16},{1,17},{2,18},{3,19},{4,20},{5,21},{6,22},{7,23},{8,24},{9,... | collective-permute-start | bytes 786440 | tf_op jit(solution)/shard_map/ppermute | solution.py:276
  35.7 5.9 %collective-permute-start.12 = (s16[32,1024]{1,0:T(8,128)(2,1)S(1)}, s16[32,1024]{1,0:T(8,128)(2,1)S(1)}, u32[]{:S(2)}, u32[]{:S(2)}) collective-permute-start(s16[32,1024]{1,0:T(8,128)(2,1)S(1)} %get-tuple-element.40), channel_id=1, source_target_pairs={{0,2},{1,3},{2,0},{3,1},{4,6},{5,7},{6,4},{7,5},{8,10},{9,11},{10,... | collective-permute-start | bytes 196616 | tf_op jit(solution)/shard_map/ppermute | solution.py:276
  38.1 5.2 %collective-permute-start.13 = (s16[32,1024]{1,0:T(8,128)(2,1)S(1)}, s16[32,1024]{1,0:T(8,128)(2,1)S(1)}, u32[]{:S(2)}, u32[]{:S(2)}) collective-permute-start(s16[32,1024]{1,0:T(8,128)(2,1)S(1)} %get-tuple-element.41), channel_id=1, source_target_pairs={{0,4},{1,5},{2,6},{3,7},{4,0},{5,1},{6,2},{7,3},{8,12},{9,13},{10,... | collective-permute-start | bytes 196616 | tf_op jit(solution)/shard_map/ppermute | solution.py:276
  40.2 6.2 %collective-permute-start.14 = (s16[32,1024]{1,0:T(8,128)(2,1)S(1)}, s16[32,1024]{1,0:T(8,128)(2,1)S(1)}, u32[]{:S(2)}, u32[]{:S(2)}) collective-permute-start(s16[32,1024]{1,0:T(8,128)(2,1)S(1)} %get-tuple-element.42), channel_id=1, source_target_pairs={{0,6},{1,7},{2,4},{3,5},{4,2},{5,3},{6,0},{7,1},{8,14},{9,15},{10,... | collective-permute-start | bytes 196616 | tf_op jit(solution)/shard_map/ppermute | solution.py:276
  46.4 2.0 %collective-permute-start.15 = (s16[256,1024]{1,0:T(8,128)(2,1)S(1)}, s16[256,1024]{1,0:T(8,128)(2,1)S(1)}, u32[]{:S(2)}, u32[]{:S(2)}) collective-permute-start(s16[256,1024]{1,0:T(8,128)(2,1)S(1)} %rows_of_other_core.1), channel_id=1, source_target_pairs={{0,1},{1,0},{2,3},{3,2},{4,5},{5,4},{6,7},{7,6},{8,9},{9,8},{10,11... | collective-permute-start | bytes 1572872 | tf_op jit(solution)/shard_map/ppermute | solution.py:276

commit v9 on v8

--- a/solution.py
+++ b/solution.py
@@ -54,6 +54,12 @@
     return pl.CostEstimate(flops=flops, bytes_accessed=2 * tile.shape[-2] * tile.shape[-1], transcendentals=0)
 
 
+def blk_steps(blk_count, core):
+    near = blk_count - 2
+    steps = [slot + 1 + core * (near - 1 - 2 * slot) for slot in range(near)]
+    return [0] + steps + [blk_count - 1]
+
+
 def start_all(copies):
     for copy in copies:
         copy.start()
@@ -68,9 +74,9 @@
     outgoing, sems = rest[:-1], rest[-1]
     blk, grp = lax.axis_index("blk"), lax.axis_index("grp")
     copies = []
-    for step, picked in enumerate(outgoing):
+    for slot, step in enumerate(blk_steps(len(outgoing), grp % CORES)):
         cd = tile_cd[jnp.bitwise_xor(blk, step), grp]
-        copies.append(pltpu.make_async_copy(amplitudes.at[cd], picked, sems.at[step]))
+        copies.append(pltpu.make_async_copy(amplitudes.at[cd], outgoing[slot], sems.at[slot]))
     start_all(copies)
     wait_all(copies)
 
@@ -100,27 +106,30 @@
         coded[first : first + chip_rows, LANES:] = tail
 
 
-def own_kernel(rows, far_picked, tile, *rest):
-    outgoing, (far_rows, product) = rest[:-2], rest[-2:]
-    far_rows[...] = far_picked[...]
+def own_kernel(rows, tile, far_picked, *rest):
+    outgoing, (tile_out, far_out, product, sem) = rest[:-4], rest[-4:]
+    copy = pltpu.make_async_copy(tile, tile_out, sem)
+    copy.start()
+    far_out[...] = far_picked[...]
     code_chips(rows, tile, product, outgoing, 0)
-
-
-def contract_own(rows, far_picked, tile, chips):
+    copy.wait()
+
+
+def contract_own(rows, tile, far_picked, chips):
     group_rows, tile_width = rows.shape[0], tile.shape[1]
     coded = jax.ShapeDtypeStruct((group_rows // chips, tile_width), jnp.int16)
     product = jax.ShapeDtypeStruct((group_rows, tile_width), jnp.float32)
-    outputs = [coded] * chips + [jax.ShapeDtypeStruct(rows.shape, rows.dtype)]
+    outputs = [coded] * chips + [jax.ShapeDtypeStruct(array.shape, array.dtype) for array in (tile, far_picked)]
     return pl.pallas_call(
         own_kernel,
         out_shape=outputs,
         in_specs=[VMEM] * 3,
         out_specs=[VMEM] * len(outputs),
-        scratch_shapes=[pltpu.VMEM(product.shape, product.dtype)],
-        compiler_params=vmem_limit(rows, far_picked, tile, *outputs, product),
+        scratch_shapes=[pltpu.VMEM(product.shape, product.dtype), pltpu.SemaphoreType.DMA],
+        compiler_params=vmem_limit(rows, tile, far_picked, *outputs, product),
         cost_estimate=cost(group_rows, tile),
         name="contract_own_group",
-    )(rows, far_picked, tile)
+    )(rows, tile, far_picked)
 
 
 def near_kernel(near, *refs):
@@ -229,16 +238,19 @@
 
     lax.fori_loop(0, ab_tiles, hold, 0)
     pieces = pieces_of(arrays, owner_rows)
-    own = grp % CORES * owner_rows
+    core = grp % CORES
+    steps_here, steps_there = blk_steps(tile_ab.shape[0], core), blk_steps(tile_ab.shape[0], 1 - core)
+    own = core * owner_rows
     for start in range(0, len(pieces), chips):
         terms = []
         for index in range(start, start + chips):
             array, first = pieces[index]
-            p = jnp.bitwise_xor(blk, index // chips)
+            p_here = jnp.bitwise_xor(blk, steps_here[index // chips])
+            p_there = jnp.bitwise_xor(blk, steps_there[index // chips])
             g = jnp.bitwise_xor(grp, index % chips * CORES)
             here = pl.ds(pl.multiple_of(first + own, owner_rows), owner_rows)
             there = pl.ds(index * owner_rows, owner_rows)
-            for source, span, column in ((array, here, g), (swapped, there, jnp.bitwise_xor(g, 1))):
+            for source, span, p, column in ((array, here, p_here, g), (swapped, there, p_there, jnp.bitwise_xor(g, 1))):
                 kept = pair_screen[tile_cd[p, column], grp].astype(jnp.float32)
                 scale = row_scale(source[span, :LANES]) * kept
                 terms.append((source, span, scale, tile_ab[p, column]))
@@ -270,19 +282,20 @@
     owner_rows = residual_in.shape[0]
     far = blk_count - 1
 
-    def swap(value, blk_step, chip_step, core_step=0):
-        step = blk_step * grp_count + chip_step * CORES + core_step
-        pairs = [(device, device ^ step) for device in range(blk_count * grp_count)]
+    def swap(value, slot, chip_step, core_step=0):
+        pairs = []
+        for device in range(blk_count * grp_count):
+            blk_step = blk_steps(blk_count, device % CORES)[slot]
+            pairs.append((device, device ^ (blk_step * grp_count + chip_step * CORES + core_step)))
         return lax.ppermute(value, ("blk", "grp"), pairs)
 
     def along_chips(outgoing):
         arrived = {step: swap(outgoing[step], 0, step) for step in reversed(range(1, chips))}
         return [outgoing[0]] + [arrived[step] for step in range(1, chips)]
 
-    tile = integrals[0]
     own_rows, *near_picked, far_picked = pick(tile_cd, amplitudes)
     near_rows = [swap(rows, index + 1, 0) for index, rows in enumerate(near_picked)]
-    *own_out, far_picked = contract_own(own_rows, far_picked, tile, chips)
+    *own_out, tile, far_picked = contract_own(own_rows, integrals[0], far_picked, chips)
     own_in = along_chips(own_out)
     far_rows = swap(far_picked, far, 0)
     near_in = along_chips(contract_near(near_rows, tile, chips))

time: 51.8 us -> 47.2 us (0.911)
  waiting for transfers between devices: 13.6 us -> 10.8 us
  local copies, waits for them, and re-layouts: 5.11 us -> 3.51 us
    ppermute x16, waiting for transfers between devices: 13.6 us -> 10.8 us  [swap(): return lax.ppermute(value, ('blk', 'grp'), pairs)]
    unnamed x18 -> x14, local copies, waits for them, and re-layouts: 5.11 us -> 3.51 us
  transfers between devices with their start and end apart: 16 -> 16, of which waited for: 6 -> 5; matrix products, arithmetic and copies ran while one was open for 0% -> 0% of each run, Pallas kernels for 5% -> 6%
where the time goes in v9:
time: 47.2 us; the launch traced here: 47 us
  starting transfers between devices  26 us (55%)
  waiting for transfers between devices  10.8 us (23%)
  Pallas kernels  6.62 us (14%)
  local copies, waits for them, and re-layouts  3.51 us (7%)
    ppermute x16, starting transfers between devices, swap(): return lax.ppermute(value, ('blk', 'grp'), pairs)  26 us
    ppermute x16, waiting for transfers between devices, swap(): return lax.ppermute(value, ('blk', 'grp'), pairs)  10.8 us
    unnamed x14, local copies, waits for them, and re-layouts  3.51 us
    pallas_call x1, Pallas kernels, add_blocks(): pl.pallas_call(lambda *refs: add_kernel(parts, *refs), out_shape=jax.Shap...  3.12 us
    pallas_call x1, Pallas kernels, contract_near(): pl.pallas_call(lambda *refs: near_kernel(len(groups), *refs), out_shape=[...  1.13 us
  transfers between devices with their start and end apart: 16, of which 5 were waited for; matrix products, arithmetic and copies ran while one was open for 0% of the time, Pallas kernels for 6%

profile of v9, /device:TPU:0, one launch (start us, length us, event | category | flops | bytes accessed | tf_op | source)
XLA Modules:
  0.0 47.0 jit_solution(5363604299191459591)
XLA Ops:
  0.0 0.0 copy-start.2
  0.0 1.2 %copy-done.2 = bf16[4,128,1024]{2,1,0:T(8,128)(2,1)S(1)} copy-done((bf16[4,128,1024]{2,1,0:T(8,128)(2,1)S(1)}, bf16[4,128,1024]{2,1,0:T(8,128)(2,1)}, u32[]{:S(2)}) %copy-start.2) | copy-done | bytes 1048600
  1.2 0.0 copy-start.3
  1.2 0.7 %copy-done.3 = s32[4,8]{1,0:T(4,128)S(1)} copy-done((s32[4,8]{1,0:T(4,128)S(1)}, s32[4,8]{1,0:T(4,128)}, u32[]{:S(2)}) %copy-start.3) | copy-done | bytes 152
  1.9 0.7 %pick_cd_blocks.1 = (bf16[128,1024]{1,0:T(8,128)(2,1)S(1)}, bf16[128,1024]{1,0:T(8,128)(2,1)S(1)}, bf16[128,1024]{1,0:T(8,128)(2,1)S(1)}, bf16[128,1024]{1,0:T(8,128)(2,1)S(1)}) custom-call(s32[4,8]{1,0:T(4,128)S(1)} %copy-done.3, bf16[4,128,1024]{2,1,0:T(8,128)(2,1)S(1)} %copy-done.2), custom_call_target="tpu_custom_call" | custom-call | tf_op jit(solution)/shard_map/pick_cd_blocks/pallas_call | solution.py:87
  2.6 3.0 %collective-permute-start.3 = (bf16[128,1024]{1,0:T(8,128)(2,1)S(1)}, bf16[128,1024]{1,0:T(8,128)(2,1)S(1)}, u32[]{:S(2)}, u32[]{:S(2)}) collective-permute-start(bf16[128,1024]{1,0:T(8,128)(2,1)S(1)} %get-tuple-element.31), channel_id=1, source_target_pairs={{0,8},{1,17},{2,10},{3,19},{4,12},{5,21},{6,14},{7,23},{8,0},{9,25... | collective-permute-start | bytes 786440 | tf_op jit(solution)/shard_map/ppermute | solution.py:290
  5.6 1.5 %collective-permute-start.4 = (bf16[128,1024]{1,0:T(8,128)(2,1)S(1)}, bf16[128,1024]{1,0:T(8,128)(2,1)S(1)}, u32[]{:S(2)}, u32[]{:S(2)}) collective-permute-start(bf16[128,1024]{1,0:T(8,128)(2,1)S(1)} %get-tuple-element.32), channel_id=1, source_target_pairs={{0,16},{1,9},{2,18},{3,11},{4,20},{5,13},{6,22},{7,15},{8,24},{9,1... | collective-permute-start | bytes 786440 | tf_op jit(solution)/shard_map/ppermute | solution.py:290
  7.1 0.0 copy-start.1
  7.1 1.6 %copy-done.1 = bf16[1,1024,1024]{2,1,0:T(8,128)(2,1)S(1)} copy-done((bf16[1,1024,1024]{2,1,0:T(8,128)(2,1)S(1)}, bf16[1,1024,1024]{2,1,0:T(8,128)(2,1)}, u32[]{:S(2)}) %copy-start.1) | copy-done | bytes 2097176
  8.7 0.9 %contract_own_group.1 = (s16[32,1024]{1,0:T(8,128)(2,1)S(1)}, s16[32,1024]{1,0:T(8,128)(2,1)S(1)}, s16[32,1024]{1,0:T(8,128)(2,1)S(1)}, s16[32,1024]{1,0:T(8,128...) custom-call(bf16[128,1024]{1,0:T(8,128)(2,1)S(1)} %get-tuple-element.25.rows, ...), custom_call_target="tpu_custom_call" | custom-call | flops 268435456 | bytes 2097152 | tf_op jit(solution)/shard_map/contract_own_group/pallas_call | solution.py:123
  9.6 0.1 collective-permute-start.10
  9.7 2.0 %collective-permute-start = (s16[32,1024]{1,0:T(8,128)(2,1)S(1)}, s16[32,1024]{1,0:T(8,128)(2,1)S(1)}, u32[]{:S(2)}, u32[]{:S(2)}) collective-permute-start(s16[32,1024]{1,0:T(8,128)(2,1)S(1)} %get-tuple-element.28), channel_id=1, source_target_pairs={{0,2},{1,3},{2,0},{3,1},{4,6},{5,7},{6,4},{7,5},{8,10},{9,11},{10,... | collective-permute-start | bytes 196616 | tf_op jit(solution)/shard_map/ppermute | solution.py:290
  11.7 2.6 %collective-permute-start.1 = (s16[32,1024]{1,0:T(8,128)(2,1)S(1)}, s16[32,1024]{1,0:T(8,128)(2,1)S(1)}, u32[]{:S(2)}, u32[]{:S(2)}) collective-permute-start(s16[32,1024]{1,0:T(8,128)(2,1)S(1)} %get-tuple-element.29), channel_id=1, source_target_pairs={{0,4},{1,5},{2,6},{3,7},{4,0},{5,1},{6,2},{7,3},{8,12},{9,13},{10,... | collective-permute-start | bytes 196616 | tf_op jit(solution)/shard_map/ppermute | solution.py:290
  14.3 0.0 collective-permute-done.3.refs_0_
  14.3 2.5 %collective-permute-start.2 = (s16[32,1024]{1,0:T(8,128)(2,1)S(1)}, s16[32,1024]{1,0:T(8,128)(2,1)S(1)}, u32[]{:S(2)}, u32[]{:S(2)}) collective-permute-start(s16[32,1024]{1,0:T(8,128)(2,1)S(1)} %get-tuple-element.30), channel_id=1, source_target_pairs={{0,6},{1,7},{2,4},{3,5},{4,2},{5,3},{6,0},{7,1},{8,14},{9,15},{10,... | collective-permute-start | bytes 196616 | tf_op jit(solution)/shard_map/ppermute | solution.py:290
  16.8 0.0 collective-permute-done.4.refs_1_
  16.8 0.0 copy-start
  16.8 0.0 copy-start.4
  16.8 0.0 copy-start.5
  16.8 0.0 copy-start.6
  16.8 1.1 %contract_near_groups.1 = (s16[64,1024]{1,0:T(8,128)(2,1)S(1)}, s16[64,1024]{1,0:T(8,128)(2,1)S(1)}, s16[64,1024]{1,0:T(8,128)(2,1)S(1)}, s16[64,1024]{1,0:T(8,128)(2,1)S(1)}) custom-call(bf16[128,1024]{1,0:T(8,128)(2,1)S(1)} %collective-permute-done.3.refs_0_, bf16[128,1024]{1,0:T(8,128)(2,1)S(1)} %collective-permute-done.4.refs_1_, ...), custom_call_target="tpu_custom_call" | custom-call | flops 536870912 | bytes 2097152 | tf_op jit(solution)/shard_map/contract_near_groups/pallas_call | solution.py:146
  18.0 0.1 collective-permute-start.5
  18.0 0.0 collective-permute-done.refs_2_.refs_1_.refs_4_
  18.1 1.9 %collective-permute-start.6 = (s16[64,1024]{1,0:T(8,128)(2,1)S(1)}, s16[64,1024]{1,0:T(8,128)(2,1)S(1)}, u32[]{:S(2)}, u32[]{:S(2)}) collective-permute-start(s16[64,1024]{1,0:T(8,128)(2,1)S(1)} %get-tuple-element.36), channel_id=1, source_target_pairs={{0,4},{1,5},{2,6},{3,7},{4,0},{5,1},{6,2},{7,3},{8,12},{9,13},{10,... | collective-permute-start | bytes 393224 | tf_op jit(solution)/shard_map/ppermute | solution.py:290
  19.9 0.0 collective-permute-done.1.refs_3_.refs_2_.refs_5_
  19.9 2.5 %collective-permute-start.7 = (s16[64,1024]{1,0:T(8,128)(2,1)S(1)}, s16[64,1024]{1,0:T(8,128)(2,1)S(1)}, u32[]{:S(2)}, u32[]{:S(2)}) collective-permute-start(s16[64,1024]{1,0:T(8,128)(2,1)S(1)} %get-tuple-element.37), channel_id=1, source_target_pairs={{0,6},{1,7},{2,4},{3,5},{4,2},{5,3},{6,0},{7,1},{8,14},{9,15},{10,... | collective-permute-start | bytes 393224 | tf_op jit(solution)/shard_map/ppermute | solution.py:290
  22.4 0.0 collective-permute-done.2.refs_4_.refs_3_.refs_6_
  22.4 0.0 collective-permute-done.10.refs_0_
  22.4 0.7 %contract_far_group.1 = s16[128,1024]{1,0:T(8,128)(2,1)S(1)} custom-call(bf16[128,1024]{1,0:T(8,128)(2,1)S(1)} %collective-permute-done.10.refs_0_, bf16[1024,1024]{1,0:T(8,128)(2,1)S(1)} %get-tuple-element.33.refs_2_.refs_1_, s16[32,1024]{1,0:T(8,128)(2,1)S(1)} %collective-permute-done.refs_2_.refs_1_.refs_4_, ...), custom_call_target="tpu_custom_call" | custom-call | flops 268435456 | bytes 2097152 | tf_op jit(solution)/shard_map/contract_far_group/pallas_call | solution.py:168
  23.1 2.6 %collective-permute-start.11 = (s16[128,1024]{1,0:T(8,128)(2,1)S(1)}, s16[128,1024]{1,0:T(8,128)(2,1)S(1)}, u32[]{:S(2)}, u32[]{:S(2)}) collective-permute-start(s16[128,1024]{1,0:T(8,128)(2,1)S(1)} %contract_far_group.1), channel_id=1, source_target_pairs={{0,24},{1,25},{2,26},{3,27},{4,28},{5,29},{6,30},{7,31},{8,16},{9,... | collective-permute-start | bytes 786440 | tf_op jit(solution)/shard_map/ppermute | solution.py:290
  25.7 0.0 collective-permute-done.5.refs_1_
  25.7 4.1 %collective-permute-done.6.refs_2_ = s16[64,1024]{1,0:T(8,128)(2,1)S(1)} collective-permute-done((s16[64,1024]{1,0:T(8,128)(2,1)S(1)}, s16[64,1024]{1,0:T(8,128)(2,1)S(1)}, u32[]{:S(2)}, u32[]{:S(2)}) %collective-permute-start.6) | collective-permute-done | bytes 131104 | tf_op jit(solution)/shard_map/ppermute | solution.py:290
  29.9 0.0 collective-permute-done.7.refs_3_
  29.9 1.6 %collective-permute-start.8 = (s16[128,1024]{1,0:T(8,128)(2,1)S(1)}, s16[128,1024]{1,0:T(8,128)(2,1)S(1)}, u32[]{:S(2)}, u32[]{:S(2)}) collective-permute-start(s16[128,1024]{1,0:T(8,128)(2,1)S(1)} %get-tuple-element.38), channel_id=1, source_target_pairs={{0,8},{1,17},{2,10},{3,19},{4,12},{5,21},{6,14},{7,23},{8,0},{9,25... | collective-permute-start | bytes 786440 | tf_op jit(solution)/shard_map/ppermute | solution.py:290
  31.5 1.2 %collective-permute-start.9 = (s16[128,1024]{1,0:T(8,128)(2,1)S(1)}, s16[128,1024]{1,0:T(8,128)(2,1)S(1)}, u32[]{:S(2)}, u32[]{:S(2)}) collective-permute-start(s16[128,1024]{1,0:T(8,128)(2,1)S(1)} %get-tuple-element.39), channel_id=1, source_target_pairs={{0,16},{1,9},{2,18},{3,11},{4,20},{5,13},{6,22},{7,15},{8,24},{9,1... | collective-permute-start | bytes 786440 | tf_op jit(solution)/shard_map/ppermute | solution.py:290
  32.7 0.0 collective-permute-done.11.refs_0_
  32.7 2.0 %collective-permute-start.12 = (s16[32,1024]{1,0:T(8,128)(2,1)S(1)}, s16[32,1024]{1,0:T(8,128)(2,1)S(1)}, u32[]{:S(2)}, u32[]{:S(2)}) collective-permute-start(s16[32,1024]{1,0:T(8,128)(2,1)S(1)} %get-tuple-element.42), channel_id=1, source_target_pairs={{0,2},{1,3},{2,0},{3,1},{4,6},{5,7},{6,4},{7,5},{8,10},{9,11},{10,... | collective-permute-start | bytes 196616 | tf_op jit(solution)/shard_map/ppermute | solution.py:290
  34.7 1.0 %collective-permute-start.13 = (s16[32,1024]{1,0:T(8,128)(2,1)S(1)}, s16[32,1024]{1,0:T(8,128)(2,1)S(1)}, u32[]{:S(2)}, u32[]{:S(2)}) collective-permute-start(s16[32,1024]{1,0:T(8,128)(2,1)S(1)} %get-tuple-element.43), channel_id=1, source_target_pairs={{0,4},{1,5},{2,6},{3,7},{4,0},{5,1},{6,2},{7,3},{8,12},{9,13},{10,... | collective-permute-start | bytes 196616 | tf_op jit(solution)/shard_map/ppermute | solution.py:290
  35.7 1.5 %collective-permute-start.14 = (s16[32,1024]{1,0:T(8,128)(2,1)S(1)}, s16[32,1024]{1,0:T(8,128)(2,1)S(1)}, u32[]{:S(2)}, u32[]{:S(2)}) collective-permute-start(s16[32,1024]{1,0:T(8,128)(2,1)S(1)} %get-tuple-element.44), channel_id=1, source_target_pairs={{0,6},{1,7},{2,4},{3,5},{4,2},{5,3},{6,0},{7,1},{8,14},{9,15},{10,... | collective-permute-start | bytes 196616 | tf_op jit(solution)/shard_map/ppermute | solution.py:290
  37.2 0.1 collective-permute-done.12.refs_7_.refs_10_
  37.2 3.4 %collective-permute-done.13.refs_8_.refs_11_ = s16[32,1024]{1,0:T(8,128)(2,1)S(1)} collective-permute-done((s16[32,1024]{1,0:T(8,128)(2,1)S(1)}, s16[32,1024]{1,0:T(8,128)(2,1)S(1)}, u32[]{:S(2)}, u32[]{:S(2)}) %collective-permute-start.13) | collective-permute-done | bytes 65568 | tf_op jit(solution)/shard_map/ppermute | solution.py:290
  40.7 1.2 %collective-permute-done.14.refs_9_.refs_12_ = s16[32,1024]{1,0:T(8,128)(2,1)S(1)} collective-permute-done((s16[32,1024]{1,0:T(8,128)(2,1)S(1)}, s16[32,1024]{1,0:T(8,128)(2,1)S(1)}, u32[]{:S(2)}, u32[]{:S(2)}) %collective-permute-start.14) | collective-permute-done | bytes 65568 | tf_op jit(solution)/shard_map/ppermute | solution.py:290
  41.9 0.0 collective-permute-done.8.refs_4_.refs_7_
  41.9 0.0 collective-permute-done.9.refs_5_.refs_8_
  41.9 0.1 collective-permute-start.15
  42.0 1.9 %collective-permute-done.15.refs_13_ = s16[256,1024]{1,0:T(8,128)(2,1)S(1)} collective-permute-done((s16[256,1024]{1,0:T(8,128)(2,1)S(1)}, s16[256,1024]{1,0:T(8,128)(2,1)S(1)}, u32[]{:S(2)}, u32[]{:S(2)}) %collective-permute-start.15) | collective-permute-done | bytes 524320 | tf_op jit(solution)/shard_map/ppermute | solution.py:290
  43.9 0.0 copy-done
  43.9 0.0 copy-done.4
  43.9 0.0 copy-done.5
  43.9 0.0 copy-done.6
  43.9 3.1 %add_contributions.1 = f32[50,16,1024]{2,1,0:T(8,128)} custom-call(s32[4,8]{1,0:T(4,128)S(1)} %copy-done.5, s32[4,8]{1,0:T(4,128)S(1)} %copy-done.4, s32[4,8]{1,0:T(4,128)S(1)} %copy-done.6, s16[32,1024]{1,0:T(8,128)(2,1)S(1)} %get-tuple-element.27.refs_0_.refs_3_, s16[32,1024]{1,0:T(8,128)(2,1)S(1)} %collective-permute-done.refs_2_.refs_1_.refs_4_, ...), custom_call_target="tpu_custom_call" | custom-call | tf_op jit(solution)/shard_map/add_contributions/pallas_call | solution.py:267
  (3 shorter events, 0.1 us)
Async XLA Ops:
  0.0 1.2 %copy-start.2 = (bf16[4,128,1024]{2,1,0:T(8,128)(2,1)S(1)}, bf16[4,128,1024]{2,1,0:T(8,128)(2,1)}, u32[]{:S(2)}) copy-start(bf16[4,128,1024]{2,1,0:T(8,128)(2,1)} %amplitudes.1) | copy-start | bytes 3145732
  1.2 0.7 %copy-start.3 = (s32[4,8]{1,0:T(4,128)S(1)}, s32[4,8]{1,0:T(4,128)}, u32[]{:S(2)}) copy-start(s32[4,8]{1,0:T(4,128)} %refs_1_.1) | copy-start | bytes 388
  2.6 11.7 %collective-permute-start.3 = (bf16[128,1024]{1,0:T(8,128)(2,1)S(1)}, bf16[128,1024]{1,0:T(8,128)(2,1)S(1)}, u32[]{:S(2)}, u32[]{:S(2)}) collective-permute-start(bf16[128,1024]{1,0:T(8,128)(2,1)S(1)} %get-tuple-element.31), channel_id=1, source_target_pairs={{0,8},{1,17},{2,10},{3,19},{4,12},{5,21},{6,14},{7,23},{8,0},{9,25... | collective-permute-start | bytes 786440 | tf_op jit(solution)/shard_map/ppermute | solution.py:290
  5.6 11.2 %collective-permute-start.4 = (bf16[128,1024]{1,0:T(8,128)(2,1)S(1)}, bf16[128,1024]{1,0:T(8,128)(2,1)S(1)}, u32[]{:S(2)}, u32[]{:S(2)}) collective-permute-start(bf16[128,1024]{1,0:T(8,128)(2,1)S(1)} %get-tuple-element.32), channel_id=1, source_target_pairs={{0,16},{1,9},{2,18},{3,11},{4,20},{5,13},{6,22},{7,15},{8,24},{9,1... | collective-permute-start | bytes 786440 | tf_op jit(solution)/shard_map/ppermute | solution.py:290
  7.1 1.6 %copy-start.1 = (bf16[1,1024,1024]{2,1,0:T(8,128)(2,1)S(1)}, bf16[1,1024,1024]{2,1,0:T(8,128)(2,1)}, u32[]{:S(2)}) copy-start(bf16[1,1024,1024]{2,1,0:T(8,128)(2,1)} %param.8) | copy-start | bytes 6291460
  9.6 12.8 %collective-permute-start.10 = (bf16[128,1024]{1,0:T(8,128)(2,1)S(1)}, bf16[128,1024]{1,0:T(8,128)(2,1)S(1)}, u32[]{:S(2)}, u32[]{:S(2)}) collective-permute-start(bf16[128,1024]{1,0:T(8,128)(2,1)S(1)} %get-tuple-element.40), channel_id=1, source_target_pairs={{0,24},{1,25},{2,26},{3,27},{4,28},{5,29},{6,30},{7,31},{8,16},{9,... | collective-permute-start | bytes 786440 | tf_op jit(solution)/shard_map/ppermute | solution.py:290
  9.7 8.3 %collective-permute-start = (s16[32,1024]{1,0:T(8,128)(2,1)S(1)}, s16[32,1024]{1,0:T(8,128)(2,1)S(1)}, u32[]{:S(2)}, u32[]{:S(2)}) collective-permute-start(s16[32,1024]{1,0:T(8,128)(2,1)S(1)} %get-tuple-element.28), channel_id=1, source_target_pairs={{0,2},{1,3},{2,0},{3,1},{4,6},{5,7},{6,4},{7,5},{8,10},{9,11},{10,... | collective-permute-start | bytes 196616 | tf_op jit(solution)/shard_map/ppermute | solution.py:290
  11.7 8.2 %collective-permute-start.1 = (s16[32,1024]{1,0:T(8,128)(2,1)S(1)}, s16[32,1024]{1,0:T(8,128)(2,1)S(1)}, u32[]{:S(2)}, u32[]{:S(2)}) collective-permute-start(s16[32,1024]{1,0:T(8,128)(2,1)S(1)} %get-tuple-element.29), channel_id=1, source_target_pairs={{0,4},{1,5},{2,6},{3,7},{4,0},{5,1},{6,2},{7,3},{8,12},{9,13},{10,... | collective-permute-start | bytes 196616 | tf_op jit(solution)/shard_map/ppermute | solution.py:290
  14.3 8.1 %collective-permute-start.2 = (s16[32,1024]{1,0:T(8,128)(2,1)S(1)}, s16[32,1024]{1,0:T(8,128)(2,1)S(1)}, u32[]{:S(2)}, u32[]{:S(2)}) collective-permute-start(s16[32,1024]{1,0:T(8,128)(2,1)S(1)} %get-tuple-element.30), channel_id=1, source_target_pairs={{0,6},{1,7},{2,4},{3,5},{4,2},{5,3},{6,0},{7,1},{8,14},{9,15},{10,... | collective-permute-start | bytes 196616 | tf_op jit(solution)/shard_map/ppermute | solution.py:290
  16.8 27.1 %copy-start = (f32[16,50,1024]{2,0,1:T(8,128)S(1)}, f32[16,50,1024]{2,0,1:T(8,128)}, u32[]{:S(2)}) copy-start(f32[16,50,1024]{2,0,1:T(8,128)} %param.11) | copy-start | bytes 9830404
  16.8 27.1 %copy-start.4 = (s32[4,8]{1,0:T(4,128)S(1)}, s32[4,8]{1,0:T(4,128)}, u32[]{:S(2)}) copy-start(s32[4,8]{1,0:T(4,128)} %refs_1_.1) | copy-start | bytes 388
  16.8 27.1 %copy-start.5 = (s32[4,8]{1,0:T(4,128)S(1)}, s32[4,8]{1,0:T(4,128)}, u32[]{:S(2)}) copy-start(s32[4,8]{1,0:T(4,128)} %refs_0_.1) | copy-start | bytes 388
  16.8 27.1 %copy-start.6 = (s32[4,8]{1,0:T(4,128)S(1)}, s32[4,8]{1,0:T(4,128)}, u32[]{:S(2)}) copy-start(s32[4,8]{1,0:T(4,128)} %refs_2_.1) | copy-start | bytes 388
  18.0 7.8 %collective-permute-start.5 = (s16[64,1024]{1,0:T(8,128)(2,1)S(1)}, s16[64,1024]{1,0:T(8,128)(2,1)S(1)}, u32[]{:S(2)}, u32[]{:S(2)}) collective-permute-start(s16[64,1024]{1,0:T(8,128)(2,1)S(1)} %get-tuple-element.35), channel_id=1, source_target_pairs={{0,2},{1,3},{2,0},{3,1},{4,6},{5,7},{6,4},{7,5},{8,10},{9,11},{10,... | collective-permute-start | bytes 393224 | tf_op jit(solution)/shard_map/ppermute | solution.py:290
  18.1 11.8 %collective-permute-start.6 = (s16[64,1024]{1,0:T(8,128)(2,1)S(1)}, s16[64,1024]{1,0:T(8,128)(2,1)S(1)}, u32[]{:S(2)}, u32[]{:S(2)}) collective-permute-start(s16[64,1024]{1,0:T(8,128)(2,1)S(1)} %get-tuple-element.36), channel_id=1, source_target_pairs={{0,4},{1,5},{2,6},{3,7},{4,0},{5,1},{6,2},{7,3},{8,12},{9,13},{10,... | collective-permute-start | bytes 393224 | tf_op jit(solution)/shard_map/ppermute | solution.py:290
  19.9 9.9 %collective-permute-start.7 = (s16[64,1024]{1,0:T(8,128)(2,1)S(1)}, s16[64,1024]{1,0:T(8,128)(2,1)S(1)}, u32[]{:S(2)}, u32[]{:S(2)}) collective-permute-start(s16[64,1024]{1,0:T(8,128)(2,1)S(1)} %get-tuple-element.37), channel_id=1, source_target_pairs={{0,6},{1,7},{2,4},{3,5},{4,2},{5,3},{6,0},{7,1},{8,14},{9,15},{10,... | collective-permute-start | bytes 393224 | tf_op jit(solution)/shard_map/ppermute | solution.py:290
  23.1 9.5 %collective-permute-start.11 = (s16[128,1024]{1,0:T(8,128)(2,1)S(1)}, s16[128,1024]{1,0:T(8,128)(2,1)S(1)}, u32[]{:S(2)}, u32[]{:S(2)}) collective-permute-start(s16[128,1024]{1,0:T(8,128)(2,1)S(1)} %contract_far_group.1), channel_id=1, source_target_pairs={{0,24},{1,25},{2,26},{3,27},{4,28},{5,29},{6,30},{7,31},{8,16},{9,... | collective-permute-start | bytes 786440 | tf_op jit(solution)/shard_map/ppermute | solution.py:290
  29.9 11.9 %collective-permute-start.8 = (s16[128,1024]{1,0:T(8,128)(2,1)S(1)}, s16[128,1024]{1,0:T(8,128)(2,1)S(1)}, u32[]{:S(2)}, u32[]{:S(2)}) collective-permute-start(s16[128,1024]{1,0:T(8,128)(2,1)S(1)} %get-tuple-element.38), channel_id=1, source_target_pairs={{0,8},{1,17},{2,10},{3,19},{4,12},{5,21},{6,14},{7,23},{8,0},{9,25... | collective-permute-start | bytes 786440 | tf_op jit(solution)/shard_map/ppermute | solution.py:290
  31.5 10.4 %collective-permute-start.9 = (s16[128,1024]{1,0:T(8,128)(2,1)S(1)}, s16[128,1024]{1,0:T(8,128)(2,1)S(1)}, u32[]{:S(2)}, u32[]{:S(2)}) collective-permute-start(s16[128,1024]{1,0:T(8,128)(2,1)S(1)} %get-tuple-element.39), channel_id=1, source_target_pairs={{0,16},{1,9},{2,18},{3,11},{4,20},{5,13},{6,22},{7,15},{8,24},{9,1... | collective-permute-start | bytes 786440 | tf_op jit(solution)/shard_map/ppermute | solution.py:290
  32.7 4.6 %collective-permute-start.12 = (s16[32,1024]{1,0:T(8,128)(2,1)S(1)}, s16[32,1024]{1,0:T(8,128)(2,1)S(1)}, u32[]{:S(2)}, u32[]{:S(2)}) collective-permute-start(s16[32,1024]{1,0:T(8,128)(2,1)S(1)} %get-tuple-element.42), channel_id=1, source_target_pairs={{0,2},{1,3},{2,0},{3,1},{4,6},{5,7},{6,4},{7,5},{8,10},{9,11},{10,... | collective-permute-start | bytes 196616 | tf_op jit(solution)/shard_map/ppermute | solution.py:290
  34.7 5.9 %collective-permute-start.13 = (s16[32,1024]{1,0:T(8,128)(2,1)S(1)}, s16[32,1024]{1,0:T(8,128)(2,1)S(1)}, u32[]{:S(2)}, u32[]{:S(2)}) collective-permute-start(s16[32,1024]{1,0:T(8,128)(2,1)S(1)} %get-tuple-element.43), channel_id=1, source_target_pairs={{0,4},{1,5},{2,6},{3,7},{4,0},{5,1},{6,2},{7,3},{8,12},{9,13},{10,... | collective-permute-start | bytes 196616 | tf_op jit(solution)/shard_map/ppermute | solution.py:290
  35.7 6.2 %collective-permute-start.14 = (s16[32,1024]{1,0:T(8,128)(2,1)S(1)}, s16[32,1024]{1,0:T(8,128)(2,1)S(1)}, u32[]{:S(2)}, u32[]{:S(2)}) collective-permute-start(s16[32,1024]{1,0:T(8,128)(2,1)S(1)} %get-tuple-element.44), channel_id=1, source_target_pairs={{0,6},{1,7},{2,4},{3,5},{4,2},{5,3},{6,0},{7,1},{8,14},{9,15},{10,... | collective-permute-start | bytes 196616 | tf_op jit(solution)/shard_map/ppermute | solution.py:290
  41.9 2.0 %collective-permute-start.15 = (s16[256,1024]{1,0:T(8,128)(2,1)S(1)}, s16[256,1024]{1,0:T(8,128)(2,1)S(1)}, u32[]{:S(2)}, u32[]{:S(2)}) collective-permute-start(s16[256,1024]{1,0:T(8,128)(2,1)S(1)} %rows_of_other_core.1), channel_id=1, source_target_pairs={{0,1},{1,0},{2,3},{3,2},{4,5},{5,4},{6,7},{7,6},{8,9},{9,8},{10,11... | collective-permute-start | bytes 1572872 | tf_op jit(solution)/shard_map/ppermute | solution.py:290

commit v10 on v9

--- a/solution.py
+++ b/solution.py
@@ -95,8 +95,7 @@
     )(tile_cd, amplitudes)
 
 
-def code_chips(rows, tile, product, outgoing, first):
-    product[...] = jnp.dot(rows[...], tile[...], preferred_element_type=jnp.float32)
+def code_chips(product, outgoing, first):
     chip_rows = product.shape[0] // len(outgoing)
     chip = lax.axis_index("grp") // CORES
     for step, coded in enumerate(outgoing):
@@ -106,60 +105,53 @@
         coded[first : first + chip_rows, LANES:] = tail
 
 
-def own_kernel(rows, tile, far_picked, *rest):
-    outgoing, (tile_out, far_out, product, sem) = rest[:-4], rest[-4:]
-    copy = pltpu.make_async_copy(tile, tile_out, sem)
-    copy.start()
-    far_out[...] = far_picked[...]
-    code_chips(rows, tile, product, outgoing, 0)
-    copy.wait()
-
-
-def contract_own(rows, tile, far_picked, chips):
-    group_rows, tile_width = rows.shape[0], tile.shape[1]
+def code_own(product, chips):
+    group_rows, tile_width = product.shape
     coded = jax.ShapeDtypeStruct((group_rows // chips, tile_width), jnp.int16)
+    return pl.pallas_call(
+        lambda product, *outgoing: code_chips(product, outgoing, 0),
+        out_shape=[coded] * chips,
+        in_specs=[VMEM],
+        out_specs=[VMEM] * chips,
+        compiler_params=vmem_limit(product, *[coded] * chips),
+        name="code_own_group",
+    )(product)
+
+
+def near_kernel(near, *refs):
+    groups, tile, own, outgoing, product = refs[:near], refs[near], refs[near + 1], refs[near + 2 : -1], refs[-1]
+    chip_rows = product.shape[0] // len(outgoing)
+    outgoing[1][near * chip_rows :, :] = own[...]
+    for index, rows in enumerate(groups):
+        product[...] = jnp.dot(rows[...], tile[...], preferred_element_type=jnp.float32)
+        code_chips(product, outgoing, index * chip_rows)
+
+
+def contract_near(groups, tile, own, chips):
+    group_rows, tile_width = groups[0].shape[0], tile.shape[1]
+    chip_rows = group_rows // chips
+    rows = [len(groups) * chip_rows] * chips
+    rows[1] += chip_rows
+    coded = [jax.ShapeDtypeStruct((count, tile_width), jnp.int16) for count in rows]
     product = jax.ShapeDtypeStruct((group_rows, tile_width), jnp.float32)
-    outputs = [coded] * chips + [jax.ShapeDtypeStruct(array.shape, array.dtype) for array in (tile, far_picked)]
-    return pl.pallas_call(
-        own_kernel,
-        out_shape=outputs,
-        in_specs=[VMEM] * 3,
-        out_specs=[VMEM] * len(outputs),
-        scratch_shapes=[pltpu.VMEM(product.shape, product.dtype), pltpu.SemaphoreType.DMA],
-        compiler_params=vmem_limit(rows, tile, far_picked, *outputs, product),
-        cost_estimate=cost(group_rows, tile),
-        name="contract_own_group",
-    )(rows, tile, far_picked)
-
-
-def near_kernel(near, *refs):
-    groups, tile, outgoing, product = refs[:near], refs[near], refs[near + 1 : -1], refs[-1]
-    chip_rows = product.shape[0] // len(outgoing)
-    for index, rows in enumerate(groups):
-        code_chips(rows, tile, product, outgoing, index * chip_rows)
-
-
-def contract_near(groups, tile, chips):
-    group_rows, tile_width = groups[0].shape[0], tile.shape[1]
-    coded = jax.ShapeDtypeStruct((len(groups) * group_rows // chips, tile_width), jnp.int16)
-    product = jax.ShapeDtypeStruct((group_rows, tile_width), jnp.float32)
     return pl.pallas_call(
         lambda *refs: near_kernel(len(groups), *refs),
-        out_shape=[coded] * chips,
-        in_specs=[VMEM] * (len(groups) + 1),
+        out_shape=coded,
+        in_specs=[VMEM] * (len(groups) + 2),
         out_specs=[VMEM] * chips,
         scratch_shapes=[pltpu.VMEM(product.shape, product.dtype)],
-        compiler_params=vmem_limit(*groups, tile, *[coded] * chips, product),
+        compiler_params=vmem_limit(*groups, tile, own, *coded, product),
         cost_estimate=cost(len(groups) * group_rows, tile),
         name="contract_near_groups",
-    )(*groups, tile)
+    )(*groups, tile, own)
 
 
 def far_kernel(chips, rows, tile, *rest):
     coded, product = rest[-2:]
     chip_rows = product.shape[0] // chips
     parts = [coded.at[pl.ds(step * chip_rows, chip_rows)] for step in range(chips)]
-    code_chips(rows, tile, product, parts, 0)
+    product[...] = jnp.dot(rows[...], tile[...], preferred_element_type=jnp.float32)
+    code_chips(product, parts, 0)
 
 
 def contract_far(rows, tile, chips, earlier):
@@ -177,44 +169,37 @@
     )(rows, tile, *earlier)
 
 
-def regroup_kernel(count, *refs):
-    sources, targets = refs[:count], refs[count:]
-    part_rows = sources[0].shape[0] // len(targets)
+def regroup_kernel(count, parts, part_rows, *refs):
+    sources, targets = refs[:count], refs[-parts:]
     for j, source in enumerate(sources):
         for i, target in enumerate(targets):
             target[j * part_rows : (j + 1) * part_rows, :] = source[i * part_rows : (i + 1) * part_rows, :]
 
 
-def regroup(sources, parts, name):
-    rows, tile_width = sources[0].shape
-    target = jax.ShapeDtypeStruct((len(sources) * rows // parts, tile_width), sources[0].dtype)
-    return pl.pallas_call(
-        lambda *refs: regroup_kernel(len(sources), *refs),
+def regroup(sources, parts, part_rows, name, earlier=()):
+    target = jax.ShapeDtypeStruct((len(sources) * part_rows, sources[0].shape[1]), sources[0].dtype)
+    return pl.pallas_call(
+        lambda *refs: regroup_kernel(len(sources), parts, part_rows, *refs),
         out_shape=[target] * parts,
-        in_specs=[VMEM] * len(sources),
+        in_specs=[VMEM] * len(sources) + [ANY] * len(earlier),
         out_specs=[VMEM] * parts,
         compiler_params=vmem_limit(*sources, *[target] * parts),
         name=name,
-    )(*sources)
-
-
-def pieces_of(arrays, owner_rows):
-    return [(array, first) for array in arrays for first in range(0, array.shape[0], CORES * owner_rows)]
-
-
-def other_core_kernel(owner_rows, *refs):
+    )(*sources, *earlier)
+
+
+def other_core_kernel(pieces, owner_rows, *refs):
     arrays, halves = refs[:-1], refs[-1]
     other = 1 - lax.axis_index("grp") % CORES
-    for index, (array, first) in enumerate(pieces_of(arrays, owner_rows)):
+    for index, (array, first) in enumerate(pieces):
         source = pl.multiple_of(first + other * owner_rows, owner_rows)
-        halves[index * owner_rows : (index + 1) * owner_rows, :] = array[pl.ds(source, owner_rows), :]
-
-
-def other_core_rows(arrays, owner_rows):
-    rows = sum(array.shape[0] for array in arrays) // CORES
-    halves = jax.ShapeDtypeStruct((rows, arrays[0].shape[1]), arrays[0].dtype)
-    return pl.pallas_call(
-        lambda *refs: other_core_kernel(owner_rows, *refs),
+        halves[index * owner_rows : (index + 1) * owner_rows, :] = arrays[array][pl.ds(source, owner_rows), :]
+
+
+def other_core_rows(arrays, pieces, owner_rows):
+    halves = jax.ShapeDtypeStruct((len(pieces) * owner_rows, arrays[0].shape[1]), arrays[0].dtype)
+    return pl.pallas_call(
+        lambda *refs: other_core_kernel(pieces, owner_rows, *refs),
         out_shape=halves,
         in_specs=[VMEM] * len(arrays),
         out_specs=VMEM,
@@ -223,7 +208,7 @@
     )(*arrays)
 
 
-def add_kernel(parts, tile_ab, tile_cd, pair_screen, *rest):
+def add_kernel(parts, pieces, tile_ab, tile_cd, pair_screen, *rest):
     arrays, (swapped, residual_in, residual, held, sems) = rest[:-5], rest[-5:]
     blk, grp = lax.axis_index("blk"), lax.axis_index("grp")
     ab_tiles, owner_rows, tile_width = residual.shape
@@ -237,14 +222,13 @@
         return carry
 
     lax.fori_loop(0, ab_tiles, hold, 0)
-    pieces = pieces_of(arrays, owner_rows)
     core = grp % CORES
     steps_here, steps_there = blk_steps(tile_ab.shape[0], core), blk_steps(tile_ab.shape[0], 1 - core)
     own = core * owner_rows
     for start in range(0, len(pieces), chips):
         terms = []
         for index in range(start, start + chips):
-            array, first = pieces[index]
+            array, first = arrays[pieces[index][0]], pieces[index][1]
             p_here = jnp.bitwise_xor(blk, steps_here[index // chips])
             p_there = jnp.bitwise_xor(blk, steps_there[index // chips])
             g = jnp.bitwise_xor(grp, index % chips * CORES)
@@ -262,10 +246,10 @@
     wait_all(leaves)
 
 
-def add_blocks(tile_ab, tile_cd, pair_screen, arrays, swapped, residual_in):
+def add_blocks(tile_ab, tile_cd, pair_screen, arrays, pieces, swapped, residual_in):
     parts = 5
     return pl.pallas_call(
-        lambda *refs: add_kernel(parts, *refs),
+        lambda *refs: add_kernel(parts, pieces, *refs),
         out_shape=jax.ShapeDtypeStruct(residual_in.shape, residual_in.dtype),
         in_specs=[SMEM] * 3 + [VMEM] * (len(arrays) + 2),
         out_specs=ANY,
@@ -293,20 +277,32 @@
         arrived = {step: swap(outgoing[step], 0, step) for step in reversed(range(1, chips))}
         return [outgoing[0]] + [arrived[step] for step in range(1, chips)]
 
+    tile = integrals[0]
+    near = blk_count - 2
+    chip_rows = CORES * owner_rows
     own_rows, *near_picked, far_picked = pick(tile_cd, amplitudes)
     near_rows = [swap(rows, index + 1, 0) for index, rows in enumerate(near_picked)]
-    *own_out, tile, far_picked = contract_own(own_rows, integrals[0], far_picked, chips)
-    own_in = along_chips(own_out)
+    own_product = jnp.dot(own_rows, tile, preferred_element_type=jnp.float32)
+    own_out = code_own(own_product, chips)
+    own_in = [swap(own_out[step], 0, step) for step in range(2, chips)]
+    (far_picked,) = regroup([far_picked], 1, far_picked.shape[0], "far_rows_after_near", [own_out[0]])
     far_rows = swap(far_picked, far, 0)
-    near_in = along_chips(contract_near(near_rows, tile, chips))
-    near_back = regroup(near_in, blk_count - 2, "regroup_by_group")
-    near_in = [swap(rows, index + 1, 0) for index, rows in enumerate(near_back)]
-    far_back = swap(contract_far(far_rows, tile, chips, own_in[1:]), far, 0)
-    far_in = along_chips(regroup([far_back], chips, "regroup_by_chip"))
-    arrays = [*own_in, *near_in, *far_in]
-    swapped = swap(other_core_rows(arrays, owner_rows), 0, 0, 1)
+    near_out = contract_near(near_rows, tile, own_out[1], chips)
+    near_in = along_chips(near_out)
+    far_back = swap(contract_far(far_rows, tile, chips, [*own_in, near_out[0]]), far, 0)
+    far_out = regroup([far_back], chips, chip_rows, "regroup_by_chip")
+    far_in = along_chips(far_out)
+    near_back = regroup(near_in, near, chip_rows, "regroup_by_group")
+    back_in = [swap(rows, index + 1, 0) for index, rows in enumerate(near_back)]
+
+    arrays = [own_out[0], near_in[1], *own_in, *back_in, *far_in]
+    pieces = [(0, 0), (1, near * chip_rows)] + [(step, 0) for step in range(2, chips)]
+    for group in range(near):
+        pieces += [(chips + group, step * chip_rows) for step in range(chips)]
+    pieces += [(chips + near + step, 0) for step in range(chips)]
+    swapped = swap(other_core_rows(arrays, pieces, owner_rows), 0, 0, 1)
     by_tile = jnp.transpose(residual_in, (1, 0, 2))
-    added = add_blocks(tile_ab, tile_cd, pair_screen, arrays, swapped, by_tile)
+    added = add_blocks(tile_ab, tile_cd, pair_screen, arrays, pieces, swapped, by_tile)
     return jnp.transpose(added, (1, 0, 2))
 
 

time: 47.2 us -> 49 us (1.038)
  waiting for transfers between devices: 10.8 us -> 14.2 us
  matrix products: 0 us -> 2.03 us
  local copies, waits for them, and re-layouts: 3.51 us -> 1.93 us
  starting transfers between devices: 26 us -> 24.5 us
  Pallas kernels: 6.62 us -> 6.03 us
    ppermute x16 -> x15, waiting for transfers between devices: 10.8 us -> 14.2 us  [swap(): return lax.ppermute(value, ('blk', 'grp'), pairs)]
    dot_general x0 -> x1, matrix products: none -> 2.03 us  [shards(): own_product = jnp.dot(own_rows, tile, preferred_element_type=jnp.float32)]
    unnamed x14, local copies, waits for them, and re-layouts: 3.51 us -> 1.93 us
    ppermute x16 -> x15, starting transfers between devices: 26 us -> 24.5 us  [swap(): return lax.ppermute(value, ('blk', 'grp'), pairs)]
    pallas_call x6 -> x7, Pallas kernels: 5.22 us -> 4.63 us  [the longest x1 3.12 us: add_blocks(): pl.pallas_call(lambda *refs: add_kernel(parts, pieces, *refs), out_shape=...]
  transfers between devices with their start and end apart: 16 -> 15, of which waited for: 5 -> 4; matrix products, arithmetic and copies ran while one was open for 0% -> 4% of each run, Pallas kernels for 6% -> 4%
where the time goes in v10:
time: 49 us; the launch traced here: 48.8 us
  starting transfers between devices  24.5 us (50%)
  waiting for transfers between devices  14.2 us (29%)
  Pallas kernels  6.03 us (12%)
  matrix products  2.03 us (4%)
  local copies, waits for them, and re-layouts  1.93 us (4%)
    ppermute x15, starting transfers between devices, swap(): return lax.ppermute(value, ('blk', 'grp'), pairs)  24.5 us
    ppermute x15, waiting for transfers between devices, swap(): return lax.ppermute(value, ('blk', 'grp'), pairs)  14.2 us
    pallas_call x1, Pallas kernels, add_blocks(): pl.pallas_call(lambda *refs: add_kernel(parts, pieces, *refs), out_shape=...  3.12 us
    dot_general x1, matrix products, shards(): own_product = jnp.dot(own_rows, tile, preferred_element_type=jnp.float32)  2.03 us
    unnamed x14, local copies, waits for them, and re-layouts  1.93 us
    pallas_call x1, Pallas kernels, contract_near(): pl.pallas_call(lambda *refs: near_kernel(len(groups), *refs), out_shape=c...  1.13 us
  transfers between devices with their start and end apart: 15, of which 4 were waited for; matrix products, arithmetic and copies ran while one was open for 4% of the time, Pallas kernels for 4%

profile of v10, /device:TPU:0, one launch (start us, length us, event | category | flops | bytes accessed | tf_op | source)
XLA Modules:
  0.0 48.8 jit_solution(4910100583520811738)
XLA Ops:
  0.0 0.0 copy-start.2
  0.0 1.2 %copy-done.2 = bf16[4,128,1024]{2,1,0:T(8,128)(2,1)S(1)} copy-done((bf16[4,128,1024]{2,1,0:T(8,128)(2,1)S(1)}, bf16[4,128,1024]{2,1,0:T(8,128)(2,1)}, u32[]{:S(2)}) %copy-start.2) | copy-done | bytes 1048600
  1.2 0.0 copy-start.3
  1.2 0.7 %copy-done.3 = s32[4,8]{1,0:T(4,128)S(1)} copy-done((s32[4,8]{1,0:T(4,128)S(1)}, s32[4,8]{1,0:T(4,128)}, u32[]{:S(2)}) %copy-start.3) | copy-done | bytes 152
  1.9 0.7 %pick_cd_blocks.1 = (bf16[128,1024]{1,0:T(8,128)(2,1)S(1)}, bf16[128,1024]{1,0:T(8,128)(2,1)S(1)}, bf16[128,1024]{1,0:T(8,128)(2,1)S(1)}, bf16[128,1024]{1,0:T(8,128)(2,1)S(1)}) custom-call(s32[4,8]{1,0:T(4,128)S(1)} %copy-done.3, bf16[4,128,1024]{2,1,0:T(8,128)(2,1)S(1)} %copy-done.2), custom_call_target="tpu_custom_call" | custom-call | tf_op jit(solution)/shard_map/pick_cd_blocks/pallas_call | solution.py:87
  2.6 0.0 copy-start
  2.6 3.0 %collective-permute-start = (bf16[128,1024]{1,0:T(8,128)(2,1)S(1)}, bf16[128,1024]{1,0:T(8,128)(2,1)S(1)}, u32[]{:S(2)}, u32[]{:S(2)}) collective-permute-start(bf16[128,1024]{1,0:T(8,128)(2,1)S(1)} %get-tuple-element.25), channel_id=1, source_target_pairs={{0,8},{1,17},{2,10},{3,19},{4,12},{5,21},{6,14},{7,23},{8,0},{9,25... | collective-permute-start | bytes 786440 | tf_op jit(solution)/shard_map/ppermute | solution.py:274
  5.6 1.5 %collective-permute-start.1 = (bf16[128,1024]{1,0:T(8,128)(2,1)S(1)}, bf16[128,1024]{1,0:T(8,128)(2,1)S(1)}, u32[]{:S(2)}, u32[]{:S(2)}) collective-permute-start(bf16[128,1024]{1,0:T(8,128)(2,1)S(1)} %get-tuple-element.26), channel_id=1, source_target_pairs={{0,16},{1,9},{2,18},{3,11},{4,20},{5,13},{6,22},{7,15},{8,24},{9,1... | collective-permute-start | bytes 786440 | tf_op jit(solution)/shard_map/ppermute | solution.py:274
  7.2 2.0 %fusion.product = f32[128,1024]{1,0:T(8,128)S(1)} fusion(bf16[128,1024]{1,0:T(8,128)(2,1)S(1)} %get-tuple-element.23, bf16[1,1024,1024]{2,1,0:T(8,128)(2,1)} %param.8), kind=kOutput, calls=%fused_computation | convolution fusion | flops 268435456 | bytes 2883584 | tf_op jit(solution)/shard_map/dot_general | solution.py:285
  9.2 0.3 code_own_group.1
  9.5 0.1 collective-permute-start.9
  9.6 3.0 %collective-permute-start.3 = (s16[32,1024]{1,0:T(8,128)(2,1)S(1)}, s16[32,1024]{1,0:T(8,128)(2,1)S(1)}, u32[]{:S(2)}, u32[]{:S(2)}) collective-permute-start(s16[32,1024]{1,0:T(8,128)(2,1)S(1)} %get-tuple-element.29), channel_id=1, source_target_pairs={{0,4},{1,5},{2,6},{3,7},{4,0},{5,1},{6,2},{7,3},{8,12},{9,13},{10,... | collective-permute-start | bytes 196616 | tf_op jit(solution)/shard_map/ppermute | solution.py:274
  12.6 0.0 collective-permute-done.refs_0_
  12.6 0.0 collective-permute-done.1.refs_1_
  12.6 0.0 copy-done
  12.6 1.1 %contract_near_groups.1 = (s16[64,1024]{1,0:T(8,128)(2,1)S(1)}, s16[96,1024]{1,0:T(8,128)(2,1)S(1)}, s16[64,1024]{1,0:T(8,128)(2,1)S(1)}, s16[64,1024]{1,0:T(8,128)(2,1)S(1)}) custom-call(bf16[128,1024]{1,0:T(8,128)(2,1)S(1)} %collective-permute-done.refs_0_, bf16[128,1024]{1,0:T(8,128)(2,1)S(1)} %collective-permute-done.1.refs_1_, ...), custom_call_target="tpu_custom_call" | custom-call | flops 536870912 | bytes 2097152 | tf_op jit(solution)/shard_map/contract_near_groups/pallas_call | solution.py:137
  13.8 2.2 %collective-permute-start.2 = (s16[96,1024]{1,0:T(8,128)(2,1)S(1)}, s16[96,1024]{1,0:T(8,128)(2,1)S(1)}, u32[]{:S(2)}, u32[]{:S(2)}) collective-permute-start(s16[96,1024]{1,0:T(8,128)(2,1)S(1)} %get-tuple-element.28), channel_id=1, source_target_pairs={{0,2},{1,3},{2,0},{3,1},{4,6},{5,7},{6,4},{7,5},{8,10},{9,11},{10,... | collective-permute-start | bytes 589832 | tf_op jit(solution)/shard_map/ppermute | solution.py:274
  16.0 2.5 %collective-permute-start.4 = (s16[32,1024]{1,0:T(8,128)(2,1)S(1)}, s16[32,1024]{1,0:T(8,128)(2,1)S(1)}, u32[]{:S(2)}, u32[]{:S(2)}) collective-permute-start(s16[32,1024]{1,0:T(8,128)(2,1)S(1)} %get-tuple-element.30), channel_id=1, source_target_pairs={{0,6},{1,7},{2,4},{3,5},{4,2},{5,3},{6,0},{7,1},{8,14},{9,15},{10,... | collective-permute-start | bytes 196616 | tf_op jit(solution)/shard_map/ppermute | solution.py:274
  18.5 0.1 collective-permute-start.5
  18.6 0.0 collective-permute-done.3.refs_2_.refs_5_
  18.6 2.9 %collective-permute-start.6 = (s16[64,1024]{1,0:T(8,128)(2,1)S(1)}, s16[64,1024]{1,0:T(8,128)(2,1)S(1)}, u32[]{:S(2)}, u32[]{:S(2)}) collective-permute-start(s16[64,1024]{1,0:T(8,128)(2,1)S(1)} %get-tuple-element.33), channel_id=1, source_target_pairs={{0,6},{1,7},{2,4},{3,5},{4,2},{5,3},{6,0},{7,1},{8,14},{9,15},{10,... | collective-permute-start | bytes 393224 | tf_op jit(solution)/shard_map/ppermute | solution.py:274
  21.5 4.2 %collective-permute-done.4.refs_3_.refs_6_ = s16[32,1024]{1,0:T(8,128)(2,1)S(1)} collective-permute-done((s16[32,1024]{1,0:T(8,128)(2,1)S(1)}, s16[32,1024]{1,0:T(8,128)(2,1)S(1)}, u32[]{:S(2)}, u32[]{:S(2)}) %collective-permute-start.4) | collective-permute-done | bytes 65568 | tf_op jit(solution)/shard_map/ppermute | solution.py:274
  25.7 0.0 collective-permute-done.9.refs_0_
  25.7 0.0 copy-start.1
  25.7 0.0 copy-start.4
  25.7 0.0 copy-start.5
  25.7 0.0 copy-start.6
  25.7 0.7 %contract_far_group.1 = s16[128,1024]{1,0:T(8,128)(2,1)S(1)} custom-call(bf16[128,1024]{1,0:T(8,128)(2,1)S(1)} %collective-permute-done.9.refs_0_, bf16[1024,1024]{1,0:T(8,128)(2,1)S(1)} %bitcast.7, s16[32,1024]{1,0:T(8,128)(2,1)S(1)} %collective-permute-done.3.refs_2_.refs_5_, s16[32,1024]{1,0:T(8,128)(2,1)S(1)} %collective-permute-done.4.refs_3_.refs_6_, ...), custom_call_target="tpu_custom_call" | custom-call | flops 268435456 | bytes 2097152 | tf_op jit(solution)/shard_map/contract_far_group/pallas_call | solution.py:160
  26.4 2.6 %collective-permute-start.10 = (s16[128,1024]{1,0:T(8,128)(2,1)S(1)}, s16[128,1024]{1,0:T(8,128)(2,1)S(1)}, u32[]{:S(2)}, u32[]{:S(2)}) collective-permute-start(s16[128,1024]{1,0:T(8,128)(2,1)S(1)} %contract_far_group.1), channel_id=1, source_target_pairs={{0,24},{1,25},{2,26},{3,27},{4,28},{5,29},{6,30},{7,31},{8,16},{9,... | collective-permute-start | bytes 786440 | tf_op jit(solution)/shard_map/ppermute | solution.py:274
  29.0 3.6 %collective-permute-done.5.refs_2_ = s16[64,1024]{1,0:T(8,128)(2,1)S(1)} collective-permute-done((s16[64,1024]{1,0:T(8,128)(2,1)S(1)}, s16[64,1024]{1,0:T(8,128)(2,1)S(1)}, u32[]{:S(2)}, u32[]{:S(2)}) %collective-permute-start.5) | collective-permute-done | bytes 131104 | tf_op jit(solution)/shard_map/ppermute | solution.py:274
  32.6 0.0 collective-permute-done.6.refs_3_
  32.6 0.0 collective-permute-done.2.refs_1_.refs_4_
  32.7 1.6 %collective-permute-start.7 = (s16[128,1024]{1,0:T(8,128)(2,1)S(1)}, s16[128,1024]{1,0:T(8,128)(2,1)S(1)}, u32[]{:S(2)}, u32[]{:S(2)}) collective-permute-start(s16[128,1024]{1,0:T(8,128)(2,1)S(1)} %get-tuple-element.34), channel_id=1, source_target_pairs={{0,8},{1,17},{2,10},{3,19},{4,12},{5,21},{6,14},{7,23},{8,0},{9,25... | collective-permute-start | bytes 786440 | tf_op jit(solution)/shard_map/ppermute | solution.py:274
  34.2 0.0 collective-permute-start.8
  34.2 0.0 collective-permute-done.10.refs_0_
  34.2 2.4 %collective-permute-start.11 = (s16[32,1024]{1,0:T(8,128)(2,1)S(1)}, s16[32,1024]{1,0:T(8,128)(2,1)S(1)}, u32[]{:S(2)}, u32[]{:S(2)}) collective-permute-start(s16[32,1024]{1,0:T(8,128)(2,1)S(1)} %get-tuple-element.38), channel_id=1, source_target_pairs={{0,2},{1,3},{2,0},{3,1},{4,6},{5,7},{6,4},{7,5},{8,10},{9,11},{10,... | collective-permute-start | bytes 196616 | tf_op jit(solution)/shard_map/ppermute | solution.py:274
  36.7 0.6 %collective-permute-start.12 = (s16[32,1024]{1,0:T(8,128)(2,1)S(1)}, s16[32,1024]{1,0:T(8,128)(2,1)S(1)}, u32[]{:S(2)}, u32[]{:S(2)}) collective-permute-start(s16[32,1024]{1,0:T(8,128)(2,1)S(1)} %get-tuple-element.39), channel_id=1, source_target_pairs={{0,4},{1,5},{2,6},{3,7},{4,0},{5,1},{6,2},{7,3},{8,12},{9,13},{10,... | collective-permute-start | bytes 196616 | tf_op jit(solution)/shard_map/ppermute | solution.py:274
  37.2 1.9 %collective-permute-start.13 = (s16[32,1024]{1,0:T(8,128)(2,1)S(1)}, s16[32,1024]{1,0:T(8,128)(2,1)S(1)}, u32[]{:S(2)}, u32[]{:S(2)}) collective-permute-start(s16[32,1024]{1,0:T(8,128)(2,1)S(1)} %get-tuple-element.40), channel_id=1, source_target_pairs={{0,6},{1,7},{2,4},{3,5},{4,2},{5,3},{6,0},{7,1},{8,14},{9,15},{10,... | collective-permute-start | bytes 196616 | tf_op jit(solution)/shard_map/ppermute | solution.py:274
  39.1 0.0 collective-permute-done.11.refs_7_.refs_10_
  39.2 4.5 %collective-permute-done.12.refs_8_.refs_11_ = s16[32,1024]{1,0:T(8,128)(2,1)S(1)} collective-permute-done((s16[32,1024]{1,0:T(8,128)(2,1)S(1)}, s16[32,1024]{1,0:T(8,128)(2,1)S(1)}, u32[]{:S(2)}, u32[]{:S(2)}) %collective-permute-start.12) | collective-permute-done | bytes 65568 | tf_op jit(solution)/shard_map/ppermute | solution.py:274
  43.6 0.0 collective-permute-done.13.refs_9_.refs_12_
  43.6 0.0 collective-permute-done.7.refs_4_.refs_7_
  43.6 0.0 collective-permute-done.8.refs_5_.refs_8_
  43.6 0.1 rows_of_other_core.1
  43.7 0.1 collective-permute-start.14
  43.8 1.9 %collective-permute-done.14.refs_13_ = s16[256,1024]{1,0:T(8,128)(2,1)S(1)} collective-permute-done((s16[256,1024]{1,0:T(8,128)(2,1)S(1)}, s16[256,1024]{1,0:T(8,128)(2,1)S(1)}, u32[]{:S(2)}, u32[]{:S(2)}) %collective-permute-start.14) | collective-permute-done | bytes 524320 | tf_op jit(solution)/shard_map/ppermute | solution.py:274
  45.7 0.0 copy-done.1
  45.7 0.0 copy-done.4
  45.7 0.0 copy-done.5
  45.7 0.0 copy-done.6
  45.7 3.1 %add_contributions.1 = f32[50,16,1024]{2,1,0:T(8,128)} custom-call(s32[4,8]{1,0:T(4,128)S(1)} %copy-done.5, s32[4,8]{1,0:T(4,128)S(1)} %copy-done.4, s32[4,8]{1,0:T(4,128)S(1)} %copy-done.6, s16[32,1024]{1,0:T(8,128)(2,1)S(1)} %get-tuple-element.24.refs_1_.refs_0_.refs_3_, s16[96,1024]{1,0:T(8,128)(2,1)S(1)} %collective-permute-done.2.refs_1_.refs_4_, ...), custom_call_target="tpu_custom_call" | custom-call | tf_op jit(solution)/shard_map/add_contributions/pallas_call | solution.py:251
  (3 shorter events, 0.1 us)
Async XLA Ops:
  0.0 1.2 %copy-start.2 = (bf16[4,128,1024]{2,1,0:T(8,128)(2,1)S(1)}, bf16[4,128,1024]{2,1,0:T(8,128)(2,1)}, u32[]{:S(2)}) copy-start(bf16[4,128,1024]{2,1,0:T(8,128)(2,1)} %amplitudes.1) | copy-start | bytes 3145732
  1.2 0.7 %copy-start.3 = (s32[4,8]{1,0:T(4,128)S(1)}, s32[4,8]{1,0:T(4,128)}, u32[]{:S(2)}) copy-start(s32[4,8]{1,0:T(4,128)} %refs_1_.1) | copy-start | bytes 388
  2.6 10.0 %copy-start = (bf16[1,1024,1024]{2,1,0:T(8,128)(2,1)S(1)}, bf16[1,1024,1024]{2,1,0:T(8,128)(2,1)}, u32[]{:S(2)}) copy-start(bf16[1,1024,1024]{2,1,0:T(8,128)(2,1)} %param.8) | copy-start | bytes 6291460
  2.6 10.0 %collective-permute-start = (bf16[128,1024]{1,0:T(8,128)(2,1)S(1)}, bf16[128,1024]{1,0:T(8,128)(2,1)S(1)}, u32[]{:S(2)}, u32[]{:S(2)}) collective-permute-start(bf16[128,1024]{1,0:T(8,128)(2,1)S(1)} %get-tuple-element.25), channel_id=1, source_target_pairs={{0,8},{1,17},{2,10},{3,19},{4,12},{5,21},{6,14},{7,23},{8,0},{9,25... | collective-permute-start | bytes 786440 | tf_op jit(solution)/shard_map/ppermute | solution.py:274
  5.6 7.0 %collective-permute-start.1 = (bf16[128,1024]{1,0:T(8,128)(2,1)S(1)}, bf16[128,1024]{1,0:T(8,128)(2,1)S(1)}, u32[]{:S(2)}, u32[]{:S(2)}) collective-permute-start(bf16[128,1024]{1,0:T(8,128)(2,1)S(1)} %get-tuple-element.26), channel_id=1, source_target_pairs={{0,16},{1,9},{2,18},{3,11},{4,20},{5,13},{6,22},{7,15},{8,24},{9,1... | collective-permute-start | bytes 786440 | tf_op jit(solution)/shard_map/ppermute | solution.py:274
  9.5 16.2 %collective-permute-start.9 = (bf16[128,1024]{1,0:T(8,128)(2,1)S(1)}, bf16[128,1024]{1,0:T(8,128)(2,1)S(1)}, u32[]{:S(2)}, u32[]{:S(2)}) collective-permute-start(bf16[128,1024]{1,0:T(8,128)(2,1)S(1)} %far_rows_after_near.1), channel_id=1, source_target_pairs={{0,24},{1,25},{2,26},{3,27},{4,28},{5,29},{6,30},{7,31},{8,16},{9,... | collective-permute-start | bytes 786440 | tf_op jit(solution)/shard_map/ppermute | solution.py:274
  9.6 9.0 %collective-permute-start.3 = (s16[32,1024]{1,0:T(8,128)(2,1)S(1)}, s16[32,1024]{1,0:T(8,128)(2,1)S(1)}, u32[]{:S(2)}, u32[]{:S(2)}) collective-permute-start(s16[32,1024]{1,0:T(8,128)(2,1)S(1)} %get-tuple-element.29), channel_id=1, source_target_pairs={{0,4},{1,5},{2,6},{3,7},{4,0},{5,1},{6,2},{7,3},{8,12},{9,13},{10,... | collective-permute-start | bytes 196616 | tf_op jit(solution)/shard_map/ppermute | solution.py:274
  13.8 18.9 %collective-permute-start.2 = (s16[96,1024]{1,0:T(8,128)(2,1)S(1)}, s16[96,1024]{1,0:T(8,128)(2,1)S(1)}, u32[]{:S(2)}, u32[]{:S(2)}) collective-permute-start(s16[96,1024]{1,0:T(8,128)(2,1)S(1)} %get-tuple-element.28), channel_id=1, source_target_pairs={{0,2},{1,3},{2,0},{3,1},{4,6},{5,7},{6,4},{7,5},{8,10},{9,11},{10,... | collective-permute-start | bytes 589832 | tf_op jit(solution)/shard_map/ppermute | solution.py:274
  16.0 9.7 %collective-permute-start.4 = (s16[32,1024]{1,0:T(8,128)(2,1)S(1)}, s16[32,1024]{1,0:T(8,128)(2,1)S(1)}, u32[]{:S(2)}, u32[]{:S(2)}) collective-permute-start(s16[32,1024]{1,0:T(8,128)(2,1)S(1)} %get-tuple-element.30), channel_id=1, source_target_pairs={{0,6},{1,7},{2,4},{3,5},{4,2},{5,3},{6,0},{7,1},{8,14},{9,15},{10,... | collective-permute-start | bytes 196616 | tf_op jit(solution)/shard_map/ppermute | solution.py:274
  18.5 14.1 %collective-permute-start.5 = (s16[64,1024]{1,0:T(8,128)(2,1)S(1)}, s16[64,1024]{1,0:T(8,128)(2,1)S(1)}, u32[]{:S(2)}, u32[]{:S(2)}) collective-permute-start(s16[64,1024]{1,0:T(8,128)(2,1)S(1)} %get-tuple-element.32), channel_id=1, source_target_pairs={{0,4},{1,5},{2,6},{3,7},{4,0},{5,1},{6,2},{7,3},{8,12},{9,13},{10,... | collective-permute-start | bytes 393224 | tf_op jit(solution)/shard_map/ppermute | solution.py:274
  18.6 14.0 %collective-permute-start.6 = (s16[64,1024]{1,0:T(8,128)(2,1)S(1)}, s16[64,1024]{1,0:T(8,128)(2,1)S(1)}, u32[]{:S(2)}, u32[]{:S(2)}) collective-permute-start(s16[64,1024]{1,0:T(8,128)(2,1)S(1)} %get-tuple-element.33), channel_id=1, source_target_pairs={{0,6},{1,7},{2,4},{3,5},{4,2},{5,3},{6,0},{7,1},{8,14},{9,15},{10,... | collective-permute-start | bytes 393224 | tf_op jit(solution)/shard_map/ppermute | solution.py:274
  25.7 20.0 %copy-start.1 = (f32[16,50,1024]{2,0,1:T(8,128)S(1)}, f32[16,50,1024]{2,0,1:T(8,128)}, u32[]{:S(2)}) copy-start(f32[16,50,1024]{2,0,1:T(8,128)} %param.11) | copy-start | bytes 9830404
  25.7 20.0 %copy-start.4 = (s32[4,8]{1,0:T(4,128)S(1)}, s32[4,8]{1,0:T(4,128)}, u32[]{:S(2)}) copy-start(s32[4,8]{1,0:T(4,128)} %refs_1_.1) | copy-start | bytes 388
  25.7 20.0 %copy-start.5 = (s32[4,8]{1,0:T(4,128)S(1)}, s32[4,8]{1,0:T(4,128)}, u32[]{:S(2)}) copy-start(s32[4,8]{1,0:T(4,128)} %refs_0_.1) | copy-start | bytes 388
  25.7 20.0 %copy-start.6 = (s32[4,8]{1,0:T(4,128)S(1)}, s32[4,8]{1,0:T(4,128)}, u32[]{:S(2)}) copy-start(s32[4,8]{1,0:T(4,128)} %refs_2_.1) | copy-start | bytes 388
  26.4 7.8 %collective-permute-start.10 = (s16[128,1024]{1,0:T(8,128)(2,1)S(1)}, s16[128,1024]{1,0:T(8,128)(2,1)S(1)}, u32[]{:S(2)}, u32[]{:S(2)}) collective-permute-start(s16[128,1024]{1,0:T(8,128)(2,1)S(1)} %contract_far_group.1), channel_id=1, source_target_pairs={{0,24},{1,25},{2,26},{3,27},{4,28},{5,29},{6,30},{7,31},{8,16},{9,... | collective-permute-start | bytes 786440 | tf_op jit(solution)/shard_map/ppermute | solution.py:274
  32.7 11.0 %collective-permute-start.7 = (s16[128,1024]{1,0:T(8,128)(2,1)S(1)}, s16[128,1024]{1,0:T(8,128)(2,1)S(1)}, u32[]{:S(2)}, u32[]{:S(2)}) collective-permute-start(s16[128,1024]{1,0:T(8,128)(2,1)S(1)} %get-tuple-element.34), channel_id=1, source_target_pairs={{0,8},{1,17},{2,10},{3,19},{4,12},{5,21},{6,14},{7,23},{8,0},{9,25... | collective-permute-start | bytes 786440 | tf_op jit(solution)/shard_map/ppermute | solution.py:274
  34.2 9.4 %collective-permute-start.8 = (s16[128,1024]{1,0:T(8,128)(2,1)S(1)}, s16[128,1024]{1,0:T(8,128)(2,1)S(1)}, u32[]{:S(2)}, u32[]{:S(2)}) collective-permute-start(s16[128,1024]{1,0:T(8,128)(2,1)S(1)} %get-tuple-element.35), channel_id=1, source_target_pairs={{0,16},{1,9},{2,18},{3,11},{4,20},{5,13},{6,22},{7,15},{8,24},{9,1... | collective-permute-start | bytes 786440 | tf_op jit(solution)/shard_map/ppermute | solution.py:274
  34.2 4.9 %collective-permute-start.11 = (s16[32,1024]{1,0:T(8,128)(2,1)S(1)}, s16[32,1024]{1,0:T(8,128)(2,1)S(1)}, u32[]{:S(2)}, u32[]{:S(2)}) collective-permute-start(s16[32,1024]{1,0:T(8,128)(2,1)S(1)} %get-tuple-element.38), channel_id=1, source_target_pairs={{0,2},{1,3},{2,0},{3,1},{4,6},{5,7},{6,4},{7,5},{8,10},{9,11},{10,... | collective-permute-start | bytes 196616 | tf_op jit(solution)/shard_map/ppermute | solution.py:274
  36.7 6.9 %collective-permute-start.12 = (s16[32,1024]{1,0:T(8,128)(2,1)S(1)}, s16[32,1024]{1,0:T(8,128)(2,1)S(1)}, u32[]{:S(2)}, u32[]{:S(2)}) collective-permute-start(s16[32,1024]{1,0:T(8,128)(2,1)S(1)} %get-tuple-element.39), channel_id=1, source_target_pairs={{0,4},{1,5},{2,6},{3,7},{4,0},{5,1},{6,2},{7,3},{8,12},{9,13},{10,... | collective-permute-start | bytes 196616 | tf_op jit(solution)/shard_map/ppermute | solution.py:274
  37.2 6.4 %collective-permute-start.13 = (s16[32,1024]{1,0:T(8,128)(2,1)S(1)}, s16[32,1024]{1,0:T(8,128)(2,1)S(1)}, u32[]{:S(2)}, u32[]{:S(2)}) collective-permute-start(s16[32,1024]{1,0:T(8,128)(2,1)S(1)} %get-tuple-element.40), channel_id=1, source_target_pairs={{0,6},{1,7},{2,4},{3,5},{4,2},{5,3},{6,0},{7,1},{8,14},{9,15},{10,... | collective-permute-start | bytes 196616 | tf_op jit(solution)/shard_map/ppermute | solution.py:274
  43.7 2.0 %collective-permute-start.14 = (s16[256,1024]{1,0:T(8,128)(2,1)S(1)}, s16[256,1024]{1,0:T(8,128)(2,1)S(1)}, u32[]{:S(2)}, u32[]{:S(2)}) collective-permute-start(s16[256,1024]{1,0:T(8,128)(2,1)S(1)} %rows_of_other_core.1), channel_id=1, source_target_pairs={{0,1},{1,0},{2,3},{3,2},{4,5},{5,4},{6,7},{7,6},{8,9},{9,8},{10,11... | collective-permute-start | bytes 1572872 | tf_op jit(solution)/shard_map/ppermute | solution.py:274

commit v11 on v9

--- a/solution.py
+++ b/solution.py
@@ -14,6 +14,7 @@
 LANES = 128
 CORES = 2
 MEBIBYTE = 1 << 20
+PICK_LIMIT = 209 * MEBIBYTE // 4
 SMEM = pl.BlockSpec(memory_space=pltpu.SMEM)
 VMEM = pl.BlockSpec(memory_space=pltpu.VMEM)
 ANY = pl.BlockSpec(memory_space=pl.ANY)
@@ -60,6 +61,10 @@
     return [0] + steps + [blk_count - 1]
 
 
+def chip_steps(chips):
+    return [0] + list(reversed(range(1, chips)))
+
+
 def start_all(copies):
     for copy in copies:
         copy.start()
@@ -90,7 +95,7 @@
         in_specs=[SMEM, ANY],
         out_specs=[VMEM] * groups,
         scratch_shapes=[pltpu.SemaphoreType.DMA((groups,))],
-        compiler_params=vmem_limit(*[block] * groups),
+        compiler_params=pltpu.CompilerParams(vmem_limit_bytes=PICK_LIMIT),
         name="pick_cd_blocks",
     )(tile_cd, amplitudes)
 
@@ -99,7 +104,7 @@
     product[...] = jnp.dot(rows[...], tile[...], preferred_element_type=jnp.float32)
     chip_rows = product.shape[0] // len(outgoing)
     chip = lax.axis_index("grp") // CORES
-    for step, coded in enumerate(outgoing):
+    for step, coded in zip(chip_steps(len(outgoing)), outgoing):
         source = pl.multiple_of(jnp.bitwise_xor(chip, step) * chip_rows, chip_rows)
         code, tail = encode(product[pl.ds(source, chip_rows), :])
         coded[first : first + chip_rows, :LANES] = code
@@ -199,22 +204,21 @@
 
 
 def pieces_of(arrays, owner_rows):
-    return [(array, first) for array in arrays for first in range(0, array.shape[0], CORES * owner_rows)]
-
-
-def other_core_kernel(owner_rows, *refs):
+    return [(i, first) for i, array in enumerate(arrays) for first in range(0, array.shape[0], CORES * owner_rows)]
+
+
+def other_core_kernel(pieces, owner_rows, *refs):
     arrays, halves = refs[:-1], refs[-1]
     other = 1 - lax.axis_index("grp") % CORES
-    for index, (array, first) in enumerate(pieces_of(arrays, owner_rows)):
+    for index, (array, first) in enumerate(pieces):
         source = pl.multiple_of(first + other * owner_rows, owner_rows)
-        halves[index * owner_rows : (index + 1) * owner_rows, :] = array[pl.ds(source, owner_rows), :]
-
-
-def other_core_rows(arrays, owner_rows):
-    rows = sum(array.shape[0] for array in arrays) // CORES
-    halves = jax.ShapeDtypeStruct((rows, arrays[0].shape[1]), arrays[0].dtype)
-    return pl.pallas_call(
-        lambda *refs: other_core_kernel(owner_rows, *refs),
+        halves[index * owner_rows : (index + 1) * owner_rows, :] = arrays[array][pl.ds(source, owner_rows), :]
+
+
+def other_core_rows(arrays, pieces, owner_rows):
+    halves = jax.ShapeDtypeStruct((len(pieces) * owner_rows, arrays[0].shape[1]), arrays[0].dtype)
+    return pl.pallas_call(
+        lambda *refs: other_core_kernel(pieces, owner_rows, *refs),
         out_shape=halves,
         in_specs=[VMEM] * len(arrays),
         out_specs=VMEM,
@@ -223,56 +227,105 @@
     )(*arrays)
 
 
-def add_kernel(parts, tile_ab, tile_cd, pair_screen, *rest):
-    arrays, (swapped, residual_in, residual, held, sems) = rest[:-5], rest[-5:]
+def add_rows(rows, tables, blk, grp, held):
+    tile_ab, tile_cd, pair_screen = tables
+    terms = []
+    for source, span, p, g in rows:
+        kept = pair_screen[tile_cd[p, g], grp].astype(jnp.float32)
+        terms.append((source, span, row_scale(source[span, :LANES]) * kept, tile_ab[p, g]))
+    for source, span, scale, ab in terms:
+        for lane in range(0, held.shape[2], LANES):
+            term = source[span, lane : lane + LANES].astype(jnp.float32) * scale
+            held[ab, :, lane : lane + LANES] = held[ab, :, lane : lane + LANES] + term
+
+
+def tile_of(index, blk, grp, core, chips, blk_count):
+    p = jnp.bitwise_xor(blk, blk_steps(blk_count, core)[index // chips])
+    chip_step = chip_steps(chips)[index % chips]
+    return p, (jnp.bitwise_xor(grp // CORES, chip_step)) * CORES + core
+
+
+def add_here_kernel(pieces, tile_ab, tile_cd, pair_screen, *rest):
+    arrays, residual_in, held = rest[:-2], rest[-2], rest[-1]
     blk, grp = lax.axis_index("blk"), lax.axis_index("grp")
-    ab_tiles, owner_rows, tile_width = residual.shape
-    chips = tile_ab.shape[1] // CORES
-    bounds = [ab_tiles * part // parts for part in range(parts + 1)]
-    spans = [pl.ds(low, high - low) for low, high in zip(bounds[:-1], bounds[1:])]
-    leaves = [pltpu.make_async_copy(held.at[span], residual.at[span], sems.at[i]) for i, span in enumerate(spans)]
+    ab_tiles, owner_rows, _ = held.shape
+    blk_count, chips = tile_ab.shape[0], tile_ab.shape[1] // CORES
+    core = grp % CORES
 
     def hold(ab, carry):
         held[ab] = residual_in[ab]
         return carry
 
     lax.fori_loop(0, ab_tiles, hold, 0)
-    pieces = pieces_of(arrays, owner_rows)
-    core = grp % CORES
-    steps_here, steps_there = blk_steps(tile_ab.shape[0], core), blk_steps(tile_ab.shape[0], 1 - core)
-    own = core * owner_rows
-    for start in range(0, len(pieces), chips):
-        terms = []
-        for index in range(start, start + chips):
+    for start in range(0, len(pieces), 2 * chips):
+        rows = []
+        for index in range(start, min(start + 2 * chips, len(pieces))):
             array, first = pieces[index]
-            p_here = jnp.bitwise_xor(blk, steps_here[index // chips])
-            p_there = jnp.bitwise_xor(blk, steps_there[index // chips])
-            g = jnp.bitwise_xor(grp, index % chips * CORES)
-            here = pl.ds(pl.multiple_of(first + own, owner_rows), owner_rows)
-            there = pl.ds(index * owner_rows, owner_rows)
-            for source, span, p, column in ((array, here, p_here, g), (swapped, there, p_there, jnp.bitwise_xor(g, 1))):
-                kept = pair_screen[tile_cd[p, column], grp].astype(jnp.float32)
-                scale = row_scale(source[span, :LANES]) * kept
-                terms.append((source, span, scale, tile_ab[p, column]))
-        for source, span, scale, ab in terms:
-            for lane in range(0, tile_width, LANES):
-                term = source[span, lane : lane + LANES].astype(jnp.float32) * scale
-                held[ab, :, lane : lane + LANES] = held[ab, :, lane : lane + LANES] + term
-    start_all(leaves)
-    wait_all(leaves)
-
-
-def add_blocks(tile_ab, tile_cd, pair_screen, arrays, swapped, residual_in):
-    parts = 5
-    return pl.pallas_call(
-        lambda *refs: add_kernel(parts, *refs),
+            span = pl.ds(pl.multiple_of(first + core * owner_rows, owner_rows), owner_rows)
+            rows.append((arrays[array], span, *tile_of(index, blk, grp, core, chips, blk_count)))
+        add_rows(rows, (tile_ab, tile_cd, pair_screen), blk, grp, held)
+
+
+def add_here(tables, arrays, pieces, residual_in):
+    return pl.pallas_call(
+        lambda *refs: add_here_kernel(pieces, *refs),
         out_shape=jax.ShapeDtypeStruct(residual_in.shape, residual_in.dtype),
-        in_specs=[SMEM] * 3 + [VMEM] * (len(arrays) + 2),
+        in_specs=[SMEM] * 3 + [VMEM] * (len(arrays) + 1),
+        out_specs=VMEM,
+        compiler_params=vmem_limit(*arrays, residual_in, residual_in),
+        name="add_contributions_here",
+    )(*tables, *arrays, residual_in)
+
+
+def add_there_kernel(parts, tile_ab, tile_cd, pair_screen, swapped, partial, residual, held, touched, part_sems, tile_sems):
+    blk, grp = lax.axis_index("blk"), lax.axis_index("grp")
+    ab_tiles, owner_rows, _ = residual.shape
+    blk_count, chips = tile_ab.shape[0], tile_ab.shape[1] // CORES
+    core = 1 - grp % CORES
+    bounds = [ab_tiles * part // parts for part in range(parts + 1)]
+    spans = [pl.ds(low, high - low) for low, high in zip(bounds[:-1], bounds[1:])]
+    bulk = [pltpu.make_async_copy(partial.at[span], residual.at[span], part_sems.at[i]) for i, span in enumerate(spans)]
+    start_all(bulk)
+
+    def clear(ab, carry):
+        touched[ab] = 0
+        return carry
+
+    lax.fori_loop(0, ab_tiles, clear, 0)
+    rows, fresh = [], []
+    for index in range(blk_count * chips):
+        span = pl.ds(index * owner_rows, owner_rows)
+        rows.append((swapped, span, *tile_of(index, blk, grp, core, chips, blk_count)))
+    for _, _, p, g in rows:
+        ab = tile_ab[p, g]
+        fresh.append((ab, touched[ab] == 0))
+        touched[ab] = 1
+        held[ab] = partial[ab]
+    for start in range(0, len(rows), 2 * chips):
+        add_rows(rows[start : start + 2 * chips], (tile_ab, tile_cd, pair_screen), blk, grp, held)
+    wait_all(bulk)
+    for action in ("start", "wait"):
+        for index, (ab, first) in enumerate(fresh):
+            copy = pltpu.make_async_copy(held.at[ab], residual.at[ab], tile_sems.at[index])
+            pl.when(first)(getattr(copy, action))
+
+
+def add_there(tables, swapped, partial):
+    parts, owner_rows = 5, partial.shape[1]
+    return pl.pallas_call(
+        lambda *refs: add_there_kernel(parts, *refs),
+        out_shape=jax.ShapeDtypeStruct(partial.shape, partial.dtype),
+        in_specs=[SMEM] * 3 + [VMEM] * 2,
         out_specs=ANY,
-        scratch_shapes=[pltpu.VMEM(residual_in.shape, residual_in.dtype), pltpu.SemaphoreType.DMA((parts,))],
-        compiler_params=vmem_limit(*arrays, swapped, residual_in, residual_in),
-        name="add_contributions",
-    )(tile_ab, tile_cd, pair_screen, *arrays, swapped, residual_in)
+        scratch_shapes=[
+            pltpu.VMEM(partial.shape, partial.dtype),
+            pltpu.SMEM((partial.shape[0],), jnp.int32),
+            pltpu.SemaphoreType.DMA((parts,)),
+            pltpu.SemaphoreType.DMA((swapped.shape[0] // owner_rows,)),
+        ],
+        compiler_params=vmem_limit(swapped, partial, partial),
+        name="add_contributions_there",
+    )(*tables, swapped, partial)
 
 
 def shards(amplitudes, pair_screen, integrals, tile_ab, tile_cd, residual_in):
@@ -290,8 +343,8 @@
         return lax.ppermute(value, ("blk", "grp"), pairs)
 
     def along_chips(outgoing):
-        arrived = {step: swap(outgoing[step], 0, step) for step in reversed(range(1, chips))}
-        return [outgoing[0]] + [arrived[step] for step in range(1, chips)]
+        steps = chip_steps(chips)
+        return [outgoing[0]] + [swap(outgoing[slot], 0, steps[slot]) for slot in range(1, chips)]
 
     own_rows, *near_picked, far_picked = pick(tile_cd, amplitudes)
     near_rows = [swap(rows, index + 1, 0) for index, rows in enumerate(near_picked)]
@@ -304,10 +357,11 @@
     far_back = swap(contract_far(far_rows, tile, chips, own_in[1:]), far, 0)
     far_in = along_chips(regroup([far_back], chips, "regroup_by_chip"))
     arrays = [*own_in, *near_in, *far_in]
-    swapped = swap(other_core_rows(arrays, owner_rows), 0, 0, 1)
-    by_tile = jnp.transpose(residual_in, (1, 0, 2))
-    added = add_blocks(tile_ab, tile_cd, pair_screen, arrays, swapped, by_tile)
-    return jnp.transpose(added, (1, 0, 2))
+    pieces = pieces_of(arrays, owner_rows)
+    swapped = swap(other_core_rows(arrays, pieces, owner_rows), 0, 0, 1)
+    tables = (tile_ab, tile_cd, pair_screen)
+    partial = add_here(tables, arrays, pieces, jnp.transpose(residual_in, (1, 0, 2)))
+    return jnp.transpose(add_there(tables, swapped, partial), (1, 0, 2))
 
 
 def solution(mesh):

time: 47.2 us -> 47.3 us (level)
  starting transfers between devices: 26 us -> 23.1 us
  Pallas kernels: 6.62 us -> 9.19 us
  waiting for transfers between devices: 10.8 us -> 12.4 us
  local copies, waits for them, and re-layouts: 3.51 us -> 2.28 us
    ppermute x16, starting transfers between devices: 26 us -> 23.1 us  [swap(): return lax.ppermute(value, ('blk', 'grp'), pairs)]
    ppermute x16, waiting for transfers between devices: 10.8 us -> 12.4 us  [swap(): return lax.ppermute(value, ('blk', 'grp'), pairs)]
    pallas_call x2 -> x3, Pallas kernels: 3.16 us -> 4.65 us  [the longest x1 3.39 us: add_there(): pl.pallas_call(lambda *refs: add_there_kernel(parts, *refs), out_shape=ja...]
    unnamed x14 -> x10, local copies, waits for them, and re-layouts: 3.51 us -> 2.28 us
    pallas_call x1, Pallas kernels: 0.7 us -> 1.8 us  [pick(): pl.pallas_call(pick_kernel, out_shape=[block] * groups, in_specs=[SMEM, A...]
  transfers between devices with their start and end apart: 16 -> 16, of which waited for: 5 -> 6; matrix products, arithmetic and copies ran while one was open for 0% -> 0% of each run, Pallas kernels for 6% -> 8%
where the time goes in v11:
time: 47.3 us; the launch traced here: 47.2 us
  starting transfers between devices  23.1 us (49%)
  waiting for transfers between devices  12.4 us (26%)
  Pallas kernels  9.19 us (19%)
  local copies, waits for them, and re-layouts  2.28 us (5%)
    ppermute x16, starting transfers between devices, swap(): return lax.ppermute(value, ('blk', 'grp'), pairs)  23.1 us
    ppermute x16, waiting for transfers between devices, swap(): return lax.ppermute(value, ('blk', 'grp'), pairs)  12.4 us
    pallas_call x1, Pallas kernels, add_there(): pl.pallas_call(lambda *refs: add_there_kernel(parts, *refs), out_shape=ja...  3.39 us
    unnamed x10, local copies, waits for them, and re-layouts  2.28 us
    pallas_call x1, Pallas kernels, pick(): pl.pallas_call(pick_kernel, out_shape=[block] * groups, in_specs=[SMEM, A...  1.8 us
    pallas_call x1, Pallas kernels, add_here(): pl.pallas_call(lambda *refs: add_here_kernel(pieces, *refs), out_shape=ja...  1.2 us
    pallas_call x1, Pallas kernels, contract_near(): pl.pallas_call(lambda *refs: near_kernel(len(groups), *refs), out_shape=[...  1.12 us
  transfers between devices with their start and end apart: 16, of which 6 were waited for; matrix products, arithmetic and copies ran while one was open for 0% of the time, Pallas kernels for 8%

profile of v11, /device:TPU:0, one launch (start us, length us, event | category | flops | bytes accessed | tf_op | source)
XLA Modules:
  0.0 47.2 jit_solution(9945841704595013389)
XLA Ops:
  0.0 0.0 copy-start.2
  0.0 0.7 %copy-done.2 = s32[4,8]{1,0:T(4,128)S(1)} copy-done((s32[4,8]{1,0:T(4,128)S(1)}, s32[4,8]{1,0:T(4,128)}, u32[]{:S(2)}) %copy-start.2) | copy-done | bytes 152
  0.7 1.8 %pick_cd_blocks.1 = (bf16[128,1024]{1,0:T(8,128)(2,1)S(1)}, bf16[128,1024]{1,0:T(8,128)(2,1)S(1)}, bf16[128,1024]{1,0:T(8,128)(2,1)S(1)}, bf16[128,1024]{1,0:T(8,128)(2,1)S(1)}) custom-call(s32[4,8]{1,0:T(4,128)S(1)} %copy-done.2, bf16[4,128,1024]{2,1,0:T(8,128)(2,1)} %amplitudes.1), custom_call_target="tpu_custom_call" | custom-call | tf_op jit(solution)/shard_map/pick_cd_blocks/pallas_call | solution.py:92
  2.5 3.0 %collective-permute-start.3 = (bf16[128,1024]{1,0:T(8,128)(2,1)S(1)}, bf16[128,1024]{1,0:T(8,128)(2,1)S(1)}, u32[]{:S(2)}, u32[]{:S(2)}) collective-permute-start(bf16[128,1024]{1,0:T(8,128)(2,1)S(1)} %get-tuple-element.31), channel_id=1, source_target_pairs={{0,8},{1,17},{2,10},{3,19},{4,12},{5,21},{6,14},{7,23},{8,0},{9,25... | collective-permute-start | bytes 786440 | tf_op jit(solution)/shard_map/ppermute | solution.py:343
  5.5 1.5 %collective-permute-start.4 = (bf16[128,1024]{1,0:T(8,128)(2,1)S(1)}, bf16[128,1024]{1,0:T(8,128)(2,1)S(1)}, u32[]{:S(2)}, u32[]{:S(2)}) collective-permute-start(bf16[128,1024]{1,0:T(8,128)(2,1)S(1)} %get-tuple-element.32), channel_id=1, source_target_pairs={{0,16},{1,9},{2,18},{3,11},{4,20},{5,13},{6,22},{7,15},{8,24},{9,1... | collective-permute-start | bytes 786440 | tf_op jit(solution)/shard_map/ppermute | solution.py:343
  7.0 0.0 copy-start.1
  7.0 1.6 %copy-done.1 = bf16[1,1024,1024]{2,1,0:T(8,128)(2,1)S(1)} copy-done((bf16[1,1024,1024]{2,1,0:T(8,128)(2,1)S(1)}, bf16[1,1024,1024]{2,1,0:T(8,128)(2,1)}, u32[]{:S(2)}) %copy-start.1) | copy-done | bytes 2097176
  8.6 0.9 %contract_own_group.1 = (s16[32,1024]{1,0:T(8,128)(2,1)S(1)}, s16[32,1024]{1,0:T(8,128)(2,1)S(1)}, s16[32,1024]{1,0:T(8,128)(2,1)S(1)}, s16[32,1024]{1,0:T(8,128...) custom-call(bf16[128,1024]{1,0:T(8,128)(2,1)S(1)} %get-tuple-element.25.rows, ...), custom_call_target="tpu_custom_call" | custom-call | flops 268435456 | bytes 2097152 | tf_op jit(solution)/shard_map/contract_own_group/pallas_call | solution.py:128
  9.5 0.1 collective-permute-start.10
  9.6 4.0 %collective-permute-start = (s16[32,1024]{1,0:T(8,128)(2,1)S(1)}, s16[32,1024]{1,0:T(8,128)(2,1)S(1)}, u32[]{:S(2)}, u32[]{:S(2)}) collective-permute-start(s16[32,1024]{1,0:T(8,128)(2,1)S(1)} %get-tuple-element.28), channel_id=1, source_target_pairs={{0,6},{1,7},{2,4},{3,5},{4,2},{5,3},{6,0},{7,1},{8,14},{9,15},{10,... | collective-permute-start | bytes 196616 | tf_op jit(solution)/shard_map/ppermute | solution.py:343
  13.6 0.0 collective-permute-start.1
  13.6 0.0 collective-permute-done.3.refs_0_
  13.6 1.0 %collective-permute-start.2 = (s16[32,1024]{1,0:T(8,128)(2,1)S(1)}, s16[32,1024]{1,0:T(8,128)(2,1)S(1)}, u32[]{:S(2)}, u32[]{:S(2)}) collective-permute-start(s16[32,1024]{1,0:T(8,128)(2,1)S(1)} %get-tuple-element.30), channel_id=1, source_target_pairs={{0,2},{1,3},{2,0},{3,1},{4,6},{5,7},{6,4},{7,5},{8,10},{9,11},{10,... | collective-permute-start | bytes 196616 | tf_op jit(solution)/shard_map/ppermute | solution.py:343
  14.7 0.0 collective-permute-done.4.refs_1_
  14.7 0.0 copy-start
  14.7 0.0 copy-start.3
  14.7 0.0 copy-start.4
  14.7 1.1 %contract_near_groups.1 = (s16[64,1024]{1,0:T(8,128)(2,1)S(1)}, s16[64,1024]{1,0:T(8,128)(2,1)S(1)}, s16[64,1024]{1,0:T(8,128)(2,1)S(1)}, s16[64,1024]{1,0:T(8,128)(2,1)S(1)}) custom-call(bf16[128,1024]{1,0:T(8,128)(2,1)S(1)} %collective-permute-done.3.refs_0_, bf16[128,1024]{1,0:T(8,128)(2,1)S(1)} %collective-permute-done.4.refs_1_, ...), custom_call_target="tpu_custom_call" | custom-call | flops 536870912 | bytes 2097152 | tf_op jit(solution)/shard_map/contract_near_groups/pallas_call | solution.py:151
  15.8 3.4 %collective-permute-start.5 = (s16[64,1024]{1,0:T(8,128)(2,1)S(1)}, s16[64,1024]{1,0:T(8,128)(2,1)S(1)}, u32[]{:S(2)}, u32[]{:S(2)}) collective-permute-start(s16[64,1024]{1,0:T(8,128)(2,1)S(1)} %get-tuple-element.35), channel_id=1, source_target_pairs={{0,6},{1,7},{2,4},{3,5},{4,2},{5,3},{6,0},{7,1},{8,14},{9,15},{10,... | collective-permute-start | bytes 393224 | tf_op jit(solution)/shard_map/ppermute | solution.py:343
  19.2 0.0 collective-permute-done.refs_2_.refs_1_.refs_4_
  19.2 0.0 collective-permute-start.6
  19.2 4.4 %collective-permute-done.1.refs_3_.refs_2_.refs_5_ = s16[32,1024]{1,0:T(8,128)(2,1)S(1)} collective-permute-done((s16[32,1024]{1,0:T(8,128)(2,1)S(1)}, s16[32,1024]{1,0:T(8,128)(2,1)S(1)}, u32[]{:S(2)}, u32[]{:S(2)}) %collective-permute-start.1) | collective-permute-done | bytes 65568 | tf_op jit(solution)/shard_map/ppermute | solution.py:343
  23.7 0.0 collective-permute-start.7
  23.7 0.0 collective-permute-done.2.refs_4_.refs_3_.refs_6_
  23.7 0.0 collective-permute-done.10.refs_0_
  23.7 0.7 %contract_far_group.1 = s16[128,1024]{1,0:T(8,128)(2,1)S(1)} custom-call(bf16[128,1024]{1,0:T(8,128)(2,1)S(1)} %collective-permute-done.10.refs_0_, bf16[1024,1024]{1,0:T(8,128)(2,1)S(1)} %get-tuple-element.33.refs_2_.refs_1_, s16[32,1024]{1,0:T(8,128)(2,1)S(1)} %collective-permute-done.refs_2_.refs_1_.refs_4_, ...), custom_call_target="tpu_custom_call" | custom-call | flops 268435456 | bytes 2097152 | tf_op jit(solution)/shard_map/contract_far_group/pallas_call | solution.py:173
  24.4 2.6 %collective-permute-start.11 = (s16[128,1024]{1,0:T(8,128)(2,1)S(1)}, s16[128,1024]{1,0:T(8,128)(2,1)S(1)}, u32[]{:S(2)}, u32[]{:S(2)}) collective-permute-start(s16[128,1024]{1,0:T(8,128)(2,1)S(1)} %contract_far_group.1), channel_id=1, source_target_pairs={{0,24},{1,25},{2,26},{3,27},{4,28},{5,29},{6,30},{7,31},{8,16},{9,... | collective-permute-start | bytes 786440 | tf_op jit(solution)/shard_map/ppermute | solution.py:343
  27.0 0.0 collective-permute-done.5.refs_1_
  27.0 3.3 %collective-permute-done.6.refs_2_ = s16[64,1024]{1,0:T(8,128)(2,1)S(1)} collective-permute-done((s16[64,1024]{1,0:T(8,128)(2,1)S(1)}, s16[64,1024]{1,0:T(8,128)(2,1)S(1)}, u32[]{:S(2)}, u32[]{:S(2)}) %collective-permute-start.6) | collective-permute-done | bytes 131104 | tf_op jit(solution)/shard_map/ppermute | solution.py:343
  30.3 0.9 %collective-permute-done.7.refs_3_ = s16[64,1024]{1,0:T(8,128)(2,1)S(1)} collective-permute-done((s16[64,1024]{1,0:T(8,128)(2,1)S(1)}, s16[64,1024]{1,0:T(8,128)(2,1)S(1)}, u32[]{:S(2)}, u32[]{:S(2)}) %collective-permute-start.7) | collective-permute-done | bytes 131104 | tf_op jit(solution)/shard_map/ppermute | solution.py:343
  31.2 1.6 %collective-permute-start.8 = (s16[128,1024]{1,0:T(8,128)(2,1)S(1)}, s16[128,1024]{1,0:T(8,128)(2,1)S(1)}, u32[]{:S(2)}, u32[]{:S(2)}) collective-permute-start(s16[128,1024]{1,0:T(8,128)(2,1)S(1)} %get-tuple-element.38), channel_id=1, source_target_pairs={{0,8},{1,17},{2,10},{3,19},{4,12},{5,21},{6,14},{7,23},{8,0},{9,25... | collective-permute-start | bytes 786440 | tf_op jit(solution)/shard_map/ppermute | solution.py:343
  32.8 1.4 %collective-permute-start.9 = (s16[128,1024]{1,0:T(8,128)(2,1)S(1)}, s16[128,1024]{1,0:T(8,128)(2,1)S(1)}, u32[]{:S(2)}, u32[]{:S(2)}) collective-permute-start(s16[128,1024]{1,0:T(8,128)(2,1)S(1)} %get-tuple-element.39), channel_id=1, source_target_pairs={{0,16},{1,9},{2,18},{3,11},{4,20},{5,13},{6,22},{7,15},{8,24},{9,1... | collective-permute-start | bytes 786440 | tf_op jit(solution)/shard_map/ppermute | solution.py:343
  34.1 0.0 collective-permute-done.11.refs_0_
  34.1 1.5 %collective-permute-start.12 = (s16[32,1024]{1,0:T(8,128)(2,1)S(1)}, s16[32,1024]{1,0:T(8,128)(2,1)S(1)}, u32[]{:S(2)}, u32[]{:S(2)}) collective-permute-start(s16[32,1024]{1,0:T(8,128)(2,1)S(1)} %get-tuple-element.42), channel_id=1, source_target_pairs={{0,6},{1,7},{2,4},{3,5},{4,2},{5,3},{6,0},{7,1},{8,14},{9,15},{10,... | collective-permute-start | bytes 196616 | tf_op jit(solution)/shard_map/ppermute | solution.py:343
  35.7 0.6 %collective-permute-start.13 = (s16[32,1024]{1,0:T(8,128)(2,1)S(1)}, s16[32,1024]{1,0:T(8,128)(2,1)S(1)}, u32[]{:S(2)}, u32[]{:S(2)}) collective-permute-start(s16[32,1024]{1,0:T(8,128)(2,1)S(1)} %get-tuple-element.43), channel_id=1, source_target_pairs={{0,4},{1,5},{2,6},{3,7},{4,0},{5,1},{6,2},{7,3},{8,12},{9,13},{10,... | collective-permute-start | bytes 196616 | tf_op jit(solution)/shard_map/ppermute | solution.py:343
  36.2 2.4 %collective-permute-start.14 = (s16[32,1024]{1,0:T(8,128)(2,1)S(1)}, s16[32,1024]{1,0:T(8,128)(2,1)S(1)}, u32[]{:S(2)}, u32[]{:S(2)}) collective-permute-start(s16[32,1024]{1,0:T(8,128)(2,1)S(1)} %get-tuple-element.44), channel_id=1, source_target_pairs={{0,2},{1,3},{2,0},{3,1},{4,6},{5,7},{6,4},{7,5},{8,10},{9,11},{10,... | collective-permute-start | bytes 196616 | tf_op jit(solution)/shard_map/ppermute | solution.py:343
  38.6 1.8 %collective-permute-done.12.refs_7_.refs_10_ = s16[32,1024]{1,0:T(8,128)(2,1)S(1)} collective-permute-done((s16[32,1024]{1,0:T(8,128)(2,1)S(1)}, s16[32,1024]{1,0:T(8,128)(2,1)S(1)}, u32[]{:S(2)}, u32[]{:S(2)}) %collective-permute-start.12) | collective-permute-done | bytes 65568 | tf_op jit(solution)/shard_map/ppermute | solution.py:343
  40.4 1.4 %collective-permute-done.13.refs_8_.refs_11_ = s16[32,1024]{1,0:T(8,128)(2,1)S(1)} collective-permute-done((s16[32,1024]{1,0:T(8,128)(2,1)S(1)}, s16[32,1024]{1,0:T(8,128)(2,1)S(1)}, u32[]{:S(2)}, u32[]{:S(2)}) %collective-permute-start.13) | collective-permute-done | bytes 65568 | tf_op jit(solution)/shard_map/ppermute | solution.py:343
  41.7 0.0 collective-permute-done.14.refs_9_.refs_12_
  41.7 0.0 collective-permute-done.8.refs_4_.refs_7_
  41.7 0.0 collective-permute-done.9.refs_5_.refs_8_
  41.7 0.1 rows_of_other_core.1
  41.8 0.1 collective-permute-start.15
  41.9 0.0 copy-done
  41.9 0.0 copy-done.3
  41.9 0.0 copy-done.4
  41.9 1.2 %add_contributions_here.1.refs_4_ = f32[50,16,1024]{2,1,0:T(8,128)S(1)} custom-call(s32[4,8]{1,0:T(4,128)S(1)} %copy-done.3, s32[4,8]{1,0:T(4,128)S(1)} %copy-done.2, s32[4,8]{1,0:T(4,128)S(1)} %copy-done.4, s16[32,1024]{1,0:T(8,128)(2,1)S(1)} %get-tuple-element.27.refs_0_.refs_3_, s16[32,1024]{1,0:T(8,128)(2,1)S(1)} %collective-permute-done.refs_2_.refs_1_.refs_4_, ...), custom_call_target="tpu_custom_call" | custom-call | tf_op jit(solution)/shard_map/add_contributions_here/pallas_call | solution.py:270
  43.1 0.7 %collective-permute-done.15.refs_3_ = s16[256,1024]{1,0:T(8,128)(2,1)S(1)} collective-permute-done((s16[256,1024]{1,0:T(8,128)(2,1)S(1)}, s16[256,1024]{1,0:T(8,128)(2,1)S(1)}, u32[]{:S(2)}, u32[]{:S(2)}) %collective-permute-start.15) | collective-permute-done | bytes 524320 | tf_op jit(solution)/shard_map/ppermute | solution.py:343
  43.8 3.4 %add_contributions_there.1 = f32[50,16,1024]{2,1,0:T(8,128)} custom-call(s32[4,8]{1,0:T(4,128)S(1)} %copy-done.3, s32[4,8]{1,0:T(4,128)S(1)} %copy-done.2, s32[4,8]{1,0:T(4,128)S(1)} %copy-done.4, s16[256,1024]{1,0:T(8,128)(2,1)S(1)} %collective-permute-done.15.refs_3_, f32[50,16,1024]{2,1,0:T(8,128)S(1)} %add_contributions_here.1.refs_4_), custom_call_target="tpu_custom_call" | custom-call | tf_op jit(solution)/shard_map/add_contributions_there/pallas_call | solution.py:315
  (2 shorter events, 0.1 us)
Async XLA Ops:
  0.0 0.7 %copy-start.2 = (s32[4,8]{1,0:T(4,128)S(1)}, s32[4,8]{1,0:T(4,128)}, u32[]{:S(2)}) copy-start(s32[4,8]{1,0:T(4,128)} %refs_1_.3) | copy-start | bytes 388
  2.5 11.1 %collective-permute-start.3 = (bf16[128,1024]{1,0:T(8,128)(2,1)S(1)}, bf16[128,1024]{1,0:T(8,128)(2,1)S(1)}, u32[]{:S(2)}, u32[]{:S(2)}) collective-permute-start(bf16[128,1024]{1,0:T(8,128)(2,1)S(1)} %get-tuple-element.31), channel_id=1, source_target_pairs={{0,8},{1,17},{2,10},{3,19},{4,12},{5,21},{6,14},{7,23},{8,0},{9,25... | collective-permute-start | bytes 786440 | tf_op jit(solution)/shard_map/ppermute | solution.py:343
  5.5 9.2 %collective-permute-start.4 = (bf16[128,1024]{1,0:T(8,128)(2,1)S(1)}, bf16[128,1024]{1,0:T(8,128)(2,1)S(1)}, u32[]{:S(2)}, u32[]{:S(2)}) collective-permute-start(bf16[128,1024]{1,0:T(8,128)(2,1)S(1)} %get-tuple-element.32), channel_id=1, source_target_pairs={{0,16},{1,9},{2,18},{3,11},{4,20},{5,13},{6,22},{7,15},{8,24},{9,1... | collective-permute-start | bytes 786440 | tf_op jit(solution)/shard_map/ppermute | solution.py:343
  7.0 1.6 %copy-start.1 = (bf16[1,1024,1024]{2,1,0:T(8,128)(2,1)S(1)}, bf16[1,1024,1024]{2,1,0:T(8,128)(2,1)}, u32[]{:S(2)}) copy-start(bf16[1,1024,1024]{2,1,0:T(8,128)(2,1)} %param.8) | copy-start | bytes 6291460
  9.5 14.2 %collective-permute-start.10 = (bf16[128,1024]{1,0:T(8,128)(2,1)S(1)}, bf16[128,1024]{1,0:T(8,128)(2,1)S(1)}, u32[]{:S(2)}, u32[]{:S(2)}) collective-permute-start(bf16[128,1024]{1,0:T(8,128)(2,1)S(1)} %get-tuple-element.40), channel_id=1, source_target_pairs={{0,24},{1,25},{2,26},{3,27},{4,28},{5,29},{6,30},{7,31},{8,16},{9,... | collective-permute-start | bytes 786440 | tf_op jit(solution)/shard_map/ppermute | solution.py:343
  9.6 9.7 %collective-permute-start = (s16[32,1024]{1,0:T(8,128)(2,1)S(1)}, s16[32,1024]{1,0:T(8,128)(2,1)S(1)}, u32[]{:S(2)}, u32[]{:S(2)}) collective-permute-start(s16[32,1024]{1,0:T(8,128)(2,1)S(1)} %get-tuple-element.28), channel_id=1, source_target_pairs={{0,6},{1,7},{2,4},{3,5},{4,2},{5,3},{6,0},{7,1},{8,14},{9,15},{10,... | collective-permute-start | bytes 196616 | tf_op jit(solution)/shard_map/ppermute | solution.py:343
  13.6 10.1 %collective-permute-start.1 = (s16[32,1024]{1,0:T(8,128)(2,1)S(1)}, s16[32,1024]{1,0:T(8,128)(2,1)S(1)}, u32[]{:S(2)}, u32[]{:S(2)}) collective-permute-start(s16[32,1024]{1,0:T(8,128)(2,1)S(1)} %get-tuple-element.29), channel_id=1, source_target_pairs={{0,4},{1,5},{2,6},{3,7},{4,0},{5,1},{6,2},{7,3},{8,12},{9,13},{10,... | collective-permute-start | bytes 196616 | tf_op jit(solution)/shard_map/ppermute | solution.py:343
  13.6 10.1 %collective-permute-start.2 = (s16[32,1024]{1,0:T(8,128)(2,1)S(1)}, s16[32,1024]{1,0:T(8,128)(2,1)S(1)}, u32[]{:S(2)}, u32[]{:S(2)}) collective-permute-start(s16[32,1024]{1,0:T(8,128)(2,1)S(1)} %get-tuple-element.30), channel_id=1, source_target_pairs={{0,2},{1,3},{2,0},{3,1},{4,6},{5,7},{6,4},{7,5},{8,10},{9,11},{10,... | collective-permute-start | bytes 196616 | tf_op jit(solution)/shard_map/ppermute | solution.py:343
  14.7 27.2 %copy-start = (f32[16,50,1024]{2,0,1:T(8,128)S(1)}, f32[16,50,1024]{2,0,1:T(8,128)}, u32[]{:S(2)}) copy-start(f32[16,50,1024]{2,0,1:T(8,128)} %param.11) | copy-start | bytes 9830404
  14.7 27.2 %copy-start.3 = (s32[4,8]{1,0:T(4,128)S(1)}, s32[4,8]{1,0:T(4,128)}, u32[]{:S(2)}) copy-start(s32[4,8]{1,0:T(4,128)} %refs_0_.3) | copy-start | bytes 388
  14.7 27.2 %copy-start.4 = (s32[4,8]{1,0:T(4,128)S(1)}, s32[4,8]{1,0:T(4,128)}, u32[]{:S(2)}) copy-start(s32[4,8]{1,0:T(4,128)} %refs_2_.3) | copy-start | bytes 388
  15.8 11.2 %collective-permute-start.5 = (s16[64,1024]{1,0:T(8,128)(2,1)S(1)}, s16[64,1024]{1,0:T(8,128)(2,1)S(1)}, u32[]{:S(2)}, u32[]{:S(2)}) collective-permute-start(s16[64,1024]{1,0:T(8,128)(2,1)S(1)} %get-tuple-element.35), channel_id=1, source_target_pairs={{0,6},{1,7},{2,4},{3,5},{4,2},{5,3},{6,0},{7,1},{8,14},{9,15},{10,... | collective-permute-start | bytes 393224 | tf_op jit(solution)/shard_map/ppermute | solution.py:343
  19.2 11.0 %collective-permute-start.6 = (s16[64,1024]{1,0:T(8,128)(2,1)S(1)}, s16[64,1024]{1,0:T(8,128)(2,1)S(1)}, u32[]{:S(2)}, u32[]{:S(2)}) collective-permute-start(s16[64,1024]{1,0:T(8,128)(2,1)S(1)} %get-tuple-element.36), channel_id=1, source_target_pairs={{0,4},{1,5},{2,6},{3,7},{4,0},{5,1},{6,2},{7,3},{8,12},{9,13},{10,... | collective-permute-start | bytes 393224 | tf_op jit(solution)/shard_map/ppermute | solution.py:343
  23.7 7.5 %collective-permute-start.7 = (s16[64,1024]{1,0:T(8,128)(2,1)S(1)}, s16[64,1024]{1,0:T(8,128)(2,1)S(1)}, u32[]{:S(2)}, u32[]{:S(2)}) collective-permute-start(s16[64,1024]{1,0:T(8,128)(2,1)S(1)} %get-tuple-element.37), channel_id=1, source_target_pairs={{0,2},{1,3},{2,0},{3,1},{4,6},{5,7},{6,4},{7,5},{8,10},{9,11},{10,... | collective-permute-start | bytes 393224 | tf_op jit(solution)/shard_map/ppermute | solution.py:343
  24.4 9.7 %collective-permute-start.11 = (s16[128,1024]{1,0:T(8,128)(2,1)S(1)}, s16[128,1024]{1,0:T(8,128)(2,1)S(1)}, u32[]{:S(2)}, u32[]{:S(2)}) collective-permute-start(s16[128,1024]{1,0:T(8,128)(2,1)S(1)} %contract_far_group.1), channel_id=1, source_target_pairs={{0,24},{1,25},{2,26},{3,27},{4,28},{5,29},{6,30},{7,31},{8,16},{9,... | collective-permute-start | bytes 786440 | tf_op jit(solution)/shard_map/ppermute | solution.py:343
  31.2 10.5 %collective-permute-start.8 = (s16[128,1024]{1,0:T(8,128)(2,1)S(1)}, s16[128,1024]{1,0:T(8,128)(2,1)S(1)}, u32[]{:S(2)}, u32[]{:S(2)}) collective-permute-start(s16[128,1024]{1,0:T(8,128)(2,1)S(1)} %get-tuple-element.38), channel_id=1, source_target_pairs={{0,8},{1,17},{2,10},{3,19},{4,12},{5,21},{6,14},{7,23},{8,0},{9,25... | collective-permute-start | bytes 786440 | tf_op jit(solution)/shard_map/ppermute | solution.py:343
  32.8 9.0 %collective-permute-start.9 = (s16[128,1024]{1,0:T(8,128)(2,1)S(1)}, s16[128,1024]{1,0:T(8,128)(2,1)S(1)}, u32[]{:S(2)}, u32[]{:S(2)}) collective-permute-start(s16[128,1024]{1,0:T(8,128)(2,1)S(1)} %get-tuple-element.39), channel_id=1, source_target_pairs={{0,16},{1,9},{2,18},{3,11},{4,20},{5,13},{6,22},{7,15},{8,24},{9,1... | collective-permute-start | bytes 786440 | tf_op jit(solution)/shard_map/ppermute | solution.py:343
  34.1 6.2 %collective-permute-start.12 = (s16[32,1024]{1,0:T(8,128)(2,1)S(1)}, s16[32,1024]{1,0:T(8,128)(2,1)S(1)}, u32[]{:S(2)}, u32[]{:S(2)}) collective-permute-start(s16[32,1024]{1,0:T(8,128)(2,1)S(1)} %get-tuple-element.42), channel_id=1, source_target_pairs={{0,6},{1,7},{2,4},{3,5},{4,2},{5,3},{6,0},{7,1},{8,14},{9,15},{10,... | collective-permute-start | bytes 196616 | tf_op jit(solution)/shard_map/ppermute | solution.py:343
  35.7 6.0 %collective-permute-start.13 = (s16[32,1024]{1,0:T(8,128)(2,1)S(1)}, s16[32,1024]{1,0:T(8,128)(2,1)S(1)}, u32[]{:S(2)}, u32[]{:S(2)}) collective-permute-start(s16[32,1024]{1,0:T(8,128)(2,1)S(1)} %get-tuple-element.43), channel_id=1, source_target_pairs={{0,4},{1,5},{2,6},{3,7},{4,0},{5,1},{6,2},{7,3},{8,12},{9,13},{10,... | collective-permute-start | bytes 196616 | tf_op jit(solution)/shard_map/ppermute | solution.py:343
  36.2 5.5 %collective-permute-start.14 = (s16[32,1024]{1,0:T(8,128)(2,1)S(1)}, s16[32,1024]{1,0:T(8,128)(2,1)S(1)}, u32[]{:S(2)}, u32[]{:S(2)}) collective-permute-start(s16[32,1024]{1,0:T(8,128)(2,1)S(1)} %get-tuple-element.44), channel_id=1, source_target_pairs={{0,2},{1,3},{2,0},{3,1},{4,6},{5,7},{6,4},{7,5},{8,10},{9,11},{10,... | collective-permute-start | bytes 196616 | tf_op jit(solution)/shard_map/ppermute | solution.py:343
  41.8 2.0 %collective-permute-start.15 = (s16[256,1024]{1,0:T(8,128)(2,1)S(1)}, s16[256,1024]{1,0:T(8,128)(2,1)S(1)}, u32[]{:S(2)}, u32[]{:S(2)}) collective-permute-start(s16[256,1024]{1,0:T(8,128)(2,1)S(1)} %rows_of_other_core.1), channel_id=1, source_target_pairs={{0,1},{1,0},{2,3},{3,2},{4,5},{5,4},{6,7},{7,6},{8,9},{9,8},{10,11... | collective-permute-start | bytes 1572872 | tf_op jit(solution)/shard_map/ppermute | solution.py:343

commit v12 on v11

v12 whole, which is shorter than its diff:
```python
import math

import jax
import jax.numpy as jnp
from jax import lax
from jax.experimental import pallas as pl
from jax.experimental.pallas import tpu as pltpu
from jax.sharding import PartitionSpec as P

LARGEST = 32766.0
SCALE_STEPS = 64.0
SCALE_SHIFT = 8192
SCALE_BITS = 16
LANES = 128
CORES = 2
MEBIBYTE = 1 << 20
SMEM = pl.BlockSpec(memory_space=pltpu.SMEM)
VMEM = pl.BlockSpec(memory_space=pltpu.VMEM)
ANY = pl.BlockSpec(memory_space=pl.ANY)


def vmem_limit(*arrays):
    total = sum(math.prod(array.shape) * jnp.dtype(array.dtype).itemsize for array in arrays)
    return pltpu.CompilerParams(vmem_limit_bytes=total + 4 * MEBIBYTE)


def encode(values):
    largest = jnp.max(jnp.abs(values), axis=1, keepdims=True)
    logarithm = jnp.log2(jnp.maximum(largest, 2.0**-100))
    exponent = jnp.floor(logarithm * SCALE_STEPS) + 2.0
    scaled = values * (LARGEST * jnp.exp2(exponent * (-1.0 / SCALE_STEPS)))
    scaled = jnp.clip(scaled, -LARGEST, LARGEST)
    code = jnp.floor(scaled + 0.5).astype(jnp.int32)
    head = code[:, :LANES]
    lane = lax.broadcasted_iota(jnp.int32, head.shape, 1)
    stored = exponent.astype(jnp.int32) + SCALE_SHIFT
    stored = jnp.broadcast_to(stored, head.shape)
    bit = lax.shift_right_logical(stored, jnp.minimum(lane, SCALE_BITS)) & 1
    head = jnp.where(lane < SCALE_BITS, (head & -2) | bit, head)
    return head.astype(jnp.int16), code[:, LANES:].astype(jnp.int16)


def row_scale(head):
    head = head.astype(jnp.int32)
    lane = lax.broadcasted_iota(jnp.int32, head.shape, 1)
    bits = lax.shift_left(head & 1, jnp.minimum(lane, SCALE_BITS))
    bits = jnp.where(lane < SCALE_BITS, bits, 0).astype(jnp.float32)
    stored = jnp.broadcast_to(jnp.sum(bits, axis=1, keepdims=True), head.shape)
    return jnp.exp2((stored - SCALE_SHIFT) * (1.0 / SCALE_STEPS)) * (1.0 / LARGEST)


def cost(rows, tile):
    flops = 2 * rows * tile.shape[-2] * tile.shape[-1]
    return pl.CostEstimate(flops=flops, bytes_accessed=2 * tile.shape[-2] * tile.shape[-1], transcendentals=0)


def blk_steps(blk_count, core):
    near = blk_count - 2
    steps = [slot + 1 + core * (near - 1 - 2 * slot) for slot in range(near)]
    return [0] + steps + [blk_count - 1]


def chip_steps(chips):
    return [0] + list(reversed(range(1, chips)))


def start_all(copies):
    for copy in copies:
        copy.start()


def wait_all(copies):
    for copy in copies:
        copy.wait()


def pick_kernel(tile_cd, amplitudes, *rest):
    outgoing, sems = rest[:-1], rest[-1]
    blk, grp = lax.axis_index("blk"), lax.axis_index("grp")
    copies = []
    for slot, step in enumerate(blk_steps(len(outgoing), grp % CORES)):
        cd = tile_cd[jnp.bitwise_xor(blk, step), grp]
        copies.append(pltpu.make_async_copy(amplitudes.at[cd], outgoing[slot], sems.at[slot]))
    start_all(copies)
    wait_all(copies)


def pick(tile_cd, amplitudes):
    groups = tile_cd.shape[0]
    block = jax.ShapeDtypeStruct(amplitudes.shape[1:], amplitudes.dtype)
    return pl.pallas_call(
        pick_kernel,
        out_shape=[block] * groups,
        in_specs=[SMEM, ANY],
        out_specs=[VMEM] * groups,
        scratch_shapes=[pltpu.SemaphoreType.DMA((groups,))],
        compiler_params=vmem_limit(*[block] * groups),
        name="pick_cd_blocks",
    )(tile_cd, amplitudes)


def code_chips(product, outgoing, first):
    chip_rows = product.shape[0] // len(outgoing)
    chip = lax.axis_index("grp") // CORES
    for step, coded in zip(chip_steps(len(outgoing)), outgoing):
        source = pl.multiple_of(jnp.bitwise_xor(chip, step) * chip_rows, chip_rows)
        code, tail = encode(product[pl.ds(source, chip_rows), :])
        coded[first : first + chip_rows, :LANES] = code
        coded[first : first + chip_rows, LANES:] = tail


def chips_kernel(chips, before, passed, rows, tile, *rest):
    front, rest = rest[:before], rest[before:]
    handed, outgoing, product = rest[:passed], rest[-chips - passed - 1 : -1], rest[-1]
    for source, target in zip(handed, outgoing[chips:]):
        target[...] = source[...]
    product[...] = jnp.dot(rows[...], tile[...], preferred_element_type=jnp.float32)
    first = outgoing[0].shape[0] - product.shape[0] // chips
    for source, target in zip(front, outgoing):
        target[:first, :] = source[...]
    code_chips(product, outgoing[:chips], first)


def contract_for_chips(rows, tile, chips, front=(), passed=(), earlier=()):
    group_rows, tile_width = rows.shape[0], tile.shape[1]
    coded_rows = group_rows // chips + sum(array.shape[0] for array in front[:1])
    coded = jax.ShapeDtypeStruct((coded_rows, tile_width), jnp.int16)
    product = jax.ShapeDtypeStruct((group_rows, tile_width), jnp.float32)
    outputs = [coded] * chips + [jax.ShapeDtypeStruct(array.shape, array.dtype) for array in passed]
    inputs = [rows, tile, *front, *passed]
    return pl.pallas_call(
        lambda *refs: chips_kernel(chips, len(front), len(passed), *refs),
        out_shape=outputs,
        in_specs=[VMEM] * len(inputs) + [ANY] * len(earlier),
        out_specs=[VMEM] * len(outputs),
        scratch_shapes=[pltpu.VMEM(product.shape, product.dtype)],
        compiler_params=vmem_limit(*inputs, *outputs, product),
        cost_estimate=cost(group_rows, tile),
        name="contract_for_chips",
    )(*inputs, *earlier)


def one_kernel(chips, rows, tile, *rest):
    coded, product = rest[-2:]
    chip_rows = product.shape[0] // chips
    product[...] = jnp.dot(rows[...], tile[...], preferred_element_type=jnp.float32)
    code_chips(product, [coded.at[pl.ds(slot * chip_rows, chip_rows)] for slot in range(chips)], 0)


def contract_whole(rows, tile, chips, earlier):
    coded = jax.ShapeDtypeStruct((rows.shape[0], tile.shape[1]), jnp.int16)
    product = jax.ShapeDtypeStruct(coded.shape, jnp.float32)
    return pl.pallas_call(
        lambda *refs: one_kernel(chips, *refs),
        out_shape=coded,
        in_specs=[VMEM] * 2 + [ANY] * len(earlier),
        out_specs=VMEM,
        scratch_shapes=[pltpu.VMEM(product.shape, product.dtype)],
        compiler_params=vmem_limit(rows, tile, coded, product),
        cost_estimate=cost(rows.shape[0], tile),
        name="contract_far_group",
    )(rows, tile, *earlier)


def split_kernel(source, *targets):
    part_rows = targets[0].shape[0]
    for slot, target in enumerate(targets):
        target[...] = source[slot * part_rows : (slot + 1) * part_rows, :]


def split(source, parts):
    rows, tile_width = source.shape
    target = jax.ShapeDtypeStruct((rows // parts, tile_width), source.dtype)
    return pl.pallas_call(
        split_kernel,
        out_shape=[target] * parts,
        in_specs=[VMEM],
        out_specs=[VMEM] * parts,
        compiler_params=vmem_limit(source, source),
        name="split_by_chip",
    )(source)


def last_rows_kernel(count, *refs):
    sources, target = refs[:count], refs[-1]
    part_rows = target.shape[0] // count
    for slot, source in enumerate(sources):
        target[slot * part_rows : (slot + 1) * part_rows, :] = source[source.shape[0] - part_rows :, :]


def last_rows(sources, part_rows, earlier=()):
    target = jax.ShapeDtypeStruct((len(sources) * part_rows, sources[0].shape[1]), sources[0].dtype)
    return pl.pallas_call(
        lambda *refs: last_rows_kernel(len(sources), *refs),
        out_shape=target,
        in_specs=[VMEM] * len(sources) + [ANY] * len(earlier),
        out_specs=VMEM,
        compiler_params=vmem_limit(*sources, target),
        name="rows_of_one_group",
    )(*sources, *earlier)


def other_core_kernel(pieces, owner_rows, *refs):
    arrays, halves = refs[:-1], refs[-1]
    other = 1 - lax.axis_index("grp") % CORES
    for index, (array, first) in enumerate(pieces):
        source = pl.multiple_of(first + other * owner_rows, owner_rows)
        halves[index * owner_rows : (index + 1) * owner_rows, :] = arrays[array][pl.ds(source, owner_rows), :]


def other_core_rows(arrays, pieces, owner_rows):
    halves = jax.ShapeDtypeStruct((len(pieces) * owner_rows, arrays[0].shape[1]), arrays[0].dtype)
    return pl.pallas_call(
        lambda *refs: other_core_kernel(pieces, owner_rows, *refs),
        out_shape=halves,
        in_specs=[VMEM] * len(arrays),
        out_specs=VMEM,
        compiler_params=vmem_limit(*arrays, halves),
        name="rows_of_other_core",
    )(*arrays)


def add_rows(rows, tables, grp, held):
    tile_ab, tile_cd, pair_screen = tables
    terms = []
    for source, span, p, g in rows:
        kept = pair_screen[tile_cd[p, g], grp].astype(jnp.float32)
        terms.append((source, span, row_scale(source[span, :LANES]) * kept, tile_ab[p, g]))
    for source, span, scale, ab in terms:
        for lane in range(0, held.shape[2], LANES):
            term = source[span, lane : lane + LANES].astype(jnp.float32) * scale
            held[ab, :, lane : lane + LANES] = held[ab, :, lane : lane + LANES] + term


def tile_of(index, blk, grp, core, chips, blk_count):
    p = jnp.bitwise_xor(blk, blk_steps(blk_count, core)[index // chips])
    chip_step = chip_steps(chips)[index % chips]
    return p, (jnp.bitwise_xor(grp // CORES, chip_step)) * CORES + core


def write_kernel(parts, residual_in, *rest):
    residual, token, sems = rest[-3:]
    token[...] = jnp.zeros_like(token)
    ab_tiles = residual.shape[0]
    bounds = [ab_tiles * part // parts for part in range(parts + 1)]
    spans = [pl.ds(low, high - low) for low, high in zip(bounds[:-1], bounds[1:])]
    copies = [pltpu.make_async_copy(residual_in.at[span], residual.at[span], sems.at[i]) for i, span in enumerate(spans)]
    start_all(copies)
    wait_all(copies)


def write_residual(residual_in, earlier):
    parts = 5
    token = jax.ShapeDtypeStruct((8, LANES), jnp.int32)
    return pl.pallas_call(
        lambda *refs: write_kernel(parts, *refs),
        out_shape=[jax.ShapeDtypeStruct(residual_in.shape, residual_in.dtype), token],
        in_specs=[VMEM] + [ANY] * len(earlier),
        out_specs=[ANY, VMEM],
        scratch_shapes=[pltpu.SemaphoreType.DMA((parts,))],
        compiler_params=vmem_limit(residual_in),
        name="write_residual",
    )(residual_in, *earlier)


def add_and_write(rows, tables, grp, before, held, residual, touched, sems):
    def clear(ab, carry):
        touched[ab] = 0
        return carry

    lax.fori_loop(0, residual.shape[0], clear, 0)
    tile_ab = tables[0]
    fresh = []
    for _, _, p, g in rows:
        ab = tile_ab[p, g]
        fresh.append((ab, touched[ab] == 0))
        touched[ab] = 1
        if before is not None:
            held[ab] = before[ab]
    group = 8
    for start in range(0, len(rows), group):
        add_rows(rows[start : start + group], tables, grp, held)
    for action in ("start", "wait"):
        for index, (ab, first) in enumerate(fresh):
            copy = pltpu.make_async_copy(held.at[ab], residual.at[ab], sems.at[index])
            pl.when(first)(getattr(copy, action))


def add_here_kernel(pieces, *refs):
    tables, arrays, (residual_in, _, residual, held, touched, sems) = refs[:3], refs[3:-6], refs[-6:]
    blk, grp = lax.axis_index("blk"), lax.axis_index("grp")
    ab_tiles, owner_rows, _ = held.shape
    blk_count, chips = tables[0].shape[0], tables[0].shape[1] // CORES
    core = grp % CORES

    def hold(ab, carry):
        held[ab] = residual_in[ab]
        return carry

    lax.fori_loop(0, ab_tiles, hold, 0)
    rows = []
    for index, (array, first) in enumerate(pieces):
        span = pl.ds(pl.multiple_of(first + core * owner_rows, owner_rows), owner_rows)
        rows.append((arrays[array], span, *tile_of(index, blk, grp, core, chips, blk_count)))
    add_and_write(rows, tables, grp, None, held, residual, touched, sems)


def add_here(tables, arrays, pieces, residual_in, written):
    whole = jax.ShapeDtypeStruct(residual_in.shape, residual_in.dtype)
    return pl.pallas_call(
        lambda *refs: add_here_kernel(pieces, *refs),
        out_shape=[whole, whole],
        in_specs=[SMEM] * 3 + [VMEM] * (len(arrays) + 1) + [ANY],
        out_specs=[ANY, VMEM],
        scratch_shapes=[pltpu.SMEM(whole.shape[:1], jnp.int32), pltpu.SemaphoreType.DMA((len(pieces),))],
        input_output_aliases={3 + len(arrays) + 1: 0},
        compiler_params=vmem_limit(*arrays, residual_in, residual_in),
        name="add_contributions_here",
    )(*tables, *arrays, residual_in, written)


def add_there_kernel(*refs):
    tables, (swapped, partial, _, residual, held, touched, sems) = refs[:3], refs[3:]
    blk, grp = lax.axis_index("blk"), lax.axis_index("grp")
    owner_rows = residual.shape[1]
    blk_count, chips = tables[0].shape[0], tables[0].shape[1] // CORES
    core = 1 - grp % CORES
    rows = []
    for index in range(blk_count * chips):
        span = pl.ds(index * owner_rows, owner_rows)
        rows.append((swapped, span, *tile_of(index, blk, grp, core, chips, blk_count)))
    add_and_write(rows, tables, grp, partial, held, residual, touched, sems)


def add_there(tables, swapped, partial, written):
    whole, pieces = jax.ShapeDtypeStruct(partial.shape, partial.dtype), swapped.shape[0] // partial.shape[1]
    return pl.pallas_call(
        add_there_kernel,
        out_shape=whole,
        in_specs=[SMEM] * 3 + [VMEM] * 2 + [ANY],
        out_specs=ANY,
        scratch_shapes=[
            pltpu.VMEM(whole.shape, whole.dtype),
            pltpu.SMEM(whole.shape[:1], jnp.int32),
            pltpu.SemaphoreType.DMA((pieces,)),
        ],
        input_output_aliases={5: 0},
        compiler_params=vmem_limit(swapped, partial, partial),
        name="add_contributions_there",
    )(*tables, swapped, partial, written)


def shards(amplitudes, pair_screen, integrals, tile_ab, tile_cd, residual_in):
    blk_count = lax.axis_size("blk")
    grp_count = lax.axis_size("grp")
    chips = grp_count // CORES
    owner_rows = residual_in.shape[0]
    far = blk_count - 1

    def swap(value, slot, chip_step, core_step=0):
        pairs = []
        for device in range(blk_count * grp_count):
            blk_step = blk_steps(blk_count, device % CORES)[slot]
            pairs.append((device, device ^ (blk_step * grp_count + chip_step * CORES + core_step)))
        return lax.ppermute(value, ("blk", "grp"), pairs)

    def along_chips(outgoing):
        steps = chip_steps(chips)
        return [outgoing[0]] + [swap(outgoing[slot], 0, steps[slot]) for slot in range(1, chips)]

    chip_rows = CORES * owner_rows
    tile = integrals[0]
    own_rows, *near_picked, far_picked = pick(tile_cd, amplitudes)
    near_rows = [swap(rows, index + 1, 0) for index, rows in enumerate(near_picked)]
    *own_out, far_picked = contract_for_chips(own_rows, tile, chips, passed=[far_picked])
    far_rows = swap(far_picked, far, 0)
    by_tile = jnp.transpose(residual_in, (1, 0, 2))
    back_in = []
    near_in, front = [], own_out
    for rows in near_rows:
        near_in.append(along_chips(contract_for_chips(rows, tile, chips, front=front)))
        front = []
    far_coded = contract_whole(far_rows, tile, chips, [])
    written, token = write_residual(by_tile, [far_coded])
    for index, arrived in enumerate(near_in):
        back = last_rows(arrived, chip_rows, [token] if index else [])
        back_in.append(swap(back, index + 1, 0))
    far_in = along_chips(split(swap(far_coded, far, 0), chips))
    pieces = [(slot, 0) for slot in range(chips)]
    arrays = [*near_in[0], *back_in, *far_in]
    pieces += [(chips + group, slot * chip_rows) for group in range(len(back_in)) for slot in range(chips)]
    pieces += [(chips + len(back_in) + slot, 0) for slot in range(chips)]
    swapped = swap(other_core_rows(arrays, pieces, owner_rows), 0, 0, 1)
    tables = (tile_ab, tile_cd, pair_screen)
    written, partial = add_here(tables, arrays, pieces, by_tile, written)
    return jnp.transpose(add_there(tables, swapped, partial, written), (1, 0, 2))


def solution(mesh):
    in_specs = (
        P(None, "blk", None),
        P(None, "blk"),
        P(("blk", "grp"), None, None),
        P(),
        P(),
        P(("blk", "grp"), None, None),
    )
    out_specs = P(("blk", "grp"), None, None)
    return jax.shard_map(shards, mesh=mesh, in_specs=in_specs, out_specs=out_specs, check_vma=False)
```

time: 47.3 us -> 54.1 us (1.14)
  waiting for transfers between devices: 12.4 us -> 16.9 us
  local copies, waits for them, and re-layouts: 2.28 us -> 3.52 us
  Pallas kernels: 9.19 us -> 10 us
    ppermute x16, waiting for transfers between devices: 12.4 us -> 16.9 us  [swap(): return lax.ppermute(value, ('blk', 'grp'), pairs)]
    pallas_call x7 -> x10, Pallas kernels: 7.33 us -> 9.31 us  [the longest x1 2.55 us: add_here(): pl.pallas_call(lambda *refs: add_here_kernel(pieces, *refs), out_shape=[w...]
    unnamed x10 -> x16, local copies, waits for them, and re-layouts: 2.28 us -> 3.52 us
    pallas_call x1, Pallas kernels: 1.8 us -> 0.7 us  [pick(): pl.pallas_call(pick_kernel, out_shape=[block] * groups, in_specs=[SMEM, A...]
  transfers between devices with their start and end apart: 16 -> 16, of which waited for: 6 -> 6; matrix products, arithmetic and copies ran while one was open for 0% -> 0% of each run, Pallas kernels for 8% -> 13%
where the time goes in v12:
time: 54.1 us; the launch traced here: 53.9 us
  starting transfers between devices  23.2 us (43%)
  waiting for transfers between devices  16.9 us (31%)
  Pallas kernels  10 us (18%)
  local copies, waits for them, and re-layouts  3.52 us (7%)
    ppermute x16, starting transfers between devices, swap(): return lax.ppermute(value, ('blk', 'grp'), pairs)  23.2 us
    ppermute x16, waiting for transfers between devices, swap(): return lax.ppermute(value, ('blk', 'grp'), pairs)  16.9 us
    unnamed x16, local copies, waits for them, and re-layouts  3.52 us
    pallas_call x1, Pallas kernels, add_here(): pl.pallas_call(lambda *refs: add_here_kernel(pieces, *refs), out_shape=[w...  2.55 us
    pallas_call x1, Pallas kernels, add_there(): pl.pallas_call(add_there_kernel, out_shape=whole, in_specs=[SMEM] * 3 + [...  2.17 us
    pallas_call x3, Pallas kernels, contract_for_chips(): pl.pallas_call(lambda *refs: chips_kernel(chips, len(front), len(passed),...  2.1 us
    pallas_call x1, Pallas kernels, write_residual(): pl.pallas_call(lambda *refs: write_kernel(parts, *refs), out_shape=[jax.S...  1.75 us
  transfers between devices with their start and end apart: 16, of which 6 were waited for; matrix products, arithmetic and copies ran while one was open for 0% of the time, Pallas kernels for 13%

profile of v12, /device:TPU:0, one launch (start us, length us, event | category | flops | bytes accessed | tf_op | source)
XLA Modules:
  0.0 53.9 jit_solution(4223153204193642432)
XLA Ops:
  0.0 0.0 copy-start.3
  0.0 1.2 %copy-done.3 = bf16[4,128,1024]{2,1,0:T(8,128)(2,1)S(1)} copy-done((bf16[4,128,1024]{2,1,0:T(8,128)(2,1)S(1)}, bf16[4,128,1024]{2,1,0:T(8,128)(2,1)}, u32[]{:S(2)}) %copy-start.3) | copy-done | bytes 1048600
  1.2 0.0 copy-start.4
  1.2 0.7 %copy-done.4 = s32[4,8]{1,0:T(4,128)S(1)} copy-done((s32[4,8]{1,0:T(4,128)S(1)}, s32[4,8]{1,0:T(4,128)}, u32[]{:S(2)}) %copy-start.4) | copy-done | bytes 152
  1.9 0.7 %pick_cd_blocks.1 = (bf16[128,1024]{1,0:T(8,128)(2,1)S(1)}, bf16[128,1024]{1,0:T(8,128)(2,1)S(1)}, bf16[128,1024]{1,0:T(8,128)(2,1)S(1)}, bf16[128,1024]{1,0:T(8,128)(2,1)S(1)}) custom-call(s32[4,8]{1,0:T(4,128)S(1)} %copy-done.4, bf16[4,128,1024]{2,1,0:T(8,128)(2,1)S(1)} %copy-done.3), custom_call_target="tpu_custom_call" | custom-call | tf_op jit(solution)/shard_map/pick_cd_blocks/pallas_call | solution.py:91
  2.6 3.0 %collective-permute-start.5 = (bf16[128,1024]{1,0:T(8,128)(2,1)S(1)}, bf16[128,1024]{1,0:T(8,128)(2,1)S(1)}, u32[]{:S(2)}, u32[]{:S(2)}) collective-permute-start(bf16[128,1024]{1,0:T(8,128)(2,1)S(1)} %get-tuple-element.41), channel_id=1, source_target_pairs={{0,16},{1,9},{2,18},{3,11},{4,20},{5,13},{6,22},{7,15},{8,24},{9,1... | collective-permute-start | bytes 786440 | tf_op jit(solution)/shard_map/ppermute | solution.py:365
  5.6 1.5 %collective-permute-start = (bf16[128,1024]{1,0:T(8,128)(2,1)S(1)}, bf16[128,1024]{1,0:T(8,128)(2,1)S(1)}, u32[]{:S(2)}, u32[]{:S(2)}) collective-permute-start(bf16[128,1024]{1,0:T(8,128)(2,1)S(1)} %get-tuple-element.30), channel_id=1, source_target_pairs={{0,8},{1,17},{2,10},{3,19},{4,12},{5,21},{6,14},{7,23},{8,0},{9,25... | collective-permute-start | bytes 786440 | tf_op jit(solution)/shard_map/ppermute | solution.py:365
  7.1 0.0 copy-start
  7.1 1.6 %copy-done = bf16[1,1024,1024]{2,1,0:T(8,128)(2,1)S(1)} copy-done((bf16[1,1024,1024]{2,1,0:T(8,128)(2,1)S(1)}, bf16[1,1024,1024]{2,1,0:T(8,128)(2,1)}, u32[]{:S(2)}) %copy-start) | copy-done | bytes 2097176
  8.7 0.0 copy-start.1
  8.7 0.7 %contract_for_chips.3 = (s16[32,1024]{1,0:T(8,128)(2,1)S(1)}, s16[32,1024]{1,0:T(8,128)(2,1)S(1)}, s16[32,1024]{1,0:T(8,128)(2,1)S(1)}, s16[32,1024]{1,0:T(8,128)(2,1)S(1)}, bf16[128,1024]{1,0:T(8,128)(2,1)S(1)}) custom-call(bf16[128,1024]{1,0:T(8,128)(2,1)S(1)} %get-tuple-element.31.refs_0_, bf16[1024,1024]{1,0:T(8,128)(2,1)S(1)} %bitcast.3, ...), custom_call_target="tpu_custom_call" | custom-call | flops 268435456 | bytes 2097152 | tf_op jit(solution)/shard_map/contract_for_chips/pallas_call | solution.py:131
  9.4 0.0 copy-start.2
  9.5 0.1 collective-permute-start.9
  9.6 8.3 %collective-permute-done.5.refs_0_ = bf16[128,1024]{1,0:T(8,128)(2,1)S(1)} collective-permute-done((bf16[128,1024]{1,0:T(8,128)(2,1)S(1)}, bf16[128,1024]{1,0:T(8,128)(2,1)S(1)}, u32[]{:S(2)}, u32[]{:S(2)}) %collective-permute-start.5) | collective-permute-done | bytes 262176 | tf_op jit(solution)/shard_map/ppermute | solution.py:365
  17.9 0.0 copy-done.1
  17.9 0.7 %contract_for_chips.5 = (s16[32,1024]{1,0:T(8,128)(2,1)S(1)}, s16[32,1024]{1,0:T(8,128)(2,1)S(1)}, s16[32,1024]{1,0:T(8,128)(2,1)S(1)}, s16[32,1024]{1,0:T(8,128)(2,1)S(1)}) custom-call(bf16[128,1024]{1,0:T(8,128)(2,1)S(1)} %collective-permute-done.5.refs_0_, bf16[1024,1024]{1,0:T(8,128)(2,1)S(1)} %bitcast.4), custom_call_target="tpu_custom_call" | custom-call | flops 268435456 | bytes 2097152 | tf_op jit(solution)/shard_map/contract_for_chips/pallas_call | solution.py:131
  18.6 3.7 %collective-permute-start.6 = (s16[32,1024]{1,0:T(8,128)(2,1)S(1)}, s16[32,1024]{1,0:T(8,128)(2,1)S(1)}, u32[]{:S(2)}, u32[]{:S(2)}) collective-permute-start(s16[32,1024]{1,0:T(8,128)(2,1)S(1)} %get-tuple-element.43), channel_id=1, source_target_pairs={{0,6},{1,7},{2,4},{3,5},{4,2},{5,3},{6,0},{7,1},{8,14},{9,15},{10,... | collective-permute-start | bytes 196616 | tf_op jit(solution)/shard_map/ppermute | solution.py:365
  22.3 0.0 collective-permute-start.7
  22.3 0.0 collective-permute-done.refs_0_
  22.3 0.7 %contract_for_chips.4 = (s16[64,1024]{1,0:T(8,128)(2,1)S(1)}, s16[64,1024]{1,0:T(8,128)(2,1)S(1)}, s16[64,1024]{1,0:T(8,128)(2,1)S(1)}, s16[64,1024]{1,0:T(8,128)(2,1)S(1)}) custom-call(bf16[128,1024]{1,0:T(8,128)(2,1)S(1)} %collective-permute-done.refs_0_, bf16[1024,1024]{1,0:T(8,128)(2,1)S(1)} %bitcast.5, s16[32,1024]{1,0:T(8,128)(2,1)S(1)} %get-tuple-element.33.refs_2_, ...), custom_call_target="tpu_custom_call" | custom-call | flops 268435456 | bytes 2097152 | tf_op jit(solution)/shard_map/contract_for_chips/pallas_call | solution.py:131
  23.0 2.0 %collective-permute-start.1 = (s16[64,1024]{1,0:T(8,128)(2,1)S(1)}, s16[64,1024]{1,0:T(8,128)(2,1)S(1)}, u32[]{:S(2)}, u32[]{:S(2)}) collective-permute-start(s16[64,1024]{1,0:T(8,128)(2,1)S(1)} %get-tuple-element.38), channel_id=1, source_target_pairs={{0,6},{1,7},{2,4},{3,5},{4,2},{5,3},{6,0},{7,1},{8,14},{9,15},{10,... | collective-permute-start | bytes 393224 | tf_op jit(solution)/shard_map/ppermute | solution.py:365
  24.9 1.1 %collective-permute-start.2 = (s16[64,1024]{1,0:T(8,128)(2,1)S(1)}, s16[64,1024]{1,0:T(8,128)(2,1)S(1)}, u32[]{:S(2)}, u32[]{:S(2)}) collective-permute-start(s16[64,1024]{1,0:T(8,128)(2,1)S(1)} %get-tuple-element.39), channel_id=1, source_target_pairs={{0,4},{1,5},{2,6},{3,7},{4,0},{5,1},{6,2},{7,3},{8,12},{9,13},{10,... | collective-permute-start | bytes 393224 | tf_op jit(solution)/shard_map/ppermute | solution.py:365
  26.0 0.0 collective-permute-done.9.refs_0_
  26.0 1.4 %collective-permute-start.3 = (s16[64,1024]{1,0:T(8,128)(2,1)S(1)}, s16[64,1024]{1,0:T(8,128)(2,1)S(1)}, u32[]{:S(2)}, u32[]{:S(2)}) collective-permute-start(s16[64,1024]{1,0:T(8,128)(2,1)S(1)} %get-tuple-element.40), channel_id=1, source_target_pairs={{0,2},{1,3},{2,0},{3,1},{4,6},{5,7},{6,4},{7,5},{8,10},{9,11},{10,... | collective-permute-start | bytes 393224 | tf_op jit(solution)/shard_map/ppermute | solution.py:365
  27.4 0.7 %contract_far_group.1.refs_1_ = s16[128,1024]{1,0:T(8,128)(2,1)S(1)} custom-call(bf16[128,1024]{1,0:T(8,128)(2,1)S(1)} %collective-permute-done.9.refs_0_, bf16[1024,1024]{1,0:T(8,128)(2,1)S(1)} %bitcast.6), custom_call_target="tpu_custom_call" | custom-call | flops 268435456 | bytes 2097152 | tf_op jit(solution)/shard_map/contract_far_group/pallas_call | solution.py:153
  28.1 0.0 collective-permute-done.6.refs_1_
  28.1 1.6 %collective-permute-start.8 = (s16[32,1024]{1,0:T(8,128)(2,1)S(1)}, s16[32,1024]{1,0:T(8,128)(2,1)S(1)}, u32[]{:S(2)}, u32[]{:S(2)}) collective-permute-start(s16[32,1024]{1,0:T(8,128)(2,1)S(1)} %get-tuple-element.45), channel_id=1, source_target_pairs={{0,2},{1,3},{2,0},{3,1},{4,6},{5,7},{6,4},{7,5},{8,10},{9,11},{10,... | collective-permute-start | bytes 196616 | tf_op jit(solution)/shard_map/ppermute | solution.py:365
  29.7 2.2 %collective-permute-done.7.refs_2_ = s16[32,1024]{1,0:T(8,128)(2,1)S(1)} collective-permute-done((s16[32,1024]{1,0:T(8,128)(2,1)S(1)}, s16[32,1024]{1,0:T(8,128)(2,1)S(1)}, u32[]{:S(2)}, u32[]{:S(2)}) %collective-permute-start.7) | collective-permute-done | bytes 65568 | tf_op jit(solution)/shard_map/ppermute | solution.py:365
  31.9 0.0 collective-permute-start.11
  32.0 0.0 copy-done.2
  32.0 0.0 copy-start.5
  32.0 0.0 copy-start.6
  32.0 0.0 copy-start.7
  32.0 1.7 %write_residual.1 = (f32[50,16,1024]{2,1,0:T(8,128)}, s32[8,128]{1,0:T(8,128)S(1)}) custom-call(f32[50,16,1024]{2,1,0:T(8,128)S(1)} %bitcast.7, s16[128,1024]{1,0:T(8,128)(2,1)S(1)} %contract_far_group.1.refs_1_), custom_call_target="tpu_custom_call" | custom-call | tf_op jit(solution)/shard_map/write_residual/pallas_call | solution.py:255
  33.7 0.9 %collective-permute-done.8.refs_3_ = s16[32,1024]{1,0:T(8,128)(2,1)S(1)} collective-permute-done((s16[32,1024]{1,0:T(8,128)(2,1)S(1)}, s16[32,1024]{1,0:T(8,128)(2,1)S(1)}, u32[]{:S(2)}, u32[]{:S(2)}) %collective-permute-start.8) | collective-permute-done | bytes 65568 | tf_op jit(solution)/shard_map/ppermute | solution.py:365
  34.6 2.9 %collective-permute-start.10 = (s16[128,1024]{1,0:T(8,128)(2,1)S(1)}, s16[128,1024]{1,0:T(8,128)(2,1)S(1)}, u32[]{:S(2)}, u32[]{:S(2)}) collective-permute-start(s16[128,1024]{1,0:T(8,128)(2,1)S(1)} %rows_of_one_group.3), channel_id=1, source_target_pairs={{0,16},{1,9},{2,18},{3,11},{4,20},{5,13},{6,22},{7,15},{8,24},{9,1... | collective-permute-start | bytes 786440 | tf_op jit(solution)/shard_map/ppermute | solution.py:365
  37.5 0.0 collective-permute-done.1.refs_1_.refs_4_
  37.5 0.0 collective-permute-done.2.refs_2_.refs_5_
  37.5 0.0 collective-permute-done.3.refs_3_.refs_6_
  37.5 1.5 %collective-permute-start.4 = (s16[128,1024]{1,0:T(8,128)(2,1)S(1)}, s16[128,1024]{1,0:T(8,128)(2,1)S(1)}, u32[]{:S(2)}, u32[]{:S(2)}) collective-permute-start(s16[128,1024]{1,0:T(8,128)(2,1)S(1)} %rows_of_one_group.2), channel_id=1, source_target_pairs={{0,8},{1,17},{2,10},{3,19},{4,12},{5,21},{6,14},{7,23},{8,0},{9,25... | collective-permute-start | bytes 786440 | tf_op jit(solution)/shard_map/ppermute | solution.py:365
  39.1 2.9 %collective-permute-done.11.source = s16[128,1024]{1,0:T(8,128)(2,1)S(1)} collective-permute-done((s16[128,1024]{1,0:T(8,128)(2,1)S(1)}, s16[128,1024]{1,0:T(8,128)(2,1)S(1)}, u32[]{:S(2)}, u32[]{:S(2)}) %collective-permute-start.11) | collective-permute-done | bytes 262176 | tf_op jit(solution)/shard_map/ppermute | solution.py:365
  42.0 0.4 collective-permute-start.12
  42.4 0.0 collective-permute-start.13
  42.4 4.1 %collective-permute-start.14 = (s16[32,1024]{1,0:T(8,128)(2,1)S(1)}, s16[32,1024]{1,0:T(8,128)(2,1)S(1)}, u32[]{:S(2)}, u32[]{:S(2)}) collective-permute-start(s16[32,1024]{1,0:T(8,128)(2,1)S(1)} %get-tuple-element.51), channel_id=1, source_target_pairs={{0,2},{1,3},{2,0},{3,1},{4,6},{5,7},{6,4},{7,5},{8,10},{9,11},{10,... | collective-permute-start | bytes 196616 | tf_op jit(solution)/shard_map/ppermute | solution.py:365
  46.5 0.0 collective-permute-done.10.refs_5_.refs_8_
  46.5 1.8 %collective-permute-done.12.refs_7_.refs_10_ = s16[32,1024]{1,0:T(8,128)(2,1)S(1)} collective-permute-done((s16[32,1024]{1,0:T(8,128)(2,1)S(1)}, s16[32,1024]{1,0:T(8,128)(2,1)S(1)}, u32[]{:S(2)}, u32[]{:S(2)}) %collective-permute-start.12) | collective-permute-done | bytes 65568 | tf_op jit(solution)/shard_map/ppermute | solution.py:365
  48.3 0.7 %collective-permute-done.13.refs_8_.refs_11_ = s16[32,1024]{1,0:T(8,128)(2,1)S(1)} collective-permute-done((s16[32,1024]{1,0:T(8,128)(2,1)S(1)}, s16[32,1024]{1,0:T(8,128)(2,1)S(1)}, u32[]{:S(2)}, u32[]{:S(2)}) %collective-permute-start.13) | collective-permute-done | bytes 65568 | tf_op jit(solution)/shard_map/ppermute | solution.py:365
  49.0 0.0 collective-permute-done.14.refs_9_.refs_12_
  49.0 0.0 collective-permute-done.4.refs_4_.refs_7_
  49.0 0.1 collective-permute-start.15
  49.1 0.0 copy-done.5
  49.1 0.0 copy-done.6
  49.1 0.0 copy-done.7
  49.1 2.5 %add_contributions_here.1 = (f32[50,16,1024]{2,1,0:T(8,128)}, f32[50,16,1024]{2,1,0:T(8,128)S(1)}) custom-call(s32[4,8]{1,0:T(4,128)S(1)} %copy-done.6, s32[4,8]{1,0:T(4,128)S(1)} %copy-done.5, s32[4,8]{1,0:T(4,128)S(1)} %copy-done.7, s16[64,1024]{1,0:T(8,128)(2,1)S(1)} %get-tuple-element.37.refs_0_.refs_3_, ...), custom_call_target="tpu_custom_call", output_to_operand_aliasing={{0}: (14, {})} | custom-call | tf_op jit(solution)/shard_map/add_contributions_here/pallas_call | solution.py:310
  51.7 0.0 collective-permute-done.15.refs_3_
  51.7 2.2 %add_contributions_there.1 = f32[50,16,1024]{2,1,0:T(8,128)} custom-call(s32[4,8]{1,0:T(4,128)S(1)} %copy-done.6, s32[4,8]{1,0:T(4,128)S(1)} %copy-done.5, s32[4,8]{1,0:T(4,128)S(1)} %copy-done.7, s16[256,1024]{1,0:T(8,128)(2,1)S(1)} %collective-permute-done.15.refs_3_, ...), custom_call_target="tpu_custom_call", output_to_operand_aliasing={{}: (5, {})} | custom-call | tf_op jit(solution)/shard_map/add_contributions_there/pallas_call | solution.py:337
  (4 shorter events, 0.1 us)
Async XLA Ops:
  0.0 1.2 %copy-start.3 = (bf16[4,128,1024]{2,1,0:T(8,128)(2,1)S(1)}, bf16[4,128,1024]{2,1,0:T(8,128)(2,1)}, u32[]{:S(2)}) copy-start(bf16[4,128,1024]{2,1,0:T(8,128)(2,1)} %amplitudes.1) | copy-start | bytes 3145732
  1.2 0.7 %copy-start.4 = (s32[4,8]{1,0:T(4,128)S(1)}, s32[4,8]{1,0:T(4,128)}, u32[]{:S(2)}) copy-start(s32[4,8]{1,0:T(4,128)} %refs_1_.3) | copy-start | bytes 388
  2.6 15.3 %collective-permute-start.5 = (bf16[128,1024]{1,0:T(8,128)(2,1)S(1)}, bf16[128,1024]{1,0:T(8,128)(2,1)S(1)}, u32[]{:S(2)}, u32[]{:S(2)}) collective-permute-start(bf16[128,1024]{1,0:T(8,128)(2,1)S(1)} %get-tuple-element.41), channel_id=1, source_target_pairs={{0,16},{1,9},{2,18},{3,11},{4,20},{5,13},{6,22},{7,15},{8,24},{9,1... | collective-permute-start | bytes 786440 | tf_op jit(solution)/shard_map/ppermute | solution.py:365
  5.6 16.6 %collective-permute-start = (bf16[128,1024]{1,0:T(8,128)(2,1)S(1)}, bf16[128,1024]{1,0:T(8,128)(2,1)S(1)}, u32[]{:S(2)}, u32[]{:S(2)}) collective-permute-start(bf16[128,1024]{1,0:T(8,128)(2,1)S(1)} %get-tuple-element.30), channel_id=1, source_target_pairs={{0,8},{1,17},{2,10},{3,19},{4,12},{5,21},{6,14},{7,23},{8,0},{9,25... | collective-permute-start | bytes 786440 | tf_op jit(solution)/shard_map/ppermute | solution.py:365
  7.1 1.6 %copy-start = (bf16[1,1024,1024]{2,1,0:T(8,128)(2,1)S(1)}, bf16[1,1024,1024]{2,1,0:T(8,128)(2,1)}, u32[]{:S(2)}) copy-start(bf16[1,1024,1024]{2,1,0:T(8,128)(2,1)} %param.8) | copy-start | bytes 6291460
  8.7 9.2 %copy-start.1 = (bf16[1,1024,1024]{2,1,0:T(8,128)(2,1)S(1)}, bf16[1,1024,1024]{2,1,0:T(8,128)(2,1)}, u32[]{:S(2)}) copy-start(bf16[1,1024,1024]{2,1,0:T(8,128)(2,1)} %param.8) | copy-start | bytes 6291460
  9.4 22.5 %copy-start.2 = (f32[16,50,1024]{2,0,1:T(8,128)S(1)}, f32[16,50,1024]{2,0,1:T(8,128)}, u32[]{:S(2)}) copy-start(f32[16,50,1024]{2,0,1:T(8,128)} %param.11) | copy-start | bytes 9830404
  9.5 16.6 %collective-permute-start.9 = (bf16[128,1024]{1,0:T(8,128)(2,1)S(1)}, bf16[128,1024]{1,0:T(8,128)(2,1)S(1)}, u32[]{:S(2)}, u32[]{:S(2)}) collective-permute-start(bf16[128,1024]{1,0:T(8,128)(2,1)S(1)} %get-tuple-element.46), channel_id=1, source_target_pairs={{0,24},{1,25},{2,26},{3,27},{4,28},{5,29},{6,30},{7,31},{8,16},{9,... | collective-permute-start | bytes 786440 | tf_op jit(solution)/shard_map/ppermute | solution.py:365
  18.6 9.5 %collective-permute-start.6 = (s16[32,1024]{1,0:T(8,128)(2,1)S(1)}, s16[32,1024]{1,0:T(8,128)(2,1)S(1)}, u32[]{:S(2)}, u32[]{:S(2)}) collective-permute-start(s16[32,1024]{1,0:T(8,128)(2,1)S(1)} %get-tuple-element.43), channel_id=1, source_target_pairs={{0,6},{1,7},{2,4},{3,5},{4,2},{5,3},{6,0},{7,1},{8,14},{9,15},{10,... | collective-permute-start | bytes 196616 | tf_op jit(solution)/shard_map/ppermute | solution.py:365
  22.3 9.7 %collective-permute-start.7 = (s16[32,1024]{1,0:T(8,128)(2,1)S(1)}, s16[32,1024]{1,0:T(8,128)(2,1)S(1)}, u32[]{:S(2)}, u32[]{:S(2)}) collective-permute-start(s16[32,1024]{1,0:T(8,128)(2,1)S(1)} %get-tuple-element.44), channel_id=1, source_target_pairs={{0,4},{1,5},{2,6},{3,7},{4,0},{5,1},{6,2},{7,3},{8,12},{9,13},{10,... | collective-permute-start | bytes 196616 | tf_op jit(solution)/shard_map/ppermute | solution.py:365
  23.0 14.5 %collective-permute-start.1 = (s16[64,1024]{1,0:T(8,128)(2,1)S(1)}, s16[64,1024]{1,0:T(8,128)(2,1)S(1)}, u32[]{:S(2)}, u32[]{:S(2)}) collective-permute-start(s16[64,1024]{1,0:T(8,128)(2,1)S(1)} %get-tuple-element.38), channel_id=1, source_target_pairs={{0,6},{1,7},{2,4},{3,5},{4,2},{5,3},{6,0},{7,1},{8,14},{9,15},{10,... | collective-permute-start | bytes 393224 | tf_op jit(solution)/shard_map/ppermute | solution.py:365
  24.9 12.6 %collective-permute-start.2 = (s16[64,1024]{1,0:T(8,128)(2,1)S(1)}, s16[64,1024]{1,0:T(8,128)(2,1)S(1)}, u32[]{:S(2)}, u32[]{:S(2)}) collective-permute-start(s16[64,1024]{1,0:T(8,128)(2,1)S(1)} %get-tuple-element.39), channel_id=1, source_target_pairs={{0,4},{1,5},{2,6},{3,7},{4,0},{5,1},{6,2},{7,3},{8,12},{9,13},{10,... | collective-permute-start | bytes 393224 | tf_op jit(solution)/shard_map/ppermute | solution.py:365
  26.0 11.5 %collective-permute-start.3 = (s16[64,1024]{1,0:T(8,128)(2,1)S(1)}, s16[64,1024]{1,0:T(8,128)(2,1)S(1)}, u32[]{:S(2)}, u32[]{:S(2)}) collective-permute-start(s16[64,1024]{1,0:T(8,128)(2,1)S(1)} %get-tuple-element.40), channel_id=1, source_target_pairs={{0,2},{1,3},{2,0},{3,1},{4,6},{5,7},{6,4},{7,5},{8,10},{9,11},{10,... | collective-permute-start | bytes 393224 | tf_op jit(solution)/shard_map/ppermute | solution.py:365
  28.1 6.5 %collective-permute-start.8 = (s16[32,1024]{1,0:T(8,128)(2,1)S(1)}, s16[32,1024]{1,0:T(8,128)(2,1)S(1)}, u32[]{:S(2)}, u32[]{:S(2)}) collective-permute-start(s16[32,1024]{1,0:T(8,128)(2,1)S(1)} %get-tuple-element.45), channel_id=1, source_target_pairs={{0,2},{1,3},{2,0},{3,1},{4,6},{5,7},{6,4},{7,5},{8,10},{9,11},{10,... | collective-permute-start | bytes 196616 | tf_op jit(solution)/shard_map/ppermute | solution.py:365
  31.9 10.0 %collective-permute-start.11 = (s16[128,1024]{1,0:T(8,128)(2,1)S(1)}, s16[128,1024]{1,0:T(8,128)(2,1)S(1)}, u32[]{:S(2)}, u32[]{:S(2)}) collective-permute-start(s16[128,1024]{1,0:T(8,128)(2,1)S(1)} %contract_far_group.1.refs_1_), channel_id=1, source_target_pairs={{0,24},{1,25},{2,26},{3,27},{4,28},{5,29},{6,30},{7,31},{8,16},{9,... | collective-permute-start | bytes 786440 | tf_op jit(solution)/shard_map/ppermute | solution.py:365
  32.0 17.1 %copy-start.5 = (s32[4,8]{1,0:T(4,128)S(1)}, s32[4,8]{1,0:T(4,128)}, u32[]{:S(2)}) copy-start(s32[4,8]{1,0:T(4,128)} %refs_1_.3) | copy-start | bytes 388
  32.0 17.1 %copy-start.6 = (s32[4,8]{1,0:T(4,128)S(1)}, s32[4,8]{1,0:T(4,128)}, u32[]{:S(2)}) copy-start(s32[4,8]{1,0:T(4,128)} %refs_0_.3) | copy-start | bytes 388
  32.0 17.1 %copy-start.7 = (s32[4,8]{1,0:T(4,128)S(1)}, s32[4,8]{1,0:T(4,128)}, u32[]{:S(2)}) copy-start(s32[4,8]{1,0:T(4,128)} %refs_2_.3) | copy-start | bytes 388
  34.6 11.8 %collective-permute-start.10 = (s16[128,1024]{1,0:T(8,128)(2,1)S(1)}, s16[128,1024]{1,0:T(8,128)(2,1)S(1)}, u32[]{:S(2)}, u32[]{:S(2)}) collective-permute-start(s16[128,1024]{1,0:T(8,128)(2,1)S(1)} %rows_of_one_group.3), channel_id=1, source_target_pairs={{0,16},{1,9},{2,18},{3,11},{4,20},{5,13},{6,22},{7,15},{8,24},{9,1... | collective-permute-start | bytes 786440 | tf_op jit(solution)/shard_map/ppermute | solution.py:365
  37.5 11.4 %collective-permute-start.4 = (s16[128,1024]{1,0:T(8,128)(2,1)S(1)}, s16[128,1024]{1,0:T(8,128)(2,1)S(1)}, u32[]{:S(2)}, u32[]{:S(2)}) collective-permute-start(s16[128,1024]{1,0:T(8,128)(2,1)S(1)} %rows_of_one_group.2), channel_id=1, source_target_pairs={{0,8},{1,17},{2,10},{3,19},{4,12},{5,21},{6,14},{7,23},{8,0},{9,25... | collective-permute-start | bytes 786440 | tf_op jit(solution)/shard_map/ppermute | solution.py:365
  42.0 6.3 %collective-permute-start.12 = (s16[32,1024]{1,0:T(8,128)(2,1)S(1)}, s16[32,1024]{1,0:T(8,128)(2,1)S(1)}, u32[]{:S(2)}, u32[]{:S(2)}) collective-permute-start(s16[32,1024]{1,0:T(8,128)(2,1)S(1)} %get-tuple-element.49), channel_id=1, source_target_pairs={{0,6},{1,7},{2,4},{3,5},{4,2},{5,3},{6,0},{7,1},{8,14},{9,15},{10,... | collective-permute-start | bytes 196616 | tf_op jit(solution)/shard_map/ppermute | solution.py:365
  42.4 6.6 %collective-permute-start.13 = (s16[32,1024]{1,0:T(8,128)(2,1)S(1)}, s16[32,1024]{1,0:T(8,128)(2,1)S(1)}, u32[]{:S(2)}, u32[]{:S(2)}) collective-permute-start(s16[32,1024]{1,0:T(8,128)(2,1)S(1)} %get-tuple-element.50), channel_id=1, source_target_pairs={{0,4},{1,5},{2,6},{3,7},{4,0},{5,1},{6,2},{7,3},{8,12},{9,13},{10,... | collective-permute-start | bytes 196616 | tf_op jit(solution)/shard_map/ppermute | solution.py:365
  42.4 6.6 %collective-permute-start.14 = (s16[32,1024]{1,0:T(8,128)(2,1)S(1)}, s16[32,1024]{1,0:T(8,128)(2,1)S(1)}, u32[]{:S(2)}, u32[]{:S(2)}) collective-permute-start(s16[32,1024]{1,0:T(8,128)(2,1)S(1)} %get-tuple-element.51), channel_id=1, source_target_pairs={{0,2},{1,3},{2,0},{3,1},{4,6},{5,7},{6,4},{7,5},{8,10},{9,11},{10,... | collective-permute-start | bytes 196616 | tf_op jit(solution)/shard_map/ppermute | solution.py:365
  49.0 2.7 %collective-permute-start.15 = (s16[256,1024]{1,0:T(8,128)(2,1)S(1)}, s16[256,1024]{1,0:T(8,128)(2,1)S(1)}, u32[]{:S(2)}, u32[]{:S(2)}) collective-permute-start(s16[256,1024]{1,0:T(8,128)(2,1)S(1)} %rows_of_other_core.1), channel_id=1, source_target_pairs={{0,1},{1,0},{2,3},{3,2},{4,5},{5,4},{6,7},{7,6},{8,9},{9,8},{10,11... | collective-permute-start | bytes 1572872 | tf_op jit(solution)/shard_map/ppermute | solution.py:365

commit v13 on v12

--- a/solution.py
+++ b/solution.py
@@ -238,60 +238,15 @@
     return p, (jnp.bitwise_xor(grp // CORES, chip_step)) * CORES + core
 
 
-def write_kernel(parts, residual_in, *rest):
-    residual, token, sems = rest[-3:]
-    token[...] = jnp.zeros_like(token)
-    ab_tiles = residual.shape[0]
+def add_kernel(parts, pieces, *refs):
+    tables, arrays, (swapped, residual_in, residual, held, sems) = refs[:3], refs[3:-5], refs[-5:]
+    blk, grp = lax.axis_index("blk"), lax.axis_index("grp")
+    ab_tiles, owner_rows, _ = residual.shape
+    blk_count, chips = tables[0].shape[0], tables[0].shape[1] // CORES
+    core = grp % CORES
     bounds = [ab_tiles * part // parts for part in range(parts + 1)]
     spans = [pl.ds(low, high - low) for low, high in zip(bounds[:-1], bounds[1:])]
-    copies = [pltpu.make_async_copy(residual_in.at[span], residual.at[span], sems.at[i]) for i, span in enumerate(spans)]
-    start_all(copies)
-    wait_all(copies)
-
-
-def write_residual(residual_in, earlier):
-    parts = 5
-    token = jax.ShapeDtypeStruct((8, LANES), jnp.int32)
-    return pl.pallas_call(
-        lambda *refs: write_kernel(parts, *refs),
-        out_shape=[jax.ShapeDtypeStruct(residual_in.shape, residual_in.dtype), token],
-        in_specs=[VMEM] + [ANY] * len(earlier),
-        out_specs=[ANY, VMEM],
-        scratch_shapes=[pltpu.SemaphoreType.DMA((parts,))],
-        compiler_params=vmem_limit(residual_in),
-        name="write_residual",
-    )(residual_in, *earlier)
-
-
-def add_and_write(rows, tables, grp, before, held, residual, touched, sems):
-    def clear(ab, carry):
-        touched[ab] = 0
-        return carry
-
-    lax.fori_loop(0, residual.shape[0], clear, 0)
-    tile_ab = tables[0]
-    fresh = []
-    for _, _, p, g in rows:
-        ab = tile_ab[p, g]
-        fresh.append((ab, touched[ab] == 0))
-        touched[ab] = 1
-        if before is not None:
-            held[ab] = before[ab]
-    group = 8
-    for start in range(0, len(rows), group):
-        add_rows(rows[start : start + group], tables, grp, held)
-    for action in ("start", "wait"):
-        for index, (ab, first) in enumerate(fresh):
-            copy = pltpu.make_async_copy(held.at[ab], residual.at[ab], sems.at[index])
-            pl.when(first)(getattr(copy, action))
-
-
-def add_here_kernel(pieces, *refs):
-    tables, arrays, (residual_in, _, residual, held, touched, sems) = refs[:3], refs[3:-6], refs[-6:]
-    blk, grp = lax.axis_index("blk"), lax.axis_index("grp")
-    ab_tiles, owner_rows, _ = held.shape
-    blk_count, chips = tables[0].shape[0], tables[0].shape[1] // CORES
-    core = grp % CORES
+    leaves = [pltpu.make_async_copy(held.at[span], residual.at[span], sems.at[i]) for i, span in enumerate(spans)]
 
     def hold(ab, carry):
         held[ab] = residual_in[ab]
@@ -302,52 +257,26 @@
     for index, (array, first) in enumerate(pieces):
         span = pl.ds(pl.multiple_of(first + core * owner_rows, owner_rows), owner_rows)
         rows.append((arrays[array], span, *tile_of(index, blk, grp, core, chips, blk_count)))
-    add_and_write(rows, tables, grp, None, held, residual, touched, sems)
-
-
-def add_here(tables, arrays, pieces, residual_in, written):
-    whole = jax.ShapeDtypeStruct(residual_in.shape, residual_in.dtype)
-    return pl.pallas_call(
-        lambda *refs: add_here_kernel(pieces, *refs),
-        out_shape=[whole, whole],
-        in_specs=[SMEM] * 3 + [VMEM] * (len(arrays) + 1) + [ANY],
-        out_specs=[ANY, VMEM],
-        scratch_shapes=[pltpu.SMEM(whole.shape[:1], jnp.int32), pltpu.SemaphoreType.DMA((len(pieces),))],
-        input_output_aliases={3 + len(arrays) + 1: 0},
-        compiler_params=vmem_limit(*arrays, residual_in, residual_in),
-        name="add_contributions_here",
-    )(*tables, *arrays, residual_in, written)
-
-
-def add_there_kernel(*refs):
-    tables, (swapped, partial, _, residual, held, touched, sems) = refs[:3], refs[3:]
-    blk, grp = lax.axis_index("blk"), lax.axis_index("grp")
-    owner_rows = residual.shape[1]
-    blk_count, chips = tables[0].shape[0], tables[0].shape[1] // CORES
-    core = 1 - grp % CORES
-    rows = []
-    for index in range(blk_count * chips):
         span = pl.ds(index * owner_rows, owner_rows)
-        rows.append((swapped, span, *tile_of(index, blk, grp, core, chips, blk_count)))
-    add_and_write(rows, tables, grp, partial, held, residual, touched, sems)
-
-
-def add_there(tables, swapped, partial, written):
-    whole, pieces = jax.ShapeDtypeStruct(partial.shape, partial.dtype), swapped.shape[0] // partial.shape[1]
-    return pl.pallas_call(
-        add_there_kernel,
-        out_shape=whole,
-        in_specs=[SMEM] * 3 + [VMEM] * 2 + [ANY],
+        rows.append((swapped, span, *tile_of(index, blk, grp, 1 - core, chips, blk_count)))
+    group = 8
+    for start in range(0, len(rows), group):
+        add_rows(rows[start : start + group], tables, grp, held)
+    start_all(leaves)
+    wait_all(leaves)
+
+
+def add_blocks(tables, arrays, pieces, swapped, residual_in):
+    parts = 5
+    return pl.pallas_call(
+        lambda *refs: add_kernel(parts, pieces, *refs),
+        out_shape=jax.ShapeDtypeStruct(residual_in.shape, residual_in.dtype),
+        in_specs=[SMEM] * 3 + [VMEM] * (len(arrays) + 2),
         out_specs=ANY,
-        scratch_shapes=[
-            pltpu.VMEM(whole.shape, whole.dtype),
-            pltpu.SMEM(whole.shape[:1], jnp.int32),
-            pltpu.SemaphoreType.DMA((pieces,)),
-        ],
-        input_output_aliases={5: 0},
-        compiler_params=vmem_limit(swapped, partial, partial),
-        name="add_contributions_there",
-    )(*tables, swapped, partial, written)
+        scratch_shapes=[pltpu.VMEM(residual_in.shape, residual_in.dtype), pltpu.SemaphoreType.DMA((parts,))],
+        compiler_params=vmem_limit(*arrays, swapped, residual_in, residual_in),
+        name="add_contributions",
+    )(*tables, *arrays, swapped, residual_in)
 
 
 def shards(amplitudes, pair_screen, integrals, tile_ab, tile_cd, residual_in):
@@ -374,26 +303,23 @@
     near_rows = [swap(rows, index + 1, 0) for index, rows in enumerate(near_picked)]
     *own_out, far_picked = contract_for_chips(own_rows, tile, chips, passed=[far_picked])
     far_rows = swap(far_picked, far, 0)
-    by_tile = jnp.transpose(residual_in, (1, 0, 2))
+    near_in = []
+    for index, rows in enumerate(near_rows):
+        front = own_out if index == len(near_rows) - 1 else []
+        near_in.append(along_chips(contract_for_chips(rows, tile, chips, front=front)))
+    far_in = along_chips(split(swap(contract_whole(far_rows, tile, chips, []), far, 0), chips))
     back_in = []
-    near_in, front = [], own_out
-    for rows in near_rows:
-        near_in.append(along_chips(contract_for_chips(rows, tile, chips, front=front)))
-        front = []
-    far_coded = contract_whole(far_rows, tile, chips, [])
-    written, token = write_residual(by_tile, [far_coded])
     for index, arrived in enumerate(near_in):
-        back = last_rows(arrived, chip_rows, [token] if index else [])
-        back_in.append(swap(back, index + 1, 0))
-    far_in = along_chips(split(swap(far_coded, far, 0), chips))
+        earlier = [] if index == len(near_in) - 1 else []
+        back_in.append(swap(last_rows(arrived, chip_rows, earlier), index + 1, 0))
+    arrays = [*near_in[-1], *back_in, *far_in]
     pieces = [(slot, 0) for slot in range(chips)]
-    arrays = [*near_in[0], *back_in, *far_in]
     pieces += [(chips + group, slot * chip_rows) for group in range(len(back_in)) for slot in range(chips)]
     pieces += [(chips + len(back_in) + slot, 0) for slot in range(chips)]
     swapped = swap(other_core_rows(arrays, pieces, owner_rows), 0, 0, 1)
-    tables = (tile_ab, tile_cd, pair_screen)
-    written, partial = add_here(tables, arrays, pieces, by_tile, written)
-    return jnp.transpose(add_there(tables, swapped, partial, written), (1, 0, 2))
+    by_tile = jnp.transpose(residual_in, (1, 0, 2))
+    added = add_blocks((tile_ab, tile_cd, pair_screen), arrays, pieces, swapped, by_tile)
+    return jnp.transpose(added, (1, 0, 2))
 
 
 def solution(mesh):

time: 54.1 us -> 48.9 us (0.904)
  Pallas kernels: 10 us -> 6.72 us
  waiting for transfers between devices: 16.9 us -> 14.9 us
    pallas_call x3 -> x1, Pallas kernels: 6.46 us -> 3.12 us  [add_blocks(): pl.pallas_call(lambda *refs: add_kernel(parts, pieces, *refs), out_shape=...]
    ppermute x16, waiting for transfers between devices: 16.9 us -> 14.9 us  [swap(): return lax.ppermute(value, ('blk', 'grp'), pairs)]
  transfers between devices with their start and end apart: 16 -> 16, of which waited for: 6 -> 7; matrix products, arithmetic and copies ran while one was open for 0% -> 0% of each run, Pallas kernels for 13% -> 6%
where the time goes in v13:
time: 48.9 us; the launch traced here: 48.7 us
  starting transfers between devices  23.5 us (48%)
  waiting for transfers between devices  14.9 us (30%)
  Pallas kernels  6.72 us (14%)
  local copies, waits for them, and re-layouts  3.52 us (7%)
    ppermute x16, starting transfers between devices, swap(): return lax.ppermute(value, ('blk', 'grp'), pairs)  23.5 us
    ppermute x16, waiting for transfers between devices, swap(): return lax.ppermute(value, ('blk', 'grp'), pairs)  14.9 us
    unnamed x16, local copies, waits for them, and re-layouts  3.52 us
    pallas_call x1, Pallas kernels, add_blocks(): pl.pallas_call(lambda *refs: add_kernel(parts, pieces, *refs), out_shape=...  3.12 us
    pallas_call x3, Pallas kernels, contract_for_chips(): pl.pallas_call(lambda *refs: chips_kernel(chips, len(front), len(passed),...  2.1 us
  transfers between devices with their start and end apart: 16, of which 7 were waited for; matrix products, arithmetic and copies ran while one was open for 0% of the time, Pallas kernels for 6%

profile of v13, /device:TPU:0, one launch (start us, length us, event | category | flops | bytes accessed | tf_op | source)
XLA Modules:
  0.0 48.7 jit_solution(7429994597757612716)
XLA Ops:
  0.0 0.0 copy-start.3
  0.0 1.2 %copy-done.3 = bf16[4,128,1024]{2,1,0:T(8,128)(2,1)S(1)} copy-done((bf16[4,128,1024]{2,1,0:T(8,128)(2,1)S(1)}, bf16[4,128,1024]{2,1,0:T(8,128)(2,1)}, u32[]{:S(2)}) %copy-start.3) | copy-done | bytes 1048600
  1.2 0.0 copy-start.4
  1.2 0.7 %copy-done.4 = s32[4,8]{1,0:T(4,128)S(1)} copy-done((s32[4,8]{1,0:T(4,128)S(1)}, s32[4,8]{1,0:T(4,128)}, u32[]{:S(2)}) %copy-start.4) | copy-done | bytes 152
  1.9 0.7 %pick_cd_blocks.1 = (bf16[128,1024]{1,0:T(8,128)(2,1)S(1)}, bf16[128,1024]{1,0:T(8,128)(2,1)S(1)}, bf16[128,1024]{1,0:T(8,128)(2,1)S(1)}, bf16[128,1024]{1,0:T(8,128)(2,1)S(1)}) custom-call(s32[4,8]{1,0:T(4,128)S(1)} %copy-done.4, bf16[4,128,1024]{2,1,0:T(8,128)(2,1)S(1)} %copy-done.3), custom_call_target="tpu_custom_call" | custom-call | tf_op jit(solution)/shard_map/pick_cd_blocks/pallas_call | solution.py:91
  2.6 3.0 %collective-permute-start.4 = (bf16[128,1024]{1,0:T(8,128)(2,1)S(1)}, bf16[128,1024]{1,0:T(8,128)(2,1)S(1)}, u32[]{:S(2)}, u32[]{:S(2)}) collective-permute-start(bf16[128,1024]{1,0:T(8,128)(2,1)S(1)} %get-tuple-element.37), channel_id=1, source_target_pairs={{0,8},{1,17},{2,10},{3,19},{4,12},{5,21},{6,14},{7,23},{8,0},{9,25... | collective-permute-start | bytes 786440 | tf_op jit(solution)/shard_map/ppermute | solution.py:294
  5.6 1.5 %collective-permute-start = (bf16[128,1024]{1,0:T(8,128)(2,1)S(1)}, bf16[128,1024]{1,0:T(8,128)(2,1)S(1)}, u32[]{:S(2)}, u32[]{:S(2)}) collective-permute-start(bf16[128,1024]{1,0:T(8,128)(2,1)S(1)} %get-tuple-element.26), channel_id=1, source_target_pairs={{0,16},{1,9},{2,18},{3,11},{4,20},{5,13},{6,22},{7,15},{8,24},{9,1... | collective-permute-start | bytes 786440 | tf_op jit(solution)/shard_map/ppermute | solution.py:294
  7.1 0.0 copy-start
  7.1 1.6 %copy-done = bf16[1,1024,1024]{2,1,0:T(8,128)(2,1)S(1)} copy-done((bf16[1,1024,1024]{2,1,0:T(8,128)(2,1)S(1)}, bf16[1,1024,1024]{2,1,0:T(8,128)(2,1)}, u32[]{:S(2)}) %copy-start) | copy-done | bytes 2097176
  8.7 0.0 copy-start.1
  8.7 0.7 %contract_for_chips.3 = (s16[32,1024]{1,0:T(8,128)(2,1)S(1)}, s16[32,1024]{1,0:T(8,128)(2,1)S(1)}, s16[32,1024]{1,0:T(8,128)(2,1)S(1)}, s16[32,1024]{1,0:T(8,128)(2,1)S(1)}, bf16[128,1024]{1,0:T(8,128)(2,1)S(1)}) custom-call(bf16[128,1024]{1,0:T(8,128)(2,1)S(1)} %get-tuple-element.27.refs_0_, bf16[1024,1024]{1,0:T(8,128)(2,1)S(1)} %bitcast.3, ...), custom_call_target="tpu_custom_call" | custom-call | flops 268435456 | bytes 2097152 | tf_op jit(solution)/shard_map/contract_for_chips/pallas_call | solution.py:131
  9.4 0.1 collective-permute-start.10
  9.5 2.7 %collective-permute-done.4.refs_0_ = bf16[128,1024]{1,0:T(8,128)(2,1)S(1)} collective-permute-done((bf16[128,1024]{1,0:T(8,128)(2,1)S(1)}, bf16[128,1024]{1,0:T(8,128)(2,1)S(1)}, u32[]{:S(2)}, u32[]{:S(2)}) %collective-permute-start.4) | collective-permute-done | bytes 262176 | tf_op jit(solution)/shard_map/ppermute | solution.py:294
  12.2 0.0 copy-done.1
  12.2 0.7 %contract_for_chips.5 = (s16[32,1024]{1,0:T(8,128)(2,1)S(1)}, s16[32,1024]{1,0:T(8,128)(2,1)S(1)}, s16[32,1024]{1,0:T(8,128)(2,1)S(1)}, s16[32,1024]{1,0:T(8,128)(2,1)S(1)}) custom-call(bf16[128,1024]{1,0:T(8,128)(2,1)S(1)} %collective-permute-done.4.refs_0_, bf16[1024,1024]{1,0:T(8,128)(2,1)S(1)} %bitcast.4), custom_call_target="tpu_custom_call" | custom-call | flops 268435456 | bytes 2097152 | tf_op jit(solution)/shard_map/contract_for_chips/pallas_call | solution.py:131
  12.9 4.7 %collective-permute-start.5 = (s16[32,1024]{1,0:T(8,128)(2,1)S(1)}, s16[32,1024]{1,0:T(8,128)(2,1)S(1)}, u32[]{:S(2)}, u32[]{:S(2)}) collective-permute-start(s16[32,1024]{1,0:T(8,128)(2,1)S(1)} %get-tuple-element.39), channel_id=1, source_target_pairs={{0,6},{1,7},{2,4},{3,5},{4,2},{5,3},{6,0},{7,1},{8,14},{9,15},{10,... | collective-permute-start | bytes 196616 | tf_op jit(solution)/shard_map/ppermute | solution.py:294
  17.6 0.0 collective-permute-start.6
  17.6 0.0 collective-permute-done.refs_0_
  17.6 0.7 %contract_for_chips.4 = (s16[64,1024]{1,0:T(8,128)(2,1)S(1)}, s16[64,1024]{1,0:T(8,128)(2,1)S(1)}, s16[64,1024]{1,0:T(8,128)(2,1)S(1)}, s16[64,1024]{1,0:T(8,128)(2,1)S(1)}) custom-call(bf16[128,1024]{1,0:T(8,128)(2,1)S(1)} %collective-permute-done.refs_0_, bf16[1024,1024]{1,0:T(8,128)(2,1)S(1)} %bitcast.5, s16[32,1024]{1,0:T(8,128)(2,1)S(1)} %get-tuple-element.29.refs_2_, ...), custom_call_target="tpu_custom_call" | custom-call | flops 268435456 | bytes 2097152 | tf_op jit(solution)/shard_map/contract_for_chips/pallas_call | solution.py:131
  18.3 0.0 copy-start.2
  18.3 0.0 copy-start.5
  18.3 0.0 copy-start.6
  18.3 0.0 copy-start.7
  18.3 2.0 %collective-permute-start.1 = (s16[64,1024]{1,0:T(8,128)(2,1)S(1)}, s16[64,1024]{1,0:T(8,128)(2,1)S(1)}, u32[]{:S(2)}, u32[]{:S(2)}) collective-permute-start(s16[64,1024]{1,0:T(8,128)(2,1)S(1)} %get-tuple-element.34), channel_id=1, source_target_pairs={{0,6},{1,7},{2,4},{3,5},{4,2},{5,3},{6,0},{7,1},{8,14},{9,15},{10,... | collective-permute-start | bytes 393224 | tf_op jit(solution)/shard_map/ppermute | solution.py:294
  20.3 1.1 %collective-permute-start.2 = (s16[64,1024]{1,0:T(8,128)(2,1)S(1)}, s16[64,1024]{1,0:T(8,128)(2,1)S(1)}, u32[]{:S(2)}, u32[]{:S(2)}) collective-permute-start(s16[64,1024]{1,0:T(8,128)(2,1)S(1)} %get-tuple-element.35), channel_id=1, source_target_pairs={{0,4},{1,5},{2,6},{3,7},{4,0},{5,1},{6,2},{7,3},{8,12},{9,13},{10,... | collective-permute-start | bytes 393224 | tf_op jit(solution)/shard_map/ppermute | solution.py:294
  21.4 0.0 collective-permute-done.10.refs_0_
  21.4 1.4 %collective-permute-start.3 = (s16[64,1024]{1,0:T(8,128)(2,1)S(1)}, s16[64,1024]{1,0:T(8,128)(2,1)S(1)}, u32[]{:S(2)}, u32[]{:S(2)}) collective-permute-start(s16[64,1024]{1,0:T(8,128)(2,1)S(1)} %get-tuple-element.36), channel_id=1, source_target_pairs={{0,2},{1,3},{2,0},{3,1},{4,6},{5,7},{6,4},{7,5},{8,10},{9,11},{10,... | collective-permute-start | bytes 393224 | tf_op jit(solution)/shard_map/ppermute | solution.py:294
  22.8 0.7 %contract_far_group.1 = s16[128,1024]{1,0:T(8,128)(2,1)S(1)} custom-call(bf16[128,1024]{1,0:T(8,128)(2,1)S(1)} %collective-permute-done.10.refs_0_, bf16[1024,1024]{1,0:T(8,128)(2,1)S(1)} %bitcast.6), custom_call_target="tpu_custom_call" | custom-call | flops 268435456 | bytes 2097152 | tf_op jit(solution)/shard_map/contract_far_group/pallas_call | solution.py:153
  23.5 0.0 collective-permute-done.5.refs_1_
  23.5 1.4 %collective-permute-start.7 = (s16[32,1024]{1,0:T(8,128)(2,1)S(1)}, s16[32,1024]{1,0:T(8,128)(2,1)S(1)}, u32[]{:S(2)}, u32[]{:S(2)}) collective-permute-start(s16[32,1024]{1,0:T(8,128)(2,1)S(1)} %get-tuple-element.41), channel_id=1, source_target_pairs={{0,2},{1,3},{2,0},{3,1},{4,6},{5,7},{6,4},{7,5},{8,10},{9,11},{10,... | collective-permute-start | bytes 196616 | tf_op jit(solution)/shard_map/ppermute | solution.py:294
  24.9 3.5 %collective-permute-done.6.refs_2_ = s16[32,1024]{1,0:T(8,128)(2,1)S(1)} collective-permute-done((s16[32,1024]{1,0:T(8,128)(2,1)S(1)}, s16[32,1024]{1,0:T(8,128)(2,1)S(1)}, u32[]{:S(2)}, u32[]{:S(2)}) %collective-permute-start.6) | collective-permute-done | bytes 65568 | tf_op jit(solution)/shard_map/ppermute | solution.py:294
  28.4 1.3 %collective-permute-start.11 = (s16[128,1024]{1,0:T(8,128)(2,1)S(1)}, s16[128,1024]{1,0:T(8,128)(2,1)S(1)}, u32[]{:S(2)}, u32[]{:S(2)}) collective-permute-start(s16[128,1024]{1,0:T(8,128)(2,1)S(1)} %contract_far_group.1), channel_id=1, source_target_pairs={{0,24},{1,25},{2,26},{3,27},{4,28},{5,29},{6,30},{7,31},{8,16},{9,... | collective-permute-start | bytes 786440 | tf_op jit(solution)/shard_map/ppermute | solution.py:294
  29.7 0.0 collective-permute-done.7.refs_3_
  29.7 1.0 %collective-permute-start.8 = (s16[128,1024]{1,0:T(8,128)(2,1)S(1)}, s16[128,1024]{1,0:T(8,128)(2,1)S(1)}, u32[]{:S(2)}, u32[]{:S(2)}) collective-permute-start(s16[128,1024]{1,0:T(8,128)(2,1)S(1)} %rows_of_one_group.2), channel_id=1, source_target_pairs={{0,8},{1,17},{2,10},{3,19},{4,12},{5,21},{6,14},{7,23},{8,0},{9,25... | collective-permute-start | bytes 786440 | tf_op jit(solution)/shard_map/ppermute | solution.py:294
  30.7 0.0 collective-permute-done.1.refs_1_.refs_4_
  30.7 1.3 %collective-permute-done.2.refs_2_.refs_5_ = s16[64,1024]{1,0:T(8,128)(2,1)S(1)} collective-permute-done((s16[64,1024]{1,0:T(8,128)(2,1)S(1)}, s16[64,1024]{1,0:T(8,128)(2,1)S(1)}, u32[]{:S(2)}, u32[]{:S(2)}) %collective-permute-start.2) | collective-permute-done | bytes 131104 | tf_op jit(solution)/shard_map/ppermute | solution.py:294
  32.1 0.0 collective-permute-done.3.refs_3_.refs_6_
  32.1 1.6 %collective-permute-start.9 = (s16[128,1024]{1,0:T(8,128)(2,1)S(1)}, s16[128,1024]{1,0:T(8,128)(2,1)S(1)}, u32[]{:S(2)}, u32[]{:S(2)}) collective-permute-start(s16[128,1024]{1,0:T(8,128)(2,1)S(1)} %rows_of_one_group.3), channel_id=1, source_target_pairs={{0,16},{1,9},{2,18},{3,11},{4,20},{5,13},{6,22},{7,15},{8,24},{9,1... | collective-permute-start | bytes 786440 | tf_op jit(solution)/shard_map/ppermute | solution.py:294
  33.7 2.4 %collective-permute-done.11.source = s16[128,1024]{1,0:T(8,128)(2,1)S(1)} collective-permute-done((s16[128,1024]{1,0:T(8,128)(2,1)S(1)}, s16[128,1024]{1,0:T(8,128)(2,1)S(1)}, u32[]{:S(2)}, u32[]{:S(2)}) %collective-permute-start.11) | collective-permute-done | bytes 262176 | tf_op jit(solution)/shard_map/ppermute | solution.py:294
  36.0 1.6 %collective-permute-start.12 = (s16[32,1024]{1,0:T(8,128)(2,1)S(1)}, s16[32,1024]{1,0:T(8,128)(2,1)S(1)}, u32[]{:S(2)}, u32[]{:S(2)}) collective-permute-start(s16[32,1024]{1,0:T(8,128)(2,1)S(1)} %get-tuple-element.44), channel_id=1, source_target_pairs={{0,6},{1,7},{2,4},{3,5},{4,2},{5,3},{6,0},{7,1},{8,14},{9,15},{10,... | collective-permute-start | bytes 196616 | tf_op jit(solution)/shard_map/ppermute | solution.py:294
  37.6 0.0 collective-permute-start.13
  37.6 2.9 %collective-permute-start.14 = (s16[32,1024]{1,0:T(8,128)(2,1)S(1)}, s16[32,1024]{1,0:T(8,128)(2,1)S(1)}, u32[]{:S(2)}, u32[]{:S(2)}) collective-permute-start(s16[32,1024]{1,0:T(8,128)(2,1)S(1)} %get-tuple-element.46), channel_id=1, source_target_pairs={{0,2},{1,3},{2,0},{3,1},{4,6},{5,7},{6,4},{7,5},{8,10},{9,11},{10,... | collective-permute-start | bytes 196616 | tf_op jit(solution)/shard_map/ppermute | solution.py:294
  40.5 0.0 collective-permute-done.8.refs_4_.refs_7_
  40.5 1.7 %collective-permute-done.12.refs_7_.refs_10_ = s16[32,1024]{1,0:T(8,128)(2,1)S(1)} collective-permute-done((s16[32,1024]{1,0:T(8,128)(2,1)S(1)}, s16[32,1024]{1,0:T(8,128)(2,1)S(1)}, u32[]{:S(2)}, u32[]{:S(2)}) %collective-permute-start.12) | collective-permute-done | bytes 65568 | tf_op jit(solution)/shard_map/ppermute | solution.py:294
  42.2 1.4 %collective-permute-done.13.refs_8_.refs_11_ = s16[32,1024]{1,0:T(8,128)(2,1)S(1)} collective-permute-done((s16[32,1024]{1,0:T(8,128)(2,1)S(1)}, s16[32,1024]{1,0:T(8,128)(2,1)S(1)}, u32[]{:S(2)}, u32[]{:S(2)}) %collective-permute-start.13) | collective-permute-done | bytes 65568 | tf_op jit(solution)/shard_map/ppermute | solution.py:294
  43.6 0.0 collective-permute-done.14.refs_9_.refs_12_
  43.6 0.0 collective-permute-done.9.refs_5_.refs_8_
  43.6 0.1 collective-permute-start.15
  43.7 1.9 %collective-permute-done.15.refs_13_ = s16[256,1024]{1,0:T(8,128)(2,1)S(1)} collective-permute-done((s16[256,1024]{1,0:T(8,128)(2,1)S(1)}, s16[256,1024]{1,0:T(8,128)(2,1)S(1)}, u32[]{:S(2)}, u32[]{:S(2)}) %collective-permute-start.15) | collective-permute-done | bytes 524320 | tf_op jit(solution)/shard_map/ppermute | solution.py:294
  45.6 0.0 copy-done.2
  45.6 0.0 copy-done.5
  45.6 0.0 copy-done.6
  45.6 0.0 copy-done.7
  45.6 3.1 %add_contributions.1 = f32[50,16,1024]{2,1,0:T(8,128)} custom-call(s32[4,8]{1,0:T(4,128)S(1)} %copy-done.6, s32[4,8]{1,0:T(4,128)S(1)} %copy-done.5, s32[4,8]{1,0:T(4,128)S(1)} %copy-done.7, s16[64,1024]{1,0:T(8,128)(2,1)S(1)} %get-tuple-element.33.refs_0_.refs_3_, s16[64,1024]{1,0:T(8,128)(2,1)S(1)} %collective-permute-done.1.refs_1_.refs_4_, ...), custom_call_target="tpu_custom_call" | custom-call | tf_op jit(solution)/shard_map/add_contributions/pallas_call | solution.py:271
  (4 shorter events, 0.1 us)
Async XLA Ops:
  0.0 1.2 %copy-start.3 = (bf16[4,128,1024]{2,1,0:T(8,128)(2,1)S(1)}, bf16[4,128,1024]{2,1,0:T(8,128)(2,1)}, u32[]{:S(2)}) copy-start(bf16[4,128,1024]{2,1,0:T(8,128)(2,1)} %amplitudes.1) | copy-start | bytes 3145732
  1.2 0.7 %copy-start.4 = (s32[4,8]{1,0:T(4,128)S(1)}, s32[4,8]{1,0:T(4,128)}, u32[]{:S(2)}) copy-start(s32[4,8]{1,0:T(4,128)} %refs_1_.1) | copy-start | bytes 388
  2.6 9.6 %collective-permute-start.4 = (bf16[128,1024]{1,0:T(8,128)(2,1)S(1)}, bf16[128,1024]{1,0:T(8,128)(2,1)S(1)}, u32[]{:S(2)}, u32[]{:S(2)}) collective-permute-start(bf16[128,1024]{1,0:T(8,128)(2,1)S(1)} %get-tuple-element.37), channel_id=1, source_target_pairs={{0,8},{1,17},{2,10},{3,19},{4,12},{5,21},{6,14},{7,23},{8,0},{9,25... | collective-permute-start | bytes 786440 | tf_op jit(solution)/shard_map/ppermute | solution.py:294
  5.6 12.0 %collective-permute-start = (bf16[128,1024]{1,0:T(8,128)(2,1)S(1)}, bf16[128,1024]{1,0:T(8,128)(2,1)S(1)}, u32[]{:S(2)}, u32[]{:S(2)}) collective-permute-start(bf16[128,1024]{1,0:T(8,128)(2,1)S(1)} %get-tuple-element.26), channel_id=1, source_target_pairs={{0,16},{1,9},{2,18},{3,11},{4,20},{5,13},{6,22},{7,15},{8,24},{9,1... | collective-permute-start | bytes 786440 | tf_op jit(solution)/shard_map/ppermute | solution.py:294
  7.1 1.6 %copy-start = (bf16[1,1024,1024]{2,1,0:T(8,128)(2,1)S(1)}, bf16[1,1024,1024]{2,1,0:T(8,128)(2,1)}, u32[]{:S(2)}) copy-start(bf16[1,1024,1024]{2,1,0:T(8,128)(2,1)} %param.8) | copy-start | bytes 6291460
  8.7 3.5 %copy-start.1 = (bf16[1,1024,1024]{2,1,0:T(8,128)(2,1)S(1)}, bf16[1,1024,1024]{2,1,0:T(8,128)(2,1)}, u32[]{:S(2)}) copy-start(bf16[1,1024,1024]{2,1,0:T(8,128)(2,1)} %param.8) | copy-start | bytes 6291460
  9.4 11.9 %collective-permute-start.10 = (bf16[128,1024]{1,0:T(8,128)(2,1)S(1)}, bf16[128,1024]{1,0:T(8,128)(2,1)S(1)}, u32[]{:S(2)}, u32[]{:S(2)}) collective-permute-start(bf16[128,1024]{1,0:T(8,128)(2,1)S(1)} %get-tuple-element.42), channel_id=1, source_target_pairs={{0,24},{1,25},{2,26},{3,27},{4,28},{5,29},{6,30},{7,31},{8,16},{9,... | collective-permute-start | bytes 786440 | tf_op jit(solution)/shard_map/ppermute | solution.py:294
  12.9 10.6 %collective-permute-start.5 = (s16[32,1024]{1,0:T(8,128)(2,1)S(1)}, s16[32,1024]{1,0:T(8,128)(2,1)S(1)}, u32[]{:S(2)}, u32[]{:S(2)}) collective-permute-start(s16[32,1024]{1,0:T(8,128)(2,1)S(1)} %get-tuple-element.39), channel_id=1, source_target_pairs={{0,6},{1,7},{2,4},{3,5},{4,2},{5,3},{6,0},{7,1},{8,14},{9,15},{10,... | collective-permute-start | bytes 196616 | tf_op jit(solution)/shard_map/ppermute | solution.py:294
  17.6 10.8 %collective-permute-start.6 = (s16[32,1024]{1,0:T(8,128)(2,1)S(1)}, s16[32,1024]{1,0:T(8,128)(2,1)S(1)}, u32[]{:S(2)}, u32[]{:S(2)}) collective-permute-start(s16[32,1024]{1,0:T(8,128)(2,1)S(1)} %get-tuple-element.40), channel_id=1, source_target_pairs={{0,4},{1,5},{2,6},{3,7},{4,0},{5,1},{6,2},{7,3},{8,12},{9,13},{10,... | collective-permute-start | bytes 196616 | tf_op jit(solution)/shard_map/ppermute | solution.py:294
  18.3 27.3 %copy-start.2 = (f32[16,50,1024]{2,0,1:T(8,128)S(1)}, f32[16,50,1024]{2,0,1:T(8,128)}, u32[]{:S(2)}) copy-start(f32[16,50,1024]{2,0,1:T(8,128)} %param.11) | copy-start | bytes 9830404
  18.3 27.3 %copy-start.5 = (s32[4,8]{1,0:T(4,128)S(1)}, s32[4,8]{1,0:T(4,128)}, u32[]{:S(2)}) copy-start(s32[4,8]{1,0:T(4,128)} %refs_1_.1) | copy-start | bytes 388
  18.3 27.3 %copy-start.6 = (s32[4,8]{1,0:T(4,128)S(1)}, s32[4,8]{1,0:T(4,128)}, u32[]{:S(2)}) copy-start(s32[4,8]{1,0:T(4,128)} %refs_0_.1) | copy-start | bytes 388
  18.3 27.3 %copy-start.7 = (s32[4,8]{1,0:T(4,128)S(1)}, s32[4,8]{1,0:T(4,128)}, u32[]{:S(2)}) copy-start(s32[4,8]{1,0:T(4,128)} %refs_2_.1) | copy-start | bytes 388
  18.3 12.4 %collective-permute-start.1 = (s16[64,1024]{1,0:T(8,128)(2,1)S(1)}, s16[64,1024]{1,0:T(8,128)(2,1)S(1)}, u32[]{:S(2)}, u32[]{:S(2)}) collective-permute-start(s16[64,1024]{1,0:T(8,128)(2,1)S(1)} %get-tuple-element.34), channel_id=1, source_target_pairs={{0,6},{1,7},{2,4},{3,5},{4,2},{5,3},{6,0},{7,1},{8,14},{9,15},{10,... | collective-permute-start | bytes 393224 | tf_op jit(solution)/shard_map/ppermute | solution.py:294
  20.3 11.7 %collective-permute-start.2 = (s16[64,1024]{1,0:T(8,128)(2,1)S(1)}, s16[64,1024]{1,0:T(8,128)(2,1)S(1)}, u32[]{:S(2)}, u32[]{:S(2)}) collective-permute-start(s16[64,1024]{1,0:T(8,128)(2,1)S(1)} %get-tuple-element.35), channel_id=1, source_target_pairs={{0,4},{1,5},{2,6},{3,7},{4,0},{5,1},{6,2},{7,3},{8,12},{9,13},{10,... | collective-permute-start | bytes 393224 | tf_op jit(solution)/shard_map/ppermute | solution.py:294
  21.4 10.7 %collective-permute-start.3 = (s16[64,1024]{1,0:T(8,128)(2,1)S(1)}, s16[64,1024]{1,0:T(8,128)(2,1)S(1)}, u32[]{:S(2)}, u32[]{:S(2)}) collective-permute-start(s16[64,1024]{1,0:T(8,128)(2,1)S(1)} %get-tuple-element.36), channel_id=1, source_target_pairs={{0,2},{1,3},{2,0},{3,1},{4,6},{5,7},{6,4},{7,5},{8,10},{9,11},{10,... | collective-permute-start | bytes 393224 | tf_op jit(solution)/shard_map/ppermute | solution.py:294
  23.5 6.2 %collective-permute-start.7 = (s16[32,1024]{1,0:T(8,128)(2,1)S(1)}, s16[32,1024]{1,0:T(8,128)(2,1)S(1)}, u32[]{:S(2)}, u32[]{:S(2)}) collective-permute-start(s16[32,1024]{1,0:T(8,128)(2,1)S(1)} %get-tuple-element.41), channel_id=1, source_target_pairs={{0,2},{1,3},{2,0},{3,1},{4,6},{5,7},{6,4},{7,5},{8,10},{9,11},{10,... | collective-permute-start | bytes 196616 | tf_op jit(solution)/shard_map/ppermute | solution.py:294
  28.4 7.6 %collective-permute-start.11 = (s16[128,1024]{1,0:T(8,128)(2,1)S(1)}, s16[128,1024]{1,0:T(8,128)(2,1)S(1)}, u32[]{:S(2)}, u32[]{:S(2)}) collective-permute-start(s16[128,1024]{1,0:T(8,128)(2,1)S(1)} %contract_far_group.1), channel_id=1, source_target_pairs={{0,24},{1,25},{2,26},{3,27},{4,28},{5,29},{6,30},{7,31},{8,16},{9,... | collective-permute-start | bytes 786440 | tf_op jit(solution)/shard_map/ppermute | solution.py:294
  29.7 10.8 %collective-permute-start.8 = (s16[128,1024]{1,0:T(8,128)(2,1)S(1)}, s16[128,1024]{1,0:T(8,128)(2,1)S(1)}, u32[]{:S(2)}, u32[]{:S(2)}) collective-permute-start(s16[128,1024]{1,0:T(8,128)(2,1)S(1)} %rows_of_one_group.2), channel_id=1, source_target_pairs={{0,8},{1,17},{2,10},{3,19},{4,12},{5,21},{6,14},{7,23},{8,0},{9,25... | collective-permute-start | bytes 786440 | tf_op jit(solution)/shard_map/ppermute | solution.py:294
  32.1 11.5 %collective-permute-start.9 = (s16[128,1024]{1,0:T(8,128)(2,1)S(1)}, s16[128,1024]{1,0:T(8,128)(2,1)S(1)}, u32[]{:S(2)}, u32[]{:S(2)}) collective-permute-start(s16[128,1024]{1,0:T(8,128)(2,1)S(1)} %rows_of_one_group.3), channel_id=1, source_target_pairs={{0,16},{1,9},{2,18},{3,11},{4,20},{5,13},{6,22},{7,15},{8,24},{9,1... | collective-permute-start | bytes 786440 | tf_op jit(solution)/shard_map/ppermute | solution.py:294
  36.0 6.1 %collective-permute-start.12 = (s16[32,1024]{1,0:T(8,128)(2,1)S(1)}, s16[32,1024]{1,0:T(8,128)(2,1)S(1)}, u32[]{:S(2)}, u32[]{:S(2)}) collective-permute-start(s16[32,1024]{1,0:T(8,128)(2,1)S(1)} %get-tuple-element.44), channel_id=1, source_target_pairs={{0,6},{1,7},{2,4},{3,5},{4,2},{5,3},{6,0},{7,1},{8,14},{9,15},{10,... | collective-permute-start | bytes 196616 | tf_op jit(solution)/shard_map/ppermute | solution.py:294
  37.6 6.0 %collective-permute-start.13 = (s16[32,1024]{1,0:T(8,128)(2,1)S(1)}, s16[32,1024]{1,0:T(8,128)(2,1)S(1)}, u32[]{:S(2)}, u32[]{:S(2)}) collective-permute-start(s16[32,1024]{1,0:T(8,128)(2,1)S(1)} %get-tuple-element.45), channel_id=1, source_target_pairs={{0,4},{1,5},{2,6},{3,7},{4,0},{5,1},{6,2},{7,3},{8,12},{9,13},{10,... | collective-permute-start | bytes 196616 | tf_op jit(solution)/shard_map/ppermute | solution.py:294
  37.6 6.0 %collective-permute-start.14 = (s16[32,1024]{1,0:T(8,128)(2,1)S(1)}, s16[32,1024]{1,0:T(8,128)(2,1)S(1)}, u32[]{:S(2)}, u32[]{:S(2)}) collective-permute-start(s16[32,1024]{1,0:T(8,128)(2,1)S(1)} %get-tuple-element.46), channel_id=1, source_target_pairs={{0,2},{1,3},{2,0},{3,1},{4,6},{5,7},{6,4},{7,5},{8,10},{9,11},{10,... | collective-permute-start | bytes 196616 | tf_op jit(solution)/shard_map/ppermute | solution.py:294
  43.6 2.0 %collective-permute-start.15 = (s16[256,1024]{1,0:T(8,128)(2,1)S(1)}, s16[256,1024]{1,0:T(8,128)(2,1)S(1)}, u32[]{:S(2)}, u32[]{:S(2)}) collective-permute-start(s16[256,1024]{1,0:T(8,128)(2,1)S(1)} %rows_of_other_core.1), channel_id=1, source_target_pairs={{0,1},{1,0},{2,3},{3,2},{4,5},{5,4},{6,7},{7,6},{8,9},{9,8},{10,11... | collective-permute-start | bytes 1572872 | tf_op jit(solution)/shard_map/ppermute | solution.py:294

commit v14 on v9

--- a/solution.py
+++ b/solution.py
@@ -14,6 +14,7 @@
 LANES = 128
 CORES = 2
 MEBIBYTE = 1 << 20
+ROOMY = pltpu.CompilerParams(vmem_limit_bytes=209 * MEBIBYTE // 4)
 SMEM = pl.BlockSpec(memory_space=pltpu.SMEM)
 VMEM = pl.BlockSpec(memory_space=pltpu.VMEM)
 ANY = pl.BlockSpec(memory_space=pl.ANY)
@@ -60,6 +61,12 @@
     return [0] + steps + [blk_count - 1]
 
 
+def copies_of(source, target, parts, sems, first):
+    rows = target.shape[0] // parts
+    spans = [pl.ds(part * rows, rows) for part in range(parts)]
+    return [pltpu.make_async_copy(source.at[s], target.at[s], sems.at[first + i]) for i, s in enumerate(spans)]
+
+
 def start_all(copies):
     for copy in copies:
         copy.start()
@@ -70,33 +77,32 @@
         copy.wait()
 
 
-def pick_kernel(tile_cd, amplitudes, *rest):
+def pick_kernel(parts, tile_cd, amplitudes, *rest):
     outgoing, sems = rest[:-1], rest[-1]
     blk, grp = lax.axis_index("blk"), lax.axis_index("grp")
     copies = []
     for slot, step in enumerate(blk_steps(len(outgoing), grp % CORES)):
         cd = tile_cd[jnp.bitwise_xor(blk, step), grp]
-        copies.append(pltpu.make_async_copy(amplitudes.at[cd], outgoing[slot], sems.at[slot]))
+        copies += copies_of(amplitudes.at[cd], outgoing[slot], parts, sems, slot * parts)
     start_all(copies)
     wait_all(copies)
 
 
 def pick(tile_cd, amplitudes):
-    groups = tile_cd.shape[0]
+    groups, parts = tile_cd.shape[0], 4
     block = jax.ShapeDtypeStruct(amplitudes.shape[1:], amplitudes.dtype)
     return pl.pallas_call(
-        pick_kernel,
+        lambda *refs: pick_kernel(parts, *refs),
         out_shape=[block] * groups,
         in_specs=[SMEM, ANY],
         out_specs=[VMEM] * groups,
-        scratch_shapes=[pltpu.SemaphoreType.DMA((groups,))],
-        compiler_params=vmem_limit(*[block] * groups),
+        scratch_shapes=[pltpu.SemaphoreType.DMA((groups * parts,))],
+        compiler_params=ROOMY,
         name="pick_cd_blocks",
     )(tile_cd, amplitudes)
 
 
-def code_chips(rows, tile, product, outgoing, first):
-    product[...] = jnp.dot(rows[...], tile[...], preferred_element_type=jnp.float32)
+def code_chips(product, outgoing, first):
     chip_rows = product.shape[0] // len(outgoing)
     chip = lax.axis_index("grp") // CORES
     for step, coded in enumerate(outgoing):
@@ -106,37 +112,48 @@
         coded[first : first + chip_rows, LANES:] = tail
 
 
-def own_kernel(rows, tile, far_picked, *rest):
-    outgoing, (tile_out, far_out, product, sem) = rest[:-4], rest[-4:]
-    copy = pltpu.make_async_copy(tile, tile_out, sem)
-    copy.start()
+def own_kernel(steps, parts, rows, integrals, far_picked, *rest):
+    outgoing, (far_out, tile, product, sems) = rest[:-4], rest[-4:]
+    depth = tile.shape[0] // steps
+    spans = [pl.ds(step * depth, depth) for step in range(steps)]
+    copies = [copies_of(integrals.at[0, s], tile.at[s], parts, sems, i * parts) for i, s in enumerate(spans)]
+    for group in copies:
+        start_all(group)
     far_out[...] = far_picked[...]
-    code_chips(rows, tile, product, outgoing, 0)
-    copy.wait()
-
-
-def contract_own(rows, tile, far_picked, chips):
-    group_rows, tile_width = rows.shape[0], tile.shape[1]
+    for step, group in enumerate(copies):
+        wait_all(group)
+        here = slice(step * depth, (step + 1) * depth)
+        term = jnp.dot(rows[:, here], tile[here, :], preferred_element_type=jnp.float32)
+        product[...] = product[...] + term if step else term
+    code_chips(product, outgoing, 0)
+
+
+def contract_own(rows, integrals, far_picked, chips):
+    group_rows, (_, depth, tile_width) = rows.shape[0], integrals.shape
+    steps, parts = 4, 4
     coded = jax.ShapeDtypeStruct((group_rows // chips, tile_width), jnp.int16)
-    product = jax.ShapeDtypeStruct((group_rows, tile_width), jnp.float32)
-    outputs = [coded] * chips + [jax.ShapeDtypeStruct(array.shape, array.dtype) for array in (tile, far_picked)]
-    return pl.pallas_call(
-        own_kernel,
-        out_shape=outputs,
-        in_specs=[VMEM] * 3,
-        out_specs=[VMEM] * len(outputs),
-        scratch_shapes=[pltpu.VMEM(product.shape, product.dtype), pltpu.SemaphoreType.DMA],
-        compiler_params=vmem_limit(rows, tile, far_picked, *outputs, product),
-        cost_estimate=cost(group_rows, tile),
+    return pl.pallas_call(
+        lambda *refs: own_kernel(steps, parts, *refs),
+        out_shape=[coded] * chips + [jax.ShapeDtypeStruct(far_picked.shape, far_picked.dtype)],
+        in_specs=[VMEM, ANY, VMEM],
+        out_specs=[VMEM] * (chips + 1),
+        scratch_shapes=[
+            pltpu.VMEM((depth, tile_width), integrals.dtype),
+            pltpu.VMEM((group_rows, tile_width), jnp.float32),
+            pltpu.SemaphoreType.DMA((steps * parts,)),
+        ],
+        compiler_params=ROOMY,
+        cost_estimate=cost(group_rows, integrals),
         name="contract_own_group",
-    )(rows, tile, far_picked)
+    )(rows, integrals, far_picked)
 
 
 def near_kernel(near, *refs):
     groups, tile, outgoing, product = refs[:near], refs[near], refs[near + 1 : -1], refs[-1]
     chip_rows = product.shape[0] // len(outgoing)
     for index, rows in enumerate(groups):
-        code_chips(rows, tile, product, outgoing, index * chip_rows)
+        product[...] = jnp.dot(rows[...], tile[...], preferred_element_type=jnp.float32)
+        code_chips(product, outgoing, index * chip_rows)
 
 
 def contract_near(groups, tile, chips):
@@ -159,7 +176,8 @@
     coded, product = rest[-2:]
     chip_rows = product.shape[0] // chips
     parts = [coded.at[pl.ds(step * chip_rows, chip_rows)] for step in range(chips)]
-    code_chips(rows, tile, product, parts, 0)
+    product[...] = jnp.dot(rows[...], tile[...], preferred_element_type=jnp.float32)
+    code_chips(product, parts, 0)
 
 
 def contract_far(rows, tile, chips, earlier):
@@ -203,28 +221,30 @@
 
 
 def other_core_kernel(owner_rows, *refs):
-    arrays, halves = refs[:-1], refs[-1]
+    arrays, halves = refs[:-2], refs[-2:]
     other = 1 - lax.axis_index("grp") % CORES
-    for index, (array, first) in enumerate(pieces_of(arrays, owner_rows)):
+    pieces = pieces_of(arrays, owner_rows)
+    for index, (array, first) in enumerate(pieces):
+        half, place = divmod(index, len(pieces) // 2)
         source = pl.multiple_of(first + other * owner_rows, owner_rows)
-        halves[index * owner_rows : (index + 1) * owner_rows, :] = array[pl.ds(source, owner_rows), :]
+        halves[half][place * owner_rows : (place + 1) * owner_rows, :] = array[pl.ds(source, owner_rows), :]
 
 
 def other_core_rows(arrays, owner_rows):
     rows = sum(array.shape[0] for array in arrays) // CORES
-    halves = jax.ShapeDtypeStruct((rows, arrays[0].shape[1]), arrays[0].dtype)
+    half = jax.ShapeDtypeStruct((rows // 2, arrays[0].shape[1]), arrays[0].dtype)
     return pl.pallas_call(
         lambda *refs: other_core_kernel(owner_rows, *refs),
-        out_shape=halves,
+        out_shape=[half] * 2,
         in_specs=[VMEM] * len(arrays),
-        out_specs=VMEM,
-        compiler_params=vmem_limit(*arrays, halves),
+        out_specs=[VMEM] * 2,
+        compiler_params=vmem_limit(*arrays, half, half),
         name="rows_of_other_core",
     )(*arrays)
 
 
 def add_kernel(parts, tile_ab, tile_cd, pair_screen, *rest):
-    arrays, (swapped, residual_in, residual, held, sems) = rest[:-5], rest[-5:]
+    arrays, swapped, (residual_in, residual, held, sems) = rest[:-6], rest[-6:-4], rest[-4:]
     blk, grp = lax.axis_index("blk"), lax.axis_index("grp")
     ab_tiles, owner_rows, tile_width = residual.shape
     chips = tile_ab.shape[1] // CORES
@@ -249,8 +269,9 @@
             p_there = jnp.bitwise_xor(blk, steps_there[index // chips])
             g = jnp.bitwise_xor(grp, index % chips * CORES)
             here = pl.ds(pl.multiple_of(first + own, owner_rows), owner_rows)
-            there = pl.ds(index * owner_rows, owner_rows)
-            for source, span, p, column in ((array, here, p_here, g), (swapped, there, p_there, jnp.bitwise_xor(g, 1))):
+            half, place = divmod(index, len(pieces) // 2)
+            there = pl.ds(place * owner_rows, owner_rows)
+            for source, span, p, column in ((array, here, p_here, g), (swapped[half], there, p_there, jnp.bitwise_xor(g, 1))):
                 kept = pair_screen[tile_cd[p, column], grp].astype(jnp.float32)
                 scale = row_scale(source[span, :LANES]) * kept
                 terms.append((source, span, scale, tile_ab[p, column]))
@@ -263,16 +284,16 @@
 
 
 def add_blocks(tile_ab, tile_cd, pair_screen, arrays, swapped, residual_in):
-    parts = 5
+    parts = residual_in.shape[0] // 2
     return pl.pallas_call(
         lambda *refs: add_kernel(parts, *refs),
         out_shape=jax.ShapeDtypeStruct(residual_in.shape, residual_in.dtype),
-        in_specs=[SMEM] * 3 + [VMEM] * (len(arrays) + 2),
+        in_specs=[SMEM] * 3 + [VMEM] * (len(arrays) + 3),
         out_specs=ANY,
         scratch_shapes=[pltpu.VMEM(residual_in.shape, residual_in.dtype), pltpu.SemaphoreType.DMA((parts,))],
-        compiler_params=vmem_limit(*arrays, swapped, residual_in, residual_in),
+        compiler_params=vmem_limit(*arrays, *swapped, residual_in, residual_in),
         name="add_contributions",
-    )(tile_ab, tile_cd, pair_screen, *arrays, swapped, residual_in)
+    )(tile_ab, tile_cd, pair_screen, *arrays, *swapped, residual_in)
 
 
 def shards(amplitudes, pair_screen, integrals, tile_ab, tile_cd, residual_in):
@@ -295,7 +316,8 @@
 
     own_rows, *near_picked, far_picked = pick(tile_cd, amplitudes)
     near_rows = [swap(rows, index + 1, 0) for index, rows in enumerate(near_picked)]
-    *own_out, tile, far_picked = contract_own(own_rows, integrals[0], far_picked, chips)
+    *own_out, far_picked = contract_own(own_rows, integrals, far_picked, chips)
+    tile = integrals[0]
     own_in = along_chips(own_out)
     far_rows = swap(far_picked, far, 0)
     near_in = along_chips(contract_near(near_rows, tile, chips))
@@ -304,7 +326,7 @@
     far_back = swap(contract_far(far_rows, tile, chips, own_in[1:]), far, 0)
     far_in = along_chips(regroup([far_back], chips, "regroup_by_chip"))
     arrays = [*own_in, *near_in, *far_in]
-    swapped = swap(other_core_rows(arrays, owner_rows), 0, 0, 1)
+    swapped = [swap(half, 0, 0, 1) for half in other_core_rows(arrays, owner_rows)]
     by_tile = jnp.transpose(residual_in, (1, 0, 2))
     added = add_blocks(tile_ab, tile_cd, pair_screen, arrays, swapped, by_tile)
     return jnp.transpose(added, (1, 0, 2))

time: 47.2 us -> 47.4 us (level)
  Pallas kernels: 6.62 us -> 9.41 us
  local copies, waits for them, and re-layouts: 3.51 us -> 0.85 us
  starting transfers between devices: 26 us -> 26.5 us
  waiting for transfers between devices: 10.8 us -> 10.3 us
    unnamed x14 -> x10, local copies, waits for them, and re-layouts: 3.51 us -> 0.85 us
    pallas_call x2, Pallas kernels: 1.58 us -> 4.18 us  [the longest x1 2.22 us: contract_own(): pl.pallas_call(lambda *refs: own_kernel(steps, parts, *refs), out_shape=[...]
    ppermute x16 -> x17, starting transfers between devices: 26 us -> 26.5 us  [swap(): return lax.ppermute(value, ('blk', 'grp'), pairs)]
    ppermute x16 -> x17, waiting for transfers between devices: 10.8 us -> 10.3 us  [swap(): return lax.ppermute(value, ('blk', 'grp'), pairs)]
  transfers between devices with their start and end apart: 16 -> 17, of which waited for: 5 -> 5; matrix products, arithmetic and copies ran while one was open for 0% -> 0% of each run, Pallas kernels for 6% -> 9%
where the time goes in v14:
time: 47.4 us; the launch traced here: 47.2 us
  starting transfers between devices  26.5 us (56%)
  waiting for transfers between devices  10.3 us (22%)
  Pallas kernels  9.41 us (20%)
  local copies, waits for them, and re-layouts  0.85 us (2%)
    ppermute x17, starting transfers between devices, swap(): return lax.ppermute(value, ('blk', 'grp'), pairs)  26.5 us
    ppermute x17, waiting for transfers between devices, swap(): return lax.ppermute(value, ('blk', 'grp'), pairs)  10.3 us
    pallas_call x1, Pallas kernels, add_blocks(): pl.pallas_call(lambda *refs: add_kernel(parts, *refs), out_shape=jax.Shap...  3.28 us
    pallas_call x1, Pallas kernels, contract_own(): pl.pallas_call(lambda *refs: own_kernel(steps, parts, *refs), out_shape=[...  2.22 us
    pallas_call x1, Pallas kernels, pick(): pl.pallas_call(lambda *refs: pick_kernel(parts, *refs), out_shape=[block]...  1.95 us
    pallas_call x1, Pallas kernels, contract_near(): pl.pallas_call(lambda *refs: near_kernel(len(groups), *refs), out_shape=[...  1.15 us
  transfers between devices with their start and end apart: 17, of which 5 were waited for; matrix products, arithmetic and copies ran while one was open for 0% of the time, Pallas kernels for 9%

profile of v14, /device:TPU:0, one launch (start us, length us, event | category | flops | bytes accessed | tf_op | source)
XLA Modules:
  0.0 47.2 jit_solution(14396270719461561226)
XLA Ops:
  0.0 0.0 copy-start
  0.0 0.0 copy-start.2
  0.0 0.8 %copy-done.2 = s32[4,8]{1,0:T(4,128)S(1)} copy-done((s32[4,8]{1,0:T(4,128)S(1)}, s32[4,8]{1,0:T(4,128)}, u32[]{:S(2)}) %copy-start.2) | copy-done | bytes 152
  0.8 2.0 %pick_cd_blocks.1 = (bf16[128,1024]{1,0:T(8,128)(2,1)S(1)}, bf16[128,1024]{1,0:T(8,128)(2,1)S(1)}, bf16[128,1024]{1,0:T(8,128)(2,1)S(1)}, bf16[128,1024]{1,0:T(8,128)(2,1)S(1)}) custom-call(s32[4,8]{1,0:T(4,128)S(1)} %copy-done.2, bf16[4,128,1024]{2,1,0:T(8,128)(2,1)} %refs_1_.3), custom_call_target="tpu_custom_call" | custom-call | tf_op jit(solution)/shard_map/pick_cd_blocks/pallas_call | solution.py:94
  2.8 3.0 %collective-permute-start.3 = (bf16[128,1024]{1,0:T(8,128)(2,1)S(1)}, bf16[128,1024]{1,0:T(8,128)(2,1)S(1)}, u32[]{:S(2)}, u32[]{:S(2)}) collective-permute-start(bf16[128,1024]{1,0:T(8,128)(2,1)S(1)} %get-tuple-element.32), channel_id=1, source_target_pairs={{0,8},{1,17},{2,10},{3,19},{4,12},{5,21},{6,14},{7,23},{8,0},{9,25... | collective-permute-start | bytes 786440 | tf_op jit(solution)/shard_map/ppermute | solution.py:311
  5.8 1.5 %collective-permute-start.4 = (bf16[128,1024]{1,0:T(8,128)(2,1)S(1)}, bf16[128,1024]{1,0:T(8,128)(2,1)S(1)}, u32[]{:S(2)}, u32[]{:S(2)}) collective-permute-start(bf16[128,1024]{1,0:T(8,128)(2,1)S(1)} %get-tuple-element.33), channel_id=1, source_target_pairs={{0,16},{1,9},{2,18},{3,11},{4,20},{5,13},{6,22},{7,15},{8,24},{9,1... | collective-permute-start | bytes 786440 | tf_op jit(solution)/shard_map/ppermute | solution.py:311
  7.3 2.2 %contract_own_group.1 = (s16[32,1024]{1,0:T(8,128)(2,1)S(1)}, s16[32,1024]{1,0:T(8,128)(2,1)S(1)}, s16[32,1024]{1,0:T(8,128)(2,1)S(1)}, s16[32,1024]{1,0:T(8,128)(2,1)S(1)}, bf16[128,1024]{1,0:T(8,128)(2,1)S(1)}) custom-call(bf16[128,1024]{1,0:T(8,128)(2,1)S(1)} %get-tuple-element.26.refs_0_, bf16[1,1024,1024]{2,1,0:T(8,128)(2,1)} %refs_1_.4, ...), custom_call_target="tpu_custom_call" | custom-call | flops 268435456 | bytes 2097152 | tf_op jit(solution)/shard_map/contract_own_group/pallas_call | solution.py:135
  9.6 0.1 collective-permute-start.10
  9.6 2.0 %collective-permute-start = (s16[32,1024]{1,0:T(8,128)(2,1)S(1)}, s16[32,1024]{1,0:T(8,128)(2,1)S(1)}, u32[]{:S(2)}, u32[]{:S(2)}) collective-permute-start(s16[32,1024]{1,0:T(8,128)(2,1)S(1)} %get-tuple-element.29), channel_id=1, source_target_pairs={{0,2},{1,3},{2,0},{3,1},{4,6},{5,7},{6,4},{7,5},{8,10},{9,11},{10,... | collective-permute-start | bytes 196616 | tf_op jit(solution)/shard_map/ppermute | solution.py:311
  11.7 2.6 %collective-permute-start.1 = (s16[32,1024]{1,0:T(8,128)(2,1)S(1)}, s16[32,1024]{1,0:T(8,128)(2,1)S(1)}, u32[]{:S(2)}, u32[]{:S(2)}) collective-permute-start(s16[32,1024]{1,0:T(8,128)(2,1)S(1)} %get-tuple-element.30), channel_id=1, source_target_pairs={{0,4},{1,5},{2,6},{3,7},{4,0},{5,1},{6,2},{7,3},{8,12},{9,13},{10,... | collective-permute-start | bytes 196616 | tf_op jit(solution)/shard_map/ppermute | solution.py:311
  14.3 0.0 collective-permute-done.3.refs_0_
  14.3 2.7 %collective-permute-start.2 = (s16[32,1024]{1,0:T(8,128)(2,1)S(1)}, s16[32,1024]{1,0:T(8,128)(2,1)S(1)}, u32[]{:S(2)}, u32[]{:S(2)}) collective-permute-start(s16[32,1024]{1,0:T(8,128)(2,1)S(1)} %get-tuple-element.31), channel_id=1, source_target_pairs={{0,6},{1,7},{2,4},{3,5},{4,2},{5,3},{6,0},{7,1},{8,14},{9,15},{10,... | collective-permute-start | bytes 196616 | tf_op jit(solution)/shard_map/ppermute | solution.py:311
  17.0 0.0 collective-permute-done.4.refs_1_
  17.0 0.0 copy-done
  17.0 0.0 copy-start.1
  17.0 0.0 copy-start.3
  17.0 0.0 copy-start.4
  17.0 1.1 %contract_near_groups.1 = (s16[64,1024]{1,0:T(8,128)(2,1)S(1)}, s16[64,1024]{1,0:T(8,128)(2,1)S(1)}, s16[64,1024]{1,0:T(8,128)(2,1)S(1)}, s16[64,1024]{1,0:T(8,128)(2,1)S(1)}) custom-call(bf16[128,1024]{1,0:T(8,128)(2,1)S(1)} %collective-permute-done.3.refs_0_, bf16[128,1024]{1,0:T(8,128)(2,1)S(1)} %collective-permute-done.4.refs_1_, ...), custom_call_target="tpu_custom_call" | custom-call | flops 536870912 | bytes 2097152 | tf_op jit(solution)/shard_map/contract_near_groups/pallas_call | solution.py:163
  18.2 0.1 collective-permute-start.5
  18.2 0.0 collective-permute-done.refs_2_.refs_1_.refs_4_
  18.3 1.6 %collective-permute-start.6 = (s16[64,1024]{1,0:T(8,128)(2,1)S(1)}, s16[64,1024]{1,0:T(8,128)(2,1)S(1)}, u32[]{:S(2)}, u32[]{:S(2)}) collective-permute-start(s16[64,1024]{1,0:T(8,128)(2,1)S(1)} %get-tuple-element.36), channel_id=1, source_target_pairs={{0,4},{1,5},{2,6},{3,7},{4,0},{5,1},{6,2},{7,3},{8,12},{9,13},{10,... | collective-permute-start | bytes 393224 | tf_op jit(solution)/shard_map/ppermute | solution.py:311
  19.9 0.0 collective-permute-done.1.refs_3_.refs_2_.refs_5_
  19.9 2.7 %collective-permute-start.7 = (s16[64,1024]{1,0:T(8,128)(2,1)S(1)}, s16[64,1024]{1,0:T(8,128)(2,1)S(1)}, u32[]{:S(2)}, u32[]{:S(2)}) collective-permute-start(s16[64,1024]{1,0:T(8,128)(2,1)S(1)} %get-tuple-element.37), channel_id=1, source_target_pairs={{0,6},{1,7},{2,4},{3,5},{4,2},{5,3},{6,0},{7,1},{8,14},{9,15},{10,... | collective-permute-start | bytes 393224 | tf_op jit(solution)/shard_map/ppermute | solution.py:311
  22.6 0.0 collective-permute-done.2.refs_4_.refs_3_.refs_6_
  22.6 0.0 collective-permute-done.10.refs_0_
  22.6 0.7 %contract_far_group.1 = s16[128,1024]{1,0:T(8,128)(2,1)S(1)} custom-call(bf16[128,1024]{1,0:T(8,128)(2,1)S(1)} %collective-permute-done.10.refs_0_, bf16[1024,1024]{1,0:T(8,128)(2,1)S(1)} %bitcast.4, s16[32,1024]{1,0:T(8,128)(2,1)S(1)} %collective-permute-done.refs_2_.refs_1_.refs_4_, s16[32,1024]{1,0:T(8,128)(2,1)S(1)} %collective-permute-done.1.refs_3_.refs_2_.refs_5_, ...), custom_call_target="tpu_custom_call" | custom-call | flops 268435456 | bytes 2097152 | tf_op jit(solution)/shard_map/contract_far_group/pallas_call | solution.py:186
  23.4 2.6 %collective-permute-start.11 = (s16[128,1024]{1,0:T(8,128)(2,1)S(1)}, s16[128,1024]{1,0:T(8,128)(2,1)S(1)}, u32[]{:S(2)}, u32[]{:S(2)}) collective-permute-start(s16[128,1024]{1,0:T(8,128)(2,1)S(1)} %contract_far_group.1), channel_id=1, source_target_pairs={{0,24},{1,25},{2,26},{3,27},{4,28},{5,29},{6,30},{7,31},{8,16},{9,... | collective-permute-start | bytes 786440 | tf_op jit(solution)/shard_map/ppermute | solution.py:311
  26.0 0.0 collective-permute-done.5.refs_1_
  26.0 4.1 %collective-permute-done.6.refs_2_ = s16[64,1024]{1,0:T(8,128)(2,1)S(1)} collective-permute-done((s16[64,1024]{1,0:T(8,128)(2,1)S(1)}, s16[64,1024]{1,0:T(8,128)(2,1)S(1)}, u32[]{:S(2)}, u32[]{:S(2)}) %collective-permute-start.6) | collective-permute-done | bytes 131104 | tf_op jit(solution)/shard_map/ppermute | solution.py:311
  30.1 0.0 collective-permute-done.7.refs_3_
  30.1 1.6 %collective-permute-start.8 = (s16[128,1024]{1,0:T(8,128)(2,1)S(1)}, s16[128,1024]{1,0:T(8,128)(2,1)S(1)}, u32[]{:S(2)}, u32[]{:S(2)}) collective-permute-start(s16[128,1024]{1,0:T(8,128)(2,1)S(1)} %get-tuple-element.38), channel_id=1, source_target_pairs={{0,8},{1,17},{2,10},{3,19},{4,12},{5,21},{6,14},{7,23},{8,0},{9,25... | collective-permute-start | bytes 786440 | tf_op jit(solution)/shard_map/ppermute | solution.py:311
  31.7 0.9 %collective-permute-start.9 = (s16[128,1024]{1,0:T(8,128)(2,1)S(1)}, s16[128,1024]{1,0:T(8,128)(2,1)S(1)}, u32[]{:S(2)}, u32[]{:S(2)}) collective-permute-start(s16[128,1024]{1,0:T(8,128)(2,1)S(1)} %get-tuple-element.39), channel_id=1, source_target_pairs={{0,16},{1,9},{2,18},{3,11},{4,20},{5,13},{6,22},{7,15},{8,24},{9,1... | collective-permute-start | bytes 786440 | tf_op jit(solution)/shard_map/ppermute | solution.py:311
  32.6 0.0 collective-permute-done.11.refs_0_
  32.7 2.0 %collective-permute-start.12 = (s16[32,1024]{1,0:T(8,128)(2,1)S(1)}, s16[32,1024]{1,0:T(8,128)(2,1)S(1)}, u32[]{:S(2)}, u32[]{:S(2)}) collective-permute-start(s16[32,1024]{1,0:T(8,128)(2,1)S(1)} %get-tuple-element.42), channel_id=1, source_target_pairs={{0,2},{1,3},{2,0},{3,1},{4,6},{5,7},{6,4},{7,5},{8,10},{9,11},{10,... | collective-permute-start | bytes 196616 | tf_op jit(solution)/shard_map/ppermute | solution.py:311
  34.7 1.0 %collective-permute-start.13 = (s16[32,1024]{1,0:T(8,128)(2,1)S(1)}, s16[32,1024]{1,0:T(8,128)(2,1)S(1)}, u32[]{:S(2)}, u32[]{:S(2)}) collective-permute-start(s16[32,1024]{1,0:T(8,128)(2,1)S(1)} %get-tuple-element.43), channel_id=1, source_target_pairs={{0,4},{1,5},{2,6},{3,7},{4,0},{5,1},{6,2},{7,3},{8,12},{9,13},{10,... | collective-permute-start | bytes 196616 | tf_op jit(solution)/shard_map/ppermute | solution.py:311
  35.7 1.4 %collective-permute-start.14 = (s16[32,1024]{1,0:T(8,128)(2,1)S(1)}, s16[32,1024]{1,0:T(8,128)(2,1)S(1)}, u32[]{:S(2)}, u32[]{:S(2)}) collective-permute-start(s16[32,1024]{1,0:T(8,128)(2,1)S(1)} %get-tuple-element.44), channel_id=1, source_target_pairs={{0,6},{1,7},{2,4},{3,5},{4,2},{5,3},{6,0},{7,1},{8,14},{9,15},{10,... | collective-permute-start | bytes 196616 | tf_op jit(solution)/shard_map/ppermute | solution.py:311
  37.1 0.0 collective-permute-done.12.refs_7_.refs_10_
  37.1 3.6 %collective-permute-done.13.refs_8_.refs_11_ = s16[32,1024]{1,0:T(8,128)(2,1)S(1)} collective-permute-done((s16[32,1024]{1,0:T(8,128)(2,1)S(1)}, s16[32,1024]{1,0:T(8,128)(2,1)S(1)}, u32[]{:S(2)}, u32[]{:S(2)}) %collective-permute-start.13) | collective-permute-done | bytes 65568 | tf_op jit(solution)/shard_map/ppermute | solution.py:311
  40.7 1.2 %collective-permute-done.14.refs_9_.refs_12_ = s16[32,1024]{1,0:T(8,128)(2,1)S(1)} collective-permute-done((s16[32,1024]{1,0:T(8,128)(2,1)S(1)}, s16[32,1024]{1,0:T(8,128)(2,1)S(1)}, u32[]{:S(2)}, u32[]{:S(2)}) %collective-permute-start.14) | collective-permute-done | bytes 65568 | tf_op jit(solution)/shard_map/ppermute | solution.py:311
  41.9 0.0 collective-permute-done.8.refs_4_.refs_7_
  41.9 0.0 collective-permute-done.9.refs_5_.refs_8_
  42.0 0.1 collective-permute-start.15
  42.0 0.5 %collective-permute-start.16 = (s16[128,1024]{1,0:T(8,128)(2,1)S(1)}, s16[128,1024]{1,0:T(8,128)(2,1)S(1)}, u32[]{:S(2)}, u32[]{:S(2)}) collective-permute-start(s16[128,1024]{1,0:T(8,128)(2,1)S(1)} %get-tuple-element.46), channel_id=1, source_target_pairs={{0,1},{1,0},{2,3},{3,2},{4,5},{5,4},{6,7},{7,6},{8,9},{9,8},{10,11... | collective-permute-start | bytes 786440 | tf_op jit(solution)/shard_map/ppermute | solution.py:311
  42.5 1.0 %collective-permute-done.15.refs_13_ = s16[128,1024]{1,0:T(8,128)(2,1)S(1)} collective-permute-done((s16[128,1024]{1,0:T(8,128)(2,1)S(1)}, s16[128,1024]{1,0:T(8,128)(2,1)S(1)}, u32[]{:S(2)}, u32[]{:S(2)}) %collective-permute-start.15) | collective-permute-done | bytes 262176 | tf_op jit(solution)/shard_map/ppermute | solution.py:311
  43.6 0.4 collective-permute-done.16.refs_14_
  43.9 0.0 copy-done.1
  43.9 0.0 copy-done.3
  43.9 0.0 copy-done.4
  43.9 3.3 %add_contributions.1 = f32[50,16,1024]{2,1,0:T(8,128)} custom-call(s32[4,8]{1,0:T(4,128)S(1)} %copy-done.3, s32[4,8]{1,0:T(4,128)S(1)} %copy-done.2, s32[4,8]{1,0:T(4,128)S(1)} %copy-done.4, s16[32,1024]{1,0:T(8,128)(2,1)S(1)} %get-tuple-element.28.refs_0_.refs_3_, s16[32,1024]{1,0:T(8,128)(2,1)S(1)} %collective-permute-done.refs_2_.refs_1_.refs_4_, ...), custom_call_target="tpu_custom_call" | custom-call | tf_op jit(solution)/shard_map/add_contributions/pallas_call | solution.py:288
  (3 shorter events, 0.1 us)
Async XLA Ops:
  0.0 17.0 %copy-start = (bf16[1,1024,1024]{2,1,0:T(8,128)(2,1)S(1)}, bf16[1,1024,1024]{2,1,0:T(8,128)(2,1)}, u32[]{:S(2)}) copy-start(bf16[1,1024,1024]{2,1,0:T(8,128)(2,1)} %refs_1_.4) | copy-start | bytes 6291460
  0.0 0.8 %copy-start.2 = (s32[4,8]{1,0:T(4,128)S(1)}, s32[4,8]{1,0:T(4,128)}, u32[]{:S(2)}) copy-start(s32[4,8]{1,0:T(4,128)} %refs_1_.5) | copy-start | bytes 388
  2.8 11.5 %collective-permute-start.3 = (bf16[128,1024]{1,0:T(8,128)(2,1)S(1)}, bf16[128,1024]{1,0:T(8,128)(2,1)S(1)}, u32[]{:S(2)}, u32[]{:S(2)}) collective-permute-start(bf16[128,1024]{1,0:T(8,128)(2,1)S(1)} %get-tuple-element.32), channel_id=1, source_target_pairs={{0,8},{1,17},{2,10},{3,19},{4,12},{5,21},{6,14},{7,23},{8,0},{9,25... | collective-permute-start | bytes 786440 | tf_op jit(solution)/shard_map/ppermute | solution.py:311
  5.8 11.2 %collective-permute-start.4 = (bf16[128,1024]{1,0:T(8,128)(2,1)S(1)}, bf16[128,1024]{1,0:T(8,128)(2,1)S(1)}, u32[]{:S(2)}, u32[]{:S(2)}) collective-permute-start(bf16[128,1024]{1,0:T(8,128)(2,1)S(1)} %get-tuple-element.33), channel_id=1, source_target_pairs={{0,16},{1,9},{2,18},{3,11},{4,20},{5,13},{6,22},{7,15},{8,24},{9,1... | collective-permute-start | bytes 786440 | tf_op jit(solution)/shard_map/ppermute | solution.py:311
  9.6 13.1 %collective-permute-start.10 = (bf16[128,1024]{1,0:T(8,128)(2,1)S(1)}, bf16[128,1024]{1,0:T(8,128)(2,1)S(1)}, u32[]{:S(2)}, u32[]{:S(2)}) collective-permute-start(bf16[128,1024]{1,0:T(8,128)(2,1)S(1)} %get-tuple-element.40), channel_id=1, source_target_pairs={{0,24},{1,25},{2,26},{3,27},{4,28},{5,29},{6,30},{7,31},{8,16},{9,... | collective-permute-start | bytes 786440 | tf_op jit(solution)/shard_map/ppermute | solution.py:311
  9.6 8.6 %collective-permute-start = (s16[32,1024]{1,0:T(8,128)(2,1)S(1)}, s16[32,1024]{1,0:T(8,128)(2,1)S(1)}, u32[]{:S(2)}, u32[]{:S(2)}) collective-permute-start(s16[32,1024]{1,0:T(8,128)(2,1)S(1)} %get-tuple-element.29), channel_id=1, source_target_pairs={{0,2},{1,3},{2,0},{3,1},{4,6},{5,7},{6,4},{7,5},{8,10},{9,11},{10,... | collective-permute-start | bytes 196616 | tf_op jit(solution)/shard_map/ppermute | solution.py:311
  11.7 8.2 %collective-permute-start.1 = (s16[32,1024]{1,0:T(8,128)(2,1)S(1)}, s16[32,1024]{1,0:T(8,128)(2,1)S(1)}, u32[]{:S(2)}, u32[]{:S(2)}) collective-permute-start(s16[32,1024]{1,0:T(8,128)(2,1)S(1)} %get-tuple-element.30), channel_id=1, source_target_pairs={{0,4},{1,5},{2,6},{3,7},{4,0},{5,1},{6,2},{7,3},{8,12},{9,13},{10,... | collective-permute-start | bytes 196616 | tf_op jit(solution)/shard_map/ppermute | solution.py:311
  14.3 8.4 %collective-permute-start.2 = (s16[32,1024]{1,0:T(8,128)(2,1)S(1)}, s16[32,1024]{1,0:T(8,128)(2,1)S(1)}, u32[]{:S(2)}, u32[]{:S(2)}) collective-permute-start(s16[32,1024]{1,0:T(8,128)(2,1)S(1)} %get-tuple-element.31), channel_id=1, source_target_pairs={{0,6},{1,7},{2,4},{3,5},{4,2},{5,3},{6,0},{7,1},{8,14},{9,15},{10,... | collective-permute-start | bytes 196616 | tf_op jit(solution)/shard_map/ppermute | solution.py:311
  17.0 26.9 %copy-start.1 = (f32[16,50,1024]{2,0,1:T(8,128)S(1)}, f32[16,50,1024]{2,0,1:T(8,128)}, u32[]{:S(2)}) copy-start(f32[16,50,1024]{2,0,1:T(8,128)} %param.11) | copy-start | bytes 9830404
  17.0 26.9 %copy-start.3 = (s32[4,8]{1,0:T(4,128)S(1)}, s32[4,8]{1,0:T(4,128)}, u32[]{:S(2)}) copy-start(s32[4,8]{1,0:T(4,128)} %refs_0_.3) | copy-start | bytes 388
  17.0 26.9 %copy-start.4 = (s32[4,8]{1,0:T(4,128)S(1)}, s32[4,8]{1,0:T(4,128)}, u32[]{:S(2)}) copy-start(s32[4,8]{1,0:T(4,128)} %refs_2_.1) | copy-start | bytes 388
  18.2 7.8 %collective-permute-start.5 = (s16[64,1024]{1,0:T(8,128)(2,1)S(1)}, s16[64,1024]{1,0:T(8,128)(2,1)S(1)}, u32[]{:S(2)}, u32[]{:S(2)}) collective-permute-start(s16[64,1024]{1,0:T(8,128)(2,1)S(1)} %get-tuple-element.35), channel_id=1, source_target_pairs={{0,2},{1,3},{2,0},{3,1},{4,6},{5,7},{6,4},{7,5},{8,10},{9,11},{10,... | collective-permute-start | bytes 393224 | tf_op jit(solution)/shard_map/ppermute | solution.py:311
  18.3 11.8 %collective-permute-start.6 = (s16[64,1024]{1,0:T(8,128)(2,1)S(1)}, s16[64,1024]{1,0:T(8,128)(2,1)S(1)}, u32[]{:S(2)}, u32[]{:S(2)}) collective-permute-start(s16[64,1024]{1,0:T(8,128)(2,1)S(1)} %get-tuple-element.36), channel_id=1, source_target_pairs={{0,4},{1,5},{2,6},{3,7},{4,0},{5,1},{6,2},{7,3},{8,12},{9,13},{10,... | collective-permute-start | bytes 393224 | tf_op jit(solution)/shard_map/ppermute | solution.py:311
  19.9 10.2 %collective-permute-start.7 = (s16[64,1024]{1,0:T(8,128)(2,1)S(1)}, s16[64,1024]{1,0:T(8,128)(2,1)S(1)}, u32[]{:S(2)}, u32[]{:S(2)}) collective-permute-start(s16[64,1024]{1,0:T(8,128)(2,1)S(1)} %get-tuple-element.37), channel_id=1, source_target_pairs={{0,6},{1,7},{2,4},{3,5},{4,2},{5,3},{6,0},{7,1},{8,14},{9,15},{10,... | collective-permute-start | bytes 393224 | tf_op jit(solution)/shard_map/ppermute | solution.py:311
  23.4 9.3 %collective-permute-start.11 = (s16[128,1024]{1,0:T(8,128)(2,1)S(1)}, s16[128,1024]{1,0:T(8,128)(2,1)S(1)}, u32[]{:S(2)}, u32[]{:S(2)}) collective-permute-start(s16[128,1024]{1,0:T(8,128)(2,1)S(1)} %contract_far_group.1), channel_id=1, source_target_pairs={{0,24},{1,25},{2,26},{3,27},{4,28},{5,29},{6,30},{7,31},{8,16},{9,... | collective-permute-start | bytes 786440 | tf_op jit(solution)/shard_map/ppermute | solution.py:311
  30.1 11.8 %collective-permute-start.8 = (s16[128,1024]{1,0:T(8,128)(2,1)S(1)}, s16[128,1024]{1,0:T(8,128)(2,1)S(1)}, u32[]{:S(2)}, u32[]{:S(2)}) collective-permute-start(s16[128,1024]{1,0:T(8,128)(2,1)S(1)} %get-tuple-element.38), channel_id=1, source_target_pairs={{0,8},{1,17},{2,10},{3,19},{4,12},{5,21},{6,14},{7,23},{8,0},{9,25... | collective-permute-start | bytes 786440 | tf_op jit(solution)/shard_map/ppermute | solution.py:311
  31.7 10.2 %collective-permute-start.9 = (s16[128,1024]{1,0:T(8,128)(2,1)S(1)}, s16[128,1024]{1,0:T(8,128)(2,1)S(1)}, u32[]{:S(2)}, u32[]{:S(2)}) collective-permute-start(s16[128,1024]{1,0:T(8,128)(2,1)S(1)} %get-tuple-element.39), channel_id=1, source_target_pairs={{0,16},{1,9},{2,18},{3,11},{4,20},{5,13},{6,22},{7,15},{8,24},{9,1... | collective-permute-start | bytes 786440 | tf_op jit(solution)/shard_map/ppermute | solution.py:311
  32.7 4.5 %collective-permute-start.12 = (s16[32,1024]{1,0:T(8,128)(2,1)S(1)}, s16[32,1024]{1,0:T(8,128)(2,1)S(1)}, u32[]{:S(2)}, u32[]{:S(2)}) collective-permute-start(s16[32,1024]{1,0:T(8,128)(2,1)S(1)} %get-tuple-element.42), channel_id=1, source_target_pairs={{0,2},{1,3},{2,0},{3,1},{4,6},{5,7},{6,4},{7,5},{8,10},{9,11},{10,... | collective-permute-start | bytes 196616 | tf_op jit(solution)/shard_map/ppermute | solution.py:311
  34.7 6.0 %collective-permute-start.13 = (s16[32,1024]{1,0:T(8,128)(2,1)S(1)}, s16[32,1024]{1,0:T(8,128)(2,1)S(1)}, u32[]{:S(2)}, u32[]{:S(2)}) collective-permute-start(s16[32,1024]{1,0:T(8,128)(2,1)S(1)} %get-tuple-element.43), channel_id=1, source_target_pairs={{0,4},{1,5},{2,6},{3,7},{4,0},{5,1},{6,2},{7,3},{8,12},{9,13},{10,... | collective-permute-start | bytes 196616 | tf_op jit(solution)/shard_map/ppermute | solution.py:311
  35.7 6.2 %collective-permute-start.14 = (s16[32,1024]{1,0:T(8,128)(2,1)S(1)}, s16[32,1024]{1,0:T(8,128)(2,1)S(1)}, u32[]{:S(2)}, u32[]{:S(2)}) collective-permute-start(s16[32,1024]{1,0:T(8,128)(2,1)S(1)} %get-tuple-element.44), channel_id=1, source_target_pairs={{0,6},{1,7},{2,4},{3,5},{4,2},{5,3},{6,0},{7,1},{8,14},{9,15},{10,... | collective-permute-start | bytes 196616 | tf_op jit(solution)/shard_map/ppermute | solution.py:311
  42.0 1.6 %collective-permute-start.15 = (s16[128,1024]{1,0:T(8,128)(2,1)S(1)}, s16[128,1024]{1,0:T(8,128)(2,1)S(1)}, u32[]{:S(2)}, u32[]{:S(2)}) collective-permute-start(s16[128,1024]{1,0:T(8,128)(2,1)S(1)} %get-tuple-element.45), channel_id=1, source_target_pairs={{0,1},{1,0},{2,3},{3,2},{4,5},{5,4},{6,7},{7,6},{8,9},{9,8},{10,11... | collective-permute-start | bytes 786440 | tf_op jit(solution)/shard_map/ppermute | solution.py:311
  42.0 1.9 %collective-permute-start.16 = (s16[128,1024]{1,0:T(8,128)(2,1)S(1)}, s16[128,1024]{1,0:T(8,128)(2,1)S(1)}, u32[]{:S(2)}, u32[]{:S(2)}) collective-permute-start(s16[128,1024]{1,0:T(8,128)(2,1)S(1)} %get-tuple-element.46), channel_id=1, source_target_pairs={{0,1},{1,0},{2,3},{3,2},{4,5},{5,4},{6,7},{7,6},{8,9},{9,8},{10,11... | collective-permute-start | bytes 786440 | tf_op jit(solution)/shard_map/ppermute | solution.py:311

commit v15 on v11

--- a/solution.py
+++ b/solution.py
@@ -14,7 +14,6 @@
 LANES = 128
 CORES = 2
 MEBIBYTE = 1 << 20
-PICK_LIMIT = 209 * MEBIBYTE // 4
 SMEM = pl.BlockSpec(memory_space=pltpu.SMEM)
 VMEM = pl.BlockSpec(memory_space=pltpu.VMEM)
 ANY = pl.BlockSpec(memory_space=pl.ANY)
@@ -62,7 +61,7 @@
 
 
 def chip_steps(chips):
-    return [0] + list(reversed(range(1, chips)))
+    return list(range(chips))
 
 
 def start_all(copies):
@@ -95,7 +94,7 @@
         in_specs=[SMEM, ANY],
         out_specs=[VMEM] * groups,
         scratch_shapes=[pltpu.SemaphoreType.DMA((groups,))],
-        compiler_params=pltpu.CompilerParams(vmem_limit_bytes=PICK_LIMIT),
+        compiler_params=vmem_limit(*[block] * groups),
         name="pick_cd_blocks",
     )(tile_cd, amplitudes)
 
@@ -182,25 +181,25 @@
     )(rows, tile, *earlier)
 
 
-def regroup_kernel(count, *refs):
-    sources, targets = refs[:count], refs[count:]
-    part_rows = sources[0].shape[0] // len(targets)
+def regroup_kernel(count, parts, *refs):
+    sources, targets = refs[:count], refs[-parts:]
+    part_rows = sources[0].shape[0] // parts
     for j, source in enumerate(sources):
         for i, target in enumerate(targets):
             target[j * part_rows : (j + 1) * part_rows, :] = source[i * part_rows : (i + 1) * part_rows, :]
 
 
-def regroup(sources, parts, name):
+def regroup(sources, parts, name, earlier=()):
     rows, tile_width = sources[0].shape
     target = jax.ShapeDtypeStruct((len(sources) * rows // parts, tile_width), sources[0].dtype)
     return pl.pallas_call(
-        lambda *refs: regroup_kernel(len(sources), *refs),
+        lambda *refs: regroup_kernel(len(sources), parts, *refs),
         out_shape=[target] * parts,
-        in_specs=[VMEM] * len(sources),
+        in_specs=[VMEM] * len(sources) + [ANY] * len(earlier),
         out_specs=[VMEM] * parts,
         compiler_params=vmem_limit(*sources, *[target] * parts),
         name=name,
-    )(*sources)
+    )(*sources, *earlier)
 
 
 def pieces_of(arrays, owner_rows):
@@ -215,55 +214,82 @@
         halves[index * owner_rows : (index + 1) * owner_rows, :] = arrays[array][pl.ds(source, owner_rows), :]
 
 
-def other_core_rows(arrays, pieces, owner_rows):
+def other_core_rows(arrays, pieces, owner_rows, earlier=()):
     halves = jax.ShapeDtypeStruct((len(pieces) * owner_rows, arrays[0].shape[1]), arrays[0].dtype)
     return pl.pallas_call(
         lambda *refs: other_core_kernel(pieces, owner_rows, *refs),
         out_shape=halves,
-        in_specs=[VMEM] * len(arrays),
+        in_specs=[VMEM] * len(arrays) + [ANY] * len(earlier),
         out_specs=VMEM,
         compiler_params=vmem_limit(*arrays, halves),
         name="rows_of_other_core",
-    )(*arrays)
-
-
-def add_rows(rows, tables, blk, grp, held):
+    )(*arrays, *earlier)
+
+
+def write_kernel(parts, residual_in, *rest):
+    residual, token, sems = rest[-3:]
+    token[...] = jnp.zeros_like(token)
+    ab_tiles = residual.shape[0]
+    bounds = [ab_tiles * part // parts for part in range(parts + 1)]
+    spans = [pl.ds(low, high - low) for low, high in zip(bounds[:-1], bounds[1:])]
+    copies = [pltpu.make_async_copy(residual_in.at[span], residual.at[span], sems.at[i]) for i, span in enumerate(spans)]
+    start_all(copies)
+    wait_all(copies)
+
+
+def write_residual(residual_in, earlier):
+    parts = 5
+    token = jax.ShapeDtypeStruct((8, LANES), jnp.int32)
+    return pl.pallas_call(
+        lambda *refs: write_kernel(parts, *refs),
+        out_shape=[jax.ShapeDtypeStruct(residual_in.shape, residual_in.dtype), token],
+        in_specs=[VMEM] + [ANY] * len(earlier),
+        out_specs=[ANY, VMEM],
+        scratch_shapes=[pltpu.SemaphoreType.DMA((parts,))],
+        compiler_params=vmem_limit(residual_in),
+        name="write_residual",
+    )(residual_in, *earlier)
+
+
+def tiles_of(count, core, tile_ab):
+    blk, grp = lax.axis_index("blk"), lax.axis_index("grp")
+    blk_count, chips = tile_ab.shape[0], tile_ab.shape[1] // CORES
+    tiles = []
+    for index in range(count):
+        step = blk_steps(blk_count, core)[index // chips]
+        chip = jnp.bitwise_xor(grp // CORES, chip_steps(chips)[index % chips])
+        tiles.append((jnp.bitwise_xor(blk, step), chip * CORES + core))
+    return tiles
+
+
+def add_rows(tables, sources, tiles, held):
     tile_ab, tile_cd, pair_screen = tables
-    terms = []
-    for source, span, p, g in rows:
-        kept = pair_screen[tile_cd[p, g], grp].astype(jnp.float32)
-        terms.append((source, span, row_scale(source[span, :LANES]) * kept, tile_ab[p, g]))
-    for source, span, scale, ab in terms:
-        for lane in range(0, held.shape[2], LANES):
-            term = source[span, lane : lane + LANES].astype(jnp.float32) * scale
-            held[ab, :, lane : lane + LANES] = held[ab, :, lane : lane + LANES] + term
-
-
-def tile_of(index, blk, grp, core, chips, blk_count):
-    p = jnp.bitwise_xor(blk, blk_steps(blk_count, core)[index // chips])
-    chip_step = chip_steps(chips)[index % chips]
-    return p, (jnp.bitwise_xor(grp // CORES, chip_step)) * CORES + core
-
-
-def add_here_kernel(pieces, tile_ab, tile_cd, pair_screen, *rest):
-    arrays, residual_in, held = rest[:-2], rest[-2], rest[-1]
-    blk, grp = lax.axis_index("blk"), lax.axis_index("grp")
-    ab_tiles, owner_rows, _ = held.shape
-    blk_count, chips = tile_ab.shape[0], tile_ab.shape[1] // CORES
-    core = grp % CORES
+    grp = lax.axis_index("grp")
+    group = 8
+    for start in range(0, len(sources), group):
+        terms = []
+        for (source, span), (p, g) in zip(sources[start : start + group], tiles[start : start + group]):
+            kept = pair_screen[tile_cd[p, g], grp].astype(jnp.float32)
+            terms.append((source, span, row_scale(source[span, :LANES]) * kept, tile_ab[p, g]))
+        for source, span, scale, ab in terms:
+            for lane in range(0, held.shape[2], LANES):
+                term = source[span, lane : lane + LANES].astype(jnp.float32) * scale
+                held[ab, :, lane : lane + LANES] = held[ab, :, lane : lane + LANES] + term
+
+
+def add_here_kernel(pieces, *refs):
+    tables, arrays, (residual_in, held) = refs[:3], refs[3:-2], refs[-2:]
+    core = lax.axis_index("grp") % CORES
+    owner_rows = held.shape[1]
 
     def hold(ab, carry):
         held[ab] = residual_in[ab]
         return carry
 
-    lax.fori_loop(0, ab_tiles, hold, 0)
-    for start in range(0, len(pieces), 2 * chips):
-        rows = []
-        for index in range(start, min(start + 2 * chips, len(pieces))):
-            array, first = pieces[index]
-            span = pl.ds(pl.multiple_of(first + core * owner_rows, owner_rows), owner_rows)
-            rows.append((arrays[array], span, *tile_of(index, blk, grp, core, chips, blk_count)))
-        add_rows(rows, (tile_ab, tile_cd, pair_screen), blk, grp, held)
+    lax.fori_loop(0, held.shape[0], hold, 0)
+    spans = [pl.ds(pl.multiple_of(first + core * owner_rows, owner_rows), owner_rows) for _, first in pieces]
+    sources = [(arrays[array], span) for (array, _), span in zip(pieces, spans)]
+    add_rows(tables, sources, tiles_of(len(pieces), core, tables[0]), held)
 
 
 def add_here(tables, arrays, pieces, residual_in):
@@ -277,55 +303,57 @@
     )(*tables, *arrays, residual_in)
 
 
-def add_there_kernel(parts, tile_ab, tile_cd, pair_screen, swapped, partial, residual, held, touched, part_sems, tile_sems):
-    blk, grp = lax.axis_index("blk"), lax.axis_index("grp")
-    ab_tiles, owner_rows, _ = residual.shape
-    blk_count, chips = tile_ab.shape[0], tile_ab.shape[1] // CORES
-    core = 1 - grp % CORES
-    bounds = [ab_tiles * part // parts for part in range(parts + 1)]
-    spans = [pl.ds(low, high - low) for low, high in zip(bounds[:-1], bounds[1:])]
-    bulk = [pltpu.make_async_copy(partial.at[span], residual.at[span], part_sems.at[i]) for i, span in enumerate(spans)]
-    start_all(bulk)
+def add_there_kernel(count, *refs):
+    tables, (swapped, partial, _, residual, held, touched, sems) = refs[:3], refs[3:]
+    core = lax.axis_index("grp") % CORES
+    owner_rows = held.shape[1]
+    here, there = tiles_of(count, core, tables[0]), tiles_of(count, 1 - core, tables[0])
 
     def clear(ab, carry):
         touched[ab] = 0
         return carry
 
-    lax.fori_loop(0, ab_tiles, clear, 0)
-    rows, fresh = [], []
-    for index in range(blk_count * chips):
-        span = pl.ds(index * owner_rows, owner_rows)
-        rows.append((swapped, span, *tile_of(index, blk, grp, core, chips, blk_count)))
-    for _, _, p, g in rows:
-        ab = tile_ab[p, g]
-        fresh.append((ab, touched[ab] == 0))
+    def first_touch(tile):
+        ab = tables[0][tile]
+        fresh = touched[ab] == 0
         touched[ab] = 1
+        return ab, fresh
+
+    def copies_do(action, source, touches, first):
+        for index, (ab, fresh) in enumerate(touches):
+            copy = pltpu.make_async_copy(source.at[ab], residual.at[ab], sems.at[first + index])
+            pl.when(fresh)(getattr(copy, action))
+
+    lax.fori_loop(0, residual.shape[0], clear, 0)
+    late = [first_touch(tile) for tile in there]
+    early = [first_touch(tile) for tile in here]
+    copies_do("start", partial, early, count)
+    for ab, _ in late:
         held[ab] = partial[ab]
-    for start in range(0, len(rows), 2 * chips):
-        add_rows(rows[start : start + 2 * chips], (tile_ab, tile_cd, pair_screen), blk, grp, held)
-    wait_all(bulk)
-    for action in ("start", "wait"):
-        for index, (ab, first) in enumerate(fresh):
-            copy = pltpu.make_async_copy(held.at[ab], residual.at[ab], tile_sems.at[index])
-            pl.when(first)(getattr(copy, action))
-
-
-def add_there(tables, swapped, partial):
-    parts, owner_rows = 5, partial.shape[1]
-    return pl.pallas_call(
-        lambda *refs: add_there_kernel(parts, *refs),
-        out_shape=jax.ShapeDtypeStruct(partial.shape, partial.dtype),
-        in_specs=[SMEM] * 3 + [VMEM] * 2,
+    sources = [(swapped, pl.ds(index * owner_rows, owner_rows)) for index in range(count)]
+    add_rows(tables, sources, there, held)
+    copies_do("start", held, late, 0)
+    copies_do("wait", partial, early, count)
+    copies_do("wait", held, late, 0)
+
+
+def add_there(tables, swapped, partial, written):
+    whole = jax.ShapeDtypeStruct(partial.shape, partial.dtype)
+    count = swapped.shape[0] // partial.shape[1]
+    return pl.pallas_call(
+        lambda *refs: add_there_kernel(count, *refs),
+        out_shape=whole,
+        in_specs=[SMEM] * 3 + [VMEM] * 2 + [ANY],
         out_specs=ANY,
         scratch_shapes=[
-            pltpu.VMEM(partial.shape, partial.dtype),
-            pltpu.SMEM((partial.shape[0],), jnp.int32),
-            pltpu.SemaphoreType.DMA((parts,)),
-            pltpu.SemaphoreType.DMA((swapped.shape[0] // owner_rows,)),
+            pltpu.VMEM(whole.shape, whole.dtype),
+            pltpu.SMEM(whole.shape[:1], jnp.int32),
+            pltpu.SemaphoreType.DMA((2 * count,)),
         ],
+        input_output_aliases={5: 0},
         compiler_params=vmem_limit(swapped, partial, partial),
         name="add_contributions_there",
-    )(*tables, swapped, partial)
+    )(*tables, swapped, partial, written)
 
 
 def shards(amplitudes, pair_screen, integrals, tile_ab, tile_cd, residual_in):
@@ -352,16 +380,19 @@
     own_in = along_chips(own_out)
     far_rows = swap(far_picked, far, 0)
     near_in = along_chips(contract_near(near_rows, tile, chips))
-    near_back = regroup(near_in, blk_count - 2, "regroup_by_group")
+    by_tile = jnp.transpose(residual_in, (1, 0, 2))
+    far_coded = contract_far(far_rows, tile, chips, own_in[1:])
+    written, token = write_residual(by_tile, [far_coded])
+    near_back = regroup(near_in, blk_count - 2, "regroup_by_group", [token])
     near_in = [swap(rows, index + 1, 0) for index, rows in enumerate(near_back)]
-    far_back = swap(contract_far(far_rows, tile, chips, own_in[1:]), far, 0)
-    far_in = along_chips(regroup([far_back], chips, "regroup_by_chip"))
+    far_in = along_chips(regroup([swap(far_coded, far, 0)], chips, "regroup_by_chip"))
+
+    tables = (tile_ab, tile_cd, pair_screen)
     arrays = [*own_in, *near_in, *far_in]
     pieces = pieces_of(arrays, owner_rows)
     swapped = swap(other_core_rows(arrays, pieces, owner_rows), 0, 0, 1)
-    tables = (tile_ab, tile_cd, pair_screen)
-    partial = add_here(tables, arrays, pieces, jnp.transpose(residual_in, (1, 0, 2)))
-    return jnp.transpose(add_there(tables, swapped, partial), (1, 0, 2))
+    partial = add_here(tables, arrays, pieces, by_tile)
+    return jnp.transpose(add_there(tables, swapped, partial, written), (1, 0, 2))
 
 
 def solution(mesh):

time: 47.3 us -> 46.6 us (0.985)
  waiting for transfers between devices: 12.4 us -> 7.78 us
  starting transfers between devices: 23.1 us -> 26 us
  local copies, waits for them, and re-layouts: 2.28 us -> 3.52 us
    ppermute x16, waiting for transfers between devices: 12.4 us -> 7.78 us  [swap(): return lax.ppermute(value, ('blk', 'grp'), pairs)]
    ppermute x16, starting transfers between devices: 23.1 us -> 26 us  [swap(): return lax.ppermute(value, ('blk', 'grp'), pairs)]
    unnamed x10 -> x14, local copies, waits for them, and re-layouts: 2.28 us -> 3.52 us
    pallas_call x1, Pallas kernels: 1.8 us -> 0.7 us  [pick(): pl.pallas_call(pick_kernel, out_shape=[block] * groups, in_specs=[SMEM, A...]
    pallas_call x3 -> x4, Pallas kernels: 3.44 us -> 4.23 us  [the longest x1 2.44 us: add_there(): pl.pallas_call(lambda *refs: add_there_kernel(count, *refs), out_shape=wh...]
  transfers between devices with their start and end apart: 16 -> 16, of which waited for: 6 -> 5; matrix products, arithmetic and copies ran while one was open for 0% -> 0% of each run, Pallas kernels for 8% -> 12%
where the time goes in v15:
time: 46.6 us; the launch traced here: 46.4 us
  starting transfers between devices  26 us (56%)
  Pallas kernels  8.88 us (19%)
  waiting for transfers between devices  7.78 us (17%)
  local copies, waits for them, and re-layouts  3.52 us (8%)
    ppermute x16, starting transfers between devices, swap(): return lax.ppermute(value, ('blk', 'grp'), pairs)  26 us
    ppermute x16, waiting for transfers between devices, swap(): return lax.ppermute(value, ('blk', 'grp'), pairs)  7.78 us
    unnamed x14, local copies, waits for them, and re-layouts  3.52 us
    pallas_call x1, Pallas kernels, add_there(): pl.pallas_call(lambda *refs: add_there_kernel(count, *refs), out_shape=wh...  2.44 us
    pallas_call x1, Pallas kernels, write_residual(): pl.pallas_call(lambda *refs: write_kernel(parts, *refs), out_shape=[jax.S...  1.74 us
    pallas_call x1, Pallas kernels, add_here(): pl.pallas_call(lambda *refs: add_here_kernel(pieces, *refs), out_shape=ja...  1.2 us
    pallas_call x1, Pallas kernels, contract_near(): pl.pallas_call(lambda *refs: near_kernel(len(groups), *refs), out_shape=[...  1.13 us
  transfers between devices with their start and end apart: 16, of which 5 were waited for; matrix products, arithmetic and copies ran while one was open for 0% of the time, Pallas kernels for 12%

profile of v15, /device:TPU:0, one launch (start us, length us, event | category | flops | bytes accessed | tf_op | source)
XLA Modules:
  0.0 46.4 jit_solution(2818512631665724712)
XLA Ops:
  0.0 0.0 copy-start.2
  0.0 1.2 %copy-done.2 = bf16[4,128,1024]{2,1,0:T(8,128)(2,1)S(1)} copy-done((bf16[4,128,1024]{2,1,0:T(8,128)(2,1)S(1)}, bf16[4,128,1024]{2,1,0:T(8,128)(2,1)}, u32[]{:S(2)}) %copy-start.2) | copy-done | bytes 1048600
  1.2 0.0 copy-start.3
  1.2 0.7 %copy-done.3 = s32[4,8]{1,0:T(4,128)S(1)} copy-done((s32[4,8]{1,0:T(4,128)S(1)}, s32[4,8]{1,0:T(4,128)}, u32[]{:S(2)}) %copy-start.3) | copy-done | bytes 152
  1.9 0.7 %pick_cd_blocks.1 = (bf16[128,1024]{1,0:T(8,128)(2,1)S(1)}, bf16[128,1024]{1,0:T(8,128)(2,1)S(1)}, bf16[128,1024]{1,0:T(8,128)(2,1)S(1)}, bf16[128,1024]{1,0:T(8,128)(2,1)S(1)}) custom-call(s32[4,8]{1,0:T(4,128)S(1)} %copy-done.3, bf16[4,128,1024]{2,1,0:T(8,128)(2,1)S(1)} %copy-done.2), custom_call_target="tpu_custom_call" | custom-call | tf_op jit(solution)/shard_map/pick_cd_blocks/pallas_call | solution.py:91
  2.6 3.0 %collective-permute-start.3 = (bf16[128,1024]{1,0:T(8,128)(2,1)S(1)}, bf16[128,1024]{1,0:T(8,128)(2,1)S(1)}, u32[]{:S(2)}, u32[]{:S(2)}) collective-permute-start(bf16[128,1024]{1,0:T(8,128)(2,1)S(1)} %get-tuple-element.33), channel_id=1, source_target_pairs={{0,8},{1,17},{2,10},{3,19},{4,12},{5,21},{6,14},{7,23},{8,0},{9,25... | collective-permute-start | bytes 786440 | tf_op jit(solution)/shard_map/ppermute | solution.py:371
  5.6 1.5 %collective-permute-start.4 = (bf16[128,1024]{1,0:T(8,128)(2,1)S(1)}, bf16[128,1024]{1,0:T(8,128)(2,1)S(1)}, u32[]{:S(2)}, u32[]{:S(2)}) collective-permute-start(bf16[128,1024]{1,0:T(8,128)(2,1)S(1)} %get-tuple-element.34), channel_id=1, source_target_pairs={{0,16},{1,9},{2,18},{3,11},{4,20},{5,13},{6,22},{7,15},{8,24},{9,1... | collective-permute-start | bytes 786440 | tf_op jit(solution)/shard_map/ppermute | solution.py:371
  7.1 0.0 copy-start.1
  7.1 1.6 %copy-done.1 = bf16[1,1024,1024]{2,1,0:T(8,128)(2,1)S(1)} copy-done((bf16[1,1024,1024]{2,1,0:T(8,128)(2,1)S(1)}, bf16[1,1024,1024]{2,1,0:T(8,128)(2,1)}, u32[]{:S(2)}) %copy-start.1) | copy-done | bytes 2097176
  8.7 0.9 %contract_own_group.1 = (s16[32,1024]{1,0:T(8,128)(2,1)S(1)}, s16[32,1024]{1,0:T(8,128)(2,1)S(1)}, s16[32,1024]{1,0:T(8,128)(2,1)S(1)}, s16[32,1024]{1,0:T(8,128...) custom-call(bf16[128,1024]{1,0:T(8,128)(2,1)S(1)} %get-tuple-element.27.rows, ...), custom_call_target="tpu_custom_call" | custom-call | flops 268435456 | bytes 2097152 | tf_op jit(solution)/shard_map/contract_own_group/pallas_call | solution.py:127
  9.6 0.0 copy-start
  9.6 0.1 collective-permute-start.8
  9.7 2.0 %collective-permute-start = (s16[32,1024]{1,0:T(8,128)(2,1)S(1)}, s16[32,1024]{1,0:T(8,128)(2,1)S(1)}, u32[]{:S(2)}, u32[]{:S(2)}) collective-permute-start(s16[32,1024]{1,0:T(8,128)(2,1)S(1)} %get-tuple-element.30), channel_id=1, source_target_pairs={{0,2},{1,3},{2,0},{3,1},{4,6},{5,7},{6,4},{7,5},{8,10},{9,11},{10,... | collective-permute-start | bytes 196616 | tf_op jit(solution)/shard_map/ppermute | solution.py:371
  11.7 2.6 %collective-permute-start.1 = (s16[32,1024]{1,0:T(8,128)(2,1)S(1)}, s16[32,1024]{1,0:T(8,128)(2,1)S(1)}, u32[]{:S(2)}, u32[]{:S(2)}) collective-permute-start(s16[32,1024]{1,0:T(8,128)(2,1)S(1)} %get-tuple-element.31), channel_id=1, source_target_pairs={{0,4},{1,5},{2,6},{3,7},{4,0},{5,1},{6,2},{7,3},{8,12},{9,13},{10,... | collective-permute-start | bytes 196616 | tf_op jit(solution)/shard_map/ppermute | solution.py:371
  14.3 0.0 collective-permute-done.3.refs_0_
  14.3 2.5 %collective-permute-start.2 = (s16[32,1024]{1,0:T(8,128)(2,1)S(1)}, s16[32,1024]{1,0:T(8,128)(2,1)S(1)}, u32[]{:S(2)}, u32[]{:S(2)}) collective-permute-start(s16[32,1024]{1,0:T(8,128)(2,1)S(1)} %get-tuple-element.32), channel_id=1, source_target_pairs={{0,6},{1,7},{2,4},{3,5},{4,2},{5,3},{6,0},{7,1},{8,14},{9,15},{10,... | collective-permute-start | bytes 196616 | tf_op jit(solution)/shard_map/ppermute | solution.py:371
  16.8 0.0 collective-permute-done.4.refs_1_
  16.8 1.1 %contract_near_groups.1 = (s16[64,1024]{1,0:T(8,128)(2,1)S(1)}, s16[64,1024]{1,0:T(8,128)(2,1)S(1)}, s16[64,1024]{1,0:T(8,128)(2,1)S(1)}, s16[64,1024]{1,0:T(8,128)(2,1)S(1)}) custom-call(bf16[128,1024]{1,0:T(8,128)(2,1)S(1)} %collective-permute-done.3.refs_0_, bf16[128,1024]{1,0:T(8,128)(2,1)S(1)} %collective-permute-done.4.refs_1_, ...), custom_call_target="tpu_custom_call" | custom-call | flops 536870912 | bytes 2097152 | tf_op jit(solution)/shard_map/contract_near_groups/pallas_call | solution.py:150
  17.9 0.1 collective-permute-start.5
  18.0 0.0 collective-permute-done.refs_2_.refs_1_.refs_4_
  18.0 1.9 %collective-permute-start.6 = (s16[64,1024]{1,0:T(8,128)(2,1)S(1)}, s16[64,1024]{1,0:T(8,128)(2,1)S(1)}, u32[]{:S(2)}, u32[]{:S(2)}) collective-permute-start(s16[64,1024]{1,0:T(8,128)(2,1)S(1)} %get-tuple-element.38), channel_id=1, source_target_pairs={{0,4},{1,5},{2,6},{3,7},{4,0},{5,1},{6,2},{7,3},{8,12},{9,13},{10,... | collective-permute-start | bytes 393224 | tf_op jit(solution)/shard_map/ppermute | solution.py:371
  19.9 0.0 collective-permute-done.1.refs_3_.refs_2_.refs_5_
  19.9 2.5 %collective-permute-start.7 = (s16[64,1024]{1,0:T(8,128)(2,1)S(1)}, s16[64,1024]{1,0:T(8,128)(2,1)S(1)}, u32[]{:S(2)}, u32[]{:S(2)}) collective-permute-start(s16[64,1024]{1,0:T(8,128)(2,1)S(1)} %get-tuple-element.39), channel_id=1, source_target_pairs={{0,6},{1,7},{2,4},{3,5},{4,2},{5,3},{6,0},{7,1},{8,14},{9,15},{10,... | collective-permute-start | bytes 393224 | tf_op jit(solution)/shard_map/ppermute | solution.py:371
  22.4 0.0 collective-permute-done.2.refs_4_.refs_3_.refs_6_
  22.4 0.0 collective-permute-done.8.refs_0_
  22.4 0.7 %contract_far_group.1.refs_1_ = s16[128,1024]{1,0:T(8,128)(2,1)S(1)} custom-call(bf16[128,1024]{1,0:T(8,128)(2,1)S(1)} %collective-permute-done.8.refs_0_, bf16[1024,1024]{1,0:T(8,128)(2,1)S(1)} %get-tuple-element.35.refs_2_.refs_1_, s16[32,1024]{1,0:T(8,128)(2,1)S(1)} %collective-permute-done.refs_2_.refs_1_.refs_4_, ...), custom_call_target="tpu_custom_call" | custom-call | flops 268435456 | bytes 2097152 | tf_op jit(solution)/shard_map/contract_far_group/pallas_call | solution.py:172
  23.1 0.0 copy-start.4
  23.1 0.0 copy-start.5
  23.1 0.0 copy-start.6
  23.1 2.6 %collective-permute-start.11 = (s16[128,1024]{1,0:T(8,128)(2,1)S(1)}, s16[128,1024]{1,0:T(8,128)(2,1)S(1)}, u32[]{:S(2)}, u32[]{:S(2)}) collective-permute-start(s16[128,1024]{1,0:T(8,128)(2,1)S(1)} %contract_far_group.1.refs_1_), channel_id=1, source_target_pairs={{0,24},{1,25},{2,26},{3,27},{4,28},{5,29},{6,30},{7,31},{8,16},{9,... | collective-permute-start | bytes 786440 | tf_op jit(solution)/shard_map/ppermute | solution.py:371
  25.7 0.0 copy-done
  25.8 1.7 %write_residual.1 = (f32[50,16,1024]{2,1,0:T(8,128)}, s32[8,128]{1,0:T(8,128)S(1)}) custom-call(f32[50,16,1024]{2,1,0:T(8,128)S(1)} %bitcast.3, s16[128,1024]{1,0:T(8,128)(2,1)S(1)} %contract_far_group.1.refs_1_), custom_call_target="tpu_custom_call" | custom-call | tf_op jit(solution)/shard_map/write_residual/pallas_call | solution.py:243
  27.5 0.0 collective-permute-done.5.refs_1_
  27.5 2.4 %collective-permute-done.6.refs_2_ = s16[64,1024]{1,0:T(8,128)(2,1)S(1)} collective-permute-done((s16[64,1024]{1,0:T(8,128)(2,1)S(1)}, s16[64,1024]{1,0:T(8,128)(2,1)S(1)}, u32[]{:S(2)}, u32[]{:S(2)}) %collective-permute-start.6) | collective-permute-done | bytes 131104 | tf_op jit(solution)/shard_map/ppermute | solution.py:371
  29.9 0.0 collective-permute-done.7.refs_3_
  29.9 1.6 %collective-permute-start.9 = (s16[128,1024]{1,0:T(8,128)(2,1)S(1)}, s16[128,1024]{1,0:T(8,128)(2,1)S(1)}, u32[]{:S(2)}, u32[]{:S(2)}) collective-permute-start(s16[128,1024]{1,0:T(8,128)(2,1)S(1)} %get-tuple-element.42), channel_id=1, source_target_pairs={{0,8},{1,17},{2,10},{3,19},{4,12},{5,21},{6,14},{7,23},{8,0},{9,25... | collective-permute-start | bytes 786440 | tf_op jit(solution)/shard_map/ppermute | solution.py:371
  31.5 1.2 %collective-permute-start.10 = (s16[128,1024]{1,0:T(8,128)(2,1)S(1)}, s16[128,1024]{1,0:T(8,128)(2,1)S(1)}, u32[]{:S(2)}, u32[]{:S(2)}) collective-permute-start(s16[128,1024]{1,0:T(8,128)(2,1)S(1)} %get-tuple-element.43), channel_id=1, source_target_pairs={{0,16},{1,9},{2,18},{3,11},{4,20},{5,13},{6,22},{7,15},{8,24},{9,1... | collective-permute-start | bytes 786440 | tf_op jit(solution)/shard_map/ppermute | solution.py:371
  32.7 0.0 collective-permute-done.11.refs_0_
  32.7 2.0 %collective-permute-start.12 = (s16[32,1024]{1,0:T(8,128)(2,1)S(1)}, s16[32,1024]{1,0:T(8,128)(2,1)S(1)}, u32[]{:S(2)}, u32[]{:S(2)}) collective-permute-start(s16[32,1024]{1,0:T(8,128)(2,1)S(1)} %get-tuple-element.45), channel_id=1, source_target_pairs={{0,2},{1,3},{2,0},{3,1},{4,6},{5,7},{6,4},{7,5},{8,10},{9,11},{10,... | collective-permute-start | bytes 196616 | tf_op jit(solution)/shard_map/ppermute | solution.py:371
  34.7 1.0 %collective-permute-start.13 = (s16[32,1024]{1,0:T(8,128)(2,1)S(1)}, s16[32,1024]{1,0:T(8,128)(2,1)S(1)}, u32[]{:S(2)}, u32[]{:S(2)}) collective-permute-start(s16[32,1024]{1,0:T(8,128)(2,1)S(1)} %get-tuple-element.46), channel_id=1, source_target_pairs={{0,4},{1,5},{2,6},{3,7},{4,0},{5,1},{6,2},{7,3},{8,12},{9,13},{10,... | collective-permute-start | bytes 196616 | tf_op jit(solution)/shard_map/ppermute | solution.py:371
  35.7 1.4 %collective-permute-start.14 = (s16[32,1024]{1,0:T(8,128)(2,1)S(1)}, s16[32,1024]{1,0:T(8,128)(2,1)S(1)}, u32[]{:S(2)}, u32[]{:S(2)}) collective-permute-start(s16[32,1024]{1,0:T(8,128)(2,1)S(1)} %get-tuple-element.47), channel_id=1, source_target_pairs={{0,6},{1,7},{2,4},{3,5},{4,2},{5,3},{6,0},{7,1},{8,14},{9,15},{10,... | collective-permute-start | bytes 196616 | tf_op jit(solution)/shard_map/ppermute | solution.py:371
  37.2 0.1 collective-permute-done.12.refs_7_.refs_10_
  37.3 3.4 %collective-permute-done.13.refs_8_.refs_11_ = s16[32,1024]{1,0:T(8,128)(2,1)S(1)} collective-permute-done((s16[32,1024]{1,0:T(8,128)(2,1)S(1)}, s16[32,1024]{1,0:T(8,128)(2,1)S(1)}, u32[]{:S(2)}, u32[]{:S(2)}) %collective-permute-start.13) | collective-permute-done | bytes 65568 | tf_op jit(solution)/shard_map/ppermute | solution.py:371
  40.7 1.2 %collective-permute-done.14.refs_9_.refs_12_ = s16[32,1024]{1,0:T(8,128)(2,1)S(1)} collective-permute-done((s16[32,1024]{1,0:T(8,128)(2,1)S(1)}, s16[32,1024]{1,0:T(8,128)(2,1)S(1)}, u32[]{:S(2)}, u32[]{:S(2)}) %collective-permute-start.14) | collective-permute-done | bytes 65568 | tf_op jit(solution)/shard_map/ppermute | solution.py:371
  41.9 0.0 collective-permute-done.9.refs_4_.refs_7_
  41.9 0.0 collective-permute-done.10.refs_5_.refs_8_
  41.9 0.1 collective-permute-start.15
  42.0 0.0 copy-done.4
  42.0 0.0 copy-done.5
  42.0 0.0 copy-done.6
  42.1 1.2 %add_contributions_here.1.refs_4_ = f32[50,16,1024]{2,1,0:T(8,128)S(1)} custom-call(s32[4,8]{1,0:T(4,128)S(1)} %copy-done.5, s32[4,8]{1,0:T(4,128)S(1)} %copy-done.4, s32[4,8]{1,0:T(4,128)S(1)} %copy-done.6, s16[32,1024]{1,0:T(8,128)(2,1)S(1)} %get-tuple-element.29.refs_0_.refs_3_, s16[32,1024]{1,0:T(8,128)(2,1)S(1)} %collective-permute-done.refs_2_.refs_1_.refs_4_, ...), custom_call_target="tpu_custom_call" | custom-call | tf_op jit(solution)/shard_map/add_contributions_here/pallas_call | solution.py:296
  43.3 0.7 %collective-permute-done.15.refs_3_ = s16[256,1024]{1,0:T(8,128)(2,1)S(1)} collective-permute-done((s16[256,1024]{1,0:T(8,128)(2,1)S(1)}, s16[256,1024]{1,0:T(8,128)(2,1)S(1)}, u32[]{:S(2)}, u32[]{:S(2)}) %collective-permute-start.15) | collective-permute-done | bytes 524320 | tf_op jit(solution)/shard_map/ppermute | solution.py:371
  43.9 2.4 %add_contributions_there.1 = f32[50,16,1024]{2,1,0:T(8,128)} custom-call(s32[4,8]{1,0:T(4,128)S(1)} %copy-done.5, s32[4,8]{1,0:T(4,128)S(1)} %copy-done.4, s32[4,8]{1,0:T(4,128)S(1)} %copy-done.6, s16[256,1024]{1,0:T(8,128)(2,1)S(1)} %collective-permute-done.15.refs_3_, ...), custom_call_target="tpu_custom_call", output_to_operand_aliasing={{}: (5, {})} | custom-call | tf_op jit(solution)/shard_map/add_contributions_there/pallas_call | solution.py:343
  (3 shorter events, 0.1 us)
Async XLA Ops:
  0.0 1.2 %copy-start.2 = (bf16[4,128,1024]{2,1,0:T(8,128)(2,1)S(1)}, bf16[4,128,1024]{2,1,0:T(8,128)(2,1)}, u32[]{:S(2)}) copy-start(bf16[4,128,1024]{2,1,0:T(8,128)(2,1)} %amplitudes.1) | copy-start | bytes 3145732
  1.2 0.7 %copy-start.3 = (s32[4,8]{1,0:T(4,128)S(1)}, s32[4,8]{1,0:T(4,128)}, u32[]{:S(2)}) copy-start(s32[4,8]{1,0:T(4,128)} %refs_1_.3) | copy-start | bytes 388
  2.6 11.7 %collective-permute-start.3 = (bf16[128,1024]{1,0:T(8,128)(2,1)S(1)}, bf16[128,1024]{1,0:T(8,128)(2,1)S(1)}, u32[]{:S(2)}, u32[]{:S(2)}) collective-permute-start(bf16[128,1024]{1,0:T(8,128)(2,1)S(1)} %get-tuple-element.33), channel_id=1, source_target_pairs={{0,8},{1,17},{2,10},{3,19},{4,12},{5,21},{6,14},{7,23},{8,0},{9,25... | collective-permute-start | bytes 786440 | tf_op jit(solution)/shard_map/ppermute | solution.py:371
  5.6 11.2 %collective-permute-start.4 = (bf16[128,1024]{1,0:T(8,128)(2,1)S(1)}, bf16[128,1024]{1,0:T(8,128)(2,1)S(1)}, u32[]{:S(2)}, u32[]{:S(2)}) collective-permute-start(bf16[128,1024]{1,0:T(8,128)(2,1)S(1)} %get-tuple-element.34), channel_id=1, source_target_pairs={{0,16},{1,9},{2,18},{3,11},{4,20},{5,13},{6,22},{7,15},{8,24},{9,1... | collective-permute-start | bytes 786440 | tf_op jit(solution)/shard_map/ppermute | solution.py:371
  7.1 1.6 %copy-start.1 = (bf16[1,1024,1024]{2,1,0:T(8,128)(2,1)S(1)}, bf16[1,1024,1024]{2,1,0:T(8,128)(2,1)}, u32[]{:S(2)}) copy-start(bf16[1,1024,1024]{2,1,0:T(8,128)(2,1)} %param.8) | copy-start | bytes 6291460
  9.6 16.1 %copy-start = (f32[16,50,1024]{2,0,1:T(8,128)S(1)}, f32[16,50,1024]{2,0,1:T(8,128)}, u32[]{:S(2)}) copy-start(f32[16,50,1024]{2,0,1:T(8,128)} %param.11) | copy-start | bytes 9830404
  9.6 12.8 %collective-permute-start.8 = (bf16[128,1024]{1,0:T(8,128)(2,1)S(1)}, bf16[128,1024]{1,0:T(8,128)(2,1)S(1)}, u32[]{:S(2)}, u32[]{:S(2)}) collective-permute-start(bf16[128,1024]{1,0:T(8,128)(2,1)S(1)} %get-tuple-element.40), channel_id=1, source_target_pairs={{0,24},{1,25},{2,26},{3,27},{4,28},{5,29},{6,30},{7,31},{8,16},{9,... | collective-permute-start | bytes 786440 | tf_op jit(solution)/shard_map/ppermute | solution.py:371
  9.7 8.3 %collective-permute-start = (s16[32,1024]{1,0:T(8,128)(2,1)S(1)}, s16[32,1024]{1,0:T(8,128)(2,1)S(1)}, u32[]{:S(2)}, u32[]{:S(2)}) collective-permute-start(s16[32,1024]{1,0:T(8,128)(2,1)S(1)} %get-tuple-element.30), channel_id=1, source_target_pairs={{0,2},{1,3},{2,0},{3,1},{4,6},{5,7},{6,4},{7,5},{8,10},{9,11},{10,... | collective-permute-start | bytes 196616 | tf_op jit(solution)/shard_map/ppermute | solution.py:371
  11.7 8.2 %collective-permute-start.1 = (s16[32,1024]{1,0:T(8,128)(2,1)S(1)}, s16[32,1024]{1,0:T(8,128)(2,1)S(1)}, u32[]{:S(2)}, u32[]{:S(2)}) collective-permute-start(s16[32,1024]{1,0:T(8,128)(2,1)S(1)} %get-tuple-element.31), channel_id=1, source_target_pairs={{0,4},{1,5},{2,6},{3,7},{4,0},{5,1},{6,2},{7,3},{8,12},{9,13},{10,... | collective-permute-start | bytes 196616 | tf_op jit(solution)/shard_map/ppermute | solution.py:371
  14.3 8.1 %collective-permute-start.2 = (s16[32,1024]{1,0:T(8,128)(2,1)S(1)}, s16[32,1024]{1,0:T(8,128)(2,1)S(1)}, u32[]{:S(2)}, u32[]{:S(2)}) collective-permute-start(s16[32,1024]{1,0:T(8,128)(2,1)S(1)} %get-tuple-element.32), channel_id=1, source_target_pairs={{0,6},{1,7},{2,4},{3,5},{4,2},{5,3},{6,0},{7,1},{8,14},{9,15},{10,... | collective-permute-start | bytes 196616 | tf_op jit(solution)/shard_map/ppermute | solution.py:371
  17.9 9.6 %collective-permute-start.5 = (s16[64,1024]{1,0:T(8,128)(2,1)S(1)}, s16[64,1024]{1,0:T(8,128)(2,1)S(1)}, u32[]{:S(2)}, u32[]{:S(2)}) collective-permute-start(s16[64,1024]{1,0:T(8,128)(2,1)S(1)} %get-tuple-element.37), channel_id=1, source_target_pairs={{0,2},{1,3},{2,0},{3,1},{4,6},{5,7},{6,4},{7,5},{8,10},{9,11},{10,... | collective-permute-start | bytes 393224 | tf_op jit(solution)/shard_map/ppermute | solution.py:371
  18.0 11.8 %collective-permute-start.6 = (s16[64,1024]{1,0:T(8,128)(2,1)S(1)}, s16[64,1024]{1,0:T(8,128)(2,1)S(1)}, u32[]{:S(2)}, u32[]{:S(2)}) collective-permute-start(s16[64,1024]{1,0:T(8,128)(2,1)S(1)} %get-tuple-element.38), channel_id=1, source_target_pairs={{0,4},{1,5},{2,6},{3,7},{4,0},{5,1},{6,2},{7,3},{8,12},{9,13},{10,... | collective-permute-start | bytes 393224 | tf_op jit(solution)/shard_map/ppermute | solution.py:371
  19.9 9.9 %collective-permute-start.7 = (s16[64,1024]{1,0:T(8,128)(2,1)S(1)}, s16[64,1024]{1,0:T(8,128)(2,1)S(1)}, u32[]{:S(2)}, u32[]{:S(2)}) collective-permute-start(s16[64,1024]{1,0:T(8,128)(2,1)S(1)} %get-tuple-element.39), channel_id=1, source_target_pairs={{0,6},{1,7},{2,4},{3,5},{4,2},{5,3},{6,0},{7,1},{8,14},{9,15},{10,... | collective-permute-start | bytes 393224 | tf_op jit(solution)/shard_map/ppermute | solution.py:371
  23.1 18.9 %copy-start.4 = (s32[4,8]{1,0:T(4,128)S(1)}, s32[4,8]{1,0:T(4,128)}, u32[]{:S(2)}) copy-start(s32[4,8]{1,0:T(4,128)} %refs_1_.3) | copy-start | bytes 388
  23.1 18.9 %copy-start.5 = (s32[4,8]{1,0:T(4,128)S(1)}, s32[4,8]{1,0:T(4,128)}, u32[]{:S(2)}) copy-start(s32[4,8]{1,0:T(4,128)} %refs_0_.3) | copy-start | bytes 388
  23.1 18.9 %copy-start.6 = (s32[4,8]{1,0:T(4,128)S(1)}, s32[4,8]{1,0:T(4,128)}, u32[]{:S(2)}) copy-start(s32[4,8]{1,0:T(4,128)} %refs_2_.3) | copy-start | bytes 388
  23.1 9.5 %collective-permute-start.11 = (s16[128,1024]{1,0:T(8,128)(2,1)S(1)}, s16[128,1024]{1,0:T(8,128)(2,1)S(1)}, u32[]{:S(2)}, u32[]{:S(2)}) collective-permute-start(s16[128,1024]{1,0:T(8,128)(2,1)S(1)} %contract_far_group.1.refs_1_), channel_id=1, source_target_pairs={{0,24},{1,25},{2,26},{3,27},{4,28},{5,29},{6,30},{7,31},{8,16},{9,... | collective-permute-start | bytes 786440 | tf_op jit(solution)/shard_map/ppermute | solution.py:371
  29.9 12.0 %collective-permute-start.9 = (s16[128,1024]{1,0:T(8,128)(2,1)S(1)}, s16[128,1024]{1,0:T(8,128)(2,1)S(1)}, u32[]{:S(2)}, u32[]{:S(2)}) collective-permute-start(s16[128,1024]{1,0:T(8,128)(2,1)S(1)} %get-tuple-element.42), channel_id=1, source_target_pairs={{0,8},{1,17},{2,10},{3,19},{4,12},{5,21},{6,14},{7,23},{8,0},{9,25... | collective-permute-start | bytes 786440 | tf_op jit(solution)/shard_map/ppermute | solution.py:371
  31.5 10.4 %collective-permute-start.10 = (s16[128,1024]{1,0:T(8,128)(2,1)S(1)}, s16[128,1024]{1,0:T(8,128)(2,1)S(1)}, u32[]{:S(2)}, u32[]{:S(2)}) collective-permute-start(s16[128,1024]{1,0:T(8,128)(2,1)S(1)} %get-tuple-element.43), channel_id=1, source_target_pairs={{0,16},{1,9},{2,18},{3,11},{4,20},{5,13},{6,22},{7,15},{8,24},{9,1... | collective-permute-start | bytes 786440 | tf_op jit(solution)/shard_map/ppermute | solution.py:371
  32.7 4.6 %collective-permute-start.12 = (s16[32,1024]{1,0:T(8,128)(2,1)S(1)}, s16[32,1024]{1,0:T(8,128)(2,1)S(1)}, u32[]{:S(2)}, u32[]{:S(2)}) collective-permute-start(s16[32,1024]{1,0:T(8,128)(2,1)S(1)} %get-tuple-element.45), channel_id=1, source_target_pairs={{0,2},{1,3},{2,0},{3,1},{4,6},{5,7},{6,4},{7,5},{8,10},{9,11},{10,... | collective-permute-start | bytes 196616 | tf_op jit(solution)/shard_map/ppermute | solution.py:371
  34.7 6.0 %collective-permute-start.13 = (s16[32,1024]{1,0:T(8,128)(2,1)S(1)}, s16[32,1024]{1,0:T(8,128)(2,1)S(1)}, u32[]{:S(2)}, u32[]{:S(2)}) collective-permute-start(s16[32,1024]{1,0:T(8,128)(2,1)S(1)} %get-tuple-element.46), channel_id=1, source_target_pairs={{0,4},{1,5},{2,6},{3,7},{4,0},{5,1},{6,2},{7,3},{8,12},{9,13},{10,... | collective-permute-start | bytes 196616 | tf_op jit(solution)/shard_map/ppermute | solution.py:371
  35.7 6.2 %collective-permute-start.14 = (s16[32,1024]{1,0:T(8,128)(2,1)S(1)}, s16[32,1024]{1,0:T(8,128)(2,1)S(1)}, u32[]{:S(2)}, u32[]{:S(2)}) collective-permute-start(s16[32,1024]{1,0:T(8,128)(2,1)S(1)} %get-tuple-element.47), channel_id=1, source_target_pairs={{0,6},{1,7},{2,4},{3,5},{4,2},{5,3},{6,0},{7,1},{8,14},{9,15},{10,... | collective-permute-start | bytes 196616 | tf_op jit(solution)/shard_map/ppermute | solution.py:371
  41.9 2.0 %collective-permute-start.15 = (s16[256,1024]{1,0:T(8,128)(2,1)S(1)}, s16[256,1024]{1,0:T(8,128)(2,1)S(1)}, u32[]{:S(2)}, u32[]{:S(2)}) collective-permute-start(s16[256,1024]{1,0:T(8,128)(2,1)S(1)} %rows_of_other_core.1), channel_id=1, source_target_pairs={{0,1},{1,0},{2,3},{3,2},{4,5},{5,4},{6,7},{7,6},{8,9},{9,8},{10,11... | collective-permute-start | bytes 1572872 | tf_op jit(solution)/shard_map/ppermute | solution.py:371

commit v16 on v15

--- a/solution.py
+++ b/solution.py
@@ -160,23 +160,22 @@
 
 
 def far_kernel(chips, rows, tile, *rest):
-    coded, product = rest[-2:]
-    chip_rows = product.shape[0] // chips
-    parts = [coded.at[pl.ds(step * chip_rows, chip_rows)] for step in range(chips)]
-    code_chips(rows, tile, product, parts, 0)
+    outgoing, product = rest[-chips - 1 : -1], rest[-1]
+    code_chips(rows, tile, product, outgoing, 0)
 
 
 def contract_far(rows, tile, chips, earlier):
-    coded = jax.ShapeDtypeStruct((rows.shape[0], tile.shape[1]), jnp.int16)
-    product = jax.ShapeDtypeStruct(coded.shape, jnp.float32)
+    group_rows, tile_width = rows.shape[0], tile.shape[1]
+    coded = jax.ShapeDtypeStruct((group_rows // chips, tile_width), jnp.int16)
+    product = jax.ShapeDtypeStruct((group_rows, tile_width), jnp.float32)
     return pl.pallas_call(
         lambda *refs: far_kernel(chips, *refs),
-        out_shape=coded,
+        out_shape=[coded] * chips,
         in_specs=[VMEM] * 2 + [ANY] * len(earlier),
-        out_specs=VMEM,
+        out_specs=[VMEM] * chips,
         scratch_shapes=[pltpu.VMEM(product.shape, product.dtype)],
-        compiler_params=vmem_limit(rows, tile, coded, product),
-        cost_estimate=cost(rows.shape[0], tile),
+        compiler_params=vmem_limit(rows, tile, *[coded] * chips, product),
+        cost_estimate=cost(group_rows, tile),
         name="contract_far_group",
     )(rows, tile, *earlier)
 
@@ -382,10 +381,10 @@
     near_in = along_chips(contract_near(near_rows, tile, chips))
     by_tile = jnp.transpose(residual_in, (1, 0, 2))
     far_coded = contract_far(far_rows, tile, chips, own_in[1:])
-    written, token = write_residual(by_tile, [far_coded])
-    near_back = regroup(near_in, blk_count - 2, "regroup_by_group", [token])
+    far_in = [swap(coded, far, step) for step, coded in zip(chip_steps(chips), far_coded)]
+    written, token = write_residual(by_tile, far_coded[:1])
+    near_back = regroup(near_in, blk_count - 2, "regroup_by_group", [token, *far_in[:2]])
     near_in = [swap(rows, index + 1, 0) for index, rows in enumerate(near_back)]
-    far_in = along_chips(regroup([swap(far_coded, far, 0)], chips, "regroup_by_chip"))
 
     tables = (tile_ab, tile_cd, pair_screen)
     arrays = [*own_in, *near_in, *far_in]

time: 46.6 us -> 48.5 us (1.041)
  waiting for transfers between devices: 7.78 us -> 9.63 us
    ppermute x16, waiting for transfers between devices: 7.78 us -> 9.63 us  [swap(): return lax.ppermute(value, ('blk', 'grp'), pairs)]
  transfers between devices with their start and end apart: 16 -> 16, of which waited for: 5 -> 4; matrix products, arithmetic and copies ran while one was open for 0% -> 0% of each run, Pallas kernels for 12% -> 12%
where the time goes in v16:
time: 48.5 us; the launch traced here: 48.2 us
  starting transfers between devices  26.1 us (54%)
  waiting for transfers between devices  9.63 us (20%)
  Pallas kernels  8.85 us (18%)
  local copies, waits for them, and re-layouts  3.52 us (7%)
    ppermute x16, starting transfers between devices, swap(): return lax.ppermute(value, ('blk', 'grp'), pairs)  26.1 us
    ppermute x16, waiting for transfers between devices, swap(): return lax.ppermute(value, ('blk', 'grp'), pairs)  9.63 us
    unnamed x14, local copies, waits for them, and re-layouts  3.52 us
    pallas_call x1, Pallas kernels, add_there(): pl.pallas_call(lambda *refs: add_there_kernel(count, *refs), out_shape=wh...  2.44 us
    pallas_call x1, Pallas kernels, write_residual(): pl.pallas_call(lambda *refs: write_kernel(parts, *refs), out_shape=[jax.S...  1.74 us
    pallas_call x1, Pallas kernels, add_here(): pl.pallas_call(lambda *refs: add_here_kernel(pieces, *refs), out_shape=ja...  1.2 us
    pallas_call x1, Pallas kernels, contract_near(): pl.pallas_call(lambda *refs: near_kernel(len(groups), *refs), out_shape=[...  1.13 us
  transfers between devices with their start and end apart: 16, of which 4 were waited for; matrix products, arithmetic and copies ran while one was open for 0% of the time, Pallas kernels for 12%

profile of v16, /device:TPU:0, one launch (start us, length us, event | category | flops | bytes accessed | tf_op | source)
XLA Modules:
  0.0 48.2 jit_solution(306676043871049226)
XLA Ops:
  0.0 0.0 copy-start.2
  0.0 1.2 %copy-done.2 = bf16[4,128,1024]{2,1,0:T(8,128)(2,1)S(1)} copy-done((bf16[4,128,1024]{2,1,0:T(8,128)(2,1)S(1)}, bf16[4,128,1024]{2,1,0:T(8,128)(2,1)}, u32[]{:S(2)}) %copy-start.2) | copy-done | bytes 1048600
  1.2 0.0 copy-start.3
  1.2 0.7 %copy-done.3 = s32[4,8]{1,0:T(4,128)S(1)} copy-done((s32[4,8]{1,0:T(4,128)S(1)}, s32[4,8]{1,0:T(4,128)}, u32[]{:S(2)}) %copy-start.3) | copy-done | bytes 152
  1.9 0.7 %pick_cd_blocks.1 = (bf16[128,1024]{1,0:T(8,128)(2,1)S(1)}, bf16[128,1024]{1,0:T(8,128)(2,1)S(1)}, bf16[128,1024]{1,0:T(8,128)(2,1)S(1)}, bf16[128,1024]{1,0:T(8,128)(2,1)S(1)}) custom-call(s32[4,8]{1,0:T(4,128)S(1)} %copy-done.3, bf16[4,128,1024]{2,1,0:T(8,128)(2,1)S(1)} %copy-done.2), custom_call_target="tpu_custom_call" | custom-call | tf_op jit(solution)/shard_map/pick_cd_blocks/pallas_call | solution.py:91
  2.6 3.0 %collective-permute-start.3 = (bf16[128,1024]{1,0:T(8,128)(2,1)S(1)}, bf16[128,1024]{1,0:T(8,128)(2,1)S(1)}, u32[]{:S(2)}, u32[]{:S(2)}) collective-permute-start(bf16[128,1024]{1,0:T(8,128)(2,1)S(1)} %get-tuple-element.33), channel_id=1, source_target_pairs={{0,8},{1,17},{2,10},{3,19},{4,12},{5,21},{6,14},{7,23},{8,0},{9,25... | collective-permute-start | bytes 786440 | tf_op jit(solution)/shard_map/ppermute | solution.py:370
  5.6 1.5 %collective-permute-start.4 = (bf16[128,1024]{1,0:T(8,128)(2,1)S(1)}, bf16[128,1024]{1,0:T(8,128)(2,1)S(1)}, u32[]{:S(2)}, u32[]{:S(2)}) collective-permute-start(bf16[128,1024]{1,0:T(8,128)(2,1)S(1)} %get-tuple-element.34), channel_id=1, source_target_pairs={{0,16},{1,9},{2,18},{3,11},{4,20},{5,13},{6,22},{7,15},{8,24},{9,1... | collective-permute-start | bytes 786440 | tf_op jit(solution)/shard_map/ppermute | solution.py:370
  7.1 0.0 copy-start.1
  7.1 1.6 %copy-done.1 = bf16[1,1024,1024]{2,1,0:T(8,128)(2,1)S(1)} copy-done((bf16[1,1024,1024]{2,1,0:T(8,128)(2,1)S(1)}, bf16[1,1024,1024]{2,1,0:T(8,128)(2,1)}, u32[]{:S(2)}) %copy-start.1) | copy-done | bytes 2097176
  8.7 0.0 copy-start
  8.7 0.9 %contract_own_group.1 = (s16[32,1024]{1,0:T(8,128)(2,1)S(1)}, s16[32,1024]{1,0:T(8,128)(2,1)S(1)}, s16[32,1024]{1,0:T(8,128)(2,1)S(1)}, s16[32,1024]{1,0:T(8,128...) custom-call(bf16[128,1024]{1,0:T(8,128)(2,1)S(1)} %get-tuple-element.27.rows, ...), custom_call_target="tpu_custom_call" | custom-call | flops 268435456 | bytes 2097152 | tf_op jit(solution)/shard_map/contract_own_group/pallas_call | solution.py:127
  9.6 0.1 collective-permute-start.8
  9.7 2.0 %collective-permute-start = (s16[32,1024]{1,0:T(8,128)(2,1)S(1)}, s16[32,1024]{1,0:T(8,128)(2,1)S(1)}, u32[]{:S(2)}, u32[]{:S(2)}) collective-permute-start(s16[32,1024]{1,0:T(8,128)(2,1)S(1)} %get-tuple-element.30), channel_id=1, source_target_pairs={{0,2},{1,3},{2,0},{3,1},{4,6},{5,7},{6,4},{7,5},{8,10},{9,11},{10,... | collective-permute-start | bytes 196616 | tf_op jit(solution)/shard_map/ppermute | solution.py:370
  11.7 2.6 %collective-permute-start.1 = (s16[32,1024]{1,0:T(8,128)(2,1)S(1)}, s16[32,1024]{1,0:T(8,128)(2,1)S(1)}, u32[]{:S(2)}, u32[]{:S(2)}) collective-permute-start(s16[32,1024]{1,0:T(8,128)(2,1)S(1)} %get-tuple-element.31), channel_id=1, source_target_pairs={{0,4},{1,5},{2,6},{3,7},{4,0},{5,1},{6,2},{7,3},{8,12},{9,13},{10,... | collective-permute-start | bytes 196616 | tf_op jit(solution)/shard_map/ppermute | solution.py:370
  14.3 0.0 collective-permute-done.3.refs_0_
  14.3 2.5 %collective-permute-start.2 = (s16[32,1024]{1,0:T(8,128)(2,1)S(1)}, s16[32,1024]{1,0:T(8,128)(2,1)S(1)}, u32[]{:S(2)}, u32[]{:S(2)}) collective-permute-start(s16[32,1024]{1,0:T(8,128)(2,1)S(1)} %get-tuple-element.32), channel_id=1, source_target_pairs={{0,6},{1,7},{2,4},{3,5},{4,2},{5,3},{6,0},{7,1},{8,14},{9,15},{10,... | collective-permute-start | bytes 196616 | tf_op jit(solution)/shard_map/ppermute | solution.py:370
  16.8 0.0 collective-permute-done.4.refs_1_
  16.8 1.1 %contract_near_groups.1 = (s16[64,1024]{1,0:T(8,128)(2,1)S(1)}, s16[64,1024]{1,0:T(8,128)(2,1)S(1)}, s16[64,1024]{1,0:T(8,128)(2,1)S(1)}, s16[64,1024]{1,0:T(8,128)(2,1)S(1)}) custom-call(bf16[128,1024]{1,0:T(8,128)(2,1)S(1)} %collective-permute-done.3.refs_0_, bf16[128,1024]{1,0:T(8,128)(2,1)S(1)} %collective-permute-done.4.refs_1_, ...), custom_call_target="tpu_custom_call" | custom-call | flops 536870912 | bytes 2097152 | tf_op jit(solution)/shard_map/contract_near_groups/pallas_call | solution.py:150
  17.9 0.1 collective-permute-start.5
  18.0 0.0 collective-permute-done.refs_2_.refs_1_.refs_4_
  18.0 1.9 %collective-permute-start.6 = (s16[64,1024]{1,0:T(8,128)(2,1)S(1)}, s16[64,1024]{1,0:T(8,128)(2,1)S(1)}, u32[]{:S(2)}, u32[]{:S(2)}) collective-permute-start(s16[64,1024]{1,0:T(8,128)(2,1)S(1)} %get-tuple-element.38), channel_id=1, source_target_pairs={{0,4},{1,5},{2,6},{3,7},{4,0},{5,1},{6,2},{7,3},{8,12},{9,13},{10,... | collective-permute-start | bytes 393224 | tf_op jit(solution)/shard_map/ppermute | solution.py:370
  19.9 0.0 collective-permute-done.1.refs_3_.refs_2_.refs_5_
  19.9 2.5 %collective-permute-start.7 = (s16[64,1024]{1,0:T(8,128)(2,1)S(1)}, s16[64,1024]{1,0:T(8,128)(2,1)S(1)}, u32[]{:S(2)}, u32[]{:S(2)}) collective-permute-start(s16[64,1024]{1,0:T(8,128)(2,1)S(1)} %get-tuple-element.39), channel_id=1, source_target_pairs={{0,6},{1,7},{2,4},{3,5},{4,2},{5,3},{6,0},{7,1},{8,14},{9,15},{10,... | collective-permute-start | bytes 393224 | tf_op jit(solution)/shard_map/ppermute | solution.py:370
  22.4 0.0 collective-permute-done.2.refs_4_.refs_3_.refs_6_
  22.4 0.0 collective-permute-done.8.refs_0_
  22.4 0.7 %contract_far_group.1 = (s16[32,1024]{1,0:T(8,128)(2,1)S(1)}, s16[32,1024]{1,0:T(8,128)(2,1)S(1)}, s16[32,1024]{1,0:T(8,128)(2,1)S(1)}, s16[32,1024]{1,0:T(8,128)(2,1)S(1)}) custom-call(bf16[128,1024]{1,0:T(8,128)(2,1)S(1)} %collective-permute-done.8.refs_0_, bf16[1024,1024]{1,0:T(8,128)(2,1)S(1)} %get-tuple-element.35.refs_2_.refs_1_, ...), custom_call_target="tpu_custom_call" | custom-call | flops 268435456 | bytes 2097152 | tf_op jit(solution)/shard_map/contract_far_group/pallas_call | solution.py:171
  23.1 0.0 copy-start.4
  23.1 0.0 copy-start.5
  23.1 0.0 copy-start.6
  23.1 1.2 %collective-permute-start.10 = (s16[32,1024]{1,0:T(8,128)(2,1)S(1)}, s16[32,1024]{1,0:T(8,128)(2,1)S(1)}, u32[]{:S(2)}, u32[]{:S(2)}) collective-permute-start(s16[32,1024]{1,0:T(8,128)(2,1)S(1)} %get-tuple-element.43), channel_id=1, source_target_pairs={{0,26},{1,27},{2,24},{3,25},{4,30},{5,31},{6,28},{7,29},{8,18},{9,... | collective-permute-start | bytes 196616 | tf_op jit(solution)/shard_map/ppermute | solution.py:370
  24.4 1.4 %collective-permute-start.9 = (s16[32,1024]{1,0:T(8,128)(2,1)S(1)}, s16[32,1024]{1,0:T(8,128)(2,1)S(1)}, u32[]{:S(2)}, u32[]{:S(2)}) collective-permute-start(s16[32,1024]{1,0:T(8,128)(2,1)S(1)} %get-tuple-element.41.refs_1_), channel_id=1, source_target_pairs={{0,24},{1,25},{2,26},{3,27},{4,28},{5,29},{6,30},{7,31},{8,16},{9,... | collective-permute-start | bytes 196616 | tf_op jit(solution)/shard_map/ppermute | solution.py:370
  25.8 0.0 copy-done
  25.8 1.7 %write_residual.1 = (f32[50,16,1024]{2,1,0:T(8,128)}, s32[8,128]{1,0:T(8,128)S(1)}) custom-call(f32[50,16,1024]{2,1,0:T(8,128)S(1)} %bitcast.3, s16[32,1024]{1,0:T(8,128)(2,1)S(1)} %get-tuple-element.41.refs_1_), custom_call_target="tpu_custom_call" | custom-call | tf_op jit(solution)/shard_map/write_residual/pallas_call | solution.py:242
  27.6 4.0 %collective-permute-done.10.refs_6_.refs_7_.refs_10_ = s16[32,1024]{1,0:T(8,128)(2,1)S(1)} collective-permute-done((s16[32,1024]{1,0:T(8,128)(2,1)S(1)}, s16[32,1024]{1,0:T(8,128)(2,1)S(1)}, u32[]{:S(2)}, u32[]{:S(2)}) %collective-permute-start.10) | collective-permute-done | bytes 65568 | tf_op jit(solution)/shard_map/ppermute | solution.py:370
  31.6 0.0 collective-permute-done.9.refs_5_.refs_6_.refs_9_
  31.6 0.0 collective-permute-done.5.refs_1_
  31.6 0.0 collective-permute-done.6.refs_2_
  31.6 0.0 collective-permute-done.7.refs_3_
  31.6 0.7 %collective-permute-start.11 = (s16[128,1024]{1,0:T(8,128)(2,1)S(1)}, s16[128,1024]{1,0:T(8,128)(2,1)S(1)}, u32[]{:S(2)}, u32[]{:S(2)}) collective-permute-start(s16[128,1024]{1,0:T(8,128)(2,1)S(1)} %get-tuple-element.44), channel_id=1, source_target_pairs={{0,8},{1,17},{2,10},{3,19},{4,12},{5,21},{6,14},{7,23},{8,0},{9,25... | collective-permute-start | bytes 786440 | tf_op jit(solution)/shard_map/ppermute | solution.py:370
  32.3 1.3 %collective-permute-start.12 = (s16[128,1024]{1,0:T(8,128)(2,1)S(1)}, s16[128,1024]{1,0:T(8,128)(2,1)S(1)}, u32[]{:S(2)}, u32[]{:S(2)}) collective-permute-start(s16[128,1024]{1,0:T(8,128)(2,1)S(1)} %get-tuple-element.45), channel_id=1, source_target_pairs={{0,16},{1,9},{2,18},{3,11},{4,20},{5,13},{6,22},{7,15},{8,24},{9,1... | collective-permute-start | bytes 786440 | tf_op jit(solution)/shard_map/ppermute | solution.py:370
  33.6 2.3 %collective-permute-start.13 = (s16[32,1024]{1,0:T(8,128)(2,1)S(1)}, s16[32,1024]{1,0:T(8,128)(2,1)S(1)}, u32[]{:S(2)}, u32[]{:S(2)}) collective-permute-start(s16[32,1024]{1,0:T(8,128)(2,1)S(1)} %get-tuple-element.46), channel_id=1, source_target_pairs={{0,28},{1,29},{2,30},{3,31},{4,24},{5,25},{6,26},{7,27},{8,20},{9,... | collective-permute-start | bytes 196616 | tf_op jit(solution)/shard_map/ppermute | solution.py:370
  35.9 2.9 %collective-permute-start.14 = (s16[32,1024]{1,0:T(8,128)(2,1)S(1)}, s16[32,1024]{1,0:T(8,128)(2,1)S(1)}, u32[]{:S(2)}, u32[]{:S(2)}) collective-permute-start(s16[32,1024]{1,0:T(8,128)(2,1)S(1)} %get-tuple-element.47), channel_id=1, source_target_pairs={{0,30},{1,31},{2,28},{3,29},{4,26},{5,27},{6,24},{7,25},{8,22},{9,... | collective-permute-start | bytes 196616 | tf_op jit(solution)/shard_map/ppermute | solution.py:370
  38.8 3.2 %collective-permute-done.13.refs_8_.refs_11_ = s16[32,1024]{1,0:T(8,128)(2,1)S(1)} collective-permute-done((s16[32,1024]{1,0:T(8,128)(2,1)S(1)}, s16[32,1024]{1,0:T(8,128)(2,1)S(1)}, u32[]{:S(2)}, u32[]{:S(2)}) %collective-permute-start.13) | collective-permute-done | bytes 65568 | tf_op jit(solution)/shard_map/ppermute | solution.py:370
  42.0 1.8 %collective-permute-done.14.refs_9_.refs_12_ = s16[32,1024]{1,0:T(8,128)(2,1)S(1)} collective-permute-done((s16[32,1024]{1,0:T(8,128)(2,1)S(1)}, s16[32,1024]{1,0:T(8,128)(2,1)S(1)}, u32[]{:S(2)}, u32[]{:S(2)}) %collective-permute-start.14) | collective-permute-done | bytes 65568 | tf_op jit(solution)/shard_map/ppermute | solution.py:370
  43.8 0.0 collective-permute-done.11.refs_4_.refs_7_
  43.8 0.0 collective-permute-done.12.refs_5_.refs_8_
  43.8 0.1 collective-permute-start.15
  43.9 0.0 copy-done.4
  43.9 0.0 copy-done.5
  43.9 0.0 copy-done.6
  43.9 1.2 %add_contributions_here.1.refs_4_ = f32[50,16,1024]{2,1,0:T(8,128)S(1)} custom-call(s32[4,8]{1,0:T(4,128)S(1)} %copy-done.5, s32[4,8]{1,0:T(4,128)S(1)} %copy-done.4, s32[4,8]{1,0:T(4,128)S(1)} %copy-done.6, s16[32,1024]{1,0:T(8,128)(2,1)S(1)} %get-tuple-element.29.refs_0_.refs_3_, s16[32,1024]{1,0:T(8,128)(2,1)S(1)} %collective-permute-done.refs_2_.refs_1_.refs_4_, ...), custom_call_target="tpu_custom_call" | custom-call | tf_op jit(solution)/shard_map/add_contributions_here/pallas_call | solution.py:295
  45.1 0.7 %collective-permute-done.15.refs_3_ = s16[256,1024]{1,0:T(8,128)(2,1)S(1)} collective-permute-done((s16[256,1024]{1,0:T(8,128)(2,1)S(1)}, s16[256,1024]{1,0:T(8,128)(2,1)S(1)}, u32[]{:S(2)}, u32[]{:S(2)}) %collective-permute-start.15) | collective-permute-done | bytes 524320 | tf_op jit(solution)/shard_map/ppermute | solution.py:370
  45.8 2.4 %add_contributions_there.1 = f32[50,16,1024]{2,1,0:T(8,128)} custom-call(s32[4,8]{1,0:T(4,128)S(1)} %copy-done.5, s32[4,8]{1,0:T(4,128)S(1)} %copy-done.4, s32[4,8]{1,0:T(4,128)S(1)} %copy-done.6, s16[256,1024]{1,0:T(8,128)(2,1)S(1)} %collective-permute-done.15.refs_3_, ...), custom_call_target="tpu_custom_call", output_to_operand_aliasing={{}: (5, {})} | custom-call | tf_op jit(solution)/shard_map/add_contributions_there/pallas_call | solution.py:342
  (2 shorter events, 0.1 us)
Async XLA Ops:
  0.0 1.2 %copy-start.2 = (bf16[4,128,1024]{2,1,0:T(8,128)(2,1)S(1)}, bf16[4,128,1024]{2,1,0:T(8,128)(2,1)}, u32[]{:S(2)}) copy-start(bf16[4,128,1024]{2,1,0:T(8,128)(2,1)} %amplitudes.1) | copy-start | bytes 3145732
  1.2 0.7 %copy-start.3 = (s32[4,8]{1,0:T(4,128)S(1)}, s32[4,8]{1,0:T(4,128)}, u32[]{:S(2)}) copy-start(s32[4,8]{1,0:T(4,128)} %refs_1_.3) | copy-start | bytes 388
  2.6 11.7 %collective-permute-start.3 = (bf16[128,1024]{1,0:T(8,128)(2,1)S(1)}, bf16[128,1024]{1,0:T(8,128)(2,1)S(1)}, u32[]{:S(2)}, u32[]{:S(2)}) collective-permute-start(bf16[128,1024]{1,0:T(8,128)(2,1)S(1)} %get-tuple-element.33), channel_id=1, source_target_pairs={{0,8},{1,17},{2,10},{3,19},{4,12},{5,21},{6,14},{7,23},{8,0},{9,25... | collective-permute-start | bytes 786440 | tf_op jit(solution)/shard_map/ppermute | solution.py:370
  5.6 11.2 %collective-permute-start.4 = (bf16[128,1024]{1,0:T(8,128)(2,1)S(1)}, bf16[128,1024]{1,0:T(8,128)(2,1)S(1)}, u32[]{:S(2)}, u32[]{:S(2)}) collective-permute-start(bf16[128,1024]{1,0:T(8,128)(2,1)S(1)} %get-tuple-element.34), channel_id=1, source_target_pairs={{0,16},{1,9},{2,18},{3,11},{4,20},{5,13},{6,22},{7,15},{8,24},{9,1... | collective-permute-start | bytes 786440 | tf_op jit(solution)/shard_map/ppermute | solution.py:370
  7.1 1.6 %copy-start.1 = (bf16[1,1024,1024]{2,1,0:T(8,128)(2,1)S(1)}, bf16[1,1024,1024]{2,1,0:T(8,128)(2,1)}, u32[]{:S(2)}) copy-start(bf16[1,1024,1024]{2,1,0:T(8,128)(2,1)} %param.8) | copy-start | bytes 6291460
  8.7 17.1 %copy-start = (f32[16,50,1024]{2,0,1:T(8,128)S(1)}, f32[16,50,1024]{2,0,1:T(8,128)}, u32[]{:S(2)}) copy-start(f32[16,50,1024]{2,0,1:T(8,128)} %param.11) | copy-start | bytes 9830404
  9.6 12.8 %collective-permute-start.8 = (bf16[128,1024]{1,0:T(8,128)(2,1)S(1)}, bf16[128,1024]{1,0:T(8,128)(2,1)S(1)}, u32[]{:S(2)}, u32[]{:S(2)}) collective-permute-start(bf16[128,1024]{1,0:T(8,128)(2,1)S(1)} %get-tuple-element.40), channel_id=1, source_target_pairs={{0,24},{1,25},{2,26},{3,27},{4,28},{5,29},{6,30},{7,31},{8,16},{9,... | collective-permute-start | bytes 786440 | tf_op jit(solution)/shard_map/ppermute | solution.py:370
  9.7 8.3 %collective-permute-start = (s16[32,1024]{1,0:T(8,128)(2,1)S(1)}, s16[32,1024]{1,0:T(8,128)(2,1)S(1)}, u32[]{:S(2)}, u32[]{:S(2)}) collective-permute-start(s16[32,1024]{1,0:T(8,128)(2,1)S(1)} %get-tuple-element.30), channel_id=1, source_target_pairs={{0,2},{1,3},{2,0},{3,1},{4,6},{5,7},{6,4},{7,5},{8,10},{9,11},{10,... | collective-permute-start | bytes 196616 | tf_op jit(solution)/shard_map/ppermute | solution.py:370
  11.7 8.2 %collective-permute-start.1 = (s16[32,1024]{1,0:T(8,128)(2,1)S(1)}, s16[32,1024]{1,0:T(8,128)(2,1)S(1)}, u32[]{:S(2)}, u32[]{:S(2)}) collective-permute-start(s16[32,1024]{1,0:T(8,128)(2,1)S(1)} %get-tuple-element.31), channel_id=1, source_target_pairs={{0,4},{1,5},{2,6},{3,7},{4,0},{5,1},{6,2},{7,3},{8,12},{9,13},{10,... | collective-permute-start | bytes 196616 | tf_op jit(solution)/shard_map/ppermute | solution.py:370
  14.3 8.1 %collective-permute-start.2 = (s16[32,1024]{1,0:T(8,128)(2,1)S(1)}, s16[32,1024]{1,0:T(8,128)(2,1)S(1)}, u32[]{:S(2)}, u32[]{:S(2)}) collective-permute-start(s16[32,1024]{1,0:T(8,128)(2,1)S(1)} %get-tuple-element.32), channel_id=1, source_target_pairs={{0,6},{1,7},{2,4},{3,5},{4,2},{5,3},{6,0},{7,1},{8,14},{9,15},{10,... | collective-permute-start | bytes 196616 | tf_op jit(solution)/shard_map/ppermute | solution.py:370
  17.9 13.6 %collective-permute-start.5 = (s16[64,1024]{1,0:T(8,128)(2,1)S(1)}, s16[64,1024]{1,0:T(8,128)(2,1)S(1)}, u32[]{:S(2)}, u32[]{:S(2)}) collective-permute-start(s16[64,1024]{1,0:T(8,128)(2,1)S(1)} %get-tuple-element.37), channel_id=1, source_target_pairs={{0,2},{1,3},{2,0},{3,1},{4,6},{5,7},{6,4},{7,5},{8,10},{9,11},{10,... | collective-permute-start | bytes 393224 | tf_op jit(solution)/shard_map/ppermute | solution.py:370
  18.0 13.5 %collective-permute-start.6 = (s16[64,1024]{1,0:T(8,128)(2,1)S(1)}, s16[64,1024]{1,0:T(8,128)(2,1)S(1)}, u32[]{:S(2)}, u32[]{:S(2)}) collective-permute-start(s16[64,1024]{1,0:T(8,128)(2,1)S(1)} %get-tuple-element.38), channel_id=1, source_target_pairs={{0,4},{1,5},{2,6},{3,7},{4,0},{5,1},{6,2},{7,3},{8,12},{9,13},{10,... | collective-permute-start | bytes 393224 | tf_op jit(solution)/shard_map/ppermute | solution.py:370
  19.9 11.7 %collective-permute-start.7 = (s16[64,1024]{1,0:T(8,128)(2,1)S(1)}, s16[64,1024]{1,0:T(8,128)(2,1)S(1)}, u32[]{:S(2)}, u32[]{:S(2)}) collective-permute-start(s16[64,1024]{1,0:T(8,128)(2,1)S(1)} %get-tuple-element.39), channel_id=1, source_target_pairs={{0,6},{1,7},{2,4},{3,5},{4,2},{5,3},{6,0},{7,1},{8,14},{9,15},{10,... | collective-permute-start | bytes 393224 | tf_op jit(solution)/shard_map/ppermute | solution.py:370
  23.1 20.8 %copy-start.4 = (s32[4,8]{1,0:T(4,128)S(1)}, s32[4,8]{1,0:T(4,128)}, u32[]{:S(2)}) copy-start(s32[4,8]{1,0:T(4,128)} %refs_1_.3) | copy-start | bytes 388
  23.1 20.8 %copy-start.5 = (s32[4,8]{1,0:T(4,128)S(1)}, s32[4,8]{1,0:T(4,128)}, u32[]{:S(2)}) copy-start(s32[4,8]{1,0:T(4,128)} %refs_0_.3) | copy-start | bytes 388
  23.1 20.8 %copy-start.6 = (s32[4,8]{1,0:T(4,128)S(1)}, s32[4,8]{1,0:T(4,128)}, u32[]{:S(2)}) copy-start(s32[4,8]{1,0:T(4,128)} %refs_2_.3) | copy-start | bytes 388
  23.1 8.4 %collective-permute-start.10 = (s16[32,1024]{1,0:T(8,128)(2,1)S(1)}, s16[32,1024]{1,0:T(8,128)(2,1)S(1)}, u32[]{:S(2)}, u32[]{:S(2)}) collective-permute-start(s16[32,1024]{1,0:T(8,128)(2,1)S(1)} %get-tuple-element.43), channel_id=1, source_target_pairs={{0,26},{1,27},{2,24},{3,25},{4,30},{5,31},{6,28},{7,29},{8,18},{9,... | collective-permute-start | bytes 196616 | tf_op jit(solution)/shard_map/ppermute | solution.py:370
  24.4 7.2 %collective-permute-start.9 = (s16[32,1024]{1,0:T(8,128)(2,1)S(1)}, s16[32,1024]{1,0:T(8,128)(2,1)S(1)}, u32[]{:S(2)}, u32[]{:S(2)}) collective-permute-start(s16[32,1024]{1,0:T(8,128)(2,1)S(1)} %get-tuple-element.41.refs_1_), channel_id=1, source_target_pairs={{0,24},{1,25},{2,26},{3,27},{4,28},{5,29},{6,30},{7,31},{8,16},{9,... | collective-permute-start | bytes 196616 | tf_op jit(solution)/shard_map/ppermute | solution.py:370
  31.6 12.1 %collective-permute-start.11 = (s16[128,1024]{1,0:T(8,128)(2,1)S(1)}, s16[128,1024]{1,0:T(8,128)(2,1)S(1)}, u32[]{:S(2)}, u32[]{:S(2)}) collective-permute-start(s16[128,1024]{1,0:T(8,128)(2,1)S(1)} %get-tuple-element.44), channel_id=1, source_target_pairs={{0,8},{1,17},{2,10},{3,19},{4,12},{5,21},{6,14},{7,23},{8,0},{9,25... | collective-permute-start | bytes 786440 | tf_op jit(solution)/shard_map/ppermute | solution.py:370
  32.3 11.4 %collective-permute-start.12 = (s16[128,1024]{1,0:T(8,128)(2,1)S(1)}, s16[128,1024]{1,0:T(8,128)(2,1)S(1)}, u32[]{:S(2)}, u32[]{:S(2)}) collective-permute-start(s16[128,1024]{1,0:T(8,128)(2,1)S(1)} %get-tuple-element.45), channel_id=1, source_target_pairs={{0,16},{1,9},{2,18},{3,11},{4,20},{5,13},{6,22},{7,15},{8,24},{9,1... | collective-permute-start | bytes 786440 | tf_op jit(solution)/shard_map/ppermute | solution.py:370
  33.6 8.4 %collective-permute-start.13 = (s16[32,1024]{1,0:T(8,128)(2,1)S(1)}, s16[32,1024]{1,0:T(8,128)(2,1)S(1)}, u32[]{:S(2)}, u32[]{:S(2)}) collective-permute-start(s16[32,1024]{1,0:T(8,128)(2,1)S(1)} %get-tuple-element.46), channel_id=1, source_target_pairs={{0,28},{1,29},{2,30},{3,31},{4,24},{5,25},{6,26},{7,27},{8,20},{9,... | collective-permute-start | bytes 196616 | tf_op jit(solution)/shard_map/ppermute | solution.py:370
  35.9 7.9 %collective-permute-start.14 = (s16[32,1024]{1,0:T(8,128)(2,1)S(1)}, s16[32,1024]{1,0:T(8,128)(2,1)S(1)}, u32[]{:S(2)}, u32[]{:S(2)}) collective-permute-start(s16[32,1024]{1,0:T(8,128)(2,1)S(1)} %get-tuple-element.47), channel_id=1, source_target_pairs={{0,30},{1,31},{2,28},{3,29},{4,26},{5,27},{6,24},{7,25},{8,22},{9,... | collective-permute-start | bytes 196616 | tf_op jit(solution)/shard_map/ppermute | solution.py:370
  43.8 2.0 %collective-permute-start.15 = (s16[256,1024]{1,0:T(8,128)(2,1)S(1)}, s16[256,1024]{1,0:T(8,128)(2,1)S(1)}, u32[]{:S(2)}, u32[]{:S(2)}) collective-permute-start(s16[256,1024]{1,0:T(8,128)(2,1)S(1)} %rows_of_other_core.1), channel_id=1, source_target_pairs={{0,1},{1,0},{2,3},{3,2},{4,5},{5,4},{6,7},{7,6},{8,9},{9,8},{10,11... | collective-permute-start | bytes 1572872 | tf_op jit(solution)/shard_map/ppermute | solution.py:370

commit v17 on v15

--- a/solution.py
+++ b/solution.py
@@ -60,8 +60,8 @@
     return [0] + steps + [blk_count - 1]
 
 
-def chip_steps(chips):
-    return list(range(chips))
+def chip_steps(chips, core):
+    return [0] + [slot + core * (chips - 2 * slot) for slot in range(1, chips)]
 
 
 def start_all(copies):
@@ -102,8 +102,9 @@
 def code_chips(rows, tile, product, outgoing, first):
     product[...] = jnp.dot(rows[...], tile[...], preferred_element_type=jnp.float32)
     chip_rows = product.shape[0] // len(outgoing)
-    chip = lax.axis_index("grp") // CORES
-    for step, coded in zip(chip_steps(len(outgoing)), outgoing):
+    grp = lax.axis_index("grp")
+    chip = grp // CORES
+    for step, coded in zip(chip_steps(len(outgoing), grp % CORES), outgoing):
         source = pl.multiple_of(jnp.bitwise_xor(chip, step) * chip_rows, chip_rows)
         code, tail = encode(product[pl.ds(source, chip_rows), :])
         coded[first : first + chip_rows, :LANES] = code
@@ -257,7 +258,7 @@
     tiles = []
     for index in range(count):
         step = blk_steps(blk_count, core)[index // chips]
-        chip = jnp.bitwise_xor(grp // CORES, chip_steps(chips)[index % chips])
+        chip = jnp.bitwise_xor(grp // CORES, chip_steps(chips, core)[index % chips])
         tiles.append((jnp.bitwise_xor(blk, step), chip * CORES + core))
     return tiles
 
@@ -363,16 +364,16 @@
     owner_rows = residual_in.shape[0]
     far = blk_count - 1
 
-    def swap(value, slot, chip_step, core_step=0):
+    def swap(value, blk_slot, chip_slot, core_step=0):
         pairs = []
         for device in range(blk_count * grp_count):
-            blk_step = blk_steps(blk_count, device % CORES)[slot]
+            blk_step = blk_steps(blk_count, device % CORES)[blk_slot]
+            chip_step = chip_steps(chips, device % CORES)[chip_slot]
             pairs.append((device, device ^ (blk_step * grp_count + chip_step * CORES + core_step)))
         return lax.ppermute(value, ("blk", "grp"), pairs)
 
     def along_chips(outgoing):
-        steps = chip_steps(chips)
-        return [outgoing[0]] + [swap(outgoing[slot], 0, steps[slot]) for slot in range(1, chips)]
+        return [outgoing[0]] + [swap(outgoing[slot], 0, slot) for slot in range(1, chips)]
 
     own_rows, *near_picked, far_picked = pick(tile_cd, amplitudes)
     near_rows = [swap(rows, index + 1, 0) for index, rows in enumerate(near_picked)]

time: 46.6 us -> 46.5 us (level)
  waiting for transfers between devices: 7.78 us -> 6.84 us
  starting transfers between devices: 26 us -> 26.8 us
    ppermute x16, waiting for transfers between devices: 7.78 us -> 6.84 us  [swap(): return lax.ppermute(value, ('blk', 'grp'), pairs)]
    ppermute x16, starting transfers between devices: 26 us -> 26.8 us  [swap(): return lax.ppermute(value, ('blk', 'grp'), pairs)]
  transfers between devices with their start and end apart: 16 -> 16, of which waited for: 5 -> 4; matrix products, arithmetic and copies ran while one was open for 0% -> 0% of each run, Pallas kernels for 12% -> 12%
where the time goes in v17:
time: 46.5 us; the launch traced here: 46.3 us
  starting transfers between devices  26.8 us (58%)
  Pallas kernels  8.94 us (19%)
  waiting for transfers between devices  6.84 us (15%)
  local copies, waits for them, and re-layouts  3.52 us (8%)
    ppermute x16, starting transfers between devices, swap(): return lax.ppermute(value, ('blk', 'grp'), pairs)  26.8 us
    ppermute x16, waiting for transfers between devices, swap(): return lax.ppermute(value, ('blk', 'grp'), pairs)  6.84 us
    unnamed x14, local copies, waits for them, and re-layouts  3.52 us
    pallas_call x1, Pallas kernels, add_there(): pl.pallas_call(lambda *refs: add_there_kernel(count, *refs), out_shape=wh...  2.5 us
    pallas_call x1, Pallas kernels, write_residual(): pl.pallas_call(lambda *refs: write_kernel(parts, *refs), out_shape=[jax.S...  1.74 us
    pallas_call x1, Pallas kernels, add_here(): pl.pallas_call(lambda *refs: add_here_kernel(pieces, *refs), out_shape=ja...  1.2 us
    pallas_call x1, Pallas kernels, contract_near(): pl.pallas_call(lambda *refs: near_kernel(len(groups), *refs), out_shape=[...  1.13 us
  transfers between devices with their start and end apart: 16, of which 4 were waited for; matrix products, arithmetic and copies ran while one was open for 0% of the time, Pallas kernels for 12%

profile of v17, /device:TPU:0, one launch (start us, length us, event | category | flops | bytes accessed | tf_op | source)
XLA Modules:
  0.0 46.3 jit_solution(12290376777510887575)
XLA Ops:
  0.0 0.0 copy-start.2
  0.0 1.2 %copy-done.2 = bf16[4,128,1024]{2,1,0:T(8,128)(2,1)S(1)} copy-done((bf16[4,128,1024]{2,1,0:T(8,128)(2,1)S(1)}, bf16[4,128,1024]{2,1,0:T(8,128)(2,1)}, u32[]{:S(2)}) %copy-start.2) | copy-done | bytes 1048600
  1.2 0.0 copy-start.3
  1.2 0.7 %copy-done.3 = s32[4,8]{1,0:T(4,128)S(1)} copy-done((s32[4,8]{1,0:T(4,128)S(1)}, s32[4,8]{1,0:T(4,128)}, u32[]{:S(2)}) %copy-start.3) | copy-done | bytes 152
  1.9 0.7 %pick_cd_blocks.1 = (bf16[128,1024]{1,0:T(8,128)(2,1)S(1)}, bf16[128,1024]{1,0:T(8,128)(2,1)S(1)}, bf16[128,1024]{1,0:T(8,128)(2,1)S(1)}, bf16[128,1024]{1,0:T(8,128)(2,1)S(1)}) custom-call(s32[4,8]{1,0:T(4,128)S(1)} %copy-done.3, bf16[4,128,1024]{2,1,0:T(8,128)(2,1)S(1)} %copy-done.2), custom_call_target="tpu_custom_call" | custom-call | tf_op jit(solution)/shard_map/pick_cd_blocks/pallas_call | solution.py:91
  2.6 3.0 %collective-permute-start.3 = (bf16[128,1024]{1,0:T(8,128)(2,1)S(1)}, bf16[128,1024]{1,0:T(8,128)(2,1)S(1)}, u32[]{:S(2)}, u32[]{:S(2)}) collective-permute-start(bf16[128,1024]{1,0:T(8,128)(2,1)S(1)} %get-tuple-element.33), channel_id=1, source_target_pairs={{0,8},{1,17},{2,10},{3,19},{4,12},{5,21},{6,14},{7,23},{8,0},{9,25... | collective-permute-start | bytes 786440 | tf_op jit(solution)/shard_map/ppermute | solution.py:373
  5.6 1.5 %collective-permute-start.4 = (bf16[128,1024]{1,0:T(8,128)(2,1)S(1)}, bf16[128,1024]{1,0:T(8,128)(2,1)S(1)}, u32[]{:S(2)}, u32[]{:S(2)}) collective-permute-start(bf16[128,1024]{1,0:T(8,128)(2,1)S(1)} %get-tuple-element.34), channel_id=1, source_target_pairs={{0,16},{1,9},{2,18},{3,11},{4,20},{5,13},{6,22},{7,15},{8,24},{9,1... | collective-permute-start | bytes 786440 | tf_op jit(solution)/shard_map/ppermute | solution.py:373
  7.1 0.0 copy-start.1
  7.1 1.6 %copy-done.1 = bf16[1,1024,1024]{2,1,0:T(8,128)(2,1)S(1)} copy-done((bf16[1,1024,1024]{2,1,0:T(8,128)(2,1)S(1)}, bf16[1,1024,1024]{2,1,0:T(8,128)(2,1)}, u32[]{:S(2)}) %copy-start.1) | copy-done | bytes 2097176
  8.7 0.9 %contract_own_group.1 = (s16[32,1024]{1,0:T(8,128)(2,1)S(1)}, s16[32,1024]{1,0:T(8,128)(2,1)S(1)}, s16[32,1024]{1,0:T(8,128)(2,1)S(1)}, s16[32,1024]{1,0:T(8,128...) custom-call(bf16[128,1024]{1,0:T(8,128)(2,1)S(1)} %get-tuple-element.27.rows, ...), custom_call_target="tpu_custom_call" | custom-call | flops 268435456 | bytes 2097152 | tf_op jit(solution)/shard_map/contract_own_group/pallas_call | solution.py:128
  9.6 0.0 copy-start
  9.6 0.1 collective-permute-start.8
  9.7 2.0 %collective-permute-start = (s16[32,1024]{1,0:T(8,128)(2,1)S(1)}, s16[32,1024]{1,0:T(8,128)(2,1)S(1)}, u32[]{:S(2)}, u32[]{:S(2)}) collective-permute-start(s16[32,1024]{1,0:T(8,128)(2,1)S(1)} %get-tuple-element.30), channel_id=1, source_target_pairs={{0,2},{1,7},{2,0},{3,5},{4,6},{5,3},{6,4},{7,1},{8,10},{9,15},{10,... | collective-permute-start | bytes 196616 | tf_op jit(solution)/shard_map/ppermute | solution.py:373
  11.7 2.6 %collective-permute-start.1 = (s16[32,1024]{1,0:T(8,128)(2,1)S(1)}, s16[32,1024]{1,0:T(8,128)(2,1)S(1)}, u32[]{:S(2)}, u32[]{:S(2)}) collective-permute-start(s16[32,1024]{1,0:T(8,128)(2,1)S(1)} %get-tuple-element.31), channel_id=1, source_target_pairs={{0,4},{1,5},{2,6},{3,7},{4,0},{5,1},{6,2},{7,3},{8,12},{9,13},{10,... | collective-permute-start | bytes 196616 | tf_op jit(solution)/shard_map/ppermute | solution.py:373
  14.3 0.0 collective-permute-done.3.refs_0_
  14.3 2.5 %collective-permute-start.2 = (s16[32,1024]{1,0:T(8,128)(2,1)S(1)}, s16[32,1024]{1,0:T(8,128)(2,1)S(1)}, u32[]{:S(2)}, u32[]{:S(2)}) collective-permute-start(s16[32,1024]{1,0:T(8,128)(2,1)S(1)} %get-tuple-element.32), channel_id=1, source_target_pairs={{0,6},{1,3},{2,4},{3,1},{4,2},{5,7},{6,0},{7,5},{8,14},{9,11},{10,... | collective-permute-start | bytes 196616 | tf_op jit(solution)/shard_map/ppermute | solution.py:373
  16.8 0.0 collective-permute-done.4.refs_1_
  16.8 1.1 %contract_near_groups.1 = (s16[64,1024]{1,0:T(8,128)(2,1)S(1)}, s16[64,1024]{1,0:T(8,128)(2,1)S(1)}, s16[64,1024]{1,0:T(8,128)(2,1)S(1)}, s16[64,1024]{1,0:T(8,128)(2,1)S(1)}) custom-call(bf16[128,1024]{1,0:T(8,128)(2,1)S(1)} %collective-permute-done.3.refs_0_, bf16[128,1024]{1,0:T(8,128)(2,1)S(1)} %collective-permute-done.4.refs_1_, ...), custom_call_target="tpu_custom_call" | custom-call | flops 536870912 | bytes 2097152 | tf_op jit(solution)/shard_map/contract_near_groups/pallas_call | solution.py:151
  17.9 0.1 collective-permute-start.5
  18.0 0.0 collective-permute-done.refs_2_.refs_1_.refs_4_
  18.0 1.9 %collective-permute-start.6 = (s16[64,1024]{1,0:T(8,128)(2,1)S(1)}, s16[64,1024]{1,0:T(8,128)(2,1)S(1)}, u32[]{:S(2)}, u32[]{:S(2)}) collective-permute-start(s16[64,1024]{1,0:T(8,128)(2,1)S(1)} %get-tuple-element.38), channel_id=1, source_target_pairs={{0,4},{1,5},{2,6},{3,7},{4,0},{5,1},{6,2},{7,3},{8,12},{9,13},{10,... | collective-permute-start | bytes 393224 | tf_op jit(solution)/shard_map/ppermute | solution.py:373
  19.9 0.0 collective-permute-done.1.refs_3_.refs_2_.refs_5_
  19.9 2.5 %collective-permute-start.7 = (s16[64,1024]{1,0:T(8,128)(2,1)S(1)}, s16[64,1024]{1,0:T(8,128)(2,1)S(1)}, u32[]{:S(2)}, u32[]{:S(2)}) collective-permute-start(s16[64,1024]{1,0:T(8,128)(2,1)S(1)} %get-tuple-element.39), channel_id=1, source_target_pairs={{0,6},{1,3},{2,4},{3,1},{4,2},{5,7},{6,0},{7,5},{8,14},{9,11},{10,... | collective-permute-start | bytes 393224 | tf_op jit(solution)/shard_map/ppermute | solution.py:373
  22.4 0.0 collective-permute-done.2.refs_4_.refs_3_.refs_6_
  22.4 0.0 collective-permute-done.8.refs_0_
  22.4 0.7 %contract_far_group.1.refs_1_ = s16[128,1024]{1,0:T(8,128)(2,1)S(1)} custom-call(bf16[128,1024]{1,0:T(8,128)(2,1)S(1)} %collective-permute-done.8.refs_0_, bf16[1024,1024]{1,0:T(8,128)(2,1)S(1)} %get-tuple-element.35.refs_2_.refs_1_, s16[32,1024]{1,0:T(8,128)(2,1)S(1)} %collective-permute-done.refs_2_.refs_1_.refs_4_, ...), custom_call_target="tpu_custom_call" | custom-call | flops 268435456 | bytes 2097152 | tf_op jit(solution)/shard_map/contract_far_group/pallas_call | solution.py:173
  23.1 0.0 copy-start.4
  23.1 0.0 copy-start.5
  23.1 0.0 copy-start.6
  23.1 2.6 %collective-permute-start.11 = (s16[128,1024]{1,0:T(8,128)(2,1)S(1)}, s16[128,1024]{1,0:T(8,128)(2,1)S(1)}, u32[]{:S(2)}, u32[]{:S(2)}) collective-permute-start(s16[128,1024]{1,0:T(8,128)(2,1)S(1)} %contract_far_group.1.refs_1_), channel_id=1, source_target_pairs={{0,24},{1,25},{2,26},{3,27},{4,28},{5,29},{6,30},{7,31},{8,16},{9,... | collective-permute-start | bytes 786440 | tf_op jit(solution)/shard_map/ppermute | solution.py:373
  25.7 0.0 copy-done
  25.8 1.7 %write_residual.1 = (f32[50,16,1024]{2,1,0:T(8,128)}, s32[8,128]{1,0:T(8,128)S(1)}) custom-call(f32[50,16,1024]{2,1,0:T(8,128)S(1)} %bitcast.3, s16[128,1024]{1,0:T(8,128)(2,1)S(1)} %contract_far_group.1.refs_1_), custom_call_target="tpu_custom_call" | custom-call | tf_op jit(solution)/shard_map/write_residual/pallas_call | solution.py:244
  27.5 0.0 collective-permute-done.5.refs_1_
  27.5 1.4 %collective-permute-done.6.refs_2_ = s16[64,1024]{1,0:T(8,128)(2,1)S(1)} collective-permute-done((s16[64,1024]{1,0:T(8,128)(2,1)S(1)}, s16[64,1024]{1,0:T(8,128)(2,1)S(1)}, u32[]{:S(2)}, u32[]{:S(2)}) %collective-permute-start.6) | collective-permute-done | bytes 131104 | tf_op jit(solution)/shard_map/ppermute | solution.py:373
  28.9 0.0 collective-permute-done.7.refs_3_
  29.0 1.6 %collective-permute-start.9 = (s16[128,1024]{1,0:T(8,128)(2,1)S(1)}, s16[128,1024]{1,0:T(8,128)(2,1)S(1)}, u32[]{:S(2)}, u32[]{:S(2)}) collective-permute-start(s16[128,1024]{1,0:T(8,128)(2,1)S(1)} %get-tuple-element.42), channel_id=1, source_target_pairs={{0,8},{1,17},{2,10},{3,19},{4,12},{5,21},{6,14},{7,23},{8,0},{9,25... | collective-permute-start | bytes 786440 | tf_op jit(solution)/shard_map/ppermute | solution.py:373
  30.5 1.4 %collective-permute-start.10 = (s16[128,1024]{1,0:T(8,128)(2,1)S(1)}, s16[128,1024]{1,0:T(8,128)(2,1)S(1)}, u32[]{:S(2)}, u32[]{:S(2)}) collective-permute-start(s16[128,1024]{1,0:T(8,128)(2,1)S(1)} %get-tuple-element.43), channel_id=1, source_target_pairs={{0,16},{1,9},{2,18},{3,11},{4,20},{5,13},{6,22},{7,15},{8,24},{9,1... | collective-permute-start | bytes 786440 | tf_op jit(solution)/shard_map/ppermute | solution.py:373
  32.0 0.0 collective-permute-done.11.refs_0_
  32.0 2.5 %collective-permute-start.12 = (s16[32,1024]{1,0:T(8,128)(2,1)S(1)}, s16[32,1024]{1,0:T(8,128)(2,1)S(1)}, u32[]{:S(2)}, u32[]{:S(2)}) collective-permute-start(s16[32,1024]{1,0:T(8,128)(2,1)S(1)} %get-tuple-element.45), channel_id=1, source_target_pairs={{0,2},{1,7},{2,0},{3,5},{4,6},{5,3},{6,4},{7,1},{8,10},{9,15},{10,... | collective-permute-start | bytes 196616 | tf_op jit(solution)/shard_map/ppermute | solution.py:373
  34.5 1.1 %collective-permute-start.13 = (s16[32,1024]{1,0:T(8,128)(2,1)S(1)}, s16[32,1024]{1,0:T(8,128)(2,1)S(1)}, u32[]{:S(2)}, u32[]{:S(2)}) collective-permute-start(s16[32,1024]{1,0:T(8,128)(2,1)S(1)} %get-tuple-element.46), channel_id=1, source_target_pairs={{0,4},{1,5},{2,6},{3,7},{4,0},{5,1},{6,2},{7,3},{8,12},{9,13},{10,... | collective-permute-start | bytes 196616 | tf_op jit(solution)/shard_map/ppermute | solution.py:373
  35.7 1.4 %collective-permute-start.14 = (s16[32,1024]{1,0:T(8,128)(2,1)S(1)}, s16[32,1024]{1,0:T(8,128)(2,1)S(1)}, u32[]{:S(2)}, u32[]{:S(2)}) collective-permute-start(s16[32,1024]{1,0:T(8,128)(2,1)S(1)} %get-tuple-element.47), channel_id=1, source_target_pairs={{0,6},{1,3},{2,4},{3,1},{4,2},{5,7},{6,0},{7,5},{8,14},{9,11},{10,... | collective-permute-start | bytes 196616 | tf_op jit(solution)/shard_map/ppermute | solution.py:373
  37.0 0.0 collective-permute-done.12.refs_7_.refs_10_
  37.0 3.3 %collective-permute-done.13.refs_8_.refs_11_ = s16[32,1024]{1,0:T(8,128)(2,1)S(1)} collective-permute-done((s16[32,1024]{1,0:T(8,128)(2,1)S(1)}, s16[32,1024]{1,0:T(8,128)(2,1)S(1)}, u32[]{:S(2)}, u32[]{:S(2)}) %collective-permute-start.13) | collective-permute-done | bytes 65568 | tf_op jit(solution)/shard_map/ppermute | solution.py:373
  40.3 1.5 %collective-permute-done.14.refs_9_.refs_12_ = s16[32,1024]{1,0:T(8,128)(2,1)S(1)} collective-permute-done((s16[32,1024]{1,0:T(8,128)(2,1)S(1)}, s16[32,1024]{1,0:T(8,128)(2,1)S(1)}, u32[]{:S(2)}, u32[]{:S(2)}) %collective-permute-start.14) | collective-permute-done | bytes 65568 | tf_op jit(solution)/shard_map/ppermute | solution.py:373
  41.8 0.0 collective-permute-done.9.refs_4_.refs_7_
  41.8 0.0 collective-permute-done.10.refs_5_.refs_8_
  41.8 0.1 collective-permute-start.15
  41.9 0.0 copy-done.4
  41.9 0.0 copy-done.5
  41.9 0.0 copy-done.6
  41.9 1.2 %add_contributions_here.1.refs_4_ = f32[50,16,1024]{2,1,0:T(8,128)S(1)} custom-call(s32[4,8]{1,0:T(4,128)S(1)} %copy-done.5, s32[4,8]{1,0:T(4,128)S(1)} %copy-done.4, s32[4,8]{1,0:T(4,128)S(1)} %copy-done.6, s16[32,1024]{1,0:T(8,128)(2,1)S(1)} %get-tuple-element.29.refs_0_.refs_3_, s16[32,1024]{1,0:T(8,128)(2,1)S(1)} %collective-permute-done.refs_2_.refs_1_.refs_4_, ...), custom_call_target="tpu_custom_call" | custom-call | tf_op jit(solution)/shard_map/add_contributions_here/pallas_call | solution.py:297
  43.1 0.7 %collective-permute-done.15.refs_3_ = s16[256,1024]{1,0:T(8,128)(2,1)S(1)} collective-permute-done((s16[256,1024]{1,0:T(8,128)(2,1)S(1)}, s16[256,1024]{1,0:T(8,128)(2,1)S(1)}, u32[]{:S(2)}, u32[]{:S(2)}) %collective-permute-start.15) | collective-permute-done | bytes 524320 | tf_op jit(solution)/shard_map/ppermute | solution.py:373
  43.8 2.5 %add_contributions_there.1 = f32[50,16,1024]{2,1,0:T(8,128)} custom-call(s32[4,8]{1,0:T(4,128)S(1)} %copy-done.5, s32[4,8]{1,0:T(4,128)S(1)} %copy-done.4, s32[4,8]{1,0:T(4,128)S(1)} %copy-done.6, s16[256,1024]{1,0:T(8,128)(2,1)S(1)} %collective-permute-done.15.refs_3_, ...), custom_call_target="tpu_custom_call", output_to_operand_aliasing={{}: (5, {})} | custom-call | tf_op jit(solution)/shard_map/add_contributions_there/pallas_call | solution.py:344
  (3 shorter events, 0.1 us)
Async XLA Ops:
  0.0 1.2 %copy-start.2 = (bf16[4,128,1024]{2,1,0:T(8,128)(2,1)S(1)}, bf16[4,128,1024]{2,1,0:T(8,128)(2,1)}, u32[]{:S(2)}) copy-start(bf16[4,128,1024]{2,1,0:T(8,128)(2,1)} %amplitudes.1) | copy-start | bytes 3145732
  1.2 0.7 %copy-start.3 = (s32[4,8]{1,0:T(4,128)S(1)}, s32[4,8]{1,0:T(4,128)}, u32[]{:S(2)}) copy-start(s32[4,8]{1,0:T(4,128)} %refs_1_.3) | copy-start | bytes 388
  2.6 11.7 %collective-permute-start.3 = (bf16[128,1024]{1,0:T(8,128)(2,1)S(1)}, bf16[128,1024]{1,0:T(8,128)(2,1)S(1)}, u32[]{:S(2)}, u32[]{:S(2)}) collective-permute-start(bf16[128,1024]{1,0:T(8,128)(2,1)S(1)} %get-tuple-element.33), channel_id=1, source_target_pairs={{0,8},{1,17},{2,10},{3,19},{4,12},{5,21},{6,14},{7,23},{8,0},{9,25... | collective-permute-start | bytes 786440 | tf_op jit(solution)/shard_map/ppermute | solution.py:373
  5.6 11.2 %collective-permute-start.4 = (bf16[128,1024]{1,0:T(8,128)(2,1)S(1)}, bf16[128,1024]{1,0:T(8,128)(2,1)S(1)}, u32[]{:S(2)}, u32[]{:S(2)}) collective-permute-start(bf16[128,1024]{1,0:T(8,128)(2,1)S(1)} %get-tuple-element.34), channel_id=1, source_target_pairs={{0,16},{1,9},{2,18},{3,11},{4,20},{5,13},{6,22},{7,15},{8,24},{9,1... | collective-permute-start | bytes 786440 | tf_op jit(solution)/shard_map/ppermute | solution.py:373
  7.1 1.6 %copy-start.1 = (bf16[1,1024,1024]{2,1,0:T(8,128)(2,1)S(1)}, bf16[1,1024,1024]{2,1,0:T(8,128)(2,1)}, u32[]{:S(2)}) copy-start(bf16[1,1024,1024]{2,1,0:T(8,128)(2,1)} %param.8) | copy-start | bytes 6291460
  9.6 16.1 %copy-start = (f32[16,50,1024]{2,0,1:T(8,128)S(1)}, f32[16,50,1024]{2,0,1:T(8,128)}, u32[]{:S(2)}) copy-start(f32[16,50,1024]{2,0,1:T(8,128)} %param.11) | copy-start | bytes 9830404
  9.6 12.8 %collective-permute-start.8 = (bf16[128,1024]{1,0:T(8,128)(2,1)S(1)}, bf16[128,1024]{1,0:T(8,128)(2,1)S(1)}, u32[]{:S(2)}, u32[]{:S(2)}) collective-permute-start(bf16[128,1024]{1,0:T(8,128)(2,1)S(1)} %get-tuple-element.40), channel_id=1, source_target_pairs={{0,24},{1,25},{2,26},{3,27},{4,28},{5,29},{6,30},{7,31},{8,16},{9,... | collective-permute-start | bytes 786440 | tf_op jit(solution)/shard_map/ppermute | solution.py:373
  9.7 8.3 %collective-permute-start = (s16[32,1024]{1,0:T(8,128)(2,1)S(1)}, s16[32,1024]{1,0:T(8,128)(2,1)S(1)}, u32[]{:S(2)}, u32[]{:S(2)}) collective-permute-start(s16[32,1024]{1,0:T(8,128)(2,1)S(1)} %get-tuple-element.30), channel_id=1, source_target_pairs={{0,2},{1,7},{2,0},{3,5},{4,6},{5,3},{6,4},{7,1},{8,10},{9,15},{10,... | collective-permute-start | bytes 196616 | tf_op jit(solution)/shard_map/ppermute | solution.py:373
  11.7 8.2 %collective-permute-start.1 = (s16[32,1024]{1,0:T(8,128)(2,1)S(1)}, s16[32,1024]{1,0:T(8,128)(2,1)S(1)}, u32[]{:S(2)}, u32[]{:S(2)}) collective-permute-start(s16[32,1024]{1,0:T(8,128)(2,1)S(1)} %get-tuple-element.31), channel_id=1, source_target_pairs={{0,4},{1,5},{2,6},{3,7},{4,0},{5,1},{6,2},{7,3},{8,12},{9,13},{10,... | collective-permute-start | bytes 196616 | tf_op jit(solution)/shard_map/ppermute | solution.py:373
  14.3 8.1 %collective-permute-start.2 = (s16[32,1024]{1,0:T(8,128)(2,1)S(1)}, s16[32,1024]{1,0:T(8,128)(2,1)S(1)}, u32[]{:S(2)}, u32[]{:S(2)}) collective-permute-start(s16[32,1024]{1,0:T(8,128)(2,1)S(1)} %get-tuple-element.32), channel_id=1, source_target_pairs={{0,6},{1,3},{2,4},{3,1},{4,2},{5,7},{6,0},{7,5},{8,14},{9,11},{10,... | collective-permute-start | bytes 196616 | tf_op jit(solution)/shard_map/ppermute | solution.py:373
  17.9 9.6 %collective-permute-start.5 = (s16[64,1024]{1,0:T(8,128)(2,1)S(1)}, s16[64,1024]{1,0:T(8,128)(2,1)S(1)}, u32[]{:S(2)}, u32[]{:S(2)}) collective-permute-start(s16[64,1024]{1,0:T(8,128)(2,1)S(1)} %get-tuple-element.37), channel_id=1, source_target_pairs={{0,2},{1,7},{2,0},{3,5},{4,6},{5,3},{6,4},{7,1},{8,10},{9,15},{10,... | collective-permute-start | bytes 393224 | tf_op jit(solution)/shard_map/ppermute | solution.py:373
  18.0 10.9 %collective-permute-start.6 = (s16[64,1024]{1,0:T(8,128)(2,1)S(1)}, s16[64,1024]{1,0:T(8,128)(2,1)S(1)}, u32[]{:S(2)}, u32[]{:S(2)}) collective-permute-start(s16[64,1024]{1,0:T(8,128)(2,1)S(1)} %get-tuple-element.38), channel_id=1, source_target_pairs={{0,4},{1,5},{2,6},{3,7},{4,0},{5,1},{6,2},{7,3},{8,12},{9,13},{10,... | collective-permute-start | bytes 393224 | tf_op jit(solution)/shard_map/ppermute | solution.py:373
  19.9 9.0 %collective-permute-start.7 = (s16[64,1024]{1,0:T(8,128)(2,1)S(1)}, s16[64,1024]{1,0:T(8,128)(2,1)S(1)}, u32[]{:S(2)}, u32[]{:S(2)}) collective-permute-start(s16[64,1024]{1,0:T(8,128)(2,1)S(1)} %get-tuple-element.39), channel_id=1, source_target_pairs={{0,6},{1,3},{2,4},{3,1},{4,2},{5,7},{6,0},{7,5},{8,14},{9,11},{10,... | collective-permute-start | bytes 393224 | tf_op jit(solution)/shard_map/ppermute | solution.py:373
  23.1 18.8 %copy-start.4 = (s32[4,8]{1,0:T(4,128)S(1)}, s32[4,8]{1,0:T(4,128)}, u32[]{:S(2)}) copy-start(s32[4,8]{1,0:T(4,128)} %refs_1_.3) | copy-start | bytes 388
  23.1 18.8 %copy-start.5 = (s32[4,8]{1,0:T(4,128)S(1)}, s32[4,8]{1,0:T(4,128)}, u32[]{:S(2)}) copy-start(s32[4,8]{1,0:T(4,128)} %refs_0_.3) | copy-start | bytes 388
  23.1 18.8 %copy-start.6 = (s32[4,8]{1,0:T(4,128)S(1)}, s32[4,8]{1,0:T(4,128)}, u32[]{:S(2)}) copy-start(s32[4,8]{1,0:T(4,128)} %refs_2_.3) | copy-start | bytes 388
  23.1 8.8 %collective-permute-start.11 = (s16[128,1024]{1,0:T(8,128)(2,1)S(1)}, s16[128,1024]{1,0:T(8,128)(2,1)S(1)}, u32[]{:S(2)}, u32[]{:S(2)}) collective-permute-start(s16[128,1024]{1,0:T(8,128)(2,1)S(1)} %contract_far_group.1.refs_1_), channel_id=1, source_target_pairs={{0,24},{1,25},{2,26},{3,27},{4,28},{5,29},{6,30},{7,31},{8,16},{9,... | collective-permute-start | bytes 786440 | tf_op jit(solution)/shard_map/ppermute | solution.py:373
  29.0 12.8 %collective-permute-start.9 = (s16[128,1024]{1,0:T(8,128)(2,1)S(1)}, s16[128,1024]{1,0:T(8,128)(2,1)S(1)}, u32[]{:S(2)}, u32[]{:S(2)}) collective-permute-start(s16[128,1024]{1,0:T(8,128)(2,1)S(1)} %get-tuple-element.42), channel_id=1, source_target_pairs={{0,8},{1,17},{2,10},{3,19},{4,12},{5,21},{6,14},{7,23},{8,0},{9,25... | collective-permute-start | bytes 786440 | tf_op jit(solution)/shard_map/ppermute | solution.py:373
  30.5 11.3 %collective-permute-start.10 = (s16[128,1024]{1,0:T(8,128)(2,1)S(1)}, s16[128,1024]{1,0:T(8,128)(2,1)S(1)}, u32[]{:S(2)}, u32[]{:S(2)}) collective-permute-start(s16[128,1024]{1,0:T(8,128)(2,1)S(1)} %get-tuple-element.43), channel_id=1, source_target_pairs={{0,16},{1,9},{2,18},{3,11},{4,20},{5,13},{6,22},{7,15},{8,24},{9,1... | collective-permute-start | bytes 786440 | tf_op jit(solution)/shard_map/ppermute | solution.py:373
  32.0 5.0 %collective-permute-start.12 = (s16[32,1024]{1,0:T(8,128)(2,1)S(1)}, s16[32,1024]{1,0:T(8,128)(2,1)S(1)}, u32[]{:S(2)}, u32[]{:S(2)}) collective-permute-start(s16[32,1024]{1,0:T(8,128)(2,1)S(1)} %get-tuple-element.45), channel_id=1, source_target_pairs={{0,2},{1,7},{2,0},{3,5},{4,6},{5,3},{6,4},{7,1},{8,10},{9,15},{10,... | collective-permute-start | bytes 196616 | tf_op jit(solution)/shard_map/ppermute | solution.py:373
  34.5 5.8 %collective-permute-start.13 = (s16[32,1024]{1,0:T(8,128)(2,1)S(1)}, s16[32,1024]{1,0:T(8,128)(2,1)S(1)}, u32[]{:S(2)}, u32[]{:S(2)}) collective-permute-start(s16[32,1024]{1,0:T(8,128)(2,1)S(1)} %get-tuple-element.46), channel_id=1, source_target_pairs={{0,4},{1,5},{2,6},{3,7},{4,0},{5,1},{6,2},{7,3},{8,12},{9,13},{10,... | collective-permute-start | bytes 196616 | tf_op jit(solution)/shard_map/ppermute | solution.py:373
  35.7 6.1 %collective-permute-start.14 = (s16[32,1024]{1,0:T(8,128)(2,1)S(1)}, s16[32,1024]{1,0:T(8,128)(2,1)S(1)}, u32[]{:S(2)}, u32[]{:S(2)}) collective-permute-start(s16[32,1024]{1,0:T(8,128)(2,1)S(1)} %get-tuple-element.47), channel_id=1, source_target_pairs={{0,6},{1,3},{2,4},{3,1},{4,2},{5,7},{6,0},{7,5},{8,14},{9,11},{10,... | collective-permute-start | bytes 196616 | tf_op jit(solution)/shard_map/ppermute | solution.py:373
  41.8 2.0 %collective-permute-start.15 = (s16[256,1024]{1,0:T(8,128)(2,1)S(1)}, s16[256,1024]{1,0:T(8,128)(2,1)S(1)}, u32[]{:S(2)}, u32[]{:S(2)}) collective-permute-start(s16[256,1024]{1,0:T(8,128)(2,1)S(1)} %rows_of_other_core.1), channel_id=1, source_target_pairs={{0,1},{1,0},{2,3},{3,2},{4,5},{5,4},{6,7},{7,6},{8,9},{9,8},{10,11... | collective-permute-start | bytes 1572872 | tf_op jit(solution)/shard_map/ppermute | solution.py:373

commit v18 on v15

--- a/solution.py
+++ b/solution.py
@@ -383,8 +383,12 @@
     by_tile = jnp.transpose(residual_in, (1, 0, 2))
     far_coded = contract_far(far_rows, tile, chips, own_in[1:])
     written, token = write_residual(by_tile, [far_coded])
-    near_back = regroup(near_in, blk_count - 2, "regroup_by_group", [token])
-    near_in = [swap(rows, index + 1, 0) for index, rows in enumerate(near_back)]
+    half = chips // 2
+    first_back = regroup(near_in[:half], blk_count - 2, "regroup_first_chips", [token])
+    last_back = regroup(near_in[half:], blk_count - 2, "regroup_last_chips", [token])
+    near_in = []
+    for index in range(blk_count - 2):
+        near_in += [swap(back[index], index + 1, 0) for back in (first_back, last_back)]
     far_in = along_chips(regroup([swap(far_coded, far, 0)], chips, "regroup_by_chip"))
 
     tables = (tile_ab, tile_cd, pair_screen)

time: 46.6 us -> 49.8 us (1.069)
  starting transfers between devices: 26 us -> 29.4 us
    ppermute x16 -> x18, starting transfers between devices: 26 us -> 29.4 us  [swap(): return lax.ppermute(value, ('blk', 'grp'), pairs)]
    ppermute x16 -> x18, waiting for transfers between devices: 7.78 us -> 7.6 us  [swap(): return lax.ppermute(value, ('blk', 'grp'), pairs)]
  transfers between devices with their start and end apart: 16 -> 18, of which waited for: 5 -> 5; matrix products, arithmetic and copies ran while one was open for 0% -> 0% of each run, Pallas kernels for 12% -> 12%
where the time goes in v18:
time: 49.8 us; the launch traced here: 49.6 us
  starting transfers between devices  29.4 us (59%)
  Pallas kernels  8.91 us (18%)
  waiting for transfers between devices  7.6 us (15%)
  local copies, waits for them, and re-layouts  3.52 us (7%)
    ppermute x18, starting transfers between devices, swap(): return lax.ppermute(value, ('blk', 'grp'), pairs)  29.4 us
    ppermute x18, waiting for transfers between devices, swap(): return lax.ppermute(value, ('blk', 'grp'), pairs)  7.6 us
    unnamed x14, local copies, waits for them, and re-layouts  3.52 us
    pallas_call x1, Pallas kernels, add_there(): pl.pallas_call(lambda *refs: add_there_kernel(count, *refs), out_shape=wh...  2.46 us
    pallas_call x1, Pallas kernels, write_residual(): pl.pallas_call(lambda *refs: write_kernel(parts, *refs), out_shape=[jax.S...  1.74 us
    pallas_call x1, Pallas kernels, add_here(): pl.pallas_call(lambda *refs: add_here_kernel(pieces, *refs), out_shape=ja...  1.21 us
    pallas_call x1, Pallas kernels, contract_near(): pl.pallas_call(lambda *refs: near_kernel(len(groups), *refs), out_shape=[...  1.14 us
  transfers between devices with their start and end apart: 18, of which 5 were waited for; matrix products, arithmetic and copies ran while one was open for 0% of the time, Pallas kernels for 12%

profile of v18, /device:TPU:0, one launch (start us, length us, event | category | flops | bytes accessed | tf_op | source)
XLA Modules:
  0.0 49.6 jit_solution(6049477424197500370)
XLA Ops:
  0.0 0.0 copy-start.2
  0.0 1.2 %copy-done.2 = bf16[4,128,1024]{2,1,0:T(8,128)(2,1)S(1)} copy-done((bf16[4,128,1024]{2,1,0:T(8,128)(2,1)S(1)}, bf16[4,128,1024]{2,1,0:T(8,128)(2,1)}, u32[]{:S(2)}) %copy-start.2) | copy-done | bytes 1048600
  1.2 0.0 copy-start.3
  1.2 0.7 %copy-done.3 = s32[4,8]{1,0:T(4,128)S(1)} copy-done((s32[4,8]{1,0:T(4,128)S(1)}, s32[4,8]{1,0:T(4,128)}, u32[]{:S(2)}) %copy-start.3) | copy-done | bytes 152
  1.9 0.7 %pick_cd_blocks.1 = (bf16[128,1024]{1,0:T(8,128)(2,1)S(1)}, bf16[128,1024]{1,0:T(8,128)(2,1)S(1)}, bf16[128,1024]{1,0:T(8,128)(2,1)S(1)}, bf16[128,1024]{1,0:T(8,128)(2,1)S(1)}) custom-call(s32[4,8]{1,0:T(4,128)S(1)} %copy-done.3, bf16[4,128,1024]{2,1,0:T(8,128)(2,1)S(1)} %copy-done.2), custom_call_target="tpu_custom_call" | custom-call | tf_op jit(solution)/shard_map/pick_cd_blocks/pallas_call | solution.py:91
  2.6 3.0 %collective-permute-start.3 = (bf16[128,1024]{1,0:T(8,128)(2,1)S(1)}, bf16[128,1024]{1,0:T(8,128)(2,1)S(1)}, u32[]{:S(2)}, u32[]{:S(2)}) collective-permute-start(bf16[128,1024]{1,0:T(8,128)(2,1)S(1)} %get-tuple-element.35), channel_id=1, source_target_pairs={{0,8},{1,17},{2,10},{3,19},{4,12},{5,21},{6,14},{7,23},{8,0},{9,25... | collective-permute-start | bytes 786440 | tf_op jit(solution)/shard_map/ppermute | solution.py:371
  5.6 1.5 %collective-permute-start.4 = (bf16[128,1024]{1,0:T(8,128)(2,1)S(1)}, bf16[128,1024]{1,0:T(8,128)(2,1)S(1)}, u32[]{:S(2)}, u32[]{:S(2)}) collective-permute-start(bf16[128,1024]{1,0:T(8,128)(2,1)S(1)} %get-tuple-element.36), channel_id=1, source_target_pairs={{0,16},{1,9},{2,18},{3,11},{4,20},{5,13},{6,22},{7,15},{8,24},{9,1... | collective-permute-start | bytes 786440 | tf_op jit(solution)/shard_map/ppermute | solution.py:371
  7.1 0.0 copy-start.1
  7.1 1.6 %copy-done.1 = bf16[1,1024,1024]{2,1,0:T(8,128)(2,1)S(1)} copy-done((bf16[1,1024,1024]{2,1,0:T(8,128)(2,1)S(1)}, bf16[1,1024,1024]{2,1,0:T(8,128)(2,1)}, u32[]{:S(2)}) %copy-start.1) | copy-done | bytes 2097176
  8.7 0.9 %contract_own_group.1 = (s16[32,1024]{1,0:T(8,128)(2,1)S(1)}, s16[32,1024]{1,0:T(8,128)(2,1)S(1)}, s16[32,1024]{1,0:T(8,128)(2,1)S(1)}, s16[32,1024]{1,0:T(8,128...) custom-call(bf16[128,1024]{1,0:T(8,128)(2,1)S(1)} %get-tuple-element.29.rows, ...), custom_call_target="tpu_custom_call" | custom-call | flops 268435456 | bytes 2097152 | tf_op jit(solution)/shard_map/contract_own_group/pallas_call | solution.py:127
  9.6 0.0 copy-start
  9.6 0.1 collective-permute-start.6
  9.7 2.0 %collective-permute-start = (s16[32,1024]{1,0:T(8,128)(2,1)S(1)}, s16[32,1024]{1,0:T(8,128)(2,1)S(1)}, u32[]{:S(2)}, u32[]{:S(2)}) collective-permute-start(s16[32,1024]{1,0:T(8,128)(2,1)S(1)} %get-tuple-element.32), channel_id=1, source_target_pairs={{0,2},{1,3},{2,0},{3,1},{4,6},{5,7},{6,4},{7,5},{8,10},{9,11},{10,... | collective-permute-start | bytes 196616 | tf_op jit(solution)/shard_map/ppermute | solution.py:371
  11.7 2.6 %collective-permute-start.1 = (s16[32,1024]{1,0:T(8,128)(2,1)S(1)}, s16[32,1024]{1,0:T(8,128)(2,1)S(1)}, u32[]{:S(2)}, u32[]{:S(2)}) collective-permute-start(s16[32,1024]{1,0:T(8,128)(2,1)S(1)} %get-tuple-element.33), channel_id=1, source_target_pairs={{0,4},{1,5},{2,6},{3,7},{4,0},{5,1},{6,2},{7,3},{8,12},{9,13},{10,... | collective-permute-start | bytes 196616 | tf_op jit(solution)/shard_map/ppermute | solution.py:371
  14.3 0.0 collective-permute-done.3.refs_0_
  14.3 2.5 %collective-permute-start.2 = (s16[32,1024]{1,0:T(8,128)(2,1)S(1)}, s16[32,1024]{1,0:T(8,128)(2,1)S(1)}, u32[]{:S(2)}, u32[]{:S(2)}) collective-permute-start(s16[32,1024]{1,0:T(8,128)(2,1)S(1)} %get-tuple-element.34), channel_id=1, source_target_pairs={{0,6},{1,7},{2,4},{3,5},{4,2},{5,3},{6,0},{7,1},{8,14},{9,15},{10,... | collective-permute-start | bytes 196616 | tf_op jit(solution)/shard_map/ppermute | solution.py:371
  16.8 0.0 collective-permute-done.4.refs_1_
  16.8 1.1 %contract_near_groups.1 = (s16[64,1024]{1,0:T(8,128)(2,1)S(1)}, s16[64,1024]{1,0:T(8,128)(2,1)S(1)}, s16[64,1024]{1,0:T(8,128)(2,1)S(1)}, s16[64,1024]{1,0:T(8,128)(2,1)S(1)}) custom-call(bf16[128,1024]{1,0:T(8,128)(2,1)S(1)} %collective-permute-done.3.refs_0_, bf16[128,1024]{1,0:T(8,128)(2,1)S(1)} %collective-permute-done.4.refs_1_, ...), custom_call_target="tpu_custom_call" | custom-call | flops 536870912 | bytes 2097152 | tf_op jit(solution)/shard_map/contract_near_groups/pallas_call | solution.py:150
  17.9 0.1 collective-permute-start.8
  18.0 0.0 collective-permute-done.refs_2_.refs_1_.refs_4_
  18.0 1.9 %collective-permute-start.9 = (s16[64,1024]{1,0:T(8,128)(2,1)S(1)}, s16[64,1024]{1,0:T(8,128)(2,1)S(1)}, u32[]{:S(2)}, u32[]{:S(2)}) collective-permute-start(s16[64,1024]{1,0:T(8,128)(2,1)S(1)} %get-tuple-element.44), channel_id=1, source_target_pairs={{0,6},{1,7},{2,4},{3,5},{4,2},{5,3},{6,0},{7,1},{8,14},{9,15},{10,... | collective-permute-start | bytes 393224 | tf_op jit(solution)/shard_map/ppermute | solution.py:371
  19.9 0.0 collective-permute-done.1.refs_3_.refs_2_.refs_5_
  19.9 1.2 %collective-permute-done.2.refs_4_.refs_3_.refs_6_ = s16[32,1024]{1,0:T(8,128)(2,1)S(1)} collective-permute-done((s16[32,1024]{1,0:T(8,128)(2,1)S(1)}, s16[32,1024]{1,0:T(8,128)(2,1)S(1)}, u32[]{:S(2)}, u32[]{:S(2)}) %collective-permute-start.2) | collective-permute-done | bytes 65568 | tf_op jit(solution)/shard_map/ppermute | solution.py:371
  21.2 0.0 collective-permute-done.6.refs_0_
  21.2 0.7 %contract_far_group.1.refs_1_ = s16[128,1024]{1,0:T(8,128)(2,1)S(1)} custom-call(bf16[128,1024]{1,0:T(8,128)(2,1)S(1)} %collective-permute-done.6.refs_0_, bf16[1024,1024]{1,0:T(8,128)(2,1)S(1)} %get-tuple-element.37.refs_2_.refs_1_, s16[32,1024]{1,0:T(8,128)(2,1)S(1)} %collective-permute-done.refs_2_.refs_1_.refs_4_, ...), custom_call_target="tpu_custom_call" | custom-call | flops 268435456 | bytes 2097152 | tf_op jit(solution)/shard_map/contract_far_group/pallas_call | solution.py:172
  21.9 0.0 copy-start.4
  21.9 0.0 copy-start.5
  21.9 0.0 copy-start.6
  21.9 2.5 %collective-permute-start.13 = (s16[128,1024]{1,0:T(8,128)(2,1)S(1)}, s16[128,1024]{1,0:T(8,128)(2,1)S(1)}, u32[]{:S(2)}, u32[]{:S(2)}) collective-permute-start(s16[128,1024]{1,0:T(8,128)(2,1)S(1)} %contract_far_group.1.refs_1_), channel_id=1, source_target_pairs={{0,24},{1,25},{2,26},{3,27},{4,28},{5,29},{6,30},{7,31},{8,16},{9,... | collective-permute-start | bytes 786440 | tf_op jit(solution)/shard_map/ppermute | solution.py:371
  24.4 5.3 %collective-permute-start.5 = (s16[64,1024]{1,0:T(8,128)(2,1)S(1)}, s16[64,1024]{1,0:T(8,128)(2,1)S(1)}, u32[]{:S(2)}, u32[]{:S(2)}) collective-permute-start(s16[64,1024]{1,0:T(8,128)(2,1)S(1)} %get-tuple-element.39), channel_id=1, source_target_pairs={{0,2},{1,3},{2,0},{3,1},{4,6},{5,7},{6,4},{7,5},{8,10},{9,11},{10,... | collective-permute-start | bytes 393224 | tf_op jit(solution)/shard_map/ppermute | solution.py:371
  29.7 0.0 copy-done
  29.7 1.7 %write_residual.1 = (f32[50,16,1024]{2,1,0:T(8,128)}, s32[8,128]{1,0:T(8,128)S(1)}) custom-call(f32[50,16,1024]{2,1,0:T(8,128)S(1)} %bitcast.3, s16[128,1024]{1,0:T(8,128)(2,1)S(1)} %contract_far_group.1.refs_1_), custom_call_target="tpu_custom_call" | custom-call | tf_op jit(solution)/shard_map/write_residual/pallas_call | solution.py:243
  31.5 0.0 collective-permute-done.8.refs_0_
  31.5 0.0 collective-permute-done.9.refs_1_
  31.5 1.1 %collective-permute-start.10 = (s16[64,1024]{1,0:T(8,128)(2,1)S(1)}, s16[64,1024]{1,0:T(8,128)(2,1)S(1)}, u32[]{:S(2)}, u32[]{:S(2)}) collective-permute-start(s16[64,1024]{1,0:T(8,128)(2,1)S(1)} %get-tuple-element.45), channel_id=1, source_target_pairs={{0,8},{1,17},{2,10},{3,19},{4,12},{5,21},{6,14},{7,23},{8,0},{9,25... | collective-permute-start | bytes 393224 | tf_op jit(solution)/shard_map/ppermute | solution.py:371
  32.6 0.4 collective-permute-start.12
  33.0 0.0 collective-permute-done.5.refs_1_
  33.1 1.0 %collective-permute-start.7 = (s16[64,1024]{1,0:T(8,128)(2,1)S(1)}, s16[64,1024]{1,0:T(8,128)(2,1)S(1)}, u32[]{:S(2)}, u32[]{:S(2)}) collective-permute-start(s16[64,1024]{1,0:T(8,128)(2,1)S(1)} %get-tuple-element.42), channel_id=1, source_target_pairs={{0,8},{1,17},{2,10},{3,19},{4,12},{5,21},{6,14},{7,23},{8,0},{9,25... | collective-permute-start | bytes 393224 | tf_op jit(solution)/shard_map/ppermute | solution.py:371
  34.1 1.6 %collective-permute-start.11 = (s16[64,1024]{1,0:T(8,128)(2,1)S(1)}, s16[64,1024]{1,0:T(8,128)(2,1)S(1)}, u32[]{:S(2)}, u32[]{:S(2)}) collective-permute-start(s16[64,1024]{1,0:T(8,128)(2,1)S(1)} %get-tuple-element.46), channel_id=1, source_target_pairs={{0,16},{1,9},{2,18},{3,11},{4,20},{5,13},{6,22},{7,15},{8,24},{9,1... | collective-permute-start | bytes 393224 | tf_op jit(solution)/shard_map/ppermute | solution.py:371
  35.7 0.0 collective-permute-done.13.refs_0_
  35.8 0.6 %collective-permute-start.14 = (s16[32,1024]{1,0:T(8,128)(2,1)S(1)}, s16[32,1024]{1,0:T(8,128)(2,1)S(1)}, u32[]{:S(2)}, u32[]{:S(2)}) collective-permute-start(s16[32,1024]{1,0:T(8,128)(2,1)S(1)} %get-tuple-element.49), channel_id=1, source_target_pairs={{0,2},{1,3},{2,0},{3,1},{4,6},{5,7},{6,4},{7,5},{8,10},{9,11},{10,... | collective-permute-start | bytes 196616 | tf_op jit(solution)/shard_map/ppermute | solution.py:371
  36.3 1.1 %collective-permute-done.10.refs_5_.refs_8_ = s16[64,1024]{1,0:T(8,128)(2,1)S(1)} collective-permute-done((s16[64,1024]{1,0:T(8,128)(2,1)S(1)}, s16[64,1024]{1,0:T(8,128)(2,1)S(1)}, u32[]{:S(2)}, u32[]{:S(2)}) %collective-permute-start.10) | collective-permute-done | bytes 131104 | tf_op jit(solution)/shard_map/ppermute | solution.py:371
  37.4 1.6 %collective-permute-start.15 = (s16[32,1024]{1,0:T(8,128)(2,1)S(1)}, s16[32,1024]{1,0:T(8,128)(2,1)S(1)}, u32[]{:S(2)}, u32[]{:S(2)}) collective-permute-start(s16[32,1024]{1,0:T(8,128)(2,1)S(1)} %get-tuple-element.50), channel_id=1, source_target_pairs={{0,4},{1,5},{2,6},{3,7},{4,0},{5,1},{6,2},{7,3},{8,12},{9,13},{10,... | collective-permute-start | bytes 196616 | tf_op jit(solution)/shard_map/ppermute | solution.py:371
  39.0 0.0 collective-permute-done.12.refs_7_.refs_10_
  39.0 1.5 %collective-permute-start.16 = (s16[32,1024]{1,0:T(8,128)(2,1)S(1)}, s16[32,1024]{1,0:T(8,128)(2,1)S(1)}, u32[]{:S(2)}, u32[]{:S(2)}) collective-permute-start(s16[32,1024]{1,0:T(8,128)(2,1)S(1)} %get-tuple-element.51), channel_id=1, source_target_pairs={{0,6},{1,7},{2,4},{3,5},{4,2},{5,3},{6,0},{7,1},{8,14},{9,15},{10,... | collective-permute-start | bytes 196616 | tf_op jit(solution)/shard_map/ppermute | solution.py:371
  40.5 0.0 collective-permute-done.7.refs_4_.refs_7_
  40.5 0.0 collective-permute-done.11.refs_6_.refs_9_
  40.5 0.0 collective-permute-done.14.refs_9_.refs_12_
  40.5 2.8 %collective-permute-done.15.refs_10_.refs_13_ = s16[32,1024]{1,0:T(8,128)(2,1)S(1)} collective-permute-done((s16[32,1024]{1,0:T(8,128)(2,1)S(1)}, s16[32,1024]{1,0:T(8,128)(2,1)S(1)}, u32[]{:S(2)}, u32[]{:S(2)}) %collective-permute-start.15) | collective-permute-done | bytes 65568 | tf_op jit(solution)/shard_map/ppermute | solution.py:371
  43.3 1.8 %collective-permute-done.16.refs_11_.refs_14_ = s16[32,1024]{1,0:T(8,128)(2,1)S(1)} collective-permute-done((s16[32,1024]{1,0:T(8,128)(2,1)S(1)}, s16[32,1024]{1,0:T(8,128)(2,1)S(1)}, u32[]{:S(2)}, u32[]{:S(2)}) %collective-permute-start.16) | collective-permute-done | bytes 65568 | tf_op jit(solution)/shard_map/ppermute | solution.py:371
  45.2 0.1 collective-permute-start.17
  45.2 0.0 copy-done.4
  45.2 0.0 copy-done.5
  45.3 0.0 copy-done.6
  45.3 1.2 %add_contributions_here.1.refs_4_ = f32[50,16,1024]{2,1,0:T(8,128)S(1)} custom-call(s32[4,8]{1,0:T(4,128)S(1)} %copy-done.5, s32[4,8]{1,0:T(4,128)S(1)} %copy-done.4, s32[4,8]{1,0:T(4,128)S(1)} %copy-done.6, s16[32,1024]{1,0:T(8,128)(2,1)S(1)} %get-tuple-element.31.refs_0_.refs_3_, s16[32,1024]{1,0:T(8,128)(2,1)S(1)} %collective-permute-done.refs_2_.refs_1_.refs_4_, ...), custom_call_target="tpu_custom_call" | custom-call | tf_op jit(solution)/shard_map/add_contributions_here/pallas_call | solution.py:296
  46.5 0.7 %collective-permute-done.17.refs_3_ = s16[256,1024]{1,0:T(8,128)(2,1)S(1)} collective-permute-done((s16[256,1024]{1,0:T(8,128)(2,1)S(1)}, s16[256,1024]{1,0:T(8,128)(2,1)S(1)}, u32[]{:S(2)}, u32[]{:S(2)}) %collective-permute-start.17) | collective-permute-done | bytes 524320 | tf_op jit(solution)/shard_map/ppermute | solution.py:371
  47.1 2.5 %add_contributions_there.1 = f32[50,16,1024]{2,1,0:T(8,128)} custom-call(s32[4,8]{1,0:T(4,128)S(1)} %copy-done.5, s32[4,8]{1,0:T(4,128)S(1)} %copy-done.4, s32[4,8]{1,0:T(4,128)S(1)} %copy-done.6, s16[256,1024]{1,0:T(8,128)(2,1)S(1)} %collective-permute-done.17.refs_3_, ...), custom_call_target="tpu_custom_call", output_to_operand_aliasing={{}: (5, {})} | custom-call | tf_op jit(solution)/shard_map/add_contributions_there/pallas_call | solution.py:343
  (4 shorter events, 0.1 us)
Async XLA Ops:
  0.0 1.2 %copy-start.2 = (bf16[4,128,1024]{2,1,0:T(8,128)(2,1)S(1)}, bf16[4,128,1024]{2,1,0:T(8,128)(2,1)}, u32[]{:S(2)}) copy-start(bf16[4,128,1024]{2,1,0:T(8,128)(2,1)} %amplitudes.1) | copy-start | bytes 3145732
  1.2 0.7 %copy-start.3 = (s32[4,8]{1,0:T(4,128)S(1)}, s32[4,8]{1,0:T(4,128)}, u32[]{:S(2)}) copy-start(s32[4,8]{1,0:T(4,128)} %refs_1_.3) | copy-start | bytes 388
  2.6 11.7 %collective-permute-start.3 = (bf16[128,1024]{1,0:T(8,128)(2,1)S(1)}, bf16[128,1024]{1,0:T(8,128)(2,1)S(1)}, u32[]{:S(2)}, u32[]{:S(2)}) collective-permute-start(bf16[128,1024]{1,0:T(8,128)(2,1)S(1)} %get-tuple-element.35), channel_id=1, source_target_pairs={{0,8},{1,17},{2,10},{3,19},{4,12},{5,21},{6,14},{7,23},{8,0},{9,25... | collective-permute-start | bytes 786440 | tf_op jit(solution)/shard_map/ppermute | solution.py:371
  5.6 11.2 %collective-permute-start.4 = (bf16[128,1024]{1,0:T(8,128)(2,1)S(1)}, bf16[128,1024]{1,0:T(8,128)(2,1)S(1)}, u32[]{:S(2)}, u32[]{:S(2)}) collective-permute-start(bf16[128,1024]{1,0:T(8,128)(2,1)S(1)} %get-tuple-element.36), channel_id=1, source_target_pairs={{0,16},{1,9},{2,18},{3,11},{4,20},{5,13},{6,22},{7,15},{8,24},{9,1... | collective-permute-start | bytes 786440 | tf_op jit(solution)/shard_map/ppermute | solution.py:371
  7.1 1.6 %copy-start.1 = (bf16[1,1024,1024]{2,1,0:T(8,128)(2,1)S(1)}, bf16[1,1024,1024]{2,1,0:T(8,128)(2,1)}, u32[]{:S(2)}) copy-start(bf16[1,1024,1024]{2,1,0:T(8,128)(2,1)} %param.8) | copy-start | bytes 6291460
  9.6 20.1 %copy-start = (f32[16,50,1024]{2,0,1:T(8,128)S(1)}, f32[16,50,1024]{2,0,1:T(8,128)}, u32[]{:S(2)}) copy-start(f32[16,50,1024]{2,0,1:T(8,128)} %param.11) | copy-start | bytes 9830404
  9.6 11.5 %collective-permute-start.6 = (bf16[128,1024]{1,0:T(8,128)(2,1)S(1)}, bf16[128,1024]{1,0:T(8,128)(2,1)S(1)}, u32[]{:S(2)}, u32[]{:S(2)}) collective-permute-start(bf16[128,1024]{1,0:T(8,128)(2,1)S(1)} %get-tuple-element.40), channel_id=1, source_target_pairs={{0,24},{1,25},{2,26},{3,27},{4,28},{5,29},{6,30},{7,31},{8,16},{9,... | collective-permute-start | bytes 786440 | tf_op jit(solution)/shard_map/ppermute | solution.py:371
  9.7 8.3 %collective-permute-start = (s16[32,1024]{1,0:T(8,128)(2,1)S(1)}, s16[32,1024]{1,0:T(8,128)(2,1)S(1)}, u32[]{:S(2)}, u32[]{:S(2)}) collective-permute-start(s16[32,1024]{1,0:T(8,128)(2,1)S(1)} %get-tuple-element.32), channel_id=1, source_target_pairs={{0,2},{1,3},{2,0},{3,1},{4,6},{5,7},{6,4},{7,5},{8,10},{9,11},{10,... | collective-permute-start | bytes 196616 | tf_op jit(solution)/shard_map/ppermute | solution.py:371
  11.7 8.2 %collective-permute-start.1 = (s16[32,1024]{1,0:T(8,128)(2,1)S(1)}, s16[32,1024]{1,0:T(8,128)(2,1)S(1)}, u32[]{:S(2)}, u32[]{:S(2)}) collective-permute-start(s16[32,1024]{1,0:T(8,128)(2,1)S(1)} %get-tuple-element.33), channel_id=1, source_target_pairs={{0,4},{1,5},{2,6},{3,7},{4,0},{5,1},{6,2},{7,3},{8,12},{9,13},{10,... | collective-permute-start | bytes 196616 | tf_op jit(solution)/shard_map/ppermute | solution.py:371
  14.3 6.8 %collective-permute-start.2 = (s16[32,1024]{1,0:T(8,128)(2,1)S(1)}, s16[32,1024]{1,0:T(8,128)(2,1)S(1)}, u32[]{:S(2)}, u32[]{:S(2)}) collective-permute-start(s16[32,1024]{1,0:T(8,128)(2,1)S(1)} %get-tuple-element.34), channel_id=1, source_target_pairs={{0,6},{1,7},{2,4},{3,5},{4,2},{5,3},{6,0},{7,1},{8,14},{9,15},{10,... | collective-permute-start | bytes 196616 | tf_op jit(solution)/shard_map/ppermute | solution.py:371
  17.9 13.5 %collective-permute-start.8 = (s16[64,1024]{1,0:T(8,128)(2,1)S(1)}, s16[64,1024]{1,0:T(8,128)(2,1)S(1)}, u32[]{:S(2)}, u32[]{:S(2)}) collective-permute-start(s16[64,1024]{1,0:T(8,128)(2,1)S(1)} %get-tuple-element.43), channel_id=1, source_target_pairs={{0,4},{1,5},{2,6},{3,7},{4,0},{5,1},{6,2},{7,3},{8,12},{9,13},{10,... | collective-permute-start | bytes 393224 | tf_op jit(solution)/shard_map/ppermute | solution.py:371
  18.0 13.4 %collective-permute-start.9 = (s16[64,1024]{1,0:T(8,128)(2,1)S(1)}, s16[64,1024]{1,0:T(8,128)(2,1)S(1)}, u32[]{:S(2)}, u32[]{:S(2)}) collective-permute-start(s16[64,1024]{1,0:T(8,128)(2,1)S(1)} %get-tuple-element.44), channel_id=1, source_target_pairs={{0,6},{1,7},{2,4},{3,5},{4,2},{5,3},{6,0},{7,1},{8,14},{9,15},{10,... | collective-permute-start | bytes 393224 | tf_op jit(solution)/shard_map/ppermute | solution.py:371
  21.9 23.4 %copy-start.4 = (s32[4,8]{1,0:T(4,128)S(1)}, s32[4,8]{1,0:T(4,128)}, u32[]{:S(2)}) copy-start(s32[4,8]{1,0:T(4,128)} %refs_1_.3) | copy-start | bytes 388
  21.9 23.4 %copy-start.5 = (s32[4,8]{1,0:T(4,128)S(1)}, s32[4,8]{1,0:T(4,128)}, u32[]{:S(2)}) copy-start(s32[4,8]{1,0:T(4,128)} %refs_0_.3) | copy-start | bytes 388
  21.9 23.4 %copy-start.6 = (s32[4,8]{1,0:T(4,128)S(1)}, s32[4,8]{1,0:T(4,128)}, u32[]{:S(2)}) copy-start(s32[4,8]{1,0:T(4,128)} %refs_2_.3) | copy-start | bytes 388
  21.9 13.8 %collective-permute-start.13 = (s16[128,1024]{1,0:T(8,128)(2,1)S(1)}, s16[128,1024]{1,0:T(8,128)(2,1)S(1)}, u32[]{:S(2)}, u32[]{:S(2)}) collective-permute-start(s16[128,1024]{1,0:T(8,128)(2,1)S(1)} %contract_far_group.1.refs_1_), channel_id=1, source_target_pairs={{0,24},{1,25},{2,26},{3,27},{4,28},{5,29},{6,30},{7,31},{8,16},{9,... | collective-permute-start | bytes 786440 | tf_op jit(solution)/shard_map/ppermute | solution.py:371
  24.4 8.6 %collective-permute-start.5 = (s16[64,1024]{1,0:T(8,128)(2,1)S(1)}, s16[64,1024]{1,0:T(8,128)(2,1)S(1)}, u32[]{:S(2)}, u32[]{:S(2)}) collective-permute-start(s16[64,1024]{1,0:T(8,128)(2,1)S(1)} %get-tuple-element.39), channel_id=1, source_target_pairs={{0,2},{1,3},{2,0},{3,1},{4,6},{5,7},{6,4},{7,5},{8,10},{9,11},{10,... | collective-permute-start | bytes 393224 | tf_op jit(solution)/shard_map/ppermute | solution.py:371
  31.5 5.9 %collective-permute-start.10 = (s16[64,1024]{1,0:T(8,128)(2,1)S(1)}, s16[64,1024]{1,0:T(8,128)(2,1)S(1)}, u32[]{:S(2)}, u32[]{:S(2)}) collective-permute-start(s16[64,1024]{1,0:T(8,128)(2,1)S(1)} %get-tuple-element.45), channel_id=1, source_target_pairs={{0,8},{1,17},{2,10},{3,19},{4,12},{5,21},{6,14},{7,23},{8,0},{9,25... | collective-permute-start | bytes 393224 | tf_op jit(solution)/shard_map/ppermute | solution.py:371
  32.6 6.4 %collective-permute-start.12 = (s16[64,1024]{1,0:T(8,128)(2,1)S(1)}, s16[64,1024]{1,0:T(8,128)(2,1)S(1)}, u32[]{:S(2)}, u32[]{:S(2)}) collective-permute-start(s16[64,1024]{1,0:T(8,128)(2,1)S(1)} %get-tuple-element.47), channel_id=1, source_target_pairs={{0,16},{1,9},{2,18},{3,11},{4,20},{5,13},{6,22},{7,15},{8,24},{9,1... | collective-permute-start | bytes 393224 | tf_op jit(solution)/shard_map/ppermute | solution.py:371
  33.1 7.5 %collective-permute-start.7 = (s16[64,1024]{1,0:T(8,128)(2,1)S(1)}, s16[64,1024]{1,0:T(8,128)(2,1)S(1)}, u32[]{:S(2)}, u32[]{:S(2)}) collective-permute-start(s16[64,1024]{1,0:T(8,128)(2,1)S(1)} %get-tuple-element.42), channel_id=1, source_target_pairs={{0,8},{1,17},{2,10},{3,19},{4,12},{5,21},{6,14},{7,23},{8,0},{9,25... | collective-permute-start | bytes 393224 | tf_op jit(solution)/shard_map/ppermute | solution.py:371
  34.1 6.4 %collective-permute-start.11 = (s16[64,1024]{1,0:T(8,128)(2,1)S(1)}, s16[64,1024]{1,0:T(8,128)(2,1)S(1)}, u32[]{:S(2)}, u32[]{:S(2)}) collective-permute-start(s16[64,1024]{1,0:T(8,128)(2,1)S(1)} %get-tuple-element.46), channel_id=1, source_target_pairs={{0,16},{1,9},{2,18},{3,11},{4,20},{5,13},{6,22},{7,15},{8,24},{9,1... | collective-permute-start | bytes 393224 | tf_op jit(solution)/shard_map/ppermute | solution.py:371
  35.8 4.8 %collective-permute-start.14 = (s16[32,1024]{1,0:T(8,128)(2,1)S(1)}, s16[32,1024]{1,0:T(8,128)(2,1)S(1)}, u32[]{:S(2)}, u32[]{:S(2)}) collective-permute-start(s16[32,1024]{1,0:T(8,128)(2,1)S(1)} %get-tuple-element.49), channel_id=1, source_target_pairs={{0,2},{1,3},{2,0},{3,1},{4,6},{5,7},{6,4},{7,5},{8,10},{9,11},{10,... | collective-permute-start | bytes 196616 | tf_op jit(solution)/shard_map/ppermute | solution.py:371
  37.4 5.9 %collective-permute-start.15 = (s16[32,1024]{1,0:T(8,128)(2,1)S(1)}, s16[32,1024]{1,0:T(8,128)(2,1)S(1)}, u32[]{:S(2)}, u32[]{:S(2)}) collective-permute-start(s16[32,1024]{1,0:T(8,128)(2,1)S(1)} %get-tuple-element.50), channel_id=1, source_target_pairs={{0,4},{1,5},{2,6},{3,7},{4,0},{5,1},{6,2},{7,3},{8,12},{9,13},{10,... | collective-permute-start | bytes 196616 | tf_op jit(solution)/shard_map/ppermute | solution.py:371
  39.0 6.1 %collective-permute-start.16 = (s16[32,1024]{1,0:T(8,128)(2,1)S(1)}, s16[32,1024]{1,0:T(8,128)(2,1)S(1)}, u32[]{:S(2)}, u32[]{:S(2)}) collective-permute-start(s16[32,1024]{1,0:T(8,128)(2,1)S(1)} %get-tuple-element.51), channel_id=1, source_target_pairs={{0,6},{1,7},{2,4},{3,5},{4,2},{5,3},{6,0},{7,1},{8,14},{9,15},{10,... | collective-permute-start | bytes 196616 | tf_op jit(solution)/shard_map/ppermute | solution.py:371
  45.2 2.0 %collective-permute-start.17 = (s16[256,1024]{1,0:T(8,128)(2,1)S(1)}, s16[256,1024]{1,0:T(8,128)(2,1)S(1)}, u32[]{:S(2)}, u32[]{:S(2)}) collective-permute-start(s16[256,1024]{1,0:T(8,128)(2,1)S(1)} %rows_of_other_core.1), channel_id=1, source_target_pairs={{0,1},{1,0},{2,3},{3,2},{4,5},{5,4},{6,7},{7,6},{8,9},{9,8},{10,11... | collective-permute-start | bytes 1572872 | tf_op jit(solution)/shard_map/ppermute | solution.py:371

commit v19 on v17

--- a/solution.py
+++ b/solution.py
@@ -61,7 +61,7 @@
 
 
 def chip_steps(chips, core):
-    return [0] + [slot + core * (chips - 2 * slot) for slot in range(1, chips)]
+    return [0] + [slot + (1 - core) * (chips - 2 * slot) for slot in range(1, chips)]
 
 
 def start_all(copies):

time: 46.5 us -> 46.7 us (level)
  waiting for transfers between devices: 6.84 us -> 9.92 us
  starting transfers between devices: 26.8 us -> 24 us
    ppermute x16, waiting for transfers between devices: 6.84 us -> 9.92 us  [swap(): return lax.ppermute(value, ('blk', 'grp'), pairs)]
    ppermute x16, starting transfers between devices: 26.8 us -> 24 us  [swap(): return lax.ppermute(value, ('blk', 'grp'), pairs)]
  transfers between devices with their start and end apart: 16 -> 16, of which waited for: 4 -> 5; matrix products, arithmetic and copies ran while one was open for 0% -> 0% of each run, Pallas kernels for 12% -> 12%
where the time goes in v19:
time: 46.7 us; the launch traced here: 46.6 us
  starting transfers between devices  24 us (51%)
  waiting for transfers between devices  9.92 us (21%)
  Pallas kernels  8.93 us (19%)
  local copies, waits for them, and re-layouts  3.52 us (8%)
    ppermute x16, starting transfers between devices, swap(): return lax.ppermute(value, ('blk', 'grp'), pairs)  24 us
    ppermute x16, waiting for transfers between devices, swap(): return lax.ppermute(value, ('blk', 'grp'), pairs)  9.92 us
    unnamed x14, local copies, waits for them, and re-layouts  3.52 us
    pallas_call x1, Pallas kernels, add_there(): pl.pallas_call(lambda *refs: add_there_kernel(count, *refs), out_shape=wh...  2.46 us
    pallas_call x1, Pallas kernels, write_residual(): pl.pallas_call(lambda *refs: write_kernel(parts, *refs), out_shape=[jax.S...  1.74 us
    pallas_call x1, Pallas kernels, add_here(): pl.pallas_call(lambda *refs: add_here_kernel(pieces, *refs), out_shape=ja...  1.2 us
    pallas_call x1, Pallas kernels, contract_near(): pl.pallas_call(lambda *refs: near_kernel(len(groups), *refs), out_shape=[...  1.14 us
  transfers between devices with their start and end apart: 16, of which 5 were waited for; matrix products, arithmetic and copies ran while one was open for 0% of the time, Pallas kernels for 12%

profile of v19, /device:TPU:0, one launch (start us, length us, event | category | flops | bytes accessed | tf_op | source)
XLA Modules:
  0.0 46.6 jit_solution(646900109326880837)
XLA Ops:
  0.0 0.0 copy-start.2
  0.0 1.2 %copy-done.2 = bf16[4,128,1024]{2,1,0:T(8,128)(2,1)S(1)} copy-done((bf16[4,128,1024]{2,1,0:T(8,128)(2,1)S(1)}, bf16[4,128,1024]{2,1,0:T(8,128)(2,1)}, u32[]{:S(2)}) %copy-start.2) | copy-done | bytes 1048600
  1.2 0.0 copy-start.3
  1.2 0.7 %copy-done.3 = s32[4,8]{1,0:T(4,128)S(1)} copy-done((s32[4,8]{1,0:T(4,128)S(1)}, s32[4,8]{1,0:T(4,128)}, u32[]{:S(2)}) %copy-start.3) | copy-done | bytes 152
  1.9 0.7 %pick_cd_blocks.1 = (bf16[128,1024]{1,0:T(8,128)(2,1)S(1)}, bf16[128,1024]{1,0:T(8,128)(2,1)S(1)}, bf16[128,1024]{1,0:T(8,128)(2,1)S(1)}, bf16[128,1024]{1,0:T(8,128)(2,1)S(1)}) custom-call(s32[4,8]{1,0:T(4,128)S(1)} %copy-done.3, bf16[4,128,1024]{2,1,0:T(8,128)(2,1)S(1)} %copy-done.2), custom_call_target="tpu_custom_call" | custom-call | tf_op jit(solution)/shard_map/pick_cd_blocks/pallas_call | solution.py:91
  2.6 3.0 %collective-permute-start.3 = (bf16[128,1024]{1,0:T(8,128)(2,1)S(1)}, bf16[128,1024]{1,0:T(8,128)(2,1)S(1)}, u32[]{:S(2)}, u32[]{:S(2)}) collective-permute-start(bf16[128,1024]{1,0:T(8,128)(2,1)S(1)} %get-tuple-element.33), channel_id=1, source_target_pairs={{0,8},{1,17},{2,10},{3,19},{4,12},{5,21},{6,14},{7,23},{8,0},{9,25... | collective-permute-start | bytes 786440 | tf_op jit(solution)/shard_map/ppermute | solution.py:373
  5.6 1.5 %collective-permute-start.4 = (bf16[128,1024]{1,0:T(8,128)(2,1)S(1)}, bf16[128,1024]{1,0:T(8,128)(2,1)S(1)}, u32[]{:S(2)}, u32[]{:S(2)}) collective-permute-start(bf16[128,1024]{1,0:T(8,128)(2,1)S(1)} %get-tuple-element.34), channel_id=1, source_target_pairs={{0,16},{1,9},{2,18},{3,11},{4,20},{5,13},{6,22},{7,15},{8,24},{9,1... | collective-permute-start | bytes 786440 | tf_op jit(solution)/shard_map/ppermute | solution.py:373
  7.1 0.0 copy-start.1
  7.1 1.6 %copy-done.1 = bf16[1,1024,1024]{2,1,0:T(8,128)(2,1)S(1)} copy-done((bf16[1,1024,1024]{2,1,0:T(8,128)(2,1)S(1)}, bf16[1,1024,1024]{2,1,0:T(8,128)(2,1)}, u32[]{:S(2)}) %copy-start.1) | copy-done | bytes 2097176
  8.7 0.9 %contract_own_group.1 = (s16[32,1024]{1,0:T(8,128)(2,1)S(1)}, s16[32,1024]{1,0:T(8,128)(2,1)S(1)}, s16[32,1024]{1,0:T(8,128)(2,1)S(1)}, s16[32,1024]{1,0:T(8,128...) custom-call(bf16[128,1024]{1,0:T(8,128)(2,1)S(1)} %get-tuple-element.27.rows, ...), custom_call_target="tpu_custom_call" | custom-call | flops 268435456 | bytes 2097152 | tf_op jit(solution)/shard_map/contract_own_group/pallas_call | solution.py:128
  9.6 0.0 copy-start
  9.6 0.1 collective-permute-start.8
  9.7 4.1 %collective-permute-start = (s16[32,1024]{1,0:T(8,128)(2,1)S(1)}, s16[32,1024]{1,0:T(8,128)(2,1)S(1)}, u32[]{:S(2)}, u32[]{:S(2)}) collective-permute-start(s16[32,1024]{1,0:T(8,128)(2,1)S(1)} %get-tuple-element.30), channel_id=1, source_target_pairs={{0,6},{1,3},{2,4},{3,1},{4,2},{5,7},{6,0},{7,5},{8,14},{9,11},{10,... | collective-permute-start | bytes 196616 | tf_op jit(solution)/shard_map/ppermute | solution.py:373
  13.8 0.0 collective-permute-start.1
  13.8 0.0 collective-permute-done.3.refs_0_
  13.8 1.0 %collective-permute-start.2 = (s16[32,1024]{1,0:T(8,128)(2,1)S(1)}, s16[32,1024]{1,0:T(8,128)(2,1)S(1)}, u32[]{:S(2)}, u32[]{:S(2)}) collective-permute-start(s16[32,1024]{1,0:T(8,128)(2,1)S(1)} %get-tuple-element.32), channel_id=1, source_target_pairs={{0,2},{1,7},{2,0},{3,5},{4,6},{5,3},{6,4},{7,1},{8,10},{9,15},{10,... | collective-permute-start | bytes 196616 | tf_op jit(solution)/shard_map/ppermute | solution.py:373
  14.8 0.0 collective-permute-done.4.refs_1_
  14.8 1.1 %contract_near_groups.1 = (s16[64,1024]{1,0:T(8,128)(2,1)S(1)}, s16[64,1024]{1,0:T(8,128)(2,1)S(1)}, s16[64,1024]{1,0:T(8,128)(2,1)S(1)}, s16[64,1024]{1,0:T(8,128)(2,1)S(1)}) custom-call(bf16[128,1024]{1,0:T(8,128)(2,1)S(1)} %collective-permute-done.3.refs_0_, bf16[128,1024]{1,0:T(8,128)(2,1)S(1)} %collective-permute-done.4.refs_1_, ...), custom_call_target="tpu_custom_call" | custom-call | flops 536870912 | bytes 2097152 | tf_op jit(solution)/shard_map/contract_near_groups/pallas_call | solution.py:151
  15.9 3.4 %collective-permute-start.5 = (s16[64,1024]{1,0:T(8,128)(2,1)S(1)}, s16[64,1024]{1,0:T(8,128)(2,1)S(1)}, u32[]{:S(2)}, u32[]{:S(2)}) collective-permute-start(s16[64,1024]{1,0:T(8,128)(2,1)S(1)} %get-tuple-element.37), channel_id=1, source_target_pairs={{0,6},{1,3},{2,4},{3,1},{4,2},{5,7},{6,0},{7,5},{8,14},{9,11},{10,... | collective-permute-start | bytes 393224 | tf_op jit(solution)/shard_map/ppermute | solution.py:373
  19.4 0.0 collective-permute-done.refs_2_.refs_1_.refs_4_
  19.4 1.1 %collective-permute-start.6 = (s16[64,1024]{1,0:T(8,128)(2,1)S(1)}, s16[64,1024]{1,0:T(8,128)(2,1)S(1)}, u32[]{:S(2)}, u32[]{:S(2)}) collective-permute-start(s16[64,1024]{1,0:T(8,128)(2,1)S(1)} %get-tuple-element.38), channel_id=1, source_target_pairs={{0,4},{1,5},{2,6},{3,7},{4,0},{5,1},{6,2},{7,3},{8,12},{9,13},{10,... | collective-permute-start | bytes 393224 | tf_op jit(solution)/shard_map/ppermute | solution.py:373
  20.4 0.0 collective-permute-done.1.refs_3_.refs_2_.refs_5_
  20.4 0.0 collective-permute-start.7
  20.5 0.6 %collective-permute-done.2.refs_4_.refs_3_.refs_6_ = s16[32,1024]{1,0:T(8,128)(2,1)S(1)} collective-permute-done((s16[32,1024]{1,0:T(8,128)(2,1)S(1)}, s16[32,1024]{1,0:T(8,128)(2,1)S(1)}, u32[]{:S(2)}, u32[]{:S(2)}) %collective-permute-start.2) | collective-permute-done | bytes 65568 | tf_op jit(solution)/shard_map/ppermute | solution.py:373
  21.1 0.0 collective-permute-done.8.refs_0_
  21.1 0.7 %contract_far_group.1.refs_1_ = s16[128,1024]{1,0:T(8,128)(2,1)S(1)} custom-call(bf16[128,1024]{1,0:T(8,128)(2,1)S(1)} %collective-permute-done.8.refs_0_, bf16[1024,1024]{1,0:T(8,128)(2,1)S(1)} %get-tuple-element.35.refs_2_.refs_1_, s16[32,1024]{1,0:T(8,128)(2,1)S(1)} %collective-permute-done.refs_2_.refs_1_.refs_4_, ...), custom_call_target="tpu_custom_call" | custom-call | flops 268435456 | bytes 2097152 | tf_op jit(solution)/shard_map/contract_far_group/pallas_call | solution.py:173
  21.8 0.0 copy-start.4
  21.8 0.0 copy-start.5
  21.8 0.0 copy-start.6
  21.8 2.2 %collective-permute-start.11 = (s16[128,1024]{1,0:T(8,128)(2,1)S(1)}, s16[128,1024]{1,0:T(8,128)(2,1)S(1)}, u32[]{:S(2)}, u32[]{:S(2)}) collective-permute-start(s16[128,1024]{1,0:T(8,128)(2,1)S(1)} %contract_far_group.1.refs_1_), channel_id=1, source_target_pairs={{0,24},{1,25},{2,26},{3,27},{4,28},{5,29},{6,30},{7,31},{8,16},{9,... | collective-permute-start | bytes 786440 | tf_op jit(solution)/shard_map/ppermute | solution.py:373
  24.0 0.0 copy-done
  24.0 1.7 %write_residual.1 = (f32[50,16,1024]{2,1,0:T(8,128)}, s32[8,128]{1,0:T(8,128)S(1)}) custom-call(f32[50,16,1024]{2,1,0:T(8,128)S(1)} %bitcast.3, s16[128,1024]{1,0:T(8,128)(2,1)S(1)} %contract_far_group.1.refs_1_), custom_call_target="tpu_custom_call" | custom-call | tf_op jit(solution)/shard_map/write_residual/pallas_call | solution.py:244
  25.8 0.0 collective-permute-done.5.refs_1_
  25.8 5.0 %collective-permute-done.6.refs_2_ = s16[64,1024]{1,0:T(8,128)(2,1)S(1)} collective-permute-done((s16[64,1024]{1,0:T(8,128)(2,1)S(1)}, s16[64,1024]{1,0:T(8,128)(2,1)S(1)}, u32[]{:S(2)}, u32[]{:S(2)}) %collective-permute-start.6) | collective-permute-done | bytes 131104 | tf_op jit(solution)/shard_map/ppermute | solution.py:373
  30.8 0.0 collective-permute-done.7.refs_3_
  30.9 1.6 %collective-permute-start.9 = (s16[128,1024]{1,0:T(8,128)(2,1)S(1)}, s16[128,1024]{1,0:T(8,128)(2,1)S(1)}, u32[]{:S(2)}, u32[]{:S(2)}) collective-permute-start(s16[128,1024]{1,0:T(8,128)(2,1)S(1)} %get-tuple-element.42), channel_id=1, source_target_pairs={{0,8},{1,17},{2,10},{3,19},{4,12},{5,21},{6,14},{7,23},{8,0},{9,25... | collective-permute-start | bytes 786440 | tf_op jit(solution)/shard_map/ppermute | solution.py:373
  32.5 1.5 %collective-permute-start.10 = (s16[128,1024]{1,0:T(8,128)(2,1)S(1)}, s16[128,1024]{1,0:T(8,128)(2,1)S(1)}, u32[]{:S(2)}, u32[]{:S(2)}) collective-permute-start(s16[128,1024]{1,0:T(8,128)(2,1)S(1)} %get-tuple-element.43), channel_id=1, source_target_pairs={{0,16},{1,9},{2,18},{3,11},{4,20},{5,13},{6,22},{7,15},{8,24},{9,1... | collective-permute-start | bytes 786440 | tf_op jit(solution)/shard_map/ppermute | solution.py:373
  34.0 0.0 collective-permute-done.11.refs_0_
  34.0 2.5 %collective-permute-start.12 = (s16[32,1024]{1,0:T(8,128)(2,1)S(1)}, s16[32,1024]{1,0:T(8,128)(2,1)S(1)}, u32[]{:S(2)}, u32[]{:S(2)}) collective-permute-start(s16[32,1024]{1,0:T(8,128)(2,1)S(1)} %get-tuple-element.45), channel_id=1, source_target_pairs={{0,6},{1,3},{2,4},{3,1},{4,2},{5,7},{6,0},{7,5},{8,14},{9,11},{10,... | collective-permute-start | bytes 196616 | tf_op jit(solution)/shard_map/ppermute | solution.py:373
  36.5 0.0 collective-permute-start.13
  36.5 2.0 %collective-permute-start.14 = (s16[32,1024]{1,0:T(8,128)(2,1)S(1)}, s16[32,1024]{1,0:T(8,128)(2,1)S(1)}, u32[]{:S(2)}, u32[]{:S(2)}) collective-permute-start(s16[32,1024]{1,0:T(8,128)(2,1)S(1)} %get-tuple-element.47), channel_id=1, source_target_pairs={{0,2},{1,7},{2,0},{3,5},{4,6},{5,3},{6,4},{7,1},{8,10},{9,15},{10,... | collective-permute-start | bytes 196616 | tf_op jit(solution)/shard_map/ppermute | solution.py:373
  38.5 1.7 %collective-permute-done.12.refs_7_.refs_10_ = s16[32,1024]{1,0:T(8,128)(2,1)S(1)} collective-permute-done((s16[32,1024]{1,0:T(8,128)(2,1)S(1)}, s16[32,1024]{1,0:T(8,128)(2,1)S(1)}, u32[]{:S(2)}, u32[]{:S(2)}) %collective-permute-start.12) | collective-permute-done | bytes 65568 | tf_op jit(solution)/shard_map/ppermute | solution.py:373
  40.2 1.9 %collective-permute-done.13.refs_8_.refs_11_ = s16[32,1024]{1,0:T(8,128)(2,1)S(1)} collective-permute-done((s16[32,1024]{1,0:T(8,128)(2,1)S(1)}, s16[32,1024]{1,0:T(8,128)(2,1)S(1)}, u32[]{:S(2)}, u32[]{:S(2)}) %collective-permute-start.13) | collective-permute-done | bytes 65568 | tf_op jit(solution)/shard_map/ppermute | solution.py:373
  42.0 0.0 collective-permute-done.14.refs_9_.refs_12_
  42.0 0.0 collective-permute-done.9.refs_4_.refs_7_
  42.0 0.0 collective-permute-done.10.refs_5_.refs_8_
  42.1 0.1 rows_of_other_core.1
  42.1 0.1 collective-permute-start.15
  42.2 0.0 copy-done.4
  42.2 0.0 copy-done.5
  42.2 0.0 copy-done.6
  42.2 1.2 %add_contributions_here.1.refs_4_ = f32[50,16,1024]{2,1,0:T(8,128)S(1)} custom-call(s32[4,8]{1,0:T(4,128)S(1)} %copy-done.5, s32[4,8]{1,0:T(4,128)S(1)} %copy-done.4, s32[4,8]{1,0:T(4,128)S(1)} %copy-done.6, s16[32,1024]{1,0:T(8,128)(2,1)S(1)} %get-tuple-element.29.refs_0_.refs_3_, s16[32,1024]{1,0:T(8,128)(2,1)S(1)} %collective-permute-done.refs_2_.refs_1_.refs_4_, ...), custom_call_target="tpu_custom_call" | custom-call | tf_op jit(solution)/shard_map/add_contributions_here/pallas_call | solution.py:297
  43.4 0.7 %collective-permute-done.15.refs_3_ = s16[256,1024]{1,0:T(8,128)(2,1)S(1)} collective-permute-done((s16[256,1024]{1,0:T(8,128)(2,1)S(1)}, s16[256,1024]{1,0:T(8,128)(2,1)S(1)}, u32[]{:S(2)}, u32[]{:S(2)}) %collective-permute-start.15) | collective-permute-done | bytes 524320 | tf_op jit(solution)/shard_map/ppermute | solution.py:373
  44.1 2.5 %add_contributions_there.1 = f32[50,16,1024]{2,1,0:T(8,128)} custom-call(s32[4,8]{1,0:T(4,128)S(1)} %copy-done.5, s32[4,8]{1,0:T(4,128)S(1)} %copy-done.4, s32[4,8]{1,0:T(4,128)S(1)} %copy-done.6, s16[256,1024]{1,0:T(8,128)(2,1)S(1)} %collective-permute-done.15.refs_3_, ...), custom_call_target="tpu_custom_call", output_to_operand_aliasing={{}: (5, {})} | custom-call | tf_op jit(solution)/shard_map/add_contributions_there/pallas_call | solution.py:344
  (2 shorter events, 0.1 us)
Async XLA Ops:
  0.0 1.2 %copy-start.2 = (bf16[4,128,1024]{2,1,0:T(8,128)(2,1)S(1)}, bf16[4,128,1024]{2,1,0:T(8,128)(2,1)}, u32[]{:S(2)}) copy-start(bf16[4,128,1024]{2,1,0:T(8,128)(2,1)} %amplitudes.1) | copy-start | bytes 3145732
  1.2 0.7 %copy-start.3 = (s32[4,8]{1,0:T(4,128)S(1)}, s32[4,8]{1,0:T(4,128)}, u32[]{:S(2)}) copy-start(s32[4,8]{1,0:T(4,128)} %refs_1_.3) | copy-start | bytes 388
  2.6 11.2 %collective-permute-start.3 = (bf16[128,1024]{1,0:T(8,128)(2,1)S(1)}, bf16[128,1024]{1,0:T(8,128)(2,1)S(1)}, u32[]{:S(2)}, u32[]{:S(2)}) collective-permute-start(bf16[128,1024]{1,0:T(8,128)(2,1)S(1)} %get-tuple-element.33), channel_id=1, source_target_pairs={{0,8},{1,17},{2,10},{3,19},{4,12},{5,21},{6,14},{7,23},{8,0},{9,25... | collective-permute-start | bytes 786440 | tf_op jit(solution)/shard_map/ppermute | solution.py:373
  5.6 9.2 %collective-permute-start.4 = (bf16[128,1024]{1,0:T(8,128)(2,1)S(1)}, bf16[128,1024]{1,0:T(8,128)(2,1)S(1)}, u32[]{:S(2)}, u32[]{:S(2)}) collective-permute-start(bf16[128,1024]{1,0:T(8,128)(2,1)S(1)} %get-tuple-element.34), channel_id=1, source_target_pairs={{0,16},{1,9},{2,18},{3,11},{4,20},{5,13},{6,22},{7,15},{8,24},{9,1... | collective-permute-start | bytes 786440 | tf_op jit(solution)/shard_map/ppermute | solution.py:373
  7.1 1.6 %copy-start.1 = (bf16[1,1024,1024]{2,1,0:T(8,128)(2,1)S(1)}, bf16[1,1024,1024]{2,1,0:T(8,128)(2,1)}, u32[]{:S(2)}) copy-start(bf16[1,1024,1024]{2,1,0:T(8,128)(2,1)} %param.8) | copy-start | bytes 6291460
  9.6 14.4 %copy-start = (f32[16,50,1024]{2,0,1:T(8,128)S(1)}, f32[16,50,1024]{2,0,1:T(8,128)}, u32[]{:S(2)}) copy-start(f32[16,50,1024]{2,0,1:T(8,128)} %param.11) | copy-start | bytes 9830404
  9.6 11.5 %collective-permute-start.8 = (bf16[128,1024]{1,0:T(8,128)(2,1)S(1)}, bf16[128,1024]{1,0:T(8,128)(2,1)S(1)}, u32[]{:S(2)}, u32[]{:S(2)}) collective-permute-start(bf16[128,1024]{1,0:T(8,128)(2,1)S(1)} %get-tuple-element.40), channel_id=1, source_target_pairs={{0,24},{1,25},{2,26},{3,27},{4,28},{5,29},{6,30},{7,31},{8,16},{9,... | collective-permute-start | bytes 786440 | tf_op jit(solution)/shard_map/ppermute | solution.py:373
  9.7 9.7 %collective-permute-start = (s16[32,1024]{1,0:T(8,128)(2,1)S(1)}, s16[32,1024]{1,0:T(8,128)(2,1)S(1)}, u32[]{:S(2)}, u32[]{:S(2)}) collective-permute-start(s16[32,1024]{1,0:T(8,128)(2,1)S(1)} %get-tuple-element.30), channel_id=1, source_target_pairs={{0,6},{1,3},{2,4},{3,1},{4,2},{5,7},{6,0},{7,5},{8,14},{9,11},{10,... | collective-permute-start | bytes 196616 | tf_op jit(solution)/shard_map/ppermute | solution.py:373
  13.8 6.7 %collective-permute-start.1 = (s16[32,1024]{1,0:T(8,128)(2,1)S(1)}, s16[32,1024]{1,0:T(8,128)(2,1)S(1)}, u32[]{:S(2)}, u32[]{:S(2)}) collective-permute-start(s16[32,1024]{1,0:T(8,128)(2,1)S(1)} %get-tuple-element.31), channel_id=1, source_target_pairs={{0,4},{1,5},{2,6},{3,7},{4,0},{5,1},{6,2},{7,3},{8,12},{9,13},{10,... | collective-permute-start | bytes 196616 | tf_op jit(solution)/shard_map/ppermute | solution.py:373
  13.8 7.3 %collective-permute-start.2 = (s16[32,1024]{1,0:T(8,128)(2,1)S(1)}, s16[32,1024]{1,0:T(8,128)(2,1)S(1)}, u32[]{:S(2)}, u32[]{:S(2)}) collective-permute-start(s16[32,1024]{1,0:T(8,128)(2,1)S(1)} %get-tuple-element.32), channel_id=1, source_target_pairs={{0,2},{1,7},{2,0},{3,5},{4,6},{5,3},{6,4},{7,1},{8,10},{9,15},{10,... | collective-permute-start | bytes 196616 | tf_op jit(solution)/shard_map/ppermute | solution.py:373
  15.9 9.9 %collective-permute-start.5 = (s16[64,1024]{1,0:T(8,128)(2,1)S(1)}, s16[64,1024]{1,0:T(8,128)(2,1)S(1)}, u32[]{:S(2)}, u32[]{:S(2)}) collective-permute-start(s16[64,1024]{1,0:T(8,128)(2,1)S(1)} %get-tuple-element.37), channel_id=1, source_target_pairs={{0,6},{1,3},{2,4},{3,1},{4,2},{5,7},{6,0},{7,5},{8,14},{9,11},{10,... | collective-permute-start | bytes 393224 | tf_op jit(solution)/shard_map/ppermute | solution.py:373
  19.4 11.4 %collective-permute-start.6 = (s16[64,1024]{1,0:T(8,128)(2,1)S(1)}, s16[64,1024]{1,0:T(8,128)(2,1)S(1)}, u32[]{:S(2)}, u32[]{:S(2)}) collective-permute-start(s16[64,1024]{1,0:T(8,128)(2,1)S(1)} %get-tuple-element.38), channel_id=1, source_target_pairs={{0,4},{1,5},{2,6},{3,7},{4,0},{5,1},{6,2},{7,3},{8,12},{9,13},{10,... | collective-permute-start | bytes 393224 | tf_op jit(solution)/shard_map/ppermute | solution.py:373
  20.4 10.4 %collective-permute-start.7 = (s16[64,1024]{1,0:T(8,128)(2,1)S(1)}, s16[64,1024]{1,0:T(8,128)(2,1)S(1)}, u32[]{:S(2)}, u32[]{:S(2)}) collective-permute-start(s16[64,1024]{1,0:T(8,128)(2,1)S(1)} %get-tuple-element.39), channel_id=1, source_target_pairs={{0,2},{1,7},{2,0},{3,5},{4,6},{5,3},{6,4},{7,1},{8,10},{9,15},{10,... | collective-permute-start | bytes 393224 | tf_op jit(solution)/shard_map/ppermute | solution.py:373
  21.8 20.4 %copy-start.4 = (s32[4,8]{1,0:T(4,128)S(1)}, s32[4,8]{1,0:T(4,128)}, u32[]{:S(2)}) copy-start(s32[4,8]{1,0:T(4,128)} %refs_1_.3) | copy-start | bytes 388
  21.8 20.4 %copy-start.5 = (s32[4,8]{1,0:T(4,128)S(1)}, s32[4,8]{1,0:T(4,128)}, u32[]{:S(2)}) copy-start(s32[4,8]{1,0:T(4,128)} %refs_0_.3) | copy-start | bytes 388
  21.8 20.4 %copy-start.6 = (s32[4,8]{1,0:T(4,128)S(1)}, s32[4,8]{1,0:T(4,128)}, u32[]{:S(2)}) copy-start(s32[4,8]{1,0:T(4,128)} %refs_2_.3) | copy-start | bytes 388
  21.8 12.1 %collective-permute-start.11 = (s16[128,1024]{1,0:T(8,128)(2,1)S(1)}, s16[128,1024]{1,0:T(8,128)(2,1)S(1)}, u32[]{:S(2)}, u32[]{:S(2)}) collective-permute-start(s16[128,1024]{1,0:T(8,128)(2,1)S(1)} %contract_far_group.1.refs_1_), channel_id=1, source_target_pairs={{0,24},{1,25},{2,26},{3,27},{4,28},{5,29},{6,30},{7,31},{8,16},{9,... | collective-permute-start | bytes 786440 | tf_op jit(solution)/shard_map/ppermute | solution.py:373
  30.9 11.2 %collective-permute-start.9 = (s16[128,1024]{1,0:T(8,128)(2,1)S(1)}, s16[128,1024]{1,0:T(8,128)(2,1)S(1)}, u32[]{:S(2)}, u32[]{:S(2)}) collective-permute-start(s16[128,1024]{1,0:T(8,128)(2,1)S(1)} %get-tuple-element.42), channel_id=1, source_target_pairs={{0,8},{1,17},{2,10},{3,19},{4,12},{5,21},{6,14},{7,23},{8,0},{9,25... | collective-permute-start | bytes 786440 | tf_op jit(solution)/shard_map/ppermute | solution.py:373
  32.5 9.6 %collective-permute-start.10 = (s16[128,1024]{1,0:T(8,128)(2,1)S(1)}, s16[128,1024]{1,0:T(8,128)(2,1)S(1)}, u32[]{:S(2)}, u32[]{:S(2)}) collective-permute-start(s16[128,1024]{1,0:T(8,128)(2,1)S(1)} %get-tuple-element.43), channel_id=1, source_target_pairs={{0,16},{1,9},{2,18},{3,11},{4,20},{5,13},{6,22},{7,15},{8,24},{9,1... | collective-permute-start | bytes 786440 | tf_op jit(solution)/shard_map/ppermute | solution.py:373
  34.0 6.2 %collective-permute-start.12 = (s16[32,1024]{1,0:T(8,128)(2,1)S(1)}, s16[32,1024]{1,0:T(8,128)(2,1)S(1)}, u32[]{:S(2)}, u32[]{:S(2)}) collective-permute-start(s16[32,1024]{1,0:T(8,128)(2,1)S(1)} %get-tuple-element.45), channel_id=1, source_target_pairs={{0,6},{1,3},{2,4},{3,1},{4,2},{5,7},{6,0},{7,5},{8,14},{9,11},{10,... | collective-permute-start | bytes 196616 | tf_op jit(solution)/shard_map/ppermute | solution.py:373
  36.5 5.5 %collective-permute-start.13 = (s16[32,1024]{1,0:T(8,128)(2,1)S(1)}, s16[32,1024]{1,0:T(8,128)(2,1)S(1)}, u32[]{:S(2)}, u32[]{:S(2)}) collective-permute-start(s16[32,1024]{1,0:T(8,128)(2,1)S(1)} %get-tuple-element.46), channel_id=1, source_target_pairs={{0,4},{1,5},{2,6},{3,7},{4,0},{5,1},{6,2},{7,3},{8,12},{9,13},{10,... | collective-permute-start | bytes 196616 | tf_op jit(solution)/shard_map/ppermute | solution.py:373
  36.5 5.5 %collective-permute-start.14 = (s16[32,1024]{1,0:T(8,128)(2,1)S(1)}, s16[32,1024]{1,0:T(8,128)(2,1)S(1)}, u32[]{:S(2)}, u32[]{:S(2)}) collective-permute-start(s16[32,1024]{1,0:T(8,128)(2,1)S(1)} %get-tuple-element.47), channel_id=1, source_target_pairs={{0,2},{1,7},{2,0},{3,5},{4,6},{5,3},{6,4},{7,1},{8,10},{9,15},{10,... | collective-permute-start | bytes 196616 | tf_op jit(solution)/shard_map/ppermute | solution.py:373
  42.1 2.0 %collective-permute-start.15 = (s16[256,1024]{1,0:T(8,128)(2,1)S(1)}, s16[256,1024]{1,0:T(8,128)(2,1)S(1)}, u32[]{:S(2)}, u32[]{:S(2)}) collective-permute-start(s16[256,1024]{1,0:T(8,128)(2,1)S(1)} %rows_of_other_core.1), channel_id=1, source_target_pairs={{0,1},{1,0},{2,3},{3,2},{4,5},{5,4},{6,7},{7,6},{8,9},{9,8},{10,11... | collective-permute-start | bytes 1572872 | tf_op jit(solution)/shard_map/ppermute | solution.py:373
